TPU v7x, 128 devices: a whole 4x4x4 slice. The times are simulated.
128 devices in a mesh: lat: 8 (over z_lo, x), lon: 16 (over y, z_hi, core).
Axes of the slice: x: 4, y: 4, z: 4 (z_hi: 2, z_lo: 2; z = z_hi * 2 + z_lo), core: 2. Of those that a mesh axis runs over, the one named last changes fastest.
Arguments:
- grid_state: bfloat16 [96, 256, 1024], P('lat', 'lon'), may hold values from -7 to 7
- observations: bfloat16 [32768, 1024], P(('lat', 'lon')), may hold values from -6 to 6
- obs_tile: int32 [32768, 1], P(('lat', 'lon')), may hold values from 0 to 127; in each aligned block of 256 rows (0 to 255, 256 to 511, ...) at most 4 rows name the same one
- obs_cell: int32 [32768, 1], P(('lat', 'lon')), may hold values from 0 to 191
- cotangent: bfloat16 [96, 256, 1024], P('lat', 'lon'), may hold values from -6 to 6
- norm_gains: float32 [3, 1024], replicated, may hold values from 0.5 to 1.5
- w_cross_query: bfloat16 [1024, 1024], replicated, may hold values from -0.25 to 0.25
- w_cross_pairs: bfloat16 [1024, 2048], replicated, may hold values from -0.25 to 0.25
- w_cross_out: bfloat16 [1024, 1024], replicated, may hold values from -0.1875 to 0.1875
- w_near_proj: bfloat16 [1024, 3072], replicated, may hold values from -0.25 to 0.25
- w_near_out: bfloat16 [1024, 1024], replicated, may hold values from -0.1875 to 0.1875
- w_up: bfloat16 [1024, 2048], replicated, may hold values from -0.1875 to 0.1875
- w_down: bfloat16 [2048, 1024], replicated, may hold values from -0.125 to 0.125
Outputs:
- encoded: bfloat16 [96, 256, 1024], P('lat', 'lon')
- grid_grad: bfloat16 [96, 256, 1024], P('lat', 'lon')
- obs_grad: bfloat16 [32768, 1024], P(('lat', 'lon'))
Inputs may be any that keep to these rules, and one draw needn't show every extreme that they name: `obs_tile`: tile index of the row's observation; among the rows of one device at most 4 name one tile, and every tile is named by some row. `obs_cell`: In-tile cell of the row's observation, row-major within the tile.
All inputs are finite; a program needn't handle non-finite values.
Results may differ from a plain program's by a relative error of at most 0.035.
Values may be sent and summed in bfloat16 or wider, within the bound.
No kernel may reach another device: no remote copies, remote signals or barrier semaphores. Data moves between devices by JAX's collectives and lax.ppermute only.
A program may use at most 192 MiB of HBM per device.

v0:
```python
import jax
import jax.numpy as jnp
from jax import lax
from jax.sharding import PartitionSpec as P

HEADS = 16
RADIUS = 6


EPSILON = 1e-05
SPREAD = 32.0
LOW_SCORE = -1e30


def padded_2(value, sides, width, wrap):
    for axis, dim in sides:
        size, length = (lax.axis_size(axis), value.shape[dim])
        up = [(i, (i + 1) % size) for i in range(size if wrap else size - 1)]
        down = [(j, i) for i, j in up]
        last = lax.slice_in_dim(value, length - width, length, axis=dim)
        initial = lax.slice_in_dim(value, 0, width, axis=dim)
        before = lax.ppermute(last, axis, up)
        after = lax.ppermute(initial, axis, down)
        value = jnp.concatenate([before, value, after], axis=dim)
    return value


def passed_along(value, axis, by):
    size = lax.axis_size(axis)
    return lax.ppermute(value, axis, [(i, (i + by) % size) for i in range(size)])


def passed_along_2(value, axis, by):
    size = lax.axis_size(axis)
    pairs = [(i, i + by) for i in range(size) if 0 <= i + by < size]
    return lax.ppermute(value, axis, pairs)


def layer_norm(values, gain):
    values = values.astype(jnp.float32)
    center = values - jnp.mean(values, -1, keepdims=True)
    second = jnp.mean(center * center, -1, keepdims=True)
    return (center * lax.rsqrt(second + EPSILON) * gain).astype(jnp.bfloat16)


def matmul(left, right):
    return jnp.dot(left, right, preferred_element_type=jnp.float32)


def matmul_right_t(left, right):
    return lax.dot_general(
        left, right, (((1,), (1,)), ((), ())), preferred_element_type=jnp.float32
    )


def matmul_left_t(left, right):
    return lax.dot_general(
        left, right, (((0,), (0,)), ((), ())), preferred_element_type=jnp.float32
    )


def split_heads(values):
    return values.reshape(values.shape[0], HEADS, values.shape[1] // HEADS)


def cross_attend(queries, own_pairs, slot_pairs, slot_rows, slot_cols, slot_valid, tile_wide):
    query_count, model_width = queries.shape
    score_scale = (model_width // HEADS) ** (-0.5)
    query_heads = split_heads(queries)
    key_slots = split_heads(slot_pairs[:, :model_width])
    value_slots = split_heads(slot_pairs[:, model_width:])
    key_own = split_heads(own_pairs[:, :model_width])
    value_own = split_heads(own_pairs[:, model_width:])
    scores = (
        jnp.einsum("qhd,khd->hqk", query_heads, key_slots, preferred_element_type=jnp.float32)
        * score_scale
    )
    cell_ids = lax.iota(jnp.int32, query_count)
    row_gap = (cell_ids // tile_wide)[:, None] - slot_rows[None, :]
    col_gap = (cell_ids % tile_wide)[:, None] - slot_cols[None, :]
    locality = -(row_gap * row_gap + col_gap * col_gap).astype(jnp.float32) / SPREAD
    scores = jnp.where(slot_valid[None, None, :], scores + locality[None], LOW_SCORE)
    own_score = (
        jnp.einsum("qhd,qhd->hq", query_heads, key_own, preferred_element_type=jnp.float32)
        * score_scale
    )
    row_peak = jnp.maximum(jnp.max(scores, -1), own_score)
    weights = jnp.exp(scores - row_peak[:, :, None])
    own_weight = jnp.exp(own_score - row_peak)
    totals = jnp.sum(weights, -1) + own_weight
    weights = (weights / totals[:, :, None]).astype(jnp.bfloat16)
    own_weight = (own_weight / totals).astype(jnp.bfloat16)
    mixed_heads = jnp.einsum(
        "hqk,khd->qhd", weights, value_slots, preferred_element_type=jnp.float32
    )
    mixed_heads = mixed_heads + own_weight.astype(jnp.float32).T[:, :, None] * value_own.astype(
        jnp.float32
    )
    return mixed_heads.reshape(query_count, model_width).astype(jnp.bfloat16)


def near_attend(queries, pairs, lat_start, lat_total):
    rows_here, cols_here, model_width = queries.shape
    wide_rows, wide_cols = (pairs.shape[0], pairs.shape[1])
    query_heads = split_heads(queries.reshape(rows_here * cols_here, model_width))
    flat_pairs = pairs.reshape(wide_rows * wide_cols, 2 * model_width)
    key_cells = split_heads(flat_pairs[:, :model_width])
    value_cells = split_heads(flat_pairs[:, model_width:])
    score_scale = (model_width // HEADS) ** (-0.5)
    scores = (
        jnp.einsum("qhd,khd->hqk", query_heads, key_cells, preferred_element_type=jnp.float32)
        * score_scale
    )
    query_ids = lax.iota(jnp.int32, rows_here * cols_here)
    key_ids = lax.iota(jnp.int32, wide_rows * wide_cols)
    row_gap = (key_ids // wide_cols)[None, :] - RADIUS - (query_ids // cols_here)[:, None]
    col_gap = (key_ids % wide_cols)[None, :] - RADIUS - (query_ids % cols_here)[:, None]
    key_lat = lat_start + key_ids // wide_cols - RADIUS
    inside = (key_lat >= 0) & (key_lat < lat_total)
    allowed = (jnp.abs(row_gap) <= RADIUS) & (jnp.abs(col_gap) <= RADIUS) & inside[None, :]
    scores = jnp.where(allowed[None], scores, LOW_SCORE)
    row_peak = jnp.max(scores, -1, keepdims=True)
    weights = jnp.exp(scores - row_peak)
    weights = (weights / jnp.sum(weights, -1, keepdims=True)).astype(jnp.bfloat16)
    mixed_heads = jnp.einsum(
        "hqk,khd->qhd", weights, value_cells, preferred_element_type=jnp.float32
    )
    return mixed_heads.reshape(rows_here * cols_here, model_width).astype(jnp.bfloat16)


def route_out(payload, cell_codes):
    arrived, arrived_codes = (
        lax.all_to_all(payload, ("lat", "lon"), split_axis=0, concat_axis=0, tiled=True),
        lax.all_to_all(cell_codes, ("lat", "lon"), split_axis=0, concat_axis=0, tiled=True),
    )
    return (arrived, arrived_codes)


def route_back(payload):
    arrived = lax.all_to_all(payload, ("lat", "lon"), split_axis=0, concat_axis=0, tiled=True)
    return arrived


def extend(field):
    tall = padded_2(field, (("lat", 0),), RADIUS, False)
    return padded_2(tall, (("lon", 1),), RADIUS, True)


def fold_rims(grads):
    middle = grads[:, RADIUS:-RADIUS].astype(jnp.float32)
    from_east = passed_along(grads[:, :RADIUS], "lon", -1)
    from_west = passed_along(grads[:, -RADIUS:], "lon", 1)
    middle = middle.at[:, -RADIUS:].add(from_east.astype(jnp.float32))
    middle = middle.at[:, :RADIUS].add(from_west.astype(jnp.float32))
    middle = middle.astype(jnp.bfloat16)
    center = middle[RADIUS:-RADIUS].astype(jnp.float32)
    from_south = passed_along_2(middle[:RADIUS], "lat", -1)
    from_north = passed_along_2(middle[-RADIUS:], "lat", 1)
    center = center.at[-RADIUS:].add(from_south.astype(jnp.float32))
    center = center.at[:RADIUS].add(from_north.astype(jnp.float32))
    return center.astype(jnp.bfloat16)


def per_device(
    grid_state,
    observations,
    obs_tile,
    obs_cell,
    cotangent,
    norm_gains,
    w_cross_query,
    w_cross_pairs,
    w_cross_out,
    w_near_proj,
    w_near_out,
    w_up,
    w_down,
):
    rows_lat, rows_lon, model_width = grid_state.shape
    lat_count = lax.axis_size("lat")
    devices = lat_count * lax.axis_size("lon")
    slot_cap = max(2, 2 * observations.shape[0] // devices)
    slot_total = devices * slot_cap
    lat_start = lax.axis_index("lat") * rows_lat
    lat_total = rows_lat * lat_count
    dest_tile = obs_tile[:, 0]
    member = (dest_tile[:, None] == lax.iota(jnp.int32, devices)[None, :]).astype(jnp.int32)
    ranked = jnp.sum((jnp.cumsum(member, 0) - member) * member, 1)
    slot_row = dest_tile * slot_cap + ranked
    placing = (lax.iota(jnp.int32, slot_total)[:, None] == slot_row[None, :]).astype(jnp.bfloat16)
    cell_pair = jnp.stack(
        [obs_cell[:, 0] // rows_lon + 1, obs_cell[:, 0] % rows_lon + 1], 1
    ).astype(jnp.bfloat16)
    cell_codes = matmul(placing, cell_pair).astype(jnp.bfloat16).reshape(devices, slot_cap, 2)
    payload = (
        matmul(placing, observations).astype(jnp.bfloat16).reshape(devices, slot_cap, model_width)
    )
    arrived, arrived_codes = route_out(payload, cell_codes)
    slot_pairs = matmul(arrived.reshape(slot_total, model_width), w_cross_pairs).astype(
        jnp.bfloat16
    )
    flat_codes = arrived_codes.reshape(slot_total, 2).astype(jnp.int32)
    slot_rows = flat_codes[:, 0] - 1
    slot_cols = flat_codes[:, 1] - 1
    slot_valid = flat_codes[:, 0] > 0

    def cross_block(grid_in, pairs_in):
        flat = grid_in.reshape(rows_lat * rows_lon, model_width)
        normal = layer_norm(flat, norm_gains[0])
        queries = matmul(normal, w_cross_query).astype(jnp.bfloat16)
        own_pairs = matmul(normal, w_cross_pairs).astype(jnp.bfloat16)
        mixed = cross_attend(
            queries, own_pairs, pairs_in, slot_rows, slot_cols, slot_valid, rows_lon
        )
        return flat.astype(jnp.float32) + matmul(mixed, w_cross_out)

    def near_inputs(state):
        normal = layer_norm(state, norm_gains[1])
        both_proj = matmul(normal, w_near_proj)
        queries = both_proj[:, :model_width].astype(jnp.bfloat16)
        field = (
            both_proj[:, model_width:]
            .astype(jnp.bfloat16)
            .reshape(rows_lat, rows_lon, 2 * model_width)
        )
        return (queries, field)

    def near_block(state, queries, padded):
        mixed = near_attend(
            queries.reshape(rows_lat, rows_lon, model_width), padded, lat_start, lat_total
        )
        after = state + matmul(mixed, w_near_out)
        normal = layer_norm(after, norm_gains[2])
        hidden = jax.nn.gelu(matmul(normal, w_up)).astype(jnp.bfloat16)
        return (
            (after + matmul(hidden, w_down))
            .astype(jnp.bfloat16)
            .reshape(rows_lat, rows_lon, model_width)
        )

    state, cross_pull = jax.vjp(cross_block, grid_state, slot_pairs)
    (near_queries, near_field), near_pull = jax.vjp(near_inputs, state)
    padded = extend(near_field)
    encoded, block_pull = jax.vjp(near_block, state, near_queries, padded)
    state_grad, query_grad, padded_grad = block_pull(cotangent)
    field_grad = fold_rims(padded_grad)
    (input_grad,) = near_pull((query_grad, field_grad))
    grid_grad, pair_grads = cross_pull(state_grad + input_grad)
    slot_grads = (
        matmul_right_t(pair_grads, w_cross_pairs)
        .astype(jnp.bfloat16)
        .reshape(devices, slot_cap, model_width)
    )
    returned = route_back(slot_grads)
    obs_grad = matmul_left_t(placing, returned.reshape(slot_total, model_width)).astype(
        jnp.bfloat16
    )
    return (encoded, grid_grad, obs_grad)


def solution(mesh):
    return jax.shard_map(
        per_device,
        mesh=mesh,
        in_specs=(
            P("lat", "lon", None),
            P(("lat", "lon"), None),
            P(("lat", "lon"), None),
            P(("lat", "lon"), None),
            P("lat", "lon", None),
            P(),
            P(),
            P(),
            P(),
            P(),
            P(),
            P(),
            P(),
        ),
        out_specs=(P("lat", "lon", None), P("lat", "lon", None), P(("lat", "lon"), None)),
        check_vma=False,
    )
```

profile of v0, /device:TPU:1, one launch (start us, length us, event | category | flops | bytes accessed | tf_op | source)
XLA Modules:
  0.0 352.3 jit_solution(4769097551755704812)
XLA Ops:
  5.2 11.5 %all-to-all-start.1 = ((bf16[128,4,2]{1,2,0:T(2,128)(2,1)}), bf16[128,4,2]{1,2,0:T(2,128)(2,1)S(1)}, u32[]{:S(2)}, u32[]{:S(2)}) async-start(bf16[128,4,2]{1,2,0:T(2,128)(2,1)} %copy.83), calls=%async_computation.1 | async-start | bytes 131072 | tf_op jit(solution)/shard_map/all_to_all | solution.py:134
  22.6 2.2 convolution_convert_fusion.15
  24.8 4.1 %convolution_convert_fusion.4 = bf16[192,2048]{1,0:T(8,128)(2,1)} fusion(bf16[192,1024]{1,0:T(8,128)(2,1)S(1)} %multiply_convert_fusion.7, bf16[1024,2048]{1,0:T(8,128)(2,1)} %param.28), kind=kOutput, calls=%fused_computation.53 | convolution fusion | flops 805699584 | bytes 5373952 | tf_op jit(solution)/shard_map/jvp()/dot_general | solution.py:47
  30.6 2.5 reshape.583
  33.0 10.6 %all-to-all-start = ((bf16[128,4,1024]{2,1,0:T(4,128)(2,1)}), bf16[128,4,1024]{2,1,0:T(4,128)(2,1)}, u32[]{:S(2)}, u32[]{:S(2)}) async-start(bf16[128,4,1024]{2,1,0:T(4,128)(2,1)} %reshape.583), calls=%async_computation | async-start | bytes 2097152 | tf_op jit(solution)/shard_map/all_to_all | solution.py:133
  43.6 2.1 slice_convert_fusion.2
  45.7 2.5 copy.89
  51.9 10.1 %all-to-all-done = bf16[128,4,1024]{2,1,0:T(4,128)(2,1)} async-done(((bf16[128,4,1024]{2,1,0:T(4,128)(2,1)}), bf16[128,4,1024]{2,1,0:T(4,128)(2,1)}, u32[]{:S(2)}, u32[]{:S(2)}) %all-to-all-start) | async-done | bytes 1048608 | tf_op jit(solution)/shard_map/all_to_all | solution.py:133
  62.0 2.2 reshape.584
  64.2 4.8 %convolution_convert_fusion.1 = bf16[512,2048]{1,0:T(8,128)(2,1)S(1)} fusion(bf16[512,1024]{1,0:T(8,128)(2,1)} %reshape.584, bf16[1024,2048]{1,0:T(8,128)(2,1)} %param.28), kind=kOutput, calls=%fused_computation.47 | convolution fusion | flops 2148532224 | bytes 7340032 | tf_op jit(solution)/shard_map/dot_general | solution.py:47
  70.6 2.3 copy.87
  72.9 2.6 fusion.21
  75.6 2.1 fusion.131
  80.8 6.5 %convert_reduce_fusion.1 = (f32[16,192]{1,0:T(8,128)S(1)}, pred[16,192,512]{2,1,0:T(32,128)(4,1)}, bf16[16,192,512]{2,1,0:T(8,128)(2,1)S(1)}) fusion(f32[16,192]{1,0:T(8,128)} %copy-done.40, f32[192,512]{1,0:T(8,128)S(1)} %negate_multiply_fusion, f32[16,192,512]{2,1,0:T(8,128)} %copy-done.2, pred[512]{0:T(512)(128)(4,1)} %compare_reduce_fusion, ...), kind=kLoop, calls=%fused_computation.20 | loop fusion | flops 14152704 | bytes 11452928 | tf_op jit(solution)/shard_map/jvp()/reduce_sum | solution.py:87
  89.5 4.3 %convolution_convert_fusion = bf16[192,3072]{1,0:T(8,128)(2,1)S(1)} fusion(bf16[1024,3072]{1,0:T(8,128)(2,1)} %param.30, f32[192,1024]{1,0:T(8,128)S(1)} %get-tuple-element.93, f32[1024]{0:T(1024)S(1)} %bitcast.227, f32[192]{0:T(256)S(1)} %fusion.156, f32[192]{0:T(256)S(1)} %broadcast_multiply_fusion.2), kind=kOutput, calls=%fused_computation.38 | convolution fusion | flops 1209335808 | bytes 8263168 | tf_op jit(solution)/shard_map/jvp()/dot_general | solution.py:47
  97.5 9.2 %collective-permute-done = bf16[6,16,2048]{2,0,1:T(8,128)(2,1)S(1)} collective-permute-done((bf16[6,16,2048]{2,0,1:T(8,128)(2,1)S(1)}, bf16[6,16,2048]{2,0,1:T(8,128)(2,1)S(1)}, u32[]{:S(2)}, u32[]{:S(2)}) %collective-permute-start) | collective-permute-done | bytes 393248 | tf_op jit(solution)/shard_map/ppermute | solution.py:22
  106.7 3.8 %collective-permute-done.1 = bf16[6,16,2048]{2,0,1:T(8,128)(2,1)S(1)} collective-permute-done((bf16[6,16,2048]{2,0,1:T(8,128)(2,1)S(1)}, bf16[6,16,2048]{2,0,1:T(8,128)(2,1)S(1)}, u32[]{:S(2)}, u32[]{:S(2)}) %collective-permute-start.1) | collective-permute-done | bytes 393248 | tf_op jit(solution)/shard_map/ppermute | solution.py:23
  112.2 2.9 collective-permute-start.2
  118.6 2.4 copy.105
  123.0 5.5 %collective-permute-done.2 = bf16[24,6,2048]{2,0,1:T(8,128)(2,1)} collective-permute-done((bf16[24,6,2048]{2,0,1:T(8,128)(2,1)}, bf16[24,6,2048]{2,0,1:T(8,128)(2,1)}, u32[]{:S(2)}, u32[]{:S(2)}) %collective-permute-start.2) | collective-permute-done | bytes 589856 | tf_op jit(solution)/shard_map/ppermute | solution.py:22
  128.5 3.9 %collective-permute-done.3 = bf16[24,6,2048]{2,0,1:T(8,128)(2,1)} collective-permute-done((bf16[24,6,2048]{2,0,1:T(8,128)(2,1)}, bf16[24,6,2048]{2,0,1:T(8,128)(2,1)}, u32[]{:S(2)}, u32[]{:S(2)}) %collective-permute-start.3) | collective-permute-done | bytes 589856 | tf_op jit(solution)/shard_map/ppermute | solution.py:23
  132.4 2.4 pad_maximum_fusion
  134.8 3.2 copy.93
  138.0 4.3 %reshape.591 = bf16[672,2048]{1,0:T(8,128)(2,1)} reshape(bf16[24,28,2048]{2,1,0:T(8,128)(2,1)} %copy.93) | data formatting | bytes 5505024 | tf_op jit(solution)/shard_map/jvp()/reshape | solution.py:106
  142.3 3.5 %fusion.191 = (bf16[672,1024]{1,0:T(8,128)(2,1)}, bf16[672,1024]{1,0:T(8,128)(2,1)}) fusion(bf16[672,2048]{1,0:T(8,128)(2,1)} %reshape.591), kind=kLoop, calls=%fused_computation.296 | loop fusion | bytes 5505024 | tf_op jit(solution)/shard_map/jvp()/slice | solution.py:107
  145.9 2.5 copy.96
  148.4 3.5 fusion.5
  151.9 2.5 fusion.33
  155.6 6.1 %convert_reduce_fusion = (f32[16,192]{1,0:T(8,128)S(1)}, pred[16,192,672]{2,1,0:T(32,128)(4,1)}, bf16[16,192,672]{2,1,0:T(8,128)(2,1)}) fusion(f32[16,192]{1,0:T(8,128)S(1)} %get-tuple-element.94, f32[16,192,672]{2,1,0:T(8,128)S(1)} %get-tuple-element.95, pred[192,672]{1,0:T(8,128)(4,1)S(1)} %fusion.114, f32[16,192]{1,0:T(8,128)S(1)} %fusion.33), kind=kLoop, calls=%fused_computation.7 | loop fusion | flops 16512000 | bytes 14616576 | tf_op jit(solution)/shard_map/jvp()/reduce_sum | solution.py:122
  161.6 2.9 copy.94
  164.6 4.6 %convolution_convert_fusion.10 = bf16[16,64,192]{2,1,0:T(8,128)(2,1)S(1)} fusion(bf16[672,16,64]{0,2,1:T(8,128)(2,1)} %bitcast.191, bf16[16,192,672]{2,1,0:T(8,128)(2,1)} %get-tuple-element.67), kind=kOutput, calls=%fused_computation.101 | convolution fusion | flops 264437760 | bytes 5898240 | tf_op jit(solution)/shard_map/jvp(hqk,khd->qhd)/dot_general | solution.py:125
  171.7 2.3 fusion.115
  173.9 8.4 %multiply_reduce_fusion.3 = (f32[192]{0:T(256)S(1)}, f32[192,1024]{1,0:T(8,128)}) fusion(f32[192,1024]{1,0:T(8,128)} %copy-done.5, f32[192]{0:T(256)S(1)} %broadcast_multiply_fusion.1, f32[1024]{0:T(1024)S(1)} %bitcast.230, bf16[1024,2048]{1,0:T(8,128)(2,1)} %param.32, f32[192,2048]{1,0:T(8,128)} %fusion.115, bf16[192,1024]{1,0:T(8,128)(2,1)} %bitcast.213, ...), kind=kOutput, calls=%fused_computation.146 | convolution fusion | flops 1620049664 | bytes 11933184 | tf_op jit(solution)/shard_map/transpose(jvp())/dot_general | solution.py:47
  185.0 3.3 convolution_convert_fusion.14
  190.3 4.8 %convolution_convert_fusion.6 = bf16[16,64,672]{2,1,0:T(8,128)(2,1)} fusion(bf16[16,64,192]{2,1,0:T(8,128)(2,1)} %bitcast.208, bf16[16,192,672]{2,1,0:T(8,128)(2,1)} %get-tuple-element.67), kind=kOutput, calls=%fused_computation.67 | convolution fusion | flops 264929280 | bytes 5898240 | tf_op jit(solution)/shard_map/transpose(jvp(hqk,khd->qhd))/dot_general | solution.py:125
  195.2 8.0 %fusion.3 = (f32[16,192]{1,0:T(8,128)S(1)}, bf16[16,192,672]{2,1,0:T(8,128)(2,1)}) fusion(f32[16,192]{1,0:T(8,128)S(1)} %multiply_divide_fusion.2, f32[16,192]{1,0:T(8,128)S(1)} %get-tuple-element.94, f32[16,192,672]{2,1,0:T(8,128)} %copy-done.1, pred[192,672]{1,0:T(8,128)(4,1)S(1)} %fusion.114, bf16[16,64,192]{2,1,0:T(8,128)(2,1)S(1)} %bitcast.209, ...), kind=kOutput, calls=%fused_computation.5 | convolution fusion | flops 280753152 | bytes 14321664 | tf_op jit(solution)/shard_map/transpose(jvp(hqk,khd->qhd))/dot_general | solution.py:125
  203.1 6.0 %fusion.186 = (f32[16,192]{1,0:T(8,128)S(1)}, f32[16,192,672]{2,1,0:T(8,128)S(1)}) fusion(f32[16,192]{1,0:T(8,128)S(1)} %get-tuple-element.94, f32[16,192,672]{2,1,0:T(8,128)S(1)} %bitcast.181, pred[192,672]{1,0:T(8,128)(4,1)S(1)} %fusion.114, f32[16,192]{1,0:T(8,128)S(1)} %neg.42, f32[16,192]{1,0:T(8,128)S(1)} %fusion.33, ...), kind=kLoop, calls=%fused_computation.293 | loop fusion | flops 16512000 | bytes 20822016 | tf_op jit(solution)/shard_map/transpose(jvp())/reduce_sum | solution.py:123
  209.2 5.2 %fusion.69 = bf16[16,192,64]{1,2,0:T(8,128)(2,1)} fusion(bf16[672,16,64]{0,2,1:T(8,128)(2,1)S(1)} %bitcast.190, f32[16,192,672]{2,1,0:T(8,128)S(1)} %get-tuple-element.60, pred[16,192,672]{2,1,0:T(32,128)(4,1)} %get-tuple-element.62, f32[16,192]{1,0:T(8,128)S(1)} %negate_divide_fusion, pred[192,672]{1,0:T(8,128)(4,1)S(1)} %fusion.114), kind=kOutput, calls=%fused_computation.98 | convolution fusion | flops 272695296 | bytes 12232704 | tf_op jit(solution)/shard_map/transpose(jvp(qhd,khd->hqk))/dot_general | solution.py:111
  214.4 5.6 %fusion.42 = bf16[16,672,64]{1,2,0:T(8,128)(2,1)} fusion(bf16[192,16,64]{0,2,1:T(8,128)(2,1)} %bitcast.201, f32[16,192,672]{2,1,0:T(8,128)S(1)} %get-tuple-element.60, pred[16,192,672]{2,1,0:T(32,128)(4,1)} %get-tuple-element.62, f32[16,192]{1,0:T(8,128)S(1)} %negate_divide_fusion, pred[192,672]{1,0:T(8,128)(4,1)S(1)} %fusion.114), kind=kOutput, calls=%fused_computation.66 | convolution fusion | flops 273186816 | bytes 12232704 | tf_op jit(solution)/shard_map/transpose(jvp(qhd,khd->hqk))/dot_general | solution.py:111
  220.0 2.6 copy.98
  222.6 2.5 copy.99
  225.1 3.6 %pad_add_fusion = bf16[672,2048]{1,0:T(8,128)(2,1)} fusion(bf16[672,1024]{1,0:T(8,128)(2,1)} %copy.99, bf16[672,1024]{1,0:T(8,128)(2,1)} %copy.98), kind=kLoop, calls=%fused_computation.50 | loop fusion | flops 5505024 | bytes 5505024 | tf_op jit(solution)/shard_map/transpose(jvp())/add_any | solution.py:107
  228.7 4.3 %reshape.600 = bf16[24,28,2048]{2,1,0:T(8,128)(2,1)} reshape(bf16[672,2048]{1,0:T(8,128)(2,1)} %pad_add_fusion) | data formatting | bytes 5505024 | tf_op jit(solution)/shard_map/transpose(jvp())/reshape | solution.py:106
  233.1 2.0 fusion.190
  236.3 2.2 slice_convert_fusion
  239.7 3.2 collective-permute-start.5
  246.9 6.8 %collective-permute-done.4 = bf16[24,6,2048]{2,0,1:T(8,128)(2,1)} collective-permute-done((bf16[24,6,2048]{2,0,1:T(8,128)(2,1)}, bf16[24,6,2048]{2,0,1:T(8,128)(2,1)}, u32[]{:S(2)}, u32[]{:S(2)}) %collective-permute-start.4) | collective-permute-done | bytes 589856 | tf_op jit(solution)/shard_map/ppermute | solution.py:30
  253.7 3.2 slice_add_fusion.1
  256.9 7.9 %scatter-add.14 = f32[24,16,2048]{2,1,0:T(8,128)} dynamic-update-slice(f32[24,16,2048]{2,1,0:T(8,128)} %slice_convert_fusion, f32[24,6,2048]{2,1,0:T(8,128)} %slice_add_fusion.1, s32[]{:T(128)} %constant.236.clone.1, s32[]{:T(128)} %constant.263.clone.1, s32[]{:T(128)} %constant.236.clone.1) | dynamic-update-slice | bytes 2359300 | tf_op jit(solution)/shard_map/scatter-add | solution.py:153
  264.8 3.1 slice_add_fusion
  268.0 8.7 %scatter-add.15 = f32[24,16,2048]{2,1,0:T(8,128)} dynamic-update-slice(f32[24,16,2048]{2,1,0:T(8,128)} %scatter-add.14, f32[24,6,2048]{2,1,0:T(8,128)} %slice_add_fusion, s32[]{:T(128)} %constant.236.clone.1, s32[]{:T(128)} %constant.236.clone.1, s32[]{:T(128)} %constant.236.clone.1) | dynamic-update-slice | bytes 2359300 | tf_op jit(solution)/shard_map/scatter-add | solution.py:154
  276.6 2.3 convert_element_type.306
  279.0 3.0 collective-permute-start.7
  283.8 7.2 %collective-permute-done.6 = bf16[6,16,2048]{2,1,0:T(8,128)(2,1)S(1)} collective-permute-done((bf16[6,16,2048]{2,1,0:T(8,128)(2,1)S(1)}, bf16[6,16,2048]{2,1,0:T(8,128)(2,1)S(1)}, u32[]{:S(2)}, u32[]{:S(2)}) %collective-permute-start.6) | collective-permute-done | bytes 393248 | tf_op jit(solution)/shard_map/ppermute | solution.py:36
  291.7 2.4 multiply_reduce_fusion.2
  299.1 2.9 convolution_convert_fusion.8
  302.3 5.7 %fusion.7 = (f32[16,192]{1,0:T(8,128)S(1)}, bf16[16,192,512]{2,1,0:T(8,128)(2,1)S(1)}) fusion(f32[16,192]{1,0:T(8,128)S(1)} %copy-done.55, f32[16,192]{1,0:T(8,128)S(1)} %copy-done.47, f32[192,512]{1,0:T(8,128)S(1)} %copy-done.17, f32[16,192,512]{2,1,0:T(8,128)} %copy-done.2, pred[512]{0:T(512)(128)(4,1)S(1)} %copy-done.72, ...), kind=kOutput, calls=%fused_computation.16 | convolution fusion | flops 215479296 | bytes 11309568 | tf_op jit(solution)/shard_map/transpose(jvp(hqk,khd->qhd))/dot_general | solution.py:93
  308.1 3.2 fusion.182
  313.5 2.9 fusion.95
  316.4 3.4 fusion.60
  319.8 2.3 reshape.608
  322.1 8.7 %all-to-all-start.2 = ((bf16[128,4,1024]{2,1,0:T(4,128)(2,1)}), bf16[128,4,1024]{2,1,0:T(4,128)(2,1)}, u32[]{:S(2)}, u32[]{:S(2)}) async-start(bf16[128,4,1024]{2,1,0:T(4,128)(2,1)} %reshape.608), calls=%async_computation.2 | async-start | bytes 2097152 | tf_op jit(solution)/shard_map/all_to_all | solution.py:140
  331.7 4.1 %convolution_convert_fusion.12 = bf16[192,1024]{1,0:T(8,128)(2,1)S(1)} fusion(bf16[1024,2048]{1,0:T(8,128)(2,1)} %param.28, bf16[192,1024]{1,0:T(8,128)(2,1)} %copy.108, bf16[192,1024]{1,0:T(8,128)(2,1)} %get-tuple-element.106), kind=kOutput, calls=%fused_computation.109 | convolution fusion | flops 807075840 | bytes 5373952 | tf_op jit(solution)/shard_map/transpose(jvp())/dot_general | solution.py:47
  339.2 10.2 %all-to-all-done.2 = bf16[128,4,1024]{2,1,0:T(4,128)(2,1)} async-done(((bf16[128,4,1024]{2,1,0:T(4,128)(2,1)}), bf16[128,4,1024]{2,1,0:T(4,128)(2,1)}, u32[]{:S(2)}, u32[]{:S(2)}) %all-to-all-start.2) | async-done | bytes 1048608 | tf_op jit(solution)/shard_map/all_to_all | solution.py:140
  (272 shorter events, 64.2 us)
Async XLA Ops:
  0.6 87.8 %copy-start = (bf16[1024,1024]{1,0:T(8,128)(2,1)S(1)}, bf16[1024,1024]{1,0:T(8,128)(2,1)}, u32[]{:S(2)}) copy-start(bf16[1024,1024]{1,0:T(8,128)(2,1)} %param.29) | copy-start | bytes 6291460
  4.1 24.8 %copy-start.67 = (s32[256]{0:T(256)}, s32[256]{0:T(256)S(1)}, u32[]{:S(2)}) copy-start(s32[256]{0:T(256)S(1)} %multiply_add_fusion.3) | copy-start | bytes 3076
  5.2 27.8 %all-to-all-start.1 = ((bf16[128,4,2]{1,2,0:T(2,128)(2,1)}), bf16[128,4,2]{1,2,0:T(2,128)(2,1)S(1)}, u32[]{:S(2)}, u32[]{:S(2)}) async-start(bf16[128,4,2]{1,2,0:T(2,128)(2,1)} %copy.83), calls=%async_computation.1 | async-start | bytes 131072 | tf_op jit(solution)/shard_map/all_to_all | solution.py:134
  24.8 4.2 %copy-start.43 = (bf16[256,1024]{1,0:T(8,128)(2,1)S(1)}, bf16[256,1024]{1,0:T(8,128)(2,1)}, u32[]{:S(2)}) copy-start(bf16[256,1024]{1,0:T(8,128)(2,1)} %param.22) | copy-start | bytes 1572868
  30.6 42.3 %copy-start.20 = (bf16[192,1024]{0,1:T(8,128)(2,1)}, bf16[192,1024]{0,1:T(8,128)(2,1)S(1)}, u32[]{:S(2)}) copy-start(bf16[192,1024]{0,1:T(8,128)(2,1)S(1)} %copy.86) | copy-start | bytes 1179652
  33.0 15.2 %copy-start.48 = (bf16[128,4,2]{1,2,0:T(2,128)(2,1)}, bf16[128,4,2]{1,2,0:T(2,128)(2,1)S(1)}, u32[]{:S(2)}) copy-start(bf16[128,4,2]{1,2,0:T(2,128)(2,1)S(1)} %all-to-all-done.1) | copy-start | bytes 6148
  33.0 29.0 %all-to-all-start = ((bf16[128,4,1024]{2,1,0:T(4,128)(2,1)}), bf16[128,4,1024]{2,1,0:T(4,128)(2,1)}, u32[]{:S(2)}, u32[]{:S(2)}) async-start(bf16[128,4,1024]{2,1,0:T(4,128)(2,1)} %reshape.583), calls=%async_computation | async-start | bytes 2097152 | tf_op jit(solution)/shard_map/all_to_all | solution.py:133
  48.4 20.7 %copy-start.33 = (bf16[192,1024]{0,1:T(8,128)(2,1)}, bf16[192,1024]{0,1:T(8,128)(2,1)S(1)}, u32[]{:S(2)}) copy-start(bf16[192,1024]{0,1:T(8,128)(2,1)S(1)} %copy.117) | copy-start | bytes 1179652
  51.9 28.8 %copy-start.16 = (f32[192,512]{1,0:T(8,128)}, f32[192,512]{1,0:T(8,128)S(1)}, u32[]{:S(2)}) copy-start(f32[192,512]{1,0:T(8,128)S(1)} %negate_multiply_fusion) | copy-start | bytes 1179652
  75.6 3.2 copy-start.40
  75.6 3.8 %copy-start.27 = (bf16[512,1024]{1,0:T(8,128)(2,1)S(1)}, bf16[512,1024]{1,0:T(8,128)(2,1)}, u32[]{:S(2)}) copy-start(bf16[512,1024]{1,0:T(8,128)(2,1)} %get-tuple-element.76) | copy-start | bytes 3145732
  80.7 6.5 %copy-start.9 = (f32[192,1024]{0,1:T(8,128)S(1)}, f32[192,1024]{0,1:T(8,128)}, u32[]{:S(2)}) copy-start(f32[192,1024]{0,1:T(8,128)} %copy.89) | copy-start | bytes 2359300
  80.7 6.5 %copy-start.25 = (bf16[512,1024]{0,1:T(8,128)(2,1)S(1)}, bf16[512,1024]{0,1:T(8,128)(2,1)}, u32[]{:S(2)}) copy-start(bf16[512,1024]{0,1:T(8,128)(2,1)} %copy.82) | copy-start | bytes 3145732
  80.7 6.6 %copy-start.49 = (f32[192,16]{0,1:T(8,128)S(1)}, f32[192,16]{0,1:T(8,128)}, u32[]{:S(2)}) copy-start(f32[192,16]{0,1:T(8,128)} %fusion.144) | copy-start | bytes 36868
  89.5 4.3 %copy-start.63 = (f32[192]{0:T(256)}, f32[192]{0:T(256)S(1)}, u32[]{:S(2)}) copy-start(f32[192]{0:T(256)S(1)} %multiply_reduce_fusion.5) | copy-start | bytes 2308
  89.5 4.3 %copy-start.59 = (f32[192]{0:T(256)}, f32[192]{0:T(256)S(1)}, u32[]{:S(2)}) copy-start(f32[192]{0:T(256)S(1)} %fusion.156) | copy-start | bytes 2308
  93.8 3.7 %copy-start.13 = (bf16[192,3072]{1,0:T(8,128)(2,1)}, bf16[192,3072]{1,0:T(8,128)(2,1)S(1)}, u32[]{:S(2)}) copy-start(bf16[192,3072]{1,0:T(8,128)(2,1)S(1)} %convolution_convert_fusion) | copy-start | bytes 3538948
  94.3 21.0 %copy-start.61 = (s32[192]{0:T(256)S(1)}, s32[192]{0:T(256)}, u32[]{:S(2)}) copy-start(s32[192]{0:T(256)} %get-tuple-element.110) | copy-start | bytes 2308
  94.3 21.0 %copy-start.62 = (s32[192]{0:T(256)S(1)}, s32[192]{0:T(256)}, u32[]{:S(2)}) copy-start(s32[192]{0:T(256)} %get-tuple-element.111) | copy-start | bytes 2308
  94.4 12.3 %collective-permute-start = (bf16[6,16,2048]{2,0,1:T(8,128)(2,1)S(1)}, bf16[6,16,2048]{2,0,1:T(8,128)(2,1)S(1)}, u32[]{:S(2)}, u32[]{:S(2)}) collective-permute-start(bf16[6,16,2048]{2,0,1:T(8,128)(2,1)S(1)} %copy.90), channel_id=1, source_target_pairs={{0,16},{16,32},{32,48},{48,64},{64,80},{80,96},{96,112},{1,17},{17... | collective-permute-start | bytes 1179656 | tf_op jit(solution)/shard_map/ppermute | solution.py:22
  95.7 14.8 %collective-permute-start.1 = (bf16[6,16,2048]{2,0,1:T(8,128)(2,1)S(1)}, bf16[6,16,2048]{2,0,1:T(8,128)(2,1)S(1)}, u32[]{:S(2)}, u32[]{:S(2)}) collective-permute-start(bf16[6,16,2048]{2,0,1:T(8,128)(2,1)S(1)} %copy.91), channel_id=1, source_target_pairs={{16,0},{32,16},{48,32},{64,48},{80,64},{96,80},{112,96},{17,1},{33... | collective-permute-start | bytes 1179656 | tf_op jit(solution)/shard_map/ppermute | solution.py:23
  97.5 13.0 %copy-start.8 = (bf16[12,16,2048]{2,0,1:T(8,128)(2,1)}, bf16[12,16,2048]{2,0,1:T(8,128)(2,1)S(1)}, u32[]{:S(2)}) copy-start(bf16[12,16,2048]{2,0,1:T(8,128)(2,1)S(1)} %copy.92) | copy-start | bytes 2359300
  106.7 5.5 %copy-start.30 = (bf16[6,16,2048]{2,0,1:T(8,128)(2,1)}, bf16[6,16,2048]{2,0,1:T(8,128)(2,1)S(1)}, u32[]{:S(2)}) copy-start(bf16[6,16,2048]{2,0,1:T(8,128)(2,1)S(1)} %collective-permute-done) | copy-start | bytes 1179652
  112.2 16.3 %collective-permute-start.2 = (bf16[24,6,2048]{2,0,1:T(8,128)(2,1)}, bf16[24,6,2048]{2,0,1:T(8,128)(2,1)}, u32[]{:S(2)}, u32[]{:S(2)}) collective-permute-start(bf16[24,6,2048]{2,0,1:T(8,128)(2,1)} %get-tuple-element.73), channel_id=1, source_target_pairs={{0,1},{1,2},{2,3},{3,4},{4,5},{5,6},{6,7},{7,8},{8,9},{9,10},{10,1... | collective-permute-start | bytes 1769480 | tf_op jit(solution)/shard_map/ppermute | solution.py:22
  115.1 17.4 %collective-permute-start.3 = (bf16[24,6,2048]{2,0,1:T(8,128)(2,1)}, bf16[24,6,2048]{2,0,1:T(8,128)(2,1)}, u32[]{:S(2)}, u32[]{:S(2)}) collective-permute-start(bf16[24,6,2048]{2,0,1:T(8,128)(2,1)} %get-tuple-element.74), channel_id=1, source_target_pairs={{1,0},{2,1},{3,2},{4,3},{5,4},{6,5},{7,6},{8,7},{9,8},{10,9},{11,1... | collective-permute-start | bytes 1769480 | tf_op jit(solution)/shard_map/ppermute | solution.py:23
  151.9 3.7 %copy-start.1 = (f32[16,192,672]{2,1,0:T(8,128)}, f32[16,192,672]{2,1,0:T(8,128)S(1)}, u32[]{:S(2)}) copy-start(f32[16,192,672]{2,1,0:T(8,128)S(1)} %get-tuple-element.95) | copy-start | bytes 24772612
  164.6 4.6 %copy-start.11 = (bf16[1024,1024]{1,0:T(8,128)(2,1)S(1)}, bf16[1024,1024]{1,0:T(8,128)(2,1)}, u32[]{:S(2)}) copy-start(bf16[1024,1024]{1,0:T(8,128)(2,1)} %param.31) | copy-start | bytes 6291460
  169.9 4.0 %copy-start.5 = (f32[192,1024]{1,0:T(8,128)}, f32[192,1024]{1,0:T(8,128)S(1)}, u32[]{:S(2)}) copy-start(f32[192,1024]{1,0:T(8,128)S(1)} %get-tuple-element.97) | copy-start | bytes 2359300
  184.1 11.1 %copy-start.69 = (f32[192]{0:T(256)}, f32[192]{0:T(256)S(1)}, u32[]{:S(2)}) copy-start(f32[192]{0:T(256)S(1)} %negate_multiply_fusion.3) | copy-start | bytes 2308
  190.3 4.8 %copy-start.19 = (bf16[672,1024]{0,1:T(8,128)(2,1)S(1)}, bf16[672,1024]{0,1:T(8,128)(2,1)}, u32[]{:S(2)}) copy-start(bf16[672,1024]{0,1:T(8,128)(2,1)} %copy.94) | copy-start | bytes 4128772
  190.3 4.8 %copy-start.35 = (bf16[192,1024]{0,1:T(8,128)(2,1)S(1)}, bf16[192,1024]{0,1:T(8,128)(2,1)}, u32[]{:S(2)}) copy-start(bf16[192,1024]{0,1:T(8,128)(2,1)} %copy.97) | copy-start | bytes 1179652
  190.3 12.8 %slice-start = ((s8[9437184]{0:T(1024)(128)(4,1)}), s8[4194304]{0:T(1024)(128)(4,1)S(1)}, s32[]{:S(2)}) async-start(s8[9437184]{0:T(1024)(128)(4,1)} %bitcast.180), calls=%async_computation.3 | async-start | bytes 8388608
  195.1 8.0 %slice-start.1 = ((s8[9437184]{0:T(1024)(128)(4,1)}), s8[4194304]{0:T(1024)(128)(4,1)S(1)}, s32[]{:S(2)}) async-start(s8[9437184]{0:T(1024)(128)(4,1)} %bitcast.180), calls=%async_computation.4 | async-start | bytes 8388608
  195.1 8.0 %slice-start.2 = ((s8[9437184]{0:T(1024)(128)(4,1)}), s8[1048576]{0:T(1024)(128)(4,1)S(1)}, s32[]{:S(2)}) async-start(s8[9437184]{0:T(1024)(128)(4,1)} %bitcast.180), calls=%async_computation.5 | async-start | bytes 2097152
  203.1 6.0 %copy-start.18 = (bf16[672,1024]{0,1:T(8,128)(2,1)S(1)}, bf16[672,1024]{0,1:T(8,128)(2,1)}, u32[]{:S(2)}) copy-start(bf16[672,1024]{0,1:T(8,128)(2,1)} %copy.96) | copy-start | bytes 4128772
  233.1 3.2 copy-start.7
  235.1 7.9 %copy-start.73 = (bf16[2048,1024]{1,0:T(8,128)(2,1)S(1)}, bf16[2048,1024]{1,0:T(8,128)(2,1)}, u32[]{:S(2)}) copy-start(bf16[2048,1024]{1,0:T(8,128)(2,1)} %param.33) | copy-start | bytes 12582916
  236.3 6.7 %copy-start.6 = (f32[192,1024]{1,0:T(8,128)S(1)}, f32[192,1024]{1,0:T(8,128)}, u32[]{:S(2)}) copy-start(f32[192,1024]{1,0:T(8,128)} %copy-done.5) | copy-start | bytes 2359300
  236.3 6.7 %copy-start.36 = (f32[192,2048]{1,0:T(8,128)S(1)}, f32[192,2048]{1,0:T(8,128)}, u32[]{:S(2)}) copy-start(f32[192,2048]{1,0:T(8,128)} %fusion.115) | copy-start | bytes 4718596
  236.3 17.4 %collective-permute-start.4 = (bf16[24,6,2048]{2,0,1:T(8,128)(2,1)}, bf16[24,6,2048]{2,0,1:T(8,128)(2,1)}, u32[]{:S(2)}, u32[]{:S(2)}) collective-permute-start(bf16[24,6,2048]{2,0,1:T(8,128)(2,1)} %copy.100), channel_id=1, source_target_pairs={{0,15},{1,0},{2,1},{3,2},{4,3},{5,4},{6,5},{7,6},{8,7},{9,8},{10,9... | collective-permute-start | bytes 1769480 | tf_op jit(solution)/shard_map/ppermute | solution.py:30
  239.7 25.1 %collective-permute-start.5 = (bf16[24,6,2048]{2,0,1:T(8,128)(2,1)}, bf16[24,6,2048]{2,0,1:T(8,128)(2,1)}, u32[]{:S(2)}, u32[]{:S(2)}) collective-permute-start(bf16[24,6,2048]{2,0,1:T(8,128)(2,1)} %copy.102), channel_id=1, source_target_pairs={{0,1},{1,2},{2,3},{3,4},{4,5},{5,6},{6,7},{7,8},{8,9},{9,10},{10,1... | collective-permute-start | bytes 1769480 | tf_op jit(solution)/shard_map/ppermute | solution.py:30
  276.6 14.9 %slice-start.5 = ((s8[6291456]{0:T(1024)(128)(4,1)}), s8[4194304]{0:T(1024)(128)(4,1)S(1)}, s32[]{:S(2)}) async-start(s8[6291456]{0:T(1024)(128)(4,1)} %bitcast.187), calls=%async_computation.8 | async-start | bytes 8388608
  279.0 12.3 %collective-permute-start.7 = (bf16[6,16,2048]{2,1,0:T(8,128)(2,1)S(1)}, bf16[6,16,2048]{2,1,0:T(8,128)(2,1)S(1)}, u32[]{:S(2)}, u32[]{:S(2)}) collective-permute-start(bf16[6,16,2048]{2,1,0:T(8,128)(2,1)S(1)} %get-tuple-element.77), channel_id=1, source_target_pairs={{0,16},{16,32},{32,48},{48,64},{64,80},{80,96},{96,112},{1,17},{17... | collective-permute-start | bytes 1179656 | tf_op jit(solution)/shard_map/ppermute | solution.py:36
  282.0 9.6 %slice-start.6 = ((s8[6291456]{0:T(1024)(128)(4,1)}), s8[2097152]{0:T(1024)(128)(4,1)S(1)}, s32[]{:S(2)}) async-start(s8[6291456]{0:T(1024)(128)(4,1)} %bitcast.187), calls=%async_computation.9 | async-start | bytes 4194304
  282.0 9.1 %collective-permute-start.6 = (bf16[6,16,2048]{2,1,0:T(8,128)(2,1)S(1)}, bf16[6,16,2048]{2,1,0:T(8,128)(2,1)S(1)}, u32[]{:S(2)}, u32[]{:S(2)}) collective-permute-start(bf16[6,16,2048]{2,1,0:T(8,128)(2,1)S(1)} %get-tuple-element.78), channel_id=1, source_target_pairs={{16,0},{32,16},{48,32},{64,48},{80,64},{96,80},{112,96},{17,1},{33... | collective-permute-start | bytes 1179656 | tf_op jit(solution)/shard_map/ppermute | solution.py:36
  283.8 7.8 %copy-start.45 = (bf16[192,1024]{1,0:T(8,128)(2,1)S(1)}, bf16[192,1024]{1,0:T(8,128)(2,1)}, u32[]{:S(2)}) copy-start(bf16[192,1024]{1,0:T(8,128)(2,1)} %copy.104) | copy-start | bytes 1179652
  295.2 3.9 %copy-start.28 = (bf16[192,1024]{1,0:T(8,128)(2,1)}, bf16[192,1024]{1,0:T(8,128)(2,1)S(1)}, u32[]{:S(2)}) copy-start(bf16[192,1024]{1,0:T(8,128)(2,1)S(1)} %add_add_fusion.3) | copy-start | bytes 1179652
  299.0 3.2 copy-start.26
  299.0 3.2 copy-start.32
  299.0 3.2 copy-start.47
  299.1 3.2 copy-start.55
  299.1 3.2 copy-start.72
  302.2 5.9 %slice-start.3 = ((s8[6291456]{0:T(1024)(128)(4,1)}), s8[4194304]{0:T(1024)(128)(4,1)S(1)}, s32[]{:S(2)}) async-start(s8[6291456]{0:T(1024)(128)(4,1)} %bitcast.182), calls=%async_computation.6 | async-start | bytes 8388608
  302.3 5.7 %copy-start.41 = (f32[16,192]{1,0:T(8,128)S(1)}, f32[16,192]{1,0:T(8,128)}, u32[]{:S(2)}) copy-start(f32[16,192]{1,0:T(8,128)} %copy-done.40) | copy-start | bytes 36868
  302.3 5.7 %copy-start.44 = (f32[16,192]{1,0:T(8,128)S(1)}, f32[16,192]{1,0:T(8,128)}, u32[]{:S(2)}) copy-start(f32[16,192]{1,0:T(8,128)} %get-tuple-element.56) | copy-start | bytes 36868
  302.3 5.8 %slice-start.4 = ((s8[6291456]{0:T(1024)(128)(4,1)}), s8[2097152]{0:T(1024)(128)(4,1)S(1)}, s32[]{:S(2)}) async-start(s8[6291456]{0:T(1024)(128)(4,1)} %bitcast.182), calls=%async_computation.7 | async-start | bytes 4194304
  308.1 3.3 copy-start.21
  308.1 3.4 copy-start.37
  322.1 27.3 %all-to-all-start.2 = ((bf16[128,4,1024]{2,1,0:T(4,128)(2,1)}), bf16[128,4,1024]{2,1,0:T(4,128)(2,1)}, u32[]{:S(2)}, u32[]{:S(2)}) async-start(bf16[128,4,1024]{2,1,0:T(4,128)(2,1)} %reshape.608), calls=%async_computation.2 | async-start | bytes 2097152 | tf_op jit(solution)/shard_map/all_to_all | solution.py:140
  331.7 4.1 %copy-start.12 = (bf16[1024,1024]{1,0:T(8,128)(2,1)S(1)}, bf16[1024,1024]{1,0:T(8,128)(2,1)}, u32[]{:S(2)}) copy-start(bf16[1024,1024]{1,0:T(8,128)(2,1)} %param.27) | copy-start | bytes 6291460
  331.7 4.2 %copy-start.42 = (bf16[192,16,64]{0,2,1:T(8,128)(2,1)S(1)}, bf16[192,16,64]{0,2,1:T(8,128)(2,1)}, u32[]{:S(2)}) copy-start(bf16[192,16,64]{0,2,1:T(8,128)(2,1)} %fusion.95) | copy-start | bytes 1179652
  331.7 4.2 %copy-start.51 = (f32[1,1024]{1,0:T(1,128)S(1)}, f32[1,1024]{1,0:T(1,128)}, u32[]{:S(2)}) copy-start(f32[1,1024]{1,0:T(1,128)} %copy-done.50) | copy-start | bytes 12292
  331.7 4.2 %copy-start.53 = (f32[192]{0:T(256)S(1)}, f32[192]{0:T(256)}, u32[]{:S(2)}) copy-start(f32[192]{0:T(256)} %copy-done.52) | copy-start | bytes 2308
  336.9 13.8 %copy-start.68 = (s32[256]{0:T(256)S(1)}, s32[256]{0:T(256)}, u32[]{:S(2)}) copy-start(s32[256]{0:T(256)} %copy-done.67) | copy-start | bytes 3076
  (28 other events, 58.3 us)
where the time goes:
time: 358 us; the launch traced here: 352 us
  matrix products  97 us (27%)
  local copies, waits for them, and re-layouts  88.7 us (25%)
  other arithmetic  63.1 us (18%)
  waiting for transfers between devices  56.8 us (16%)
  starting transfers between devices  44.4 us (12%)
    dot_general x16, matrix products, matmul(): return jnp.dot(left, right, preferred_element_type=jnp.float32)  43.5 us
    dot_general x3, matrix products, near_attend(): jnp.einsum('hqk,khd->qhd', weights, value_cells, preferred_element_type=j...  17.3 us
    ppermute x2, waiting for transfers between devices, padded_2(): before = lax.ppermute(last, axis, up)  14.7 us
    dot_general x3, matrix products, near_attend(): jnp.einsum('qhd,khd->hqk', query_heads, key_cells, preferred_element_type...  14.3 us
    all_to_all x1, starting transfers between devices, route_out(): lax.all_to_all(cell_codes, ('lat', 'lon'), split_axis=0, concat_axis=0, t...  11.5 us
    all_to_all x1, starting transfers between devices, route_out(): lax.all_to_all(payload, ('lat', 'lon'), split_axis=0, concat_axis=0, tile...  10.6 us
    all_to_all x1, waiting for transfers between devices, route_back(): lax.all_to_all(payload, ('lat', 'lon'), split_axis=0, concat_axis=0, tile...  10.2 us
    all_to_all x1, waiting for transfers between devices, route_out(): lax.all_to_all(payload, ('lat', 'lon'), split_axis=0, concat_axis=0, tile...  10.1 us
  transfers between devices with their start and end apart: 11, of which 8 were waited for; matrix products, arithmetic and copies ran while one was open for 17% of the time, Pallas kernels for 0%

commit v1 on v0

v1 whole, which is shorter than its diff:
```python
import functools

import jax
import jax.numpy as jnp
import numpy as np
from jax import lax
from jax.experimental import pallas as pl
from jax.experimental.pallas import tpu as pltpu
from jax.sharding import PartitionSpec as P

HEADS = 16
RADIUS = 6
EPSILON = 1e-05
SPREAD = 32.0
LOW_SCORE = -1e30

BF = jnp.bfloat16
F32 = jnp.float32
NN = (((1,), (0,)), ((), ()))
NT = (((1,), (1,)), ((), ()))
TN = (((0,), (0,)), ((), ()))
CHUNK = 32
TILE = 256
PAIR = 128
HALF = 64
VMEM_BYTES = 56 * 2**20
GELU_C = 0.7978845608028654
GELU_A = 0.044715


def dot(left, right, dims=NN):
    return lax.dot_general(left, right, dims, preferred_element_type=F32)


def iota(shape, dim):
    return lax.broadcasted_iota(jnp.int32, shape, dim)


def tiles_of(count, body, tile=TILE):
    @pl.loop(0, count // tile)
    def _(i):
        body(pl.multiple_of(i * tile, tile))


def row_chunks(count):
    return [pl.ds(i, CHUNK) for i in range(0, count, CHUNK)]


def unit(values):
    center = values - jnp.mean(values, -1, keepdims=True)
    scale = lax.rsqrt(jnp.mean(center * center, -1, keepdims=True) + EPSILON)
    return center * scale, scale


def norm_pull(values, gain, grad):
    normed, scale = unit(values)
    inner = grad * gain
    return scale * (
        inner
        - jnp.mean(inner, -1, keepdims=True)
        - normed * jnp.mean(inner * normed, -1, keepdims=True)
    )


def head_masks():
    left = (iota((1, PAIR), 1) < HALF).astype(F32)
    return left.astype(BF), (1.0 - left).astype(BF)


def stacked(values):
    left, right = head_masks()
    return jnp.concatenate([values * left, values * right], axis=0)


def merged(values):
    count = values.shape[0] // 2
    lanes = iota((count, PAIR), 1) < HALF
    return jnp.where(lanes, values[:count], values[count:])


def lane_sums(values):
    lanes = iota(values.shape, 1) < HALF
    first = jnp.sum(jnp.where(lanes, values, 0.0), -1, keepdims=True)
    second = jnp.sum(jnp.where(lanes, 0.0, values), -1, keepdims=True)
    return first, second


def fetch(sources, targets, sems):
    copies = [
        pltpu.make_async_copy(source, target, sems.at[i])
        for i, (source, target) in enumerate(zip(sources, targets))
    ]
    for copy in copies:
        copy.start()
    return copies


def call(body, ins, kinds, outs, scratch, flops, name):
    any_spec = pl.BlockSpec(memory_space=pl.ANY)
    vmem_spec = pl.BlockSpec(memory_space=pltpu.VMEM)
    moved = sum(x.size * x.dtype.itemsize for x in ins)
    moved += sum(int(np.prod(s)) * jnp.dtype(t).itemsize for s, t in outs)
    single = len(outs) == 1
    shapes = [jax.ShapeDtypeStruct(s, t) for s, t in outs]
    return pl.pallas_call(
        body,
        name=name,
        out_shape=shapes[0] if single else shapes,
        in_specs=[any_spec if k == "h" else vmem_spec for k in kinds],
        out_specs=vmem_spec if single else [vmem_spec] * len(outs),
        scratch_shapes=scratch,
        compiler_params=pltpu.CompilerParams(vmem_limit_bytes=VMEM_BYTES),
        cost_estimate=pl.CostEstimate(
            flops=int(flops), bytes_accessed=int(moved), transcendentals=0
        ),
    )(*ins)


def place_kernel(tile_ref, cell_ref, obs_ref, pay_ref, place_ref, *, devices, cap, wide):
    rows, model = obs_ref.shape
    slots = devices * cap
    tile = tile_ref[...]
    member = tile == iota((rows, devices), 1)
    earlier = (iota((rows, rows), 1) < iota((rows, rows), 0)).astype(F32).astype(BF)
    before = dot(earlier, member.astype(F32).astype(BF))
    rank = jnp.sum(jnp.where(member, before, 0.0), -1, keepdims=True).astype(jnp.int32)
    slot = tile * cap + rank
    placing = (slot == iota((rows, slots), 1)).astype(F32).astype(BF)
    place_ref[...] = placing
    cell = cell_ref[...]
    shift = wide.bit_length() - 1
    lane = iota((rows, 128), 1)
    codes = jnp.where(
        lane == 0, (cell >> shift) + 1, jnp.where(lane == 1, (cell & (wide - 1)) + 1, 0)
    )
    pay_ref[:, model:] = dot(placing, codes.astype(F32).astype(BF), TN).astype(BF)
    for j in range(0, model, TILE):
        pay_ref[:, j : j + TILE] = dot(placing, obs_ref[:, j : j + TILE], TN).astype(BF)


def grid_kernel(
    grid_ref, cot_ref, gain_ref, wq_hbm, wp_hbm, wd_hbm, q_ref, own_ref, dh_ref,
    nrm, wq, wp, wd, sems,
):
    copies = fetch([wq_hbm, wp_hbm, wd_hbm], [wq, wp, wd], sems)
    cells, model = grid_ref.shape
    for rows in row_chunks(cells):
        normed, _ = unit(grid_ref[rows, :].astype(F32))
        nrm[rows, :] = (normed * gain_ref[0:1, :]).astype(BF)
    copies[0].wait()

    def query(j):
        q_ref[:, pl.ds(j, TILE)] = (
            dot(nrm[...], wq[:, pl.ds(j, TILE)]) * HALF ** (-0.5)
        ).astype(BF)

    tiles_of(model, query)
    copies[1].wait()

    def own(j):
        own_ref[:, pl.ds(j, TILE)] = dot(nrm[...], wp[:, pl.ds(j, TILE)]).astype(BF)

    tiles_of(2 * model, own)
    copies[2].wait()

    def hidden(j):
        dh_ref[:, pl.ds(j, TILE)] = dot(cot_ref[...], wd[pl.ds(j, TILE), :], NT).astype(BF)

    tiles_of(dh_ref.shape[1], hidden)


def cross_kernel(
    arr_ref, grid_ref, q_ref, own_ref, gain_ref, wp_hbm, wo_hbm,
    state_ref, nrm_ref, pairs_ref, wts_ref, mix_ref, ow_ref,
    wp, wo, scores, bias, sems, *, wide,
):
    copies = fetch([wp_hbm, wo_hbm], [wp, wo], sems)
    cells, model = grid_ref.shape
    slots = arr_ref.shape[0]
    pick = (iota((8, 128), 0) == iota((8, 128), 1)).astype(F32).astype(BF)
    codes = dot(pick, arr_ref[:, model:], NT)
    cell = iota((cells, slots), 0)
    shift = wide.bit_length() - 1
    row_gap = (cell >> shift).astype(F32) - (codes[0:1] - 1.0)
    col_gap = (cell & (wide - 1)).astype(F32) - (codes[1:2] - 1.0)
    near = -(row_gap * row_gap + col_gap * col_gap) * (1.0 / SPREAD)
    bias[...] = jnp.where(codes[0:1] > 0.5, near, LOW_SCORE)
    copies[0].wait()

    def project(j):
        pairs_ref[:, pl.ds(j, TILE)] = dot(
            arr_ref[:, :model], wp[:, pl.ds(j, TILE)]
        ).astype(BF)

    tiles_of(2 * model, project)

    @pl.loop(0, model // PAIR)
    def _(h):
        keys = pl.ds(pl.multiple_of(h * PAIR, PAIR), PAIR)
        vals = pl.ds(pl.multiple_of(model + h * PAIR, PAIR), PAIR)
        q = q_ref[:, keys]
        scores[...] = dot(stacked(q), pairs_ref[:, keys], NT)
        own_scores = lane_sums(q.astype(F32) * own_ref[:, keys].astype(F32))
        own_weights = []
        for side in range(2):
            parts = []
            for i in range(0, cells, CHUNK):
                own_score = own_scores[side][i : i + CHUNK]
                x = scores[pl.ds(side * cells + i, CHUNK), :] + bias[pl.ds(i, CHUNK), :]
                peak = jnp.maximum(jnp.max(x, -1, keepdims=True), own_score)
                x = jnp.exp(x - peak)
                own_weight = jnp.exp(own_score - peak)
                inverse = 1.0 / (jnp.sum(x, -1, keepdims=True) + own_weight)
                wts_ref[h, pl.ds(side * cells + i, CHUNK), :] = (x * inverse).astype(BF)
                parts.append(own_weight * inverse)
            own_weights.append(jnp.concatenate(parts, axis=0))
        lanes = iota((cells, PAIR), 1) < HALF
        weight = jnp.where(lanes, own_weights[0], own_weights[1]).astype(BF)
        ow_ref[:, keys] = weight
        mix = merged(dot(wts_ref[h], pairs_ref[:, vals]))
        mix_ref[:, keys] = (
            mix + weight.astype(F32) * own_ref[:, vals].astype(F32)
        ).astype(BF)

    copies[1].wait()

    def project_out(j):
        state_ref[:, pl.ds(j, TILE)] = grid_ref[:, pl.ds(j, TILE)].astype(F32) + dot(
            mix_ref[...], wo[:, pl.ds(j, TILE)]
        )

    tiles_of(model, project_out)
    for rows in row_chunks(cells):
        normed, _ = unit(state_ref[rows, :])
        nrm_ref[rows, :] = (normed * gain_ref[1:2, :]).astype(BF)


def near_own_kernel(nrm_ref, w_hbm, q_ref, kv_ref, w, sems):
    cells, model = nrm_ref.shape
    copies = fetch(
        [w_hbm.at[:, pl.ds(0, model)], w_hbm.at[:, pl.ds(model, 2 * model)]],
        [w.at[:, pl.ds(0, model)], w.at[:, pl.ds(model, 2 * model)]],
        sems,
    )
    copies[0].wait()

    def query(j):
        q_ref[:, pl.ds(j, TILE)] = (
            dot(nrm_ref[...], w[:, pl.ds(j, TILE)]) * HALF ** (-0.5)
        ).astype(BF)

    tiles_of(model, query)
    copies[1].wait()

    def pairs(j):
        kv_ref[:, pl.ds(j, TILE)] = dot(
            nrm_ref[...], w[:, pl.ds(pl.multiple_of(model + j, TILE), TILE)]
        ).astype(BF)

    tiles_of(2 * model, pairs)


def rim_kernel(own_ref, north_ref, south_ref, sel_ref, west_ref, east_ref, ext):
    cells, model = own_ref.shape
    rim = north_ref.shape[0]
    ext[pl.ds(0, cells), :] = own_ref[...]
    ext[pl.ds(cells, rim), :] = north_ref[...]
    ext[pl.ds(cells + rim, rim), :] = south_ref[...]
    side = west_ref.shape[0]

    def pick(j):
        both = dot(sel_ref[...], ext[:, pl.ds(j, TILE)]).astype(BF)
        west_ref[:, pl.ds(j, TILE)] = both[:side]
        east_ref[:, pl.ds(j, TILE)] = both[side:]

    tiles_of(model, pick)


def near_rows_kernel(north_ref, south_ref, w_hbm, kv_ref, x, w, sems):
    rim, model = north_ref.shape
    copies = fetch([w_hbm.at[:, pl.ds(model, 2 * model)]], [w], sems)
    x[pl.ds(0, rim), :] = north_ref[...]
    x[pl.ds(rim, rim), :] = south_ref[...]
    copies[0].wait()

    def pairs(j):
        kv_ref[:, pl.ds(j, TILE)] = dot(x[...], w[:, pl.ds(j, TILE)]).astype(BF)

    tiles_of(2 * model, pairs)


def near_kernel(
    q_ref, west_ref, east_ref, base_ref, inside_ref, state_ref, cot_ref, dh_ref, gain_ref,
    kvo_hbm, kvr_hbm, wn_hbm, wo_hbm, wu_hbm,
    after_ref, hid_ref, dwest_ref, deast_ref, dqkv_ref, drows_ref, dafter_ref,
    wkv, wo, wu, kv, dkv, x, wts, scores, ds, bias, mix, nrm, du, acc, dab, dmix, sems,
):
    cells, model = state_ref.shape
    keys_all = kv.shape[0]
    ext = 2 * cells
    side = west_ref.shape[0]
    ends = ext + 2 * side
    copies = fetch(
        [kvo_hbm, kvr_hbm, wn_hbm.at[:, pl.ds(model, 2 * model)], wo_hbm, wu_hbm],
        [kv.at[pl.ds(0, cells), :], kv.at[pl.ds(cells, cells), :], wkv, wo, wu],
        sems,
    )
    x[pl.ds(0, side), :] = west_ref[...]
    x[pl.ds(side, side), :] = east_ref[...]
    kv[pl.ds(ends, keys_all - ends), :] = jnp.zeros((keys_all - ends, 2 * model), BF)
    bias[...] = base_ref[...].astype(F32) + inside_ref[0:1, :]
    copies[0].wait()
    copies[1].wait()
    copies[2].wait()

    def project(j):
        kv[pl.ds(ext, 2 * side), pl.ds(j, TILE)] = dot(
            x[...], wkv[:, pl.ds(j, TILE)]
        ).astype(BF)

    tiles_of(2 * model, project)

    @pl.loop(0, model // PAIR)
    def _(h):
        keys = pl.ds(pl.multiple_of(h * PAIR, PAIR), PAIR)
        vals = pl.ds(pl.multiple_of(model + h * PAIR, PAIR), PAIR)
        scores[...] = dot(stacked(q_ref[:, keys]), kv[:, keys], NT)
        for start in range(0, 2 * cells, CHUNK):
            rows = pl.ds(start, CHUNK)
            v = scores[rows, :] + bias[pl.ds(start % cells, CHUNK), :]
            v = jnp.exp(v - jnp.max(v, -1, keepdims=True))
            inverse = 1.0 / jnp.sum(v, -1, keepdims=True)
            wts[h, rows, :] = (v * inverse).astype(BF)
        mix[:, keys] = merged(dot(wts[h], kv[:, vals])).astype(BF)

    copies[3].wait()

    def project_out(j):
        after_ref[:, pl.ds(j, TILE)] = state_ref[:, pl.ds(j, TILE)] + dot(
            mix[...], wo[:, pl.ds(j, TILE)]
        )

    tiles_of(model, project_out)
    for rows in row_chunks(cells):
        normed, _ = unit(after_ref[rows, :])
        nrm[rows, :] = (normed * gain_ref[2:3, :]).astype(BF)
    copies[4].wait()

    def feed(j):
        cols = pl.ds(j, TILE)
        u = dot(nrm[...], wu[:, cols])
        square = u * u
        t = jnp.tanh(GELU_C * (u + GELU_A * (square * u)))
        half = 0.5 * (1.0 + t)
        hid_ref[:, cols] = (u * half).astype(BF)
        slope = half + (0.5 * GELU_C) * u * (1.0 - t * t) * (1.0 + 3.0 * GELU_A * square)
        du[:, cols] = (dh_ref[:, cols].astype(F32) * slope).astype(BF)

    tiles_of(du.shape[1], feed)

    def feed_back(j):
        acc[:, pl.ds(j, TILE)] = dot(du[...], wu[pl.ds(j, TILE), :], NT)

    tiles_of(model, feed_back)
    for rows in row_chunks(cells):
        grad = acc[rows, :].astype(BF).astype(F32)
        total = cot_ref[rows, :].astype(F32) + norm_pull(
            after_ref[rows, :], gain_ref[2:3, :], grad
        )
        dafter_ref[rows, :] = total
        dab[rows, :] = total.astype(BF)

    def mix_back(j):
        dmix[:, pl.ds(j, TILE)] = dot(dab[...], wo[pl.ds(j, TILE), :], NT).astype(BF)

    tiles_of(model, mix_back)

    @pl.loop(0, model // PAIR)
    def _(h):
        keys = pl.ds(pl.multiple_of(h * PAIR, PAIR), PAIR)
        vals = pl.ds(pl.multiple_of(model + h * PAIR, PAIR), PAIR)
        grad = dmix[:, keys]
        grad_2 = stacked(grad)
        scores[...] = dot(grad_2, kv[:, vals], NT)
        deltas = lane_sums(grad.astype(F32) * mix[:, keys].astype(F32))
        for s in range(2):
            for i in range(0, cells, CHUNK):
                rows = pl.ds(s * cells + i, CHUNK)
                ds[rows, :] = (
                    wts[h, rows, :].astype(F32)
                    * (scores[rows, :] - deltas[s][i : i + CHUNK])
                ).astype(BF)
        dqkv_ref[:, keys] = (merged(dot(ds[...], kv[:, keys])) * HALF ** (-0.5)).astype(BF)
        dkv[:, keys] = dot(stacked(q_ref[:, keys]), ds[...], TN).T.astype(BF)
        dkv[:, vals] = dot(grad_2, wts[h], TN).T.astype(BF)

    def rim_back(j):
        both = dot(dkv[pl.ds(ext, 2 * side), :], wkv[pl.ds(j, TILE), :], NT).astype(BF)
        dwest_ref[:, pl.ds(j, TILE)] = both[:side]
        deast_ref[:, pl.ds(j, TILE)] = both[side:]

    tiles_of(model, rim_back)
    dqkv_ref[:, pl.ds(model, 2 * model)] = dkv[pl.ds(0, cells), :]
    drows_ref[...] = dkv[pl.ds(cells, cells), :]


def encode_kernel(after_ref, hid_ref, wd_hbm, enc_ref, wd, sems):
    copies = fetch([wd_hbm], [wd], sems)
    copies[0].wait()

    def down(j):
        enc_ref[:, pl.ds(j, TILE)] = (
            after_ref[:, pl.ds(j, TILE)] + dot(hid_ref[...], wd[:, pl.ds(j, TILE)])
        ).astype(BF)

    tiles_of(after_ref.shape[1], down)


def near_back_kernel(dqkv_ref, drows_ref, w_hbm, dn_ref, w, sems):
    copies = fetch([w_hbm], [w], sems)
    cells, wide = dqkv_ref.shape
    model = wide // 3
    copies[0].wait()

    def back(j):
        dn_ref[pl.ds(0, cells), pl.ds(j, TILE)] = dot(dqkv_ref[...], w[pl.ds(j, TILE), :], NT)
        dn_ref[pl.ds(cells, cells), pl.ds(j, TILE)] = dot(
            drows_ref[...], w[pl.ds(j, TILE), pl.ds(model, 2 * model)], NT
        )

    tiles_of(model, back)


def fold_kernel(dn_ref, from_east_ref, from_west_ref, sel_ref, own_ref, north_ref, south_ref, x):
    cells, model = own_ref.shape
    rim = north_ref.shape[0]
    side = from_east_ref.shape[0]
    x[pl.ds(0, side), :] = from_west_ref[...]
    x[pl.ds(side, side), :] = from_east_ref[...]

    def fold(j):
        cols = pl.ds(j, TILE)
        total = dn_ref[:, cols] + dot(sel_ref[...], x[:, cols], TN)
        own_ref[:, cols] = total[:cells]
        north_ref[:, cols] = total[cells : cells + rim].astype(BF)
        south_ref[:, cols] = total[cells + rim :].astype(BF)

    tiles_of(model, fold)


def cross_back_kernel(
    dn_ref, north_ref, south_ref, state_ref, dafter_ref, gain_ref, q_ref, own_ref, pairs_ref,
    wts_ref, mix_ref, ow_ref, wp_hbm, wo_hbm,
    dstate_ref, slot_ref, dq_ref, down_ref,
    wp, wo, dsb, dmix, dpairs, scores, ds, sems,
):
    copies = fetch([wo_hbm, wp_hbm], [wo, wp], sems)
    cells, model = state_ref.shape
    rim = north_ref.shape[0]
    for i in range(0, cells, CHUNK):
        rows = pl.ds(i, CHUNK)
        other = north_ref[rows, :] if i < rim else south_ref[pl.ds(i - rim, CHUNK), :]
        grad = (dn_ref[rows, :] + other.astype(F32)).astype(BF).astype(F32)
        total = dafter_ref[rows, :] + norm_pull(state_ref[rows, :], gain_ref[1:2, :], grad)
        dstate_ref[rows, :] = total
        dsb[rows, :] = total.astype(BF)
    copies[0].wait()

    def mix_back(j):
        dmix[:, pl.ds(j, TILE)] = dot(dsb[...], wo[pl.ds(j, TILE), :], NT).astype(BF)

    tiles_of(model, mix_back)

    @pl.loop(0, model // PAIR)
    def _(h):
        keys = pl.ds(pl.multiple_of(h * PAIR, PAIR), PAIR)
        vals = pl.ds(pl.multiple_of(model + h * PAIR, PAIR), PAIR)
        grad = dmix[:, keys]
        grad_2 = stacked(grad)
        grad_f = grad.astype(F32)
        scores[...] = dot(grad_2, pairs_ref[:, vals], NT)
        deltas = lane_sums(grad_f * mix_ref[:, keys].astype(F32))
        own_dots = lane_sums(grad_f * own_ref[:, vals].astype(F32))
        for s in range(2):
            for i in range(0, cells, CHUNK):
                rows = pl.ds(s * cells + i, CHUNK)
                ds[rows, :] = (
                    wts_ref[h, rows, :].astype(F32)
                    * (scores[rows, :] - deltas[s][i : i + CHUNK])
                ).astype(BF)
        lanes = iota((cells, PAIR), 1) < HALF
        weight = ow_ref[:, keys].astype(F32)
        own_grad = weight * jnp.where(
            lanes, own_dots[0] - deltas[0], own_dots[1] - deltas[1]
        )
        q = q_ref[:, keys]
        dq = merged(dot(ds[...], pairs_ref[:, keys])) + own_grad * own_ref[:, keys].astype(F32)
        dq_ref[:, keys] = (dq * HALF ** (-0.5)).astype(BF)
        down_ref[:, keys] = (own_grad * q.astype(F32)).astype(BF)
        down_ref[:, vals] = (weight * grad_f).astype(BF)
        dpairs[:, keys] = dot(stacked(q), ds[...], TN).T.astype(BF)
        dpairs[:, vals] = dot(grad_2, wts_ref[h], TN).T.astype(BF)

    copies[1].wait()

    def slot_back(j):
        slot_ref[:, pl.ds(j, TILE)] = dot(dpairs[...], wp[pl.ds(j, TILE), :], NT).astype(BF)

    tiles_of(model, slot_back)


def grid_back_kernel(
    grid_ref, dstate_ref, gain_ref, dq_ref, down_ref, wq_hbm, wp_hbm, out_ref, wq, wp, acc, sems
):
    copies = fetch([wq_hbm, wp_hbm], [wq, wp], sems)
    cells, model = grid_ref.shape
    for copy in copies:
        copy.wait()

    def back(j):
        acc[:, pl.ds(j, TILE)] = dot(dq_ref[...], wq[pl.ds(j, TILE), :], NT) + dot(
            down_ref[...], wp[pl.ds(j, TILE), :], NT
        )

    tiles_of(model, back)
    for rows in row_chunks(cells):
        grad = acc[rows, :].astype(BF).astype(F32)
        out_ref[rows, :] = (
            dstate_ref[rows, :]
            + norm_pull(grid_ref[rows, :].astype(F32), gain_ref[0:1, :], grad)
        ).astype(BF)


def ring(value, by):
    size = lax.axis_size("lon")
    return lax.ppermute(value, "lon", [(i, (i + by) % size) for i in range(size)])


def line(value, by):
    size = lax.axis_size("lat")
    pairs = [(i, i + by) for i in range(size) if 0 <= i + by < size]
    return lax.ppermute(value, "lat", pairs)


def key_places(rows_lat, rows_lon):
    places = [(r, c) for r in range(rows_lat) for c in range(rows_lon)]
    places += [(r, c) for r in range(-RADIUS, 0) for c in range(rows_lon)]
    places += [(rows_lat + r, c) for r in range(RADIUS) for c in range(rows_lon)]
    ext = list(places)
    tall = range(-RADIUS, rows_lat + RADIUS)
    places += [(r, c) for r in tall for c in range(-RADIUS, 0)]
    places += [(r, rows_lon + c) for r in tall for c in range(RADIUS)]
    return np.array(places), ext


def per_device(
    grid_state, observations, obs_tile, obs_cell, cotangent, norm_gains,
    w_cross_query, w_cross_pairs, w_cross_out, w_near_proj, w_near_out, w_up, w_down,
):
    rows_lat, rows_lon, model = grid_state.shape
    lat_count = lax.axis_size("lat")
    devices = lat_count * lax.axis_size("lon")
    rows_obs = observations.shape[0]
    cap = max(2, 2 * rows_obs // devices)
    slots = devices * cap
    cells = rows_lat * rows_lon
    ff = w_up.shape[1]
    pairs_n = model // PAIR
    rim = RADIUS * rows_lon
    side = RADIUS * (rows_lat + 2 * RADIUS)
    places, ext_places = key_places(rows_lat, rows_lon)
    keys_n = len(places)
    keys_all = -(-keys_n // 256) * 256
    spot = {place: i for i, place in enumerate(ext_places)}
    tall = range(-RADIUS, rows_lat + RADIUS)
    select = np.zeros((2 * side, len(ext_places)), np.float32)
    for i, r in enumerate(tall):
        for c in range(RADIUS):
            select[i * RADIUS + c, spot[(r, c)]] = 1.0
            select[side + i * RADIUS + c, spot[(r, rows_lon - RADIUS + c)]] = 1.0
    select = jnp.asarray(select.astype(jnp.bfloat16))
    base = np.full((cells, keys_all), LOW_SCORE, np.float32)
    own_rows, own_cols = places[:cells, 0], places[:cells, 1]
    allowed = (np.abs(places[None, :, 0] - own_rows[:, None]) <= RADIUS) & (
        np.abs(places[None, :, 1] - own_cols[:, None]) <= RADIUS
    )
    base[:, :keys_n][allowed] = 0.0
    base = jnp.asarray(base.astype(jnp.bfloat16))
    key_rows = np.zeros((8, keys_all), np.int32)
    key_rows[:, :keys_n] = places[None, :, 0]
    key_lat = jnp.asarray(key_rows) + lax.axis_index("lat") * rows_lat
    inside = jnp.where((key_lat >= 0) & (key_lat < rows_lat * lat_count), 0.0, LOW_SCORE)
    inside = inside.astype(F32)

    dma = pltpu.SemaphoreType.DMA
    vm = pltpu.VMEM
    flat = grid_state.reshape(cells, model)
    cot = cotangent.reshape(cells, model)

    payload, placing = call(
        functools.partial(place_kernel, devices=devices, cap=cap, wide=rows_lon),
        (obs_tile, obs_cell, observations), "vvv",
        [((slots, model + 128), BF), ((rows_obs, slots), BF)], [],
        2 * rows_obs * slots * model, "place",
    )
    arrived = lax.all_to_all(
        payload.reshape(devices, cap, model + 128), ("lat", "lon"), 0, 0, tiled=True
    ).reshape(slots, model + 128)
    q_c, own_pairs, dhid = call(
        grid_kernel,
        (flat, cot, norm_gains, w_cross_query, w_cross_pairs, w_down), "vvvhhh",
        [((cells, model), BF), ((cells, 2 * model), BF), ((cells, ff), BF)],
        [vm((cells, model), BF), vm((model, model), BF), vm((model, 2 * model), BF),
         vm((ff, model), BF), dma((3,))],
        2 * cells * model * (3 * model + ff), "grid_proj",
    )
    state, normal, slot_pairs, cross_w, cross_mix, own_w = call(
        functools.partial(cross_kernel, wide=rows_lon),
        (arrived, flat, q_c, own_pairs, norm_gains, w_cross_pairs, w_cross_out), "vvvvvhh",
        [((cells, model), F32), ((cells, model), BF), ((slots, 2 * model), BF),
         ((pairs_n, 2 * cells, slots), BF), ((cells, model), BF), ((cells, model), BF)],
        [vm((model, 2 * model), BF), vm((model, model), BF), vm((2 * cells, slots), F32),
         vm((cells, slots), F32), dma((2,))],
        2 * slots * model * 2 * model * 2, "cross",
    )
    south = line(normal[:rim], -1)
    north = line(normal[cells - rim :], 1)
    q_n, kv_own = call(
        near_own_kernel, (normal, w_near_proj), "vh",
        [((cells, model), BF), ((cells, 2 * model), BF)],
        [vm((model, 3 * model), BF), dma((2,))],
        2 * cells * model * 3 * model, "near_own",
    )
    west_send, east_send = call(
        rim_kernel, (normal, north, south, select), "vvvv",
        [((side, model), BF), ((side, model), BF)],
        [vm((cells + 2 * rim, model), BF)],
        2 * 2 * side * 2 * cells * model, "rim",
    )
    east = ring(west_send, -1)
    west = ring(east_send, 1)
    kv_rows = call(
        near_rows_kernel, (north, south, w_near_proj), "vvh",
        [((2 * rim, 2 * model), BF)],
        [vm((2 * rim, model), BF), vm((model, 2 * model), BF), dma((1,))],
        2 * 2 * rim * model * 2 * model, "near_rows",
    )
    after, hidden, dwest, deast, dqkv, drows, dafter = call(
        near_kernel,
        (q_n, west, east, base, inside, state, cot, dhid, norm_gains, kv_own, kv_rows,
         w_near_proj, w_near_out, w_up), "vvvvvvvvvhhhhh",
        [((cells, model), F32), ((cells, ff), BF), ((side, model), BF), ((side, model), BF),
         ((cells, 3 * model), BF), ((2 * rim, 2 * model), BF), ((cells, model), F32)],
        [vm((model, 2 * model), BF), vm((model, model), BF), vm((model, ff), BF),
         vm((keys_all, 2 * model), BF), vm((keys_all, 2 * model), BF),
         vm((2 * side, model), BF), vm((pairs_n, 2 * cells, keys_all), BF),
         vm((2 * cells, keys_all), F32), vm((2 * cells, keys_all), BF),
         vm((cells, keys_all), F32), vm((cells, model), BF), vm((cells, model), BF),
         vm((cells, ff), BF), vm((cells, model), F32), vm((cells, model), BF),
         vm((cells, model), BF), dma((5,))],
        2e10, "near",
    )
    from_east = ring(dwest, -1)
    from_west = ring(deast, 1)
    dn_ext = call(
        near_back_kernel, (dqkv, drows, w_near_proj), "vvh",
        [((cells + 2 * rim, model), F32)],
        [vm((model, 3 * model), BF), dma((1,))],
        2 * cells * model * 5 * model, "near_back",
    )
    dn_own, dnorth, dsouth = call(
        fold_kernel, (dn_ext, from_east, from_west, select), "vvvv",
        [((cells, model), F32), ((rim, model), BF), ((rim, model), BF)],
        [vm((2 * side, model), BF)],
        2 * 2 * side * 2 * cells * model, "fold",
    )
    from_south = line(dnorth, -1)
    from_north = line(dsouth, 1)
    encoded = call(
        encode_kernel, (after, hidden, w_down), "vvh", [((cells, model), BF)],
        [vm((ff, model), BF), dma((1,))], 2 * cells * model * ff, "encode",
    )
    dstate, slot_grads, dq, down = call(
        cross_back_kernel,
        (dn_own, from_north, from_south, state, dafter, norm_gains, q_c, own_pairs, slot_pairs,
         cross_w, cross_mix, own_w, w_cross_pairs, w_cross_out), "vvvvvvvvvvvvhh",
        [((cells, model), F32), ((slots, model), BF), ((cells, model), BF),
         ((cells, 2 * model), BF)],
        [vm((model, 2 * model), BF), vm((model, model), BF), vm((cells, model), BF),
         vm((cells, model), BF), vm((slots, 2 * model), BF), vm((2 * cells, slots), F32),
         vm((2 * cells, slots), BF), dma((2,))],
        2 * slots * model * 2 * model * 2, "cross_back",
    )
    returned = lax.all_to_all(
        slot_grads.reshape(devices, cap, model), ("lat", "lon"), 0, 0, tiled=True
    ).reshape(slots, model)
    grid_grad = call(
        grid_back_kernel,
        (flat, dstate, norm_gains, dq, down, w_cross_query, w_cross_pairs), "vvvvvhh",
        [((cells, model), BF)],
        [vm((model, model), BF), vm((model, 2 * model), BF), vm((cells, model), F32), dma((2,))],
        2 * cells * model * 3 * model, "grid_back",
    )
    obs_grad = dot(placing, returned).astype(BF)
    shape = (rows_lat, rows_lon, model)
    return encoded.reshape(shape), grid_grad.reshape(shape), obs_grad


def solution(mesh):
    return jax.shard_map(
        per_device,
        mesh=mesh,
        in_specs=(
            P("lat", "lon", None),
            P(("lat", "lon"), None),
            P(("lat", "lon"), None),
            P(("lat", "lon"), None),
            P("lat", "lon", None),
            P(), P(), P(), P(), P(), P(), P(), P(),
        ),
        out_specs=(P("lat", "lon", None), P("lat", "lon", None), P(("lat", "lon"), None)),
        check_vma=False,
    )
```

time: 358 us -> 212 us (0.59); the launches traced: 352 us -> 211 us
  Pallas kernels: 0 us -> 126 us
  matrix products: 97 us -> 1.24 us
  local copies, waits for them, and re-layouts: 88.7 us -> 14.5 us
  other arithmetic: 63.1 us -> 0.61 us
  waiting for transfers between devices: 56.8 us -> 25.6 us
    pallas_call x0 -> x12, Pallas kernels: none -> 126 us  [call(): pl.pallas_call(body, name=name, out_shape=shapes[0] if single else shapes...]
    dot_general x30 -> x1, matrix products: 97 us -> 1.24 us  [dot(): return lax.dot_general(left, right, dims, preferred_element_type=F32)]
    reduce_sum x15 -> x0, other arithmetic: 32.4 us -> none  [the longest x1 6.52 us: cross_attend(): row_peak = jnp.maximum(jnp.max(scores, -1), own_score)]
    ppermute x8, waiting for transfers between devices: 36.5 us -> 10.7 us  [the longest x4 10.7 us: line(): return lax.ppermute(value, 'lat', pairs)]
    slice x17 -> x1, local copies, waits for them, and re-layouts: 24.4 us -> 1.05 us  [per_device(): south = line(normal[:rim], -1)]
    reshape x12 -> x4, local copies, waits for them, and re-layouts: 24.2 us -> 6.91 us  [the longest x1 3.22 us: per_device(): payload.reshape(devices, cap, model + 128)]
    scatter-add x2 -> x0, local copies, waits for them, and re-layouts: 16.6 us -> none  [the longest x1 8.69 us: fold_rims(): middle = middle.at[:, :RADIUS].add(from_west.astype(jnp.float32))]
    convert_element_type x8 -> x0, local copies, waits for them, and re-layouts: 9.16 us -> none  [the longest x2 2.99 us: matmul(): return jnp.dot(left, right, preferred_element_type=jnp.float32)]
  transfers between devices with their start and end apart: 11 -> 10, of which waited for: 8 -> 6; matrix products, arithmetic and copies ran while one was open for 17% -> 0% of each run, Pallas kernels for 0% -> 22%
where the time goes in v1:
time: 212 us; the launch traced here: 211 us
  Pallas kernels  126 us (59%)
  starting transfers between devices  41.4 us (20%)
  waiting for transfers between devices  25.6 us (12%)
  local copies, waits for them, and re-layouts  14.5 us (7%)
    pallas_call x12, Pallas kernels, call(): pl.pallas_call(body, name=name, out_shape=shapes[0] if single else shapes...  126 us
    all_to_all x1, starting transfers between devices, per_device(): lax.all_to_all(slot_grads.reshape(devices, cap, model), ('lat', 'lon'), 0...  12.9 us
    all_to_all x1, starting transfers between devices, per_device(): lax.all_to_all(payload.reshape(devices, cap, model + 128), ('lat', 'lon')...  11.5 us
    ppermute x4, starting transfers between devices, line(): return lax.ppermute(value, 'lat', pairs)  10.7 us
    ppermute x4, waiting for transfers between devices, line(): return lax.ppermute(value, 'lat', pairs)  10.7 us
    all_to_all x1, waiting for transfers between devices, per_device(): lax.all_to_all(payload.reshape(devices, cap, model + 128), ('lat', 'lon')...  10.4 us
    unnamed x22, local copies, waits for them, and re-layouts  6.56 us
    ppermute x4, starting transfers between devices, ring(): lax.ppermute(value, 'lon', [(i, (i + by) % size) for i in range(size)])  6.29 us
  transfers between devices with their start and end apart: 10, of which 6 were waited for; matrix products, arithmetic and copies ran while one was open for 0% of the time, Pallas kernels for 22%

profile of v1, /device:TPU:1, one launch (start us, length us, event | category | flops | bytes accessed | tf_op | source)
XLA Modules:
  0.0 210.7 jit_solution(8210335613809747248)
XLA Ops:
  0.6 1.5 copy.19.tile_ref
  2.1 1.5 copy.20.cell_ref
  3.6 3.2 %place.1 = (bf16[512,1152]{1,0:T(8,128)(2,1)}, bf16[256,512]{1,0:T(8,128)(2,1)}) custom-call(s32[256,1]{1,0:T(8,128)} %copy.19.tile_ref, s32[256,1]{1,0:T(8,128)} %copy.20.cell_ref, bf16[256,1024]{1,0:T(8,128)(2,1)} %obs_ref.1), custom_call_target="tpu_custom_call" | custom-call | flops 268435456 | bytes 1968128 | tf_op jit(solution)/shard_map/place/pallas_call | solution.py:105
  6.7 3.2 %reshape.30 = bf16[128,4,1152]{2,1,0:T(4,128)(2,1)} reshape(bf16[512,1152]{1,0:T(8,128)(2,1)} %get-tuple-element.32) | data formatting | bytes 2359296 | tf_op jit(solution)/shard_map/reshape | solution.py:607
  10.0 11.5 %all-to-all-start = ((bf16[128,4,1152]{2,1,0:T(4,128)(2,1)}), bf16[128,4,1152]{2,1,0:T(4,128)(2,1)S(1)}, u32[]{:S(2)}, u32[]{:S(2)}) async-start(bf16[128,4,1152]{2,1,0:T(4,128)(2,1)} %reshape.30), calls=%async_computation | async-start | bytes 2359296 | tf_op jit(solution)/shard_map/all_to_all | solution.py:606
  21.5 9.9 %grid_proj.1 = (bf16[192,1024]{1,0:T(8,128)(2,1)}, bf16[192,2048]{1,0:T(8,128)(2,1)}, bf16[192,2048]{1,0:T(8,128)(2,1)}) custom-call(bf16[192,1024]{1,0:T(8,128)(2,1)} %bitcast.6, bf16[192,1024]{1,0:T(8,128)(2,1)} %bitcast.9, f32[3,1024]{1,0:T(4,128)} %gain_ref.9, bf16[1024,1024]{1,0:T(8,128)(2,1)} %wq_hbm.3, bf16[1024,2048]{1,0:T(8,128)(2,1)} %wp_hbm.7, ...), custom_call_target="tpu_custom_call" | custom-call | flops 2013265920 | bytes 13250560 | tf_op jit(solution)/shard_map/grid_proj/pallas_call | solution.py:105
  31.4 10.4 %all-to-all-done = bf16[128,4,1152]{2,1,0:T(4,128)(2,1)S(1)} async-done(((bf16[128,4,1152]{2,1,0:T(4,128)(2,1)}), bf16[128,4,1152]{2,1,0:T(4,128)(2,1)S(1)}, u32[]{:S(2)}, u32[]{:S(2)}) %all-to-all-start) | async-done | bytes 1179680 | tf_op jit(solution)/shard_map/all_to_all | solution.py:606
  41.8 1.2 reshape.31.arr_ref
  43.0 0.0 copy-start.7
  43.0 18.2 %cross.1 = (f32[192,1024]{1,0:T(8,128)}, bf16[192,1024]{1,0:T(8,128)(2,1)}, bf16[512,2048]{1,0:T(8,128)(2,1)}, bf16[8,384,512]{2,1,0:T(8,128)(2,1)}, bf16[192,10...) custom-call(bf16[512,1152]{1,0:T(8,128)(2,1)} %reshape.31.arr_ref, bf16[192,1024]{1,0:T(8,128)(2,1)} %bitcast.7, ...), custom_call_target="tpu_custom_call" | custom-call | flops 4294967296 | bytes 16265216 | tf_op jit(solution)/shard_map/cross/pallas_call | solution.py:105
  61.2 1.1 fusion.2
  62.2 1.3 collective-permute-start.1
  63.5 4.0 %collective-permute-start = (bf16[96,1024]{1,0:T(8,128)(2,1)S(1)}, bf16[96,1024]{1,0:T(8,128)(2,1)S(1)}, u32[]{:S(2)}, u32[]{:S(2)}) collective-permute-start(bf16[96,1024]{1,0:T(8,128)(2,1)S(1)} %get-tuple-element.62), channel_id=1, source_target_pairs={{0,16},{16,32},{32,48},{48,64},{64,80},{80,96},{96,112},{1,17},{17... | collective-permute-start | bytes 589832 | tf_op jit(solution)/shard_map/ppermute | solution.py:542
  67.6 3.2 %collective-permute-done.1.south_ref = bf16[96,1024]{1,0:T(8,128)(2,1)S(1)} collective-permute-done((bf16[96,1024]{1,0:T(8,128)(2,1)S(1)}, bf16[96,1024]{1,0:T(8,128)(2,1)S(1)}, u32[]{:S(2)}, u32[]{:S(2)}) %collective-permute-start.1) | collective-permute-done | bytes 196640 | tf_op jit(solution)/shard_map/ppermute | solution.py:542
  70.8 0.0 copy-start
  70.8 1.0 collective-permute-done.north_ref
  71.8 0.0 copy-done
  71.8 0.0 copy-start.1
  71.8 0.7 copy-done.1
  72.5 3.0 %rim.1 = (bf16[144,1024]{1,0:T(8,128)(2,1)}, bf16[144,1024]{1,0:T(8,128)(2,1)}) custom-call(bf16[192,1024]{1,0:T(8,128)(2,1)} %get-tuple-element.35.nrm_ref.own_ref, bf16[96,1024]{1,0:T(8,128)(2,1)} %copy-done.1, bf16[96,1024]{1,0:T(8,128)(2,1)} %copy-done, bf16[288,384]{1,0:T(8,128)(2,1)} %constant.22.clone.sel_ref), custom_call_target="tpu_custom_call" | custom-call | flops 226492416 | bytes 1597440 | tf_op jit(solution)/shard_map/rim/pallas_call | solution.py:105
  75.5 1.7 collective-permute-start.2
  77.2 0.0 collective-permute-start.3
  77.2 0.0 copy-done.7
  77.2 0.6 fusion.1.inside_ref
  77.9 7.0 %near_own.1 = (bf16[192,1024]{1,0:T(8,128)(2,1)}, bf16[192,2048]{1,0:T(8,128)(2,1)}) custom-call(bf16[192,1024]{1,0:T(8,128)(2,1)} %get-tuple-element.35.nrm_ref.own_ref, bf16[1024,3072]{1,0:T(8,128)(2,1)} %w_hbm.5), custom_call_target="tpu_custom_call" | custom-call | flops 1207959552 | bytes 7864320 | tf_op jit(solution)/shard_map/near_own/pallas_call | solution.py:105
  84.9 6.4 %near_rows.1.kvr_hbm = bf16[192,2048]{1,0:T(8,128)(2,1)} custom-call(bf16[96,1024]{1,0:T(8,128)(2,1)} %copy-done.1, bf16[96,1024]{1,0:T(8,128)(2,1)} %copy-done, bf16[1024,3072]{1,0:T(8,128)(2,1)} %w_hbm.5), custom_call_target="tpu_custom_call" | custom-call | flops 805306368 | bytes 7471104 | tf_op jit(solution)/shard_map/near_rows/pallas_call | solution.py:105
  91.4 0.0 collective-permute-done.2.west_ref
  91.4 0.0 copy-start.8
  91.4 0.0 collective-permute-done.3.east_ref
  91.4 0.0 copy-start.9
  91.4 0.7 copy-done.8
  92.1 0.1 copy-done.9
  92.2 34.5 %near.1 = (f32[192,1024]{1,0:T(8,128)}, bf16[192,2048]{1,0:T(8,128)(2,1)}, bf16[144,1024]{1,0:T(8,128)(2,1)}, bf16[144,1024]{1,0:T(8,128)(2,1)}, bf16[192,3072]{...) custom-call(bf16[192,1024]{1,0:T(8,128)(2,1)} %get-tuple-element.36.q_ref, ...), custom_call_target="tpu_custom_call" | custom-call | flops 20000000000 | bytes 22351872 | tf_op jit(solution)/shard_map/near/pallas_call | solution.py:105
  126.7 4.5 %collective-permute-start.4 = (bf16[144,1024]{1,0:T(8,128)(2,1)}, bf16[144,1024]{1,0:T(8,128)(2,1)S(1)}, u32[]{:S(2)}, u32[]{:S(2)}) collective-permute-start(bf16[144,1024]{1,0:T(8,128)(2,1)} %get-tuple-element.46), channel_id=1, source_target_pairs={{0,15},{1,0},{2,1},{3,2},{4,3},{5,4},{6,5},{7,6},{8,7},{9,8},{10,9... | collective-permute-start | bytes 884744 | tf_op jit(solution)/shard_map/ppermute | solution.py:536
  131.2 0.0 collective-permute-start.5
  131.2 9.5 %near_back.1.dn_ref = f32[384,1024]{1,0:T(8,128)} custom-call(bf16[192,3072]{1,0:T(8,128)(2,1)} %get-tuple-element.44.dqkv_ref, bf16[192,2048]{1,0:T(8,128)(2,1)} %get-tuple-element.45.drows_ref, bf16[1024,3072]{1,0:T(8,128)(2,1)} %w_hbm.5), custom_call_target="tpu_custom_call" | custom-call | flops 2013265920 | bytes 9830400 | tf_op jit(solution)/shard_map/near_back/pallas_call | solution.py:105
  140.8 0.0 collective-permute-done.4.from_east_ref
  140.8 0.0 copy-start.2
  140.8 0.0 collective-permute-done.5.from_west_ref
  140.8 0.7 copy-done.2
  141.5 0.0 copy-start.3
  141.5 0.7 copy-done.3
  142.2 3.8 %fold.1 = (f32[192,1024]{1,0:T(8,128)}, bf16[96,1024]{1,0:T(8,128)(2,1)}, bf16[96,1024]{1,0:T(8,128)(2,1)}) custom-call(f32[384,1024]{1,0:T(8,128)} %near_back.1.dn_ref, bf16[144,1024]{1,0:T(8,128)(2,1)} %copy-done.2, bf16[144,1024]{1,0:T(8,128)(2,1)} %copy-done.3, bf16[288,384]{1,0:T(8,128)(2,1)} %constant.22.clone.sel_ref), custom_call_target="tpu_custom_call" | custom-call | flops 226492416 | bytes 3563520 | tf_op jit(solution)/shard_map/fold/pallas_call | solution.py:105
  146.1 4.1 %collective-permute-start.6 = (bf16[96,1024]{1,0:T(8,128)(2,1)}, bf16[96,1024]{1,0:T(8,128)(2,1)S(1)}, u32[]{:S(2)}, u32[]{:S(2)}) collective-permute-start(bf16[96,1024]{1,0:T(8,128)(2,1)} %get-tuple-element.49), channel_id=1, source_target_pairs={{0,16},{16,32},{32,48},{48,64},{64,80},{80,96},{96,112},{1,17},{17... | collective-permute-start | bytes 589832 | tf_op jit(solution)/shard_map/ppermute | solution.py:542
  150.2 1.3 collective-permute-start.7
  151.5 2.7 %collective-permute-done.6.north_ref = bf16[96,1024]{1,0:T(8,128)(2,1)S(1)} collective-permute-done((bf16[96,1024]{1,0:T(8,128)(2,1)}, bf16[96,1024]{1,0:T(8,128)(2,1)S(1)}, u32[]{:S(2)}, u32[]{:S(2)}) %collective-permute-start.6) | collective-permute-done | bytes 196640 | tf_op jit(solution)/shard_map/ppermute | solution.py:542
  154.2 0.0 copy-start.5
  154.2 3.7 %collective-permute-done.7.south_ref = bf16[96,1024]{1,0:T(8,128)(2,1)S(1)} collective-permute-done((bf16[96,1024]{1,0:T(8,128)(2,1)}, bf16[96,1024]{1,0:T(8,128)(2,1)S(1)}, u32[]{:S(2)}, u32[]{:S(2)}) %collective-permute-start.7) | collective-permute-done | bytes 196640 | tf_op jit(solution)/shard_map/ppermute | solution.py:542
  157.9 0.0 copy-start.6
  157.9 0.0 copy-done.5
  157.9 0.7 copy-done.6
  158.6 16.5 %cross_back.1 = (f32[192,1024]{1,0:T(8,128)}, bf16[512,1024]{1,0:T(8,128)(2,1)}, bf16[192,1024]{1,0:T(8,128)(2,1)}, bf16[192,2048]{1,0:T(8,128)(2,1)}) custom-call(f32[192,1024]{1,0:T(8,128)} %get-tuple-element.48.dn_ref, bf16[96,1024]{1,0:T(8,128)(2,1)} %copy-done.5, bf16[96,1024]{1,0:T(8,128)(2,1)} %copy-done.6, f32[192,1024]{1,0:T(8,128)} %get-tuple-element.39.state_ref, ...), custom_call_target="tpu_custom_call" | custom-call | flops 4294967296 | bytes 19279872 | tf_op jit(solution)/shard_map/cross_back/pallas_call | solution.py:105
  175.1 2.3 %reshape.36 = bf16[128,4,1024]{2,1,0:T(4,128)(2,1)} reshape(bf16[512,1024]{1,0:T(8,128)(2,1)} %get-tuple-element.60) | data formatting | bytes 2097152 | tf_op jit(solution)/shard_map/reshape | solution.py:695
  177.3 12.9 %all-to-all-start.1 = ((bf16[128,4,1024]{2,1,0:T(4,128)(2,1)}), bf16[128,4,1024]{2,1,0:T(4,128)(2,1)S(1)}, u32[]{:S(2)}, u32[]{:S(2)}) async-start(bf16[128,4,1024]{2,1,0:T(4,128)(2,1)} %reshape.36), calls=%async_computation.1 | async-start | bytes 2097152 | tf_op jit(solution)/shard_map/all_to_all | solution.py:694
  190.2 5.9 %encode.1 = bf16[192,1024]{1,0:T(8,128)(2,1)} custom-call(f32[192,1024]{1,0:T(8,128)} %get-tuple-element.42.after_ref, bf16[192,2048]{1,0:T(8,128)(2,1)} %get-tuple-element.43.hid_ref, bf16[2048,1024]{1,0:T(8,128)(2,1)} %wd_hbm.3), custom_call_target="tpu_custom_call" | custom-call | flops 805306368 | bytes 6160384 | tf_op jit(solution)/shard_map/encode/pallas_call | solution.py:105
  196.2 8.4 %grid_back.1 = bf16[192,1024]{1,0:T(8,128)(2,1)} custom-call(bf16[192,1024]{1,0:T(8,128)(2,1)} %bitcast.8, f32[192,1024]{1,0:T(8,128)} %get-tuple-element.56.dstate_ref, f32[3,1024]{1,0:T(4,128)} %gain_ref.9, bf16[192,1024]{1,0:T(8,128)(2,1)} %get-tuple-element.57.dq_ref, bf16[192,2048]{1,0:T(8,128)(2,1)} %get-tuple-element.58.down_ref, ...), custom_call_target="tpu_custom_call" | custom-call | flops 1207959552 | bytes 9056256 | tf_op jit(solution)/shard_map/grid_back/pallas_call | solution.py:105
  204.6 0.0 copy-start.4
  204.6 4.6 %all-to-all-done.1 = bf16[128,4,1024]{2,1,0:T(4,128)(2,1)S(1)} async-done(((bf16[128,4,1024]{2,1,0:T(4,128)(2,1)}), bf16[128,4,1024]{2,1,0:T(4,128)(2,1)S(1)}, u32[]{:S(2)}, u32[]{:S(2)}) %all-to-all-start.1) | async-done | bytes 1048608 | tf_op jit(solution)/shard_map/all_to_all | solution.py:694
  209.2 0.3 reshape.37
  209.4 0.0 copy-done.4
  209.4 1.2 convolution_convert_fusion
Async XLA Ops:
  10.0 31.8 %all-to-all-start = ((bf16[128,4,1152]{2,1,0:T(4,128)(2,1)}), bf16[128,4,1152]{2,1,0:T(4,128)(2,1)S(1)}, u32[]{:S(2)}, u32[]{:S(2)}) async-start(bf16[128,4,1152]{2,1,0:T(4,128)(2,1)} %reshape.30), calls=%async_computation | async-start | bytes 2359296 | tf_op jit(solution)/shard_map/all_to_all | solution.py:606
  43.0 34.3 %copy-start.7 = (s32[8,768]{1,0:T(8,128)S(1)}, s32[8,768]{1,0:T(8,128)}, u32[]{:S(2)}) copy-start(s32[8,768]{1,0:T(8,128)} %constant.24.clone) | copy-start | bytes 73732
  62.2 8.5 %collective-permute-start.1 = (bf16[96,1024]{1,0:T(8,128)(2,1)S(1)}, bf16[96,1024]{1,0:T(8,128)(2,1)S(1)}, u32[]{:S(2)}, u32[]{:S(2)}) collective-permute-start(bf16[96,1024]{1,0:T(8,128)(2,1)S(1)} %get-tuple-element.61), channel_id=1, source_target_pairs={{16,0},{32,16},{48,32},{64,48},{80,64},{96,80},{112,96},{17,1},{33... | collective-permute-start | bytes 589832 | tf_op jit(solution)/shard_map/ppermute | solution.py:542
  63.5 8.2 %collective-permute-start = (bf16[96,1024]{1,0:T(8,128)(2,1)S(1)}, bf16[96,1024]{1,0:T(8,128)(2,1)S(1)}, u32[]{:S(2)}, u32[]{:S(2)}) collective-permute-start(bf16[96,1024]{1,0:T(8,128)(2,1)S(1)} %get-tuple-element.62), channel_id=1, source_target_pairs={{0,16},{16,32},{32,48},{48,64},{64,80},{80,96},{96,112},{1,17},{17... | collective-permute-start | bytes 589832 | tf_op jit(solution)/shard_map/ppermute | solution.py:542
  70.8 1.0 copy-start
  71.8 0.7 copy-start.1
  75.5 15.9 %collective-permute-start.2 = (bf16[144,1024]{1,0:T(8,128)(2,1)}, bf16[144,1024]{1,0:T(8,128)(2,1)S(1)}, u32[]{:S(2)}, u32[]{:S(2)}) collective-permute-start(bf16[144,1024]{1,0:T(8,128)(2,1)} %get-tuple-element.37), channel_id=1, source_target_pairs={{0,1},{1,2},{2,3},{3,4},{4,5},{5,6},{6,7},{7,8},{8,9},{9,10},{10,1... | collective-permute-start | bytes 884744 | tf_op jit(solution)/shard_map/ppermute | solution.py:536
  77.2 14.1 %collective-permute-start.3 = (bf16[144,1024]{1,0:T(8,128)(2,1)}, bf16[144,1024]{1,0:T(8,128)(2,1)S(1)}, u32[]{:S(2)}, u32[]{:S(2)}) collective-permute-start(bf16[144,1024]{1,0:T(8,128)(2,1)} %get-tuple-element.38), channel_id=1, source_target_pairs={{0,15},{1,0},{2,1},{3,2},{4,3},{5,4},{6,5},{7,6},{8,7},{9,8},{10,9... | collective-permute-start | bytes 884744 | tf_op jit(solution)/shard_map/ppermute | solution.py:536
  91.4 0.7 copy-start.8
  91.4 0.8 copy-start.9
  126.7 14.1 %collective-permute-start.4 = (bf16[144,1024]{1,0:T(8,128)(2,1)}, bf16[144,1024]{1,0:T(8,128)(2,1)S(1)}, u32[]{:S(2)}, u32[]{:S(2)}) collective-permute-start(bf16[144,1024]{1,0:T(8,128)(2,1)} %get-tuple-element.46), channel_id=1, source_target_pairs={{0,15},{1,0},{2,1},{3,2},{4,3},{5,4},{6,5},{7,6},{8,7},{9,8},{10,9... | collective-permute-start | bytes 884744 | tf_op jit(solution)/shard_map/ppermute | solution.py:536
  131.2 9.5 %collective-permute-start.5 = (bf16[144,1024]{1,0:T(8,128)(2,1)}, bf16[144,1024]{1,0:T(8,128)(2,1)S(1)}, u32[]{:S(2)}, u32[]{:S(2)}) collective-permute-start(bf16[144,1024]{1,0:T(8,128)(2,1)} %get-tuple-element.47), channel_id=1, source_target_pairs={{0,1},{1,2},{2,3},{3,4},{4,5},{5,6},{6,7},{7,8},{8,9},{9,10},{10,1... | collective-permute-start | bytes 884744 | tf_op jit(solution)/shard_map/ppermute | solution.py:536
  140.8 0.7 copy-start.2
  141.5 0.7 copy-start.3
  146.1 8.2 %collective-permute-start.6 = (bf16[96,1024]{1,0:T(8,128)(2,1)}, bf16[96,1024]{1,0:T(8,128)(2,1)S(1)}, u32[]{:S(2)}, u32[]{:S(2)}) collective-permute-start(bf16[96,1024]{1,0:T(8,128)(2,1)} %get-tuple-element.49), channel_id=1, source_target_pairs={{0,16},{16,32},{32,48},{48,64},{64,80},{80,96},{96,112},{1,17},{17... | collective-permute-start | bytes 589832 | tf_op jit(solution)/shard_map/ppermute | solution.py:542
  150.2 7.7 %collective-permute-start.7 = (bf16[96,1024]{1,0:T(8,128)(2,1)}, bf16[96,1024]{1,0:T(8,128)(2,1)S(1)}, u32[]{:S(2)}, u32[]{:S(2)}) collective-permute-start(bf16[96,1024]{1,0:T(8,128)(2,1)} %get-tuple-element.50), channel_id=1, source_target_pairs={{16,0},{32,16},{48,32},{64,48},{80,64},{96,80},{112,96},{17,1},{33... | collective-permute-start | bytes 589832 | tf_op jit(solution)/shard_map/ppermute | solution.py:542
  154.2 3.7 %copy-start.5 = (bf16[96,1024]{1,0:T(8,128)(2,1)}, bf16[96,1024]{1,0:T(8,128)(2,1)S(1)}, u32[]{:S(2)}) copy-start(bf16[96,1024]{1,0:T(8,128)(2,1)S(1)} %collective-permute-done.6.north_ref) | copy-start | bytes 589828
  157.9 0.7 copy-start.6
  177.3 31.8 %all-to-all-start.1 = ((bf16[128,4,1024]{2,1,0:T(4,128)(2,1)}), bf16[128,4,1024]{2,1,0:T(4,128)(2,1)S(1)}, u32[]{:S(2)}, u32[]{:S(2)}) async-start(bf16[128,4,1024]{2,1,0:T(4,128)(2,1)} %reshape.36), calls=%async_computation.1 | async-start | bytes 2097152 | tf_op jit(solution)/shard_map/all_to_all | solution.py:694
  204.6 4.9 %copy-start.4 = (bf16[256,512]{1,0:T(8,128)(2,1)S(1)}, bf16[256,512]{1,0:T(8,128)(2,1)}, u32[]{:S(2)}) copy-start(bf16[256,512]{1,0:T(8,128)(2,1)} %get-tuple-element.59) | copy-start | bytes 786436

commit v2 on v1

--- a/solution.py
+++ b/solution.py
@@ -20,10 +20,12 @@
 NT = (((1,), (1,)), ((), ()))
 TN = (((0,), (0,)), ((), ()))
 CHUNK = 32
-TILE = 256
+TILE = 1024
 PAIR = 128
 HALF = 64
-VMEM_BYTES = 56 * 2**20
+SLACK_BYTES = 8 * 2**20
+FEED_TILE = 512
+GROUP = 2
 GELU_C = 0.7978845608028654
 GELU_A = 0.044715
 
@@ -100,6 +102,11 @@
     vmem_spec = pl.BlockSpec(memory_space=pltpu.VMEM)
     moved = sum(x.size * x.dtype.itemsize for x in ins)
     moved += sum(int(np.prod(s)) * jnp.dtype(t).itemsize for s, t in outs)
+    held = sum(x.size * x.dtype.itemsize for x, k in zip(ins, kinds) if k == "v")
+    held += sum(int(np.prod(s)) * jnp.dtype(t).itemsize for s, t in outs)
+    for item in scratch:
+        if jnp.issubdtype(item.dtype, jnp.floating):
+            held += int(np.prod(item.shape)) * jnp.dtype(item.dtype).itemsize
     single = len(outs) == 1
     shapes = [jax.ShapeDtypeStruct(s, t) for s, t in outs]
     return pl.pallas_call(
@@ -109,7 +116,7 @@
         in_specs=[any_spec if k == "h" else vmem_spec for k in kinds],
         out_specs=vmem_spec if single else [vmem_spec] * len(outs),
         scratch_shapes=scratch,
-        compiler_params=pltpu.CompilerParams(vmem_limit_bytes=VMEM_BYTES),
+        compiler_params=pltpu.CompilerParams(vmem_limit_bytes=held + SLACK_BYTES),
         cost_estimate=pl.CostEstimate(
             flops=int(flops), bytes_accessed=int(moved), transcendentals=0
         ),
@@ -120,22 +127,23 @@
     rows, model = obs_ref.shape
     slots = devices * cap
     tile = tile_ref[...]
-    member = tile == iota((rows, devices), 1)
-    earlier = (iota((rows, rows), 1) < iota((rows, rows), 0)).astype(F32).astype(BF)
-    before = dot(earlier, member.astype(F32).astype(BF))
-    rank = jnp.sum(jnp.where(member, before, 0.0), -1, keepdims=True).astype(jnp.int32)
+    member = tile == iota((devices, rows), 0)
+    earlier = (iota((rows, rows), 0) < iota((rows, rows), 1)).astype(F32).astype(BF)
+    before = dot(member.astype(F32).astype(BF), earlier)
+    rank = jnp.sum(jnp.where(member, before, 0.0), 0, keepdims=True).astype(jnp.int32)
     slot = tile * cap + rank
-    placing = (slot == iota((rows, slots), 1)).astype(F32).astype(BF)
+    placing = (slot == iota((slots, rows), 0)).astype(F32).astype(BF)
     place_ref[...] = placing
     cell = cell_ref[...]
     shift = wide.bit_length() - 1
-    lane = iota((rows, 128), 1)
+    line_no = iota((128, rows), 0)
     codes = jnp.where(
-        lane == 0, (cell >> shift) + 1, jnp.where(lane == 1, (cell & (wide - 1)) + 1, 0)
-    )
-    pay_ref[:, model:] = dot(placing, codes.astype(F32).astype(BF), TN).astype(BF)
-    for j in range(0, model, TILE):
-        pay_ref[:, j : j + TILE] = dot(placing, obs_ref[:, j : j + TILE], TN).astype(BF)
+        line_no == 0, (cell >> shift) + 1, jnp.where(line_no == 1, (cell & (wide - 1)) + 1, 0)
+    )
+    code_rows = dot(placing, codes.astype(F32).astype(BF), NT).astype(BF)
+    pay_ref[:, :, model:] = code_rows.reshape(devices, cap, 128)
+    moved = dot(placing, obs_ref[...]).astype(BF)
+    pay_ref[:, :, :model] = moved.reshape(devices, cap, model)
 
 
 def grid_kernel(
@@ -171,14 +179,16 @@
 
 def cross_kernel(
     arr_ref, grid_ref, q_ref, own_ref, gain_ref, wp_hbm, wo_hbm,
-    state_ref, nrm_ref, pairs_ref, wts_ref, mix_ref, ow_ref,
-    wp, wo, scores, bias, sems, *, wide,
+    state_ref, top_ref, bottom_ref, pairs_ref, wts_ref, mix_ref, ow_ref,
+    arr, wp, wo, scores, bias, sems, *, wide,
 ):
     copies = fetch([wp_hbm, wo_hbm], [wp, wo], sems)
     cells, model = grid_ref.shape
-    slots = arr_ref.shape[0]
+    rim = top_ref.shape[0]
+    slots = arr.shape[0]
+    arr[...] = arr_ref[...].reshape(arr.shape)
     pick = (iota((8, 128), 0) == iota((8, 128), 1)).astype(F32).astype(BF)
-    codes = dot(pick, arr_ref[:, model:], NT)
+    codes = dot(pick, arr[:, model:], NT)
     cell = iota((cells, slots), 0)
     shift = wide.bit_length() - 1
     row_gap = (cell >> shift).astype(F32) - (codes[0:1] - 1.0)
@@ -189,24 +199,18 @@
 
     def project(j):
         pairs_ref[:, pl.ds(j, TILE)] = dot(
-            arr_ref[:, :model], wp[:, pl.ds(j, TILE)]
+            arr[:, :model], wp[:, pl.ds(j, TILE)]
         ).astype(BF)
 
     tiles_of(2 * model, project)
 
-    @pl.loop(0, model // PAIR)
-    def _(h):
-        keys = pl.ds(pl.multiple_of(h * PAIR, PAIR), PAIR)
-        vals = pl.ds(pl.multiple_of(model + h * PAIR, PAIR), PAIR)
-        q = q_ref[:, keys]
-        scores[...] = dot(stacked(q), pairs_ref[:, keys], NT)
-        own_scores = lane_sums(q.astype(F32) * own_ref[:, keys].astype(F32))
+    def soften(h, k, own_scores):
         own_weights = []
         for side in range(2):
             parts = []
             for i in range(0, cells, CHUNK):
                 own_score = own_scores[side][i : i + CHUNK]
-                x = scores[pl.ds(side * cells + i, CHUNK), :] + bias[pl.ds(i, CHUNK), :]
+                x = scores[k, pl.ds(side * cells + i, CHUNK), :] + bias[pl.ds(i, CHUNK), :]
                 peak = jnp.maximum(jnp.max(x, -1, keepdims=True), own_score)
                 x = jnp.exp(x - peak)
                 own_weight = jnp.exp(own_score - peak)
@@ -215,12 +219,27 @@
                 parts.append(own_weight * inverse)
             own_weights.append(jnp.concatenate(parts, axis=0))
         lanes = iota((cells, PAIR), 1) < HALF
-        weight = jnp.where(lanes, own_weights[0], own_weights[1]).astype(BF)
-        ow_ref[:, keys] = weight
-        mix = merged(dot(wts_ref[h], pairs_ref[:, vals]))
-        mix_ref[:, keys] = (
-            mix + weight.astype(F32) * own_ref[:, vals].astype(F32)
-        ).astype(BF)
+        return jnp.where(lanes, own_weights[0], own_weights[1]).astype(BF)
+
+    @pl.loop(0, model // (PAIR * GROUP))
+    def _(g):
+        heads, own_scores, weights = [], [], []
+        for k in range(GROUP):
+            h = g * GROUP + k
+            keys = pl.ds(pl.multiple_of(h * PAIR, PAIR), PAIR)
+            vals = pl.ds(pl.multiple_of(model + h * PAIR, PAIR), PAIR)
+            heads.append((h, keys, vals))
+            q = q_ref[:, keys]
+            scores[k] = dot(stacked(q), pairs_ref[:, keys], NT)
+            own_scores.append(lane_sums(q.astype(F32) * own_ref[:, keys].astype(F32)))
+        for k, (h, keys, vals) in enumerate(heads):
+            weights.append(soften(h, k, own_scores[k]))
+            ow_ref[:, keys] = weights[k]
+        for k, (h, keys, vals) in enumerate(heads):
+            mix = merged(dot(wts_ref[h], pairs_ref[:, vals]))
+            mix_ref[:, keys] = (
+                mix + weights[k].astype(F32) * own_ref[:, vals].astype(F32)
+            ).astype(BF)
 
     copies[1].wait()
 
@@ -230,23 +249,30 @@
         )
 
     tiles_of(model, project_out)
-    for rows in row_chunks(cells):
-        normed, _ = unit(state_ref[rows, :])
-        nrm_ref[rows, :] = (normed * gain_ref[1:2, :]).astype(BF)
-
-
-def near_own_kernel(nrm_ref, w_hbm, q_ref, kv_ref, w, sems):
-    cells, model = nrm_ref.shape
+    for i in range(0, cells, CHUNK):
+        normed, _ = unit(state_ref[pl.ds(i, CHUNK), :])
+        normed = (normed * gain_ref[1:2, :]).astype(BF)
+        if i < rim:
+            top_ref[pl.ds(i, CHUNK), :] = normed
+        else:
+            bottom_ref[pl.ds(i - rim, CHUNK), :] = normed
+
+
+def near_own_kernel(top_ref, bottom_ref, w_hbm, q_ref, kv_ref, nrm, w, sems):
+    cells, model = nrm.shape
+    rim = top_ref.shape[0]
     copies = fetch(
         [w_hbm.at[:, pl.ds(0, model)], w_hbm.at[:, pl.ds(model, 2 * model)]],
         [w.at[:, pl.ds(0, model)], w.at[:, pl.ds(model, 2 * model)]],
         sems,
     )
+    nrm[pl.ds(0, rim), :] = top_ref[...]
+    nrm[pl.ds(rim, rim), :] = bottom_ref[...]
     copies[0].wait()
 
     def query(j):
         q_ref[:, pl.ds(j, TILE)] = (
-            dot(nrm_ref[...], w[:, pl.ds(j, TILE)]) * HALF ** (-0.5)
+            dot(nrm[...], w[:, pl.ds(j, TILE)]) * HALF ** (-0.5)
         ).astype(BF)
 
     tiles_of(model, query)
@@ -254,18 +280,18 @@
 
     def pairs(j):
         kv_ref[:, pl.ds(j, TILE)] = dot(
-            nrm_ref[...], w[:, pl.ds(pl.multiple_of(model + j, TILE), TILE)]
+            nrm[...], w[:, pl.ds(pl.multiple_of(model + j, TILE), TILE)]
         ).astype(BF)
 
     tiles_of(2 * model, pairs)
 
 
-def rim_kernel(own_ref, north_ref, south_ref, sel_ref, west_ref, east_ref, ext):
-    cells, model = own_ref.shape
-    rim = north_ref.shape[0]
-    ext[pl.ds(0, cells), :] = own_ref[...]
-    ext[pl.ds(cells, rim), :] = north_ref[...]
-    ext[pl.ds(cells + rim, rim), :] = south_ref[...]
+def rim_kernel(
+    top_ref, bottom_ref, north_ref, south_ref, sel_ref, _, west_ref, east_ref, ext
+):
+    rim, model = north_ref.shape
+    for i, part in enumerate((top_ref, bottom_ref, north_ref, south_ref)):
+        ext[pl.ds(i * rim, rim), :] = part[...]
     side = west_ref.shape[0]
 
     def pick(j):
@@ -320,18 +346,24 @@
 
     tiles_of(2 * model, project)
 
-    @pl.loop(0, model // PAIR)
-    def _(h):
-        keys = pl.ds(pl.multiple_of(h * PAIR, PAIR), PAIR)
-        vals = pl.ds(pl.multiple_of(model + h * PAIR, PAIR), PAIR)
-        scores[...] = dot(stacked(q_ref[:, keys]), kv[:, keys], NT)
-        for start in range(0, 2 * cells, CHUNK):
-            rows = pl.ds(start, CHUNK)
-            v = scores[rows, :] + bias[pl.ds(start % cells, CHUNK), :]
-            v = jnp.exp(v - jnp.max(v, -1, keepdims=True))
-            inverse = 1.0 / jnp.sum(v, -1, keepdims=True)
-            wts[h, rows, :] = (v * inverse).astype(BF)
-        mix[:, keys] = merged(dot(wts[h], kv[:, vals])).astype(BF)
+    @pl.loop(0, model // (PAIR * GROUP))
+    def _(g):
+        heads = []
+        for k in range(GROUP):
+            h = g * GROUP + k
+            keys = pl.ds(pl.multiple_of(h * PAIR, PAIR), PAIR)
+            vals = pl.ds(pl.multiple_of(model + h * PAIR, PAIR), PAIR)
+            heads.append((h, keys, vals))
+            scores[k] = dot(stacked(q_ref[:, keys]), kv[:, keys], NT)
+        for k, (h, keys, vals) in enumerate(heads):
+            for start in range(0, 2 * cells, CHUNK):
+                rows = pl.ds(start, CHUNK)
+                v = scores[k, rows, :] + bias[pl.ds(start % cells, CHUNK), :]
+                v = jnp.exp(v - jnp.max(v, -1, keepdims=True))
+                inverse = 1.0 / jnp.sum(v, -1, keepdims=True)
+                wts[h, rows, :] = (v * inverse).astype(BF)
+        for k, (h, keys, vals) in enumerate(heads):
+            mix[:, keys] = merged(dot(wts[h], kv[:, vals])).astype(BF)
 
     copies[3].wait()
 
@@ -347,7 +379,7 @@
     copies[4].wait()
 
     def feed(j):
-        cols = pl.ds(j, TILE)
+        cols = pl.ds(j, FEED_TILE)
         u = dot(nrm[...], wu[:, cols])
         square = u * u
         t = jnp.tanh(GELU_C * (u + GELU_A * (square * u)))
@@ -356,7 +388,7 @@
         slope = half + (0.5 * GELU_C) * u * (1.0 - t * t) * (1.0 + 3.0 * GELU_A * square)
         du[:, cols] = (dh_ref[:, cols].astype(F32) * slope).astype(BF)
 
-    tiles_of(du.shape[1], feed)
+    tiles_of(du.shape[1], feed, FEED_TILE)
 
     def feed_back(j):
         acc[:, pl.ds(j, TILE)] = dot(du[...], wu[pl.ds(j, TILE), :], NT)
@@ -375,24 +407,30 @@
 
     tiles_of(model, mix_back)
 
-    @pl.loop(0, model // PAIR)
-    def _(h):
-        keys = pl.ds(pl.multiple_of(h * PAIR, PAIR), PAIR)
-        vals = pl.ds(pl.multiple_of(model + h * PAIR, PAIR), PAIR)
-        grad = dmix[:, keys]
-        grad_2 = stacked(grad)
-        scores[...] = dot(grad_2, kv[:, vals], NT)
-        deltas = lane_sums(grad.astype(F32) * mix[:, keys].astype(F32))
-        for s in range(2):
-            for i in range(0, cells, CHUNK):
-                rows = pl.ds(s * cells + i, CHUNK)
-                ds[rows, :] = (
-                    wts[h, rows, :].astype(F32)
-                    * (scores[rows, :] - deltas[s][i : i + CHUNK])
-                ).astype(BF)
-        dqkv_ref[:, keys] = (merged(dot(ds[...], kv[:, keys])) * HALF ** (-0.5)).astype(BF)
-        dkv[:, keys] = dot(stacked(q_ref[:, keys]), ds[...], TN).T.astype(BF)
-        dkv[:, vals] = dot(grad_2, wts[h], TN).T.astype(BF)
+    @pl.loop(0, model // (PAIR * GROUP))
+    def _(g):
+        heads, deltas = [], []
+        for k in range(GROUP):
+            h = g * GROUP + k
+            keys = pl.ds(pl.multiple_of(h * PAIR, PAIR), PAIR)
+            vals = pl.ds(pl.multiple_of(model + h * PAIR, PAIR), PAIR)
+            heads.append((h, keys, vals))
+            grad = dmix[:, keys]
+            scores[k] = dot(stacked(grad), kv[:, vals], NT)
+            deltas.append(lane_sums(grad.astype(F32) * mix[:, keys].astype(F32)))
+        for k, (h, keys, vals) in enumerate(heads):
+            for s in range(2):
+                for i in range(0, cells, CHUNK):
+                    rows = pl.ds(s * cells + i, CHUNK)
+                    ds[k, rows, :] = (
+                        wts[h, rows, :].astype(F32)
+                        * (scores[k, rows, :] - deltas[k][s][i : i + CHUNK])
+                    ).astype(BF)
+        for k, (h, keys, vals) in enumerate(heads):
+            dq = merged(dot(ds[k], kv[:, keys])) * HALF ** (-0.5)
+            dqkv_ref[:, keys] = dq.astype(BF)
+            dkv[:, keys] = dot(stacked(q_ref[:, keys]), ds[k], TN).T.astype(BF)
+            dkv[:, vals] = dot(stacked(dmix[:, keys]), wts[h], TN).T.astype(BF)
 
     def rim_back(j):
         both = dot(dkv[pl.ds(ext, 2 * side), :], wkv[pl.ds(j, TILE), :], NT).astype(BF)
@@ -404,7 +442,7 @@
     drows_ref[...] = dkv[pl.ds(cells, cells), :]
 
 
-def encode_kernel(after_ref, hid_ref, wd_hbm, enc_ref, wd, sems):
+def encode_kernel(after_ref, hid_ref, wd_hbm, _, enc_ref, wd, sems):
     copies = fetch([wd_hbm], [wd], sems)
     copies[0].wait()
 
@@ -416,41 +454,53 @@
     tiles_of(after_ref.shape[1], down)
 
 
-def near_back_kernel(dqkv_ref, drows_ref, w_hbm, dn_ref, w, sems):
-    copies = fetch([w_hbm], [w], sems)
-    cells, wide = dqkv_ref.shape
-    model = wide // 3
+def rows_back_kernel(drows_ref, w_hbm, dn_ref, w, sems):
+    model = dn_ref.shape[1]
+    copies = fetch([w_hbm.at[:, pl.ds(model, 2 * model)]], [w], sems)
     copies[0].wait()
 
     def back(j):
-        dn_ref[pl.ds(0, cells), pl.ds(j, TILE)] = dot(dqkv_ref[...], w[pl.ds(j, TILE), :], NT)
-        dn_ref[pl.ds(cells, cells), pl.ds(j, TILE)] = dot(
-            drows_ref[...], w[pl.ds(j, TILE), pl.ds(model, 2 * model)], NT
-        )
+        dn_ref[:, pl.ds(j, TILE)] = dot(drows_ref[...], w[pl.ds(j, TILE), :], NT)
 
     tiles_of(model, back)
 
 
-def fold_kernel(dn_ref, from_east_ref, from_west_ref, sel_ref, own_ref, north_ref, south_ref, x):
-    cells, model = own_ref.shape
-    rim = north_ref.shape[0]
+def fold_kernel(dn_ref, from_east_ref, from_west_ref, sel_ref, north_ref, south_ref, x):
+    rim, model = north_ref.shape
     side = from_east_ref.shape[0]
     x[pl.ds(0, side), :] = from_west_ref[...]
     x[pl.ds(side, side), :] = from_east_ref[...]
 
     def fold(j):
         cols = pl.ds(j, TILE)
-        total = dn_ref[:, cols] + dot(sel_ref[...], x[:, cols], TN)
-        own_ref[:, cols] = total[:cells]
-        north_ref[:, cols] = total[cells : cells + rim].astype(BF)
-        south_ref[:, cols] = total[cells + rim :].astype(BF)
+        total = (dn_ref[:, cols] + dot(sel_ref[...], x[:, cols], TN)).astype(BF)
+        north_ref[:, cols] = total[:rim]
+        south_ref[:, cols] = total[rim:]
 
     tiles_of(model, fold)
+
+
+def own_back_kernel(
+    dqkv_ref, from_east_ref, from_west_ref, sel_ref, w_hbm, _, dn_ref, x, w, sems
+):
+    copies = fetch([w_hbm], [w], sems)
+    side = from_east_ref.shape[0]
+    x[pl.ds(0, side), :] = from_west_ref[...]
+    x[pl.ds(side, side), :] = from_east_ref[...]
+    copies[0].wait()
+
+    def back(j):
+        cols = pl.ds(j, TILE)
+        dn_ref[:, cols] = dot(dqkv_ref[...], w[cols, :], NT) + dot(
+            sel_ref[...], x[:, cols], TN
+        )
+
+    tiles_of(dn_ref.shape[1], back)
 
 
 def cross_back_kernel(
     dn_ref, north_ref, south_ref, state_ref, dafter_ref, gain_ref, q_ref, own_ref, pairs_ref,
-    wts_ref, mix_ref, ow_ref, wp_hbm, wo_hbm,
+    wts_ref, mix_ref, ow_ref, wp_hbm, wo_hbm, _,
     dstate_ref, slot_ref, dq_ref, down_ref,
     wp, wo, dsb, dmix, dpairs, scores, ds, sems,
 ):
@@ -471,40 +521,48 @@
 
     tiles_of(model, mix_back)
 
-    @pl.loop(0, model // PAIR)
-    def _(h):
-        keys = pl.ds(pl.multiple_of(h * PAIR, PAIR), PAIR)
-        vals = pl.ds(pl.multiple_of(model + h * PAIR, PAIR), PAIR)
-        grad = dmix[:, keys]
-        grad_2 = stacked(grad)
-        grad_f = grad.astype(F32)
-        scores[...] = dot(grad_2, pairs_ref[:, vals], NT)
-        deltas = lane_sums(grad_f * mix_ref[:, keys].astype(F32))
-        own_dots = lane_sums(grad_f * own_ref[:, vals].astype(F32))
-        for s in range(2):
-            for i in range(0, cells, CHUNK):
-                rows = pl.ds(s * cells + i, CHUNK)
-                ds[rows, :] = (
-                    wts_ref[h, rows, :].astype(F32)
-                    * (scores[rows, :] - deltas[s][i : i + CHUNK])
-                ).astype(BF)
-        lanes = iota((cells, PAIR), 1) < HALF
-        weight = ow_ref[:, keys].astype(F32)
-        own_grad = weight * jnp.where(
-            lanes, own_dots[0] - deltas[0], own_dots[1] - deltas[1]
-        )
-        q = q_ref[:, keys]
-        dq = merged(dot(ds[...], pairs_ref[:, keys])) + own_grad * own_ref[:, keys].astype(F32)
-        dq_ref[:, keys] = (dq * HALF ** (-0.5)).astype(BF)
-        down_ref[:, keys] = (own_grad * q.astype(F32)).astype(BF)
-        down_ref[:, vals] = (weight * grad_f).astype(BF)
-        dpairs[:, keys] = dot(stacked(q), ds[...], TN).T.astype(BF)
-        dpairs[:, vals] = dot(grad_2, wts_ref[h], TN).T.astype(BF)
+    @pl.loop(0, model // (PAIR * GROUP))
+    def _(g):
+        heads, deltas, own_dots = [], [], []
+        for k in range(GROUP):
+            h = g * GROUP + k
+            keys = pl.ds(pl.multiple_of(h * PAIR, PAIR), PAIR)
+            vals = pl.ds(pl.multiple_of(model + h * PAIR, PAIR), PAIR)
+            heads.append((h, keys, vals))
+            grad = dmix[:, keys]
+            grad_f = grad.astype(F32)
+            scores[k] = dot(stacked(grad), pairs_ref[:, vals], NT)
+            deltas.append(lane_sums(grad_f * mix_ref[:, keys].astype(F32)))
+            own_dots.append(lane_sums(grad_f * own_ref[:, vals].astype(F32)))
+        for k, (h, keys, vals) in enumerate(heads):
+            for s in range(2):
+                for i in range(0, cells, CHUNK):
+                    rows = pl.ds(s * cells + i, CHUNK)
+                    ds[k, rows, :] = (
+                        wts_ref[h, rows, :].astype(F32)
+                        * (scores[k, rows, :] - deltas[k][s][i : i + CHUNK])
+                    ).astype(BF)
+        for k, (h, keys, vals) in enumerate(heads):
+            lanes = iota((cells, PAIR), 1) < HALF
+            weight = ow_ref[:, keys].astype(F32)
+            own_grad = weight * jnp.where(
+                lanes, own_dots[k][0] - deltas[k][0], own_dots[k][1] - deltas[k][1]
+            )
+            q = q_ref[:, keys]
+            grad = dmix[:, keys]
+            dq = merged(dot(ds[k], pairs_ref[:, keys]))
+            dq = dq + own_grad * own_ref[:, keys].astype(F32)
+            dq_ref[:, keys] = (dq * HALF ** (-0.5)).astype(BF)
+            down_ref[:, keys] = (own_grad * q.astype(F32)).astype(BF)
+            down_ref[:, vals] = (weight * grad.astype(F32)).astype(BF)
+            dpairs[:, keys] = dot(stacked(q), ds[k], TN).T.astype(BF)
+            dpairs[:, vals] = dot(stacked(grad), wts_ref[h], TN).T.astype(BF)
 
     copies[1].wait()
 
     def slot_back(j):
-        slot_ref[:, pl.ds(j, TILE)] = dot(dpairs[...], wp[pl.ds(j, TILE), :], NT).astype(BF)
+        grads = dot(dpairs[...], wp[pl.ds(j, TILE), :], NT).astype(BF)
+        slot_ref[:, :, pl.ds(j, TILE)] = grads.reshape(slot_ref.shape[:2] + (TILE,))
 
     tiles_of(model, slot_back)
 
@@ -578,7 +636,7 @@
         for c in range(RADIUS):
             select[i * RADIUS + c, spot[(r, c)]] = 1.0
             select[side + i * RADIUS + c, spot[(r, rows_lon - RADIUS + c)]] = 1.0
-    select = jnp.asarray(select.astype(jnp.bfloat16))
+    select = select.astype(jnp.bfloat16)
     base = np.full((cells, keys_all), LOW_SCORE, np.float32)
     own_rows, own_cols = places[:cells, 0], places[:cells, 1]
     allowed = (np.abs(places[None, :, 0] - own_rows[:, None]) <= RADIUS) & (
@@ -599,13 +657,11 @@
 
     payload, placing = call(
         functools.partial(place_kernel, devices=devices, cap=cap, wide=rows_lon),
-        (obs_tile, obs_cell, observations), "vvv",
-        [((slots, model + 128), BF), ((rows_obs, slots), BF)], [],
+        (obs_tile.reshape(1, rows_obs), obs_cell.reshape(1, rows_obs), observations), "vvv",
+        [((devices, cap, model + 128), BF), ((slots, rows_obs), BF)], [],
         2 * rows_obs * slots * model, "place",
     )
-    arrived = lax.all_to_all(
-        payload.reshape(devices, cap, model + 128), ("lat", "lon"), 0, 0, tiled=True
-    ).reshape(slots, model + 128)
+    arrived = lax.all_to_all(payload, ("lat", "lon"), 0, 0, tiled=True)
     q_c, own_pairs, dhid = call(
         grid_kernel,
         (flat, cot, norm_gains, w_cross_query, w_cross_pairs, w_down), "vvvhhh",
@@ -614,25 +670,25 @@
          vm((ff, model), BF), dma((3,))],
         2 * cells * model * (3 * model + ff), "grid_proj",
     )
-    state, normal, slot_pairs, cross_w, cross_mix, own_w = call(
+    state, top, bottom, slot_pairs, cross_w, cross_mix, own_w = call(
         functools.partial(cross_kernel, wide=rows_lon),
         (arrived, flat, q_c, own_pairs, norm_gains, w_cross_pairs, w_cross_out), "vvvvvhh",
-        [((cells, model), F32), ((cells, model), BF), ((slots, 2 * model), BF),
+        [((cells, model), F32), ((rim, model), BF), ((rim, model), BF), ((slots, 2 * model), BF),
          ((pairs_n, 2 * cells, slots), BF), ((cells, model), BF), ((cells, model), BF)],
-        [vm((model, 2 * model), BF), vm((model, model), BF), vm((2 * cells, slots), F32),
-         vm((cells, slots), F32), dma((2,))],
+        [vm((slots, model + 128), BF), vm((model, 2 * model), BF), vm((model, model), BF),
+         vm((GROUP, 2 * cells, slots), F32), vm((cells, slots), F32), dma((2,))],
         2 * slots * model * 2 * model * 2, "cross",
     )
-    south = line(normal[:rim], -1)
-    north = line(normal[cells - rim :], 1)
+    south = line(top, -1)
+    north = line(bottom, 1)
     q_n, kv_own = call(
-        near_own_kernel, (normal, w_near_proj), "vh",
+        near_own_kernel, (top, bottom, w_near_proj), "vvh",
         [((cells, model), BF), ((cells, 2 * model), BF)],
-        [vm((model, 3 * model), BF), dma((2,))],
+        [vm((cells, model), BF), vm((model, 3 * model), BF), dma((2,))],
         2 * cells * model * 3 * model, "near_own",
     )
     west_send, east_send = call(
-        rim_kernel, (normal, north, south, select), "vvvv",
+        rim_kernel, (top, bottom, north, south, jnp.asarray(select), kv_own), "vvvvvh",
         [((side, model), BF), ((side, model), BF)],
         [vm((cells + 2 * rim, model), BF)],
         2 * 2 * side * 2 * cells * model, "rim",
@@ -654,7 +710,7 @@
         [vm((model, 2 * model), BF), vm((model, model), BF), vm((model, ff), BF),
          vm((keys_all, 2 * model), BF), vm((keys_all, 2 * model), BF),
          vm((2 * side, model), BF), vm((pairs_n, 2 * cells, keys_all), BF),
-         vm((2 * cells, keys_all), F32), vm((2 * cells, keys_all), BF),
+         vm((GROUP, 2 * cells, keys_all), F32), vm((GROUP, 2 * cells, keys_all), BF),
          vm((cells, keys_all), F32), vm((cells, model), BF), vm((cells, model), BF),
          vm((cells, ff), BF), vm((cells, model), F32), vm((cells, model), BF),
          vm((cells, model), BF), dma((5,))],
@@ -662,37 +718,43 @@
     )
     from_east = ring(dwest, -1)
     from_west = ring(deast, 1)
-    dn_ext = call(
-        near_back_kernel, (dqkv, drows, w_near_proj), "vvh",
-        [((cells + 2 * rim, model), F32)],
-        [vm((model, 3 * model), BF), dma((1,))],
-        2 * cells * model * 5 * model, "near_back",
-    )
-    dn_own, dnorth, dsouth = call(
-        fold_kernel, (dn_ext, from_east, from_west, select), "vvvv",
-        [((cells, model), F32), ((rim, model), BF), ((rim, model), BF)],
+    dn_rows = call(
+        rows_back_kernel, (drows, w_near_proj), "vh", [((2 * rim, model), F32)],
+        [vm((model, 2 * model), BF), dma((1,))],
+        2 * 2 * rim * model * 2 * model, "rows_back",
+    )
+    dnorth, dsouth = call(
+        fold_kernel, (dn_rows, from_east, from_west, jnp.asarray(select[:, cells:])), "vvvv",
+        [((rim, model), BF), ((rim, model), BF)],
         [vm((2 * side, model), BF)],
-        2 * 2 * side * 2 * cells * model, "fold",
+        2 * 2 * side * 2 * rim * model, "fold",
     )
     from_south = line(dnorth, -1)
     from_north = line(dsouth, 1)
+    dn_own = call(
+        own_back_kernel,
+        (dqkv, from_east, from_west, jnp.asarray(select[:, :cells]), w_near_proj, dnorth), "vvvvhh",
+        [((cells, model), F32)],
+        [vm((2 * side, model), BF), vm((model, 3 * model), BF), dma((1,))],
+        2 * cells * model * 3 * model, "own_back",
+    )
     encoded = call(
-        encode_kernel, (after, hidden, w_down), "vvh", [((cells, model), BF)],
+        encode_kernel, (after, hidden, w_down, dsouth), "vvhh", [((cells, model), BF)],
         [vm((ff, model), BF), dma((1,))], 2 * cells * model * ff, "encode",
     )
     dstate, slot_grads, dq, down = call(
         cross_back_kernel,
         (dn_own, from_north, from_south, state, dafter, norm_gains, q_c, own_pairs, slot_pairs,
-         cross_w, cross_mix, own_w, w_cross_pairs, w_cross_out), "vvvvvvvvvvvvhh",
-        [((cells, model), F32), ((slots, model), BF), ((cells, model), BF),
+         cross_w, cross_mix, own_w, w_cross_pairs, w_cross_out, encoded), "vvvvvvvvvvvvhhh",
+        [((cells, model), F32), ((devices, cap, model), BF), ((cells, model), BF),
          ((cells, 2 * model), BF)],
         [vm((model, 2 * model), BF), vm((model, model), BF), vm((cells, model), BF),
-         vm((cells, model), BF), vm((slots, 2 * model), BF), vm((2 * cells, slots), F32),
-         vm((2 * cells, slots), BF), dma((2,))],
+         vm((cells, model), BF), vm((slots, 2 * model), BF), vm((GROUP, 2 * cells, slots), F32),
+         vm((GROUP, 2 * cells, slots), BF), dma((2,))],
         2 * slots * model * 2 * model * 2, "cross_back",
     )
     returned = lax.all_to_all(
-        slot_grads.reshape(devices, cap, model), ("lat", "lon"), 0, 0, tiled=True
+        slot_grads, ("lat", "lon"), 0, 0, tiled=True
     ).reshape(slots, model)
     grid_grad = call(
         grid_back_kernel,
@@ -701,7 +763,7 @@
         [vm((model, model), BF), vm((model, 2 * model), BF), vm((cells, model), F32), dma((2,))],
         2 * cells * model * 3 * model, "grid_back",
     )
-    obs_grad = dot(placing, returned).astype(BF)
+    obs_grad = dot(placing, returned, TN).astype(BF)
     shape = (rows_lat, rows_lon, model)
     return encoded.reshape(shape), grid_grad.reshape(shape), obs_grad
 

time: 212 us -> 174 us (0.82)
  Pallas kernels: 126 us -> 68 us
  local copies, waits for them, and re-layouts: 14.5 us -> 35.7 us
    pallas_call x12 -> x13, Pallas kernels: 126 us -> 68 us  [call(): pl.pallas_call(body, name=name, out_shape=shapes[0] if single else shapes...]
    unnamed x22 -> x100, local copies, waits for them, and re-layouts: 6.56 us -> 34.3 us
    ppermute x4, waiting for transfers between devices: 10.7 us -> 0.01 us  [line(): return lax.ppermute(value, 'lat', pairs)]
    ppermute x4, waiting for transfers between devices: 0.01 us -> 6.55 us  [ring(): lax.ppermute(value, 'lon', [(i, (i + by) % size) for i in range(size)])]
    reshape x4 -> x1, local copies, waits for them, and re-layouts: 6.91 us -> 1.34 us  [per_device(): returned = lax.all_to_all(slot_grads, ('lat', 'lon'), 0, 0, tiled=True).r...]
    all_to_all x2, waiting for transfers between devices: 15 us -> 19 us  [the longest x1 10.5 us: per_device(): lax.all_to_all(slot_grads, ('lat', 'lon'), 0, 0, tiled=True)]
    all_to_all x2, starting transfers between devices: 24.4 us -> 26.9 us  [the longest x1 15 us: per_device(): lax.all_to_all(slot_grads, ('lat', 'lon'), 0, 0, tiled=True)]
  transfers between devices with their start and end apart: 10 -> 10, of which waited for: 6 -> 6; matrix products, arithmetic and copies ran while one was open for 0% -> 0% of each run, Pallas kernels for 22% -> 13%
where the time goes in v2:
time: 174 us
  Pallas kernels  68 us (39%)
  starting transfers between devices  41.9 us (24%)
  local copies, waits for them, and re-layouts  35.7 us (21%)
  waiting for transfers between devices  25.6 us (15%)
    pallas_call x13, Pallas kernels, call(): pl.pallas_call(body, name=name, out_shape=shapes[0] if single else shapes...  68 us
    unnamed x100, local copies, waits for them, and re-layouts  34.3 us
    all_to_all x1, starting transfers between devices, per_device(): lax.all_to_all(slot_grads, ('lat', 'lon'), 0, 0, tiled=True)  15 us
    all_to_all x1, starting transfers between devices, per_device(): arrived = lax.all_to_all(payload, ('lat', 'lon'), 0, 0, tiled=True)  11.9 us
    all_to_all x1, waiting for transfers between devices, per_device(): lax.all_to_all(slot_grads, ('lat', 'lon'), 0, 0, tiled=True)  10.5 us
    ppermute x4, starting transfers between devices, line(): return lax.ppermute(value, 'lat', pairs)  9.06 us
    all_to_all x1, waiting for transfers between devices, per_device(): arrived = lax.all_to_all(payload, ('lat', 'lon'), 0, 0, tiled=True)  8.48 us
    ppermute x4, waiting for transfers between devices, ring(): lax.ppermute(value, 'lon', [(i, (i + by) % size) for i in range(size)])  6.55 us
  transfers between devices with their start and end apart: 10, of which 6 were waited for; matrix products, arithmetic and copies ran while one was open for 0% of the time, Pallas kernels for 13%

profile of v2, /device:TPU:1, one launch (start us, length us, event | category | flops | bytes accessed | tf_op | source)
XLA Modules:
  0.0 173.6 jit_solution(2261307374393698973)
XLA Ops:
  0.7 1.2 copy-done.43
  1.9 0.7 copy-done.44
  2.5 0.7 copy-done.45
  3.2 0.7 place.1
  4.0 1.0 copy-done.17
  5.0 0.7 copy-done.35
  5.7 11.9 %all-to-all-start = ((bf16[128,4,1152]{2,1,0:T(4,128)(2,1)}), bf16[128,4,1152]{2,1,0:T(4,128)(2,1)}, u32[]{:S(2)}, u32[]{:S(2)}) async-start(bf16[128,4,1152]{2,1,0:T(4,128)(2,1)} %copy-done.17), calls=%async_computation | async-start | bytes 2359296 | tf_op jit(solution)/shard_map/all_to_all | solution.py:664
  17.7 0.0 copy-start.2
  17.7 2.2 %copy-done.2 = bf16[1024,2048]{1,0:T(8,128)(2,1)S(1)} copy-done((bf16[1024,2048]{1,0:T(8,128)(2,1)S(1)}, bf16[1024,2048]{1,0:T(8,128)(2,1)}, u32[]{:S(2)}) %copy-start.2) | copy-done | bytes 4194328
  19.9 2.2 %copy-done.6 = bf16[2048,1024]{1,0:T(8,128)(2,1)S(1)} copy-done((bf16[2048,1024]{1,0:T(8,128)(2,1)S(1)}, bf16[2048,1024]{1,0:T(8,128)(2,1)}, u32[]{:S(2)}) %copy-start.6) | copy-done | bytes 4194328
  22.0 1.0 copy-done.24
  23.0 4.5 %grid_proj.1 = (bf16[192,1024]{1,0:T(8,128)(2,1)S(1)}, bf16[192,2048]{1,0:T(8,128)(2,1)S(1)}, bf16[192,2048]{1,0:T(8,128)(2,1)S(1)}) custom-call(bf16[192,1024]{1,0:T(8,128)(2,1)S(1)} %bitcast.10, bf16[192,1024]{1,0:T(8,128)(2,1)S(1)} %bitcast.14, f32[3,1024]{1,0:T(4,128)S(1)} %copy-done.38, bf16[1024,1024]{1,0:T(8,128)(2,1)S(1)} %copy-done.8, ...), custom_call_target="tpu_custom_call" | custom-call | flops 2013265920 | bytes 13250560 | tf_op jit(solution)/shard_map/grid_proj/pallas_call | solution.py:112
  27.5 0.7 copy-done.28
  28.3 0.9 copy-done.41
  29.2 8.5 %all-to-all-done.arr_ref = bf16[128,4,1152]{2,1,0:T(4,128)(2,1)} async-done(((bf16[128,4,1152]{2,1,0:T(4,128)(2,1)}), bf16[128,4,1152]{2,1,0:T(4,128)(2,1)}, u32[]{:S(2)}, u32[]{:S(2)}) %all-to-all-start) | async-done | bytes 1179680 | tf_op jit(solution)/shard_map/all_to_all | solution.py:664
  37.7 2.2 %copy-done.3 = bf16[1024,2048]{1,0:T(8,128)(2,1)S(1)} copy-done((bf16[1024,2048]{1,0:T(8,128)(2,1)S(1)}, bf16[1024,2048]{1,0:T(8,128)(2,1)}, u32[]{:S(2)}) %copy-start.3) | copy-done | bytes 4194328
  39.8 1.6 copy-done.11
  41.4 1.0 copy-done.29
  42.4 10.3 %cross.1 = (f32[192,1024]{1,0:T(8,128)S(1)}, bf16[96,1024]{1,0:T(8,128)(2,1)S(1)}, bf16[96,1024]{1,0:T(8,128)(2,1)}, bf16[512,2048]{1,0:T(8,128)(2,1)S(1)}, bf16...) custom-call(bf16[128,4,1152]{2,1,0:T(4,128)(2,1)} %all-to-all-done.arr_ref, ...), custom_call_target="tpu_custom_call" | custom-call | flops 4294967296 | bytes 16265216 | tf_op jit(solution)/shard_map/cross/pallas_call | solution.py:112
  52.8 1.6 copy-done.9
  54.4 1.3 copy-done.13
  55.7 0.9 copy-done.18
  56.6 0.7 copy-done.31
  57.4 0.8 copy-done.33
  58.1 1.3 collective-permute-start.1
  59.4 4.7 %collective-permute-start = (bf16[96,1024]{1,0:T(8,128)(2,1)}, bf16[96,1024]{1,0:T(8,128)(2,1)}, u32[]{:S(2)}, u32[]{:S(2)}) collective-permute-start(bf16[96,1024]{1,0:T(8,128)(2,1)} %get-tuple-element.36.bottom_ref), channel_id=1, source_target_pairs={{0,16},{16,32},{32,48},{48,64},{64,80},{80,96},{96,112},{1,17},{17... | collective-permute-start | bytes 589832 | tf_op jit(solution)/shard_map/ppermute | solution.py:600
  64.1 2.8 %copy-done = bf16[1024,3072]{1,0:T(8,128)(2,1)S(1)} copy-done((bf16[1024,3072]{1,0:T(8,128)(2,1)S(1)}, bf16[1024,3072]{1,0:T(8,128)(2,1)}, u32[]{:S(2)}) %copy-start) | copy-done | bytes 6291480
  66.9 3.6 %near_own.1 = (bf16[192,1024]{1,0:T(8,128)(2,1)S(1)}, bf16[192,2048]{1,0:T(8,128)(2,1)S(1)}) custom-call(bf16[96,1024]{1,0:T(8,128)(2,1)S(1)} %get-tuple-element.35.top_ref, bf16[96,1024]{1,0:T(8,128)(2,1)} %get-tuple-element.36.bottom_ref, bf16[1024,3072]{1,0:T(8,128)(2,1)S(1)} %copy-done), custom_call_target="tpu_custom_call" | custom-call | flops 1207959552 | bytes 7864320 | tf_op jit(solution)/shard_map/near_own/pallas_call | solution.py:112
  70.5 1.6 rim.1
  72.1 2.6 %collective-permute-start.2 = (bf16[144,1024]{1,0:T(8,128)(2,1)S(1)}, bf16[144,1024]{1,0:T(8,128)(2,1)S(1)}, u32[]{:S(2)}, u32[]{:S(2)}) collective-permute-start(bf16[144,1024]{1,0:T(8,128)(2,1)S(1)} %get-tuple-element.39), channel_id=1, source_target_pairs={{0,1},{1,2},{2,3},{3,4},{4,5},{5,6},{6,7},{7,8},{8,9},{9,10},{10,1... | collective-permute-start | bytes 884744 | tf_op jit(solution)/shard_map/ppermute | solution.py:594
  74.8 2.8 %copy-done.1 = bf16[1024,3072]{1,0:T(8,128)(2,1)S(1)} copy-done((bf16[1024,3072]{1,0:T(8,128)(2,1)S(1)}, bf16[1024,3072]{1,0:T(8,128)(2,1)}, u32[]{:S(2)}) %copy-start.1) | copy-done | bytes 6291480
  77.5 3.2 %near_rows.1.kvr_hbm = bf16[192,2048]{1,0:T(8,128)(2,1)S(1)} custom-call(bf16[96,1024]{1,0:T(8,128)(2,1)} %collective-permute-done.north_ref, bf16[96,1024]{1,0:T(8,128)(2,1)} %collective-permute-done.1.south_ref, bf16[1024,3072]{1,0:T(8,128)(2,1)S(1)} %copy-done.1), custom_call_target="tpu_custom_call" | custom-call | flops 805306368 | bytes 7471104 | tf_op jit(solution)/shard_map/near_rows/pallas_call | solution.py:112
  80.7 0.8 collective-permute-done.2.west_ref
  81.6 3.2 %collective-permute-done.3.east_ref = bf16[144,1024]{1,0:T(8,128)(2,1)S(1)} collective-permute-done((bf16[144,1024]{1,0:T(8,128)(2,1)S(1)}, bf16[144,1024]{1,0:T(8,128)(2,1)S(1)}, u32[]{:S(2)}, u32[]{:S(2)}) %collective-permute-start.3) | collective-permute-done | bytes 294944 | tf_op jit(solution)/shard_map/ppermute | solution.py:594
  84.8 22.5 %near.1 = (f32[192,1024]{1,0:T(8,128)S(1)}, bf16[192,2048]{1,0:T(8,128)(2,1)S(1)}, bf16[144,1024]{1,0:T(8,128)(2,1)S(1)}, bf16[144,1024]{1,0:T(8,128)(2,1)S(1)},...) custom-call(bf16[192,1024]{1,0:T(8,128)(2,1)S(1)} %get-tuple-element.37.q_ref, ...), custom_call_target="tpu_custom_call" | custom-call | flops 20000000000 | bytes 22351872 | tf_op jit(solution)/shard_map/near/pallas_call | solution.py:112
  107.3 0.1 collective-permute-start.4
  107.4 3.2 %collective-permute-start.5 = (bf16[144,1024]{1,0:T(8,128)(2,1)S(1)}, bf16[144,1024]{1,0:T(8,128)(2,1)S(1)}, u32[]{:S(2)}, u32[]{:S(2)}) collective-permute-start(bf16[144,1024]{1,0:T(8,128)(2,1)S(1)} %get-tuple-element.47), channel_id=1, source_target_pairs={{0,1},{1,2},{2,3},{3,4},{4,5},{5,6},{6,7},{7,8},{8,9},{9,10},{10,1... | collective-permute-start | bytes 884744 | tf_op jit(solution)/shard_map/ppermute | solution.py:594
  110.6 0.0 copy-start.7
  110.6 2.1 %rows_back.1.dn_ref = f32[192,1024]{1,0:T(8,128)S(1)} custom-call(bf16[192,2048]{1,0:T(8,128)(2,1)S(1)} %get-tuple-element.45.drows_ref, bf16[1024,3072]{1,0:T(8,128)(2,1)S(1)} %bitcast.9), custom_call_target="tpu_custom_call" | custom-call | flops 805306368 | bytes 7864320 | tf_op jit(solution)/shard_map/rows_back/pallas_call | solution.py:112
  112.7 2.3 %collective-permute-done.4.from_east_ref = bf16[144,1024]{1,0:T(8,128)(2,1)S(1)} collective-permute-done((bf16[144,1024]{1,0:T(8,128)(2,1)S(1)}, bf16[144,1024]{1,0:T(8,128)(2,1)S(1)}, u32[]{:S(2)}, u32[]{:S(2)}) %collective-permute-start.4) | collective-permute-done | bytes 294944 | tf_op jit(solution)/shard_map/ppermute | solution.py:594
  115.0 0.2 collective-permute-done.5.from_west_ref
  115.2 0.4 fold.1
  115.6 1.6 collective-permute-start.6
  117.2 1.5 collective-permute-start.7
  118.7 0.0 copy-start.40
  118.8 0.0 copy-start.12
  118.8 2.1 %encode.1._ = bf16[192,1024]{1,0:T(8,128)(2,1)} custom-call(f32[192,1024]{1,0:T(8,128)S(1)} %get-tuple-element.43.after_ref, bf16[192,2048]{1,0:T(8,128)(2,1)S(1)} %get-tuple-element.44.hid_ref, bf16[2048,1024]{1,0:T(8,128)(2,1)S(1)} %copy-done.7, bf16[96,1024]{1,0:T(8,128)(2,1)S(1)} %get-tuple-element.48._), custom_call_target="tpu_custom_call" | custom-call | flops 805306368 | bytes 6356992 | tf_op jit(solution)/shard_map/encode/pallas_call | solution.py:112
  120.9 2.9 %own_back.1.dn_ref = f32[192,1024]{1,0:T(8,128)S(1)} custom-call(bf16[192,3072]{1,0:T(8,128)(2,1)S(1)} %get-tuple-element.49.dqkv_ref, bf16[144,1024]{1,0:T(8,128)(2,1)S(1)} %collective-permute-done.4.from_east_ref, bf16[144,1024]{1,0:T(8,128)(2,1)S(1)} %collective-permute-done.5.from_west_ref, bf16[288,192]{1,0:T(8,128)(2,1)S(1)} %copy-done.40, ...), custom_call_target="tpu_custom_call" | custom-call | flops 1207959552 | bytes 9154560 | tf_op jit(solution)/shard_map/own_back/pallas_call | solution.py:112
  123.8 0.2 copy-done.10
  124.0 0.1 copy-done.30
  124.1 0.1 copy-done.32
  124.2 0.1 copy-done.34
  124.3 10.5 %cross_back.1 = (f32[192,1024]{1,0:T(8,128)S(1)}, bf16[128,4,1024]{2,1,0:T(4,128)(2,1)}, bf16[192,1024]{1,0:T(8,128)(2,1)S(1)}, bf16[192,2048]{1,0:T(8,128)(2,1)S(1)}) custom-call(f32[192,1024]{1,0:T(8,128)S(1)} %own_back.1.dn_ref, bf16[96,1024]{1,0:T(8,128)(2,1)S(1)} %collective-permute-done.6.north_ref, ...), custom_call_target="tpu_custom_call" | custom-call | flops 4294967296 | bytes 19673088 | tf_op jit(solution)/shard_map/cross_back/pallas_call | solution.py:112
  134.8 0.9 copy-done.20
  135.7 0.9 copy-done.22
  136.6 0.7 copy-done.26
  137.4 15.0 %all-to-all-start.1 = ((bf16[128,4,1024]{2,1,0:T(4,128)(2,1)}), bf16[128,4,1024]{2,1,0:T(4,128)(2,1)}, u32[]{:S(2)}, u32[]{:S(2)}) async-start(bf16[128,4,1024]{2,1,0:T(4,128)(2,1)} %get-tuple-element.60), calls=%async_computation.1 | async-start | bytes 2097152 | tf_op jit(solution)/shard_map/all_to_all | solution.py:756
  152.4 2.2 %copy-done.5 = bf16[1024,2048]{1,0:T(8,128)(2,1)S(1)} copy-done((bf16[1024,2048]{1,0:T(8,128)(2,1)S(1)}, bf16[1024,2048]{1,0:T(8,128)(2,1)}, u32[]{:S(2)}) %copy-start.5) | copy-done | bytes 4194328
  154.6 1.1 copy-done.23
  155.7 1.0 copy-done.27
  156.7 3.7 %grid_back.1 = bf16[192,1024]{1,0:T(8,128)(2,1)} custom-call(bf16[192,1024]{1,0:T(8,128)(2,1)S(1)} %bitcast.12, f32[192,1024]{1,0:T(8,128)S(1)} %copy-done.21, f32[3,1024]{1,0:T(4,128)S(1)} %copy-done.38, bf16[192,1024]{1,0:T(8,128)(2,1)S(1)} %copy-done.27, bf16[192,2048]{1,0:T(8,128)(2,1)S(1)} %copy-done.23, bf16[1024,1024]{1,0:T(8,128)(2,1)S(1)} %copy-done.8, ...), custom_call_target="tpu_custom_call" | custom-call | flops 1207959552 | bytes 9056256 | tf_op jit(solution)/shard_map/grid_back/pallas_call | solution.py:112
  160.4 10.5 %all-to-all-done.1 = bf16[128,4,1024]{2,1,0:T(4,128)(2,1)} async-done(((bf16[128,4,1024]{2,1,0:T(4,128)(2,1)}), bf16[128,4,1024]{2,1,0:T(4,128)(2,1)}, u32[]{:S(2)}, u32[]{:S(2)}) %all-to-all-start.1) | async-done | bytes 1048608 | tf_op jit(solution)/shard_map/all_to_all | solution.py:756
  171.0 1.3 reshape.33
  172.3 1.3 convolution_convert_fusion
  (73 shorter events, 0.2 us)
Async XLA Ops:
  0.6 17.0 %copy-start.38 = (f32[3,1024]{1,0:T(4,128)S(1)}, f32[3,1024]{1,0:T(4,128)}, u32[]{:S(2)}) copy-start(f32[3,1024]{1,0:T(4,128)} %gain_ref.9) | copy-start | bytes 36868
  0.6 17.0 %copy-start.8 = (bf16[1024,1024]{1,0:T(8,128)(2,1)S(1)}, bf16[1024,1024]{1,0:T(8,128)(2,1)}, u32[]{:S(2)}) copy-start(bf16[1024,1024]{1,0:T(8,128)(2,1)} %wq_hbm.3) | copy-start | bytes 6291460
  0.7 17.0 %copy-start.15 = (bf16[12,16,1024]{2,1,0:T(8,128)(2,1)S(1)}, bf16[12,16,1024]{2,1,0:T(8,128)(2,1)}, u32[]{:S(2)}) copy-start(bf16[12,16,1024]{2,1,0:T(8,128)(2,1)} %param.18) | copy-start | bytes 1179652
  0.7 1.2 copy-start.43
  1.9 0.7 copy-start.44
  2.5 0.7 copy-start.45
  4.0 1.1 copy-start.17
  5.0 0.7 copy-start.35
  5.7 31.9 %all-to-all-start = ((bf16[128,4,1152]{2,1,0:T(4,128)(2,1)}), bf16[128,4,1152]{2,1,0:T(4,128)(2,1)}, u32[]{:S(2)}, u32[]{:S(2)}) async-start(bf16[128,4,1152]{2,1,0:T(4,128)(2,1)} %copy-done.17), calls=%async_computation | async-start | bytes 2359296 | tf_op jit(solution)/shard_map/all_to_all | solution.py:664
  17.7 2.2 %copy-start.2 = (bf16[1024,2048]{1,0:T(8,128)(2,1)S(1)}, bf16[1024,2048]{1,0:T(8,128)(2,1)}, u32[]{:S(2)}) copy-start(bf16[1024,2048]{1,0:T(8,128)(2,1)} %wp_hbm.7) | copy-start | bytes 12582916
  19.9 2.2 %copy-start.6 = (bf16[2048,1024]{1,0:T(8,128)(2,1)S(1)}, bf16[2048,1024]{1,0:T(8,128)(2,1)}, u32[]{:S(2)}) copy-start(bf16[2048,1024]{1,0:T(8,128)(2,1)} %wd_hbm.3) | copy-start | bytes 12582916
  22.0 1.0 copy-start.24
  27.5 0.7 copy-start.28
  28.3 0.9 copy-start.41
  37.7 2.2 %copy-start.3 = (bf16[1024,2048]{1,0:T(8,128)(2,1)S(1)}, bf16[1024,2048]{1,0:T(8,128)(2,1)}, u32[]{:S(2)}) copy-start(bf16[1024,2048]{1,0:T(8,128)(2,1)} %wp_hbm.7) | copy-start | bytes 12582916
  39.8 1.6 copy-start.11
  41.4 1.0 copy-start.29
  52.8 1.6 copy-start.9
  54.4 1.3 copy-start.13
  55.7 0.9 copy-start.18
  56.6 0.7 copy-start.31
  57.4 0.8 copy-start.33
  58.1 12.4 %collective-permute-start.1 = (bf16[96,1024]{1,0:T(8,128)(2,1)S(1)}, bf16[96,1024]{1,0:T(8,128)(2,1)}, u32[]{:S(2)}, u32[]{:S(2)}) collective-permute-start(bf16[96,1024]{1,0:T(8,128)(2,1)S(1)} %get-tuple-element.35.top_ref), channel_id=1, source_target_pairs={{16,0},{32,16},{48,32},{64,48},{80,64},{96,80},{112,96},{17,1},{33... | collective-permute-start | bytes 589832 | tf_op jit(solution)/shard_map/ppermute | solution.py:600
  59.4 11.1 %collective-permute-start = (bf16[96,1024]{1,0:T(8,128)(2,1)}, bf16[96,1024]{1,0:T(8,128)(2,1)}, u32[]{:S(2)}, u32[]{:S(2)}) collective-permute-start(bf16[96,1024]{1,0:T(8,128)(2,1)} %get-tuple-element.36.bottom_ref), channel_id=1, source_target_pairs={{0,16},{16,32},{32,48},{48,64},{64,80},{80,96},{96,112},{1,17},{17... | collective-permute-start | bytes 589832 | tf_op jit(solution)/shard_map/ppermute | solution.py:600
  64.1 2.8 %copy-start = (bf16[1024,3072]{1,0:T(8,128)(2,1)S(1)}, bf16[1024,3072]{1,0:T(8,128)(2,1)}, u32[]{:S(2)}) copy-start(bf16[1024,3072]{1,0:T(8,128)(2,1)} %w_hbm.7) | copy-start | bytes 18874372
  66.9 3.7 %copy-start.37 = (bf16[288,384]{1,0:T(8,128)(2,1)S(1)}, bf16[288,384]{1,0:T(8,128)(2,1)}, u32[]{:S(2)}) copy-start(bf16[288,384]{1,0:T(8,128)(2,1)} %constant.28.clone.sel_ref) | copy-start | bytes 663556
  66.9 7.9 %copy-start.47 = (s32[8,768]{1,0:T(8,128)S(1)}, s32[8,768]{1,0:T(8,128)}, u32[]{:S(2)}) copy-start(s32[8,768]{1,0:T(8,128)} %constant.27.clone) | copy-start | bytes 73732
  72.1 9.4 %collective-permute-start.2 = (bf16[144,1024]{1,0:T(8,128)(2,1)S(1)}, bf16[144,1024]{1,0:T(8,128)(2,1)S(1)}, u32[]{:S(2)}, u32[]{:S(2)}) collective-permute-start(bf16[144,1024]{1,0:T(8,128)(2,1)S(1)} %get-tuple-element.39), channel_id=1, source_target_pairs={{0,1},{1,2},{2,3},{3,4},{4,5},{5,6},{6,7},{7,8},{8,9},{9,10},{10,1... | collective-permute-start | bytes 884744 | tf_op jit(solution)/shard_map/ppermute | solution.py:594
  74.7 10.0 %collective-permute-start.3 = (bf16[144,1024]{1,0:T(8,128)(2,1)S(1)}, bf16[144,1024]{1,0:T(8,128)(2,1)S(1)}, u32[]{:S(2)}, u32[]{:S(2)}) collective-permute-start(bf16[144,1024]{1,0:T(8,128)(2,1)S(1)} %get-tuple-element.40), channel_id=1, source_target_pairs={{0,15},{1,0},{2,1},{3,2},{4,3},{5,4},{6,5},{7,6},{8,7},{9,8},{10,9... | collective-permute-start | bytes 884744 | tf_op jit(solution)/shard_map/ppermute | solution.py:594
  74.7 2.8 %copy-start.1 = (bf16[1024,3072]{1,0:T(8,128)(2,1)S(1)}, bf16[1024,3072]{1,0:T(8,128)(2,1)}, u32[]{:S(2)}) copy-start(bf16[1024,3072]{1,0:T(8,128)(2,1)} %w_hbm.7) | copy-start | bytes 18874372
  77.5 7.2 %copy-start.19 = (f32[192,1024]{1,0:T(8,128)S(1)}, f32[192,1024]{1,0:T(8,128)}, u32[]{:S(2)}) copy-start(f32[192,1024]{1,0:T(8,128)} %copy-done.18) | copy-start | bytes 2359300
  77.5 7.2 %copy-start.25 = (bf16[12,16,1024]{2,1,0:T(8,128)(2,1)S(1)}, bf16[12,16,1024]{2,1,0:T(8,128)(2,1)}, u32[]{:S(2)}) copy-start(bf16[12,16,1024]{2,1,0:T(8,128)(2,1)} %param.22) | copy-start | bytes 1179652
  77.5 7.2 %copy-start.42 = (bf16[192,2048]{1,0:T(8,128)(2,1)S(1)}, bf16[192,2048]{1,0:T(8,128)(2,1)}, u32[]{:S(2)}) copy-start(bf16[192,2048]{1,0:T(8,128)(2,1)} %copy-done.41) | copy-start | bytes 2359300
  77.5 7.2 %copy-start.46 = (bf16[192,768]{1,0:T(8,128)(2,1)S(1)}, bf16[192,768]{1,0:T(8,128)(2,1)}, u32[]{:S(2)}) copy-start(bf16[192,768]{1,0:T(8,128)(2,1)} %constant.26.clone.base_ref) | copy-start | bytes 884740
  84.8 25.8 %slice-start = ((s8[6291456]{0:T(1024)(128)(4,1)}), s8[4194304]{0:T(1024)(128)(4,1)S(1)}, s32[]{:S(2)}) async-start(s8[6291456]{0:T(1024)(128)(4,1)} %bitcast.8), calls=%async_computation.2 | async-start | bytes 8388608
  84.8 25.8 %slice-start.1 = ((s8[6291456]{0:T(1024)(128)(4,1)}), s8[2097152]{0:T(1024)(128)(4,1)S(1)}, s32[]{:S(2)}) async-start(s8[6291456]{0:T(1024)(128)(4,1)} %bitcast.8), calls=%async_computation.3 | async-start | bytes 4194304
  107.3 7.7 %collective-permute-start.4 = (bf16[144,1024]{1,0:T(8,128)(2,1)S(1)}, bf16[144,1024]{1,0:T(8,128)(2,1)S(1)}, u32[]{:S(2)}, u32[]{:S(2)}) collective-permute-start(bf16[144,1024]{1,0:T(8,128)(2,1)S(1)} %get-tuple-element.46), channel_id=1, source_target_pairs={{0,15},{1,0},{2,1},{3,2},{4,3},{5,4},{6,5},{7,6},{8,7},{9,8},{10,9... | collective-permute-start | bytes 884744 | tf_op jit(solution)/shard_map/ppermute | solution.py:594
  107.4 7.9 %collective-permute-start.5 = (bf16[144,1024]{1,0:T(8,128)(2,1)S(1)}, bf16[144,1024]{1,0:T(8,128)(2,1)S(1)}, u32[]{:S(2)}, u32[]{:S(2)}) collective-permute-start(bf16[144,1024]{1,0:T(8,128)(2,1)S(1)} %get-tuple-element.47), channel_id=1, source_target_pairs={{0,1},{1,2},{2,3},{3,4},{4,5},{5,6},{6,7},{7,8},{8,9},{9,10},{10,1... | collective-permute-start | bytes 884744 | tf_op jit(solution)/shard_map/ppermute | solution.py:594
  110.6 4.6 %copy-start.39 = (bf16[288,192]{1,0:T(8,128)(2,1)S(1)}, bf16[288,192]{1,0:T(8,128)(2,1)}, u32[]{:S(2)}) copy-start(bf16[288,192]{1,0:T(8,128)(2,1)} %constant.29.clone.sel_ref) | copy-start | bytes 331780
  110.6 8.1 %copy-start.7 = (bf16[2048,1024]{1,0:T(8,128)(2,1)S(1)}, bf16[2048,1024]{1,0:T(8,128)(2,1)}, u32[]{:S(2)}) copy-start(bf16[2048,1024]{1,0:T(8,128)(2,1)} %wd_hbm.3) | copy-start | bytes 12582916
  115.6 8.2 %collective-permute-start.6 = (bf16[96,1024]{1,0:T(8,128)(2,1)S(1)}, bf16[96,1024]{1,0:T(8,128)(2,1)S(1)}, u32[]{:S(2)}, u32[]{:S(2)}) collective-permute-start(bf16[96,1024]{1,0:T(8,128)(2,1)S(1)} %get-tuple-element.48._), channel_id=1, source_target_pairs={{0,16},{16,32},{32,48},{48,64},{64,80},{80,96},{96,112},{1,17},{17... | collective-permute-start | bytes 589832 | tf_op jit(solution)/shard_map/ppermute | solution.py:600
  117.2 6.6 %collective-permute-start.7 = (bf16[96,1024]{1,0:T(8,128)(2,1)S(1)}, bf16[96,1024]{1,0:T(8,128)(2,1)S(1)}, u32[]{:S(2)}, u32[]{:S(2)}) collective-permute-start(bf16[96,1024]{1,0:T(8,128)(2,1)S(1)} %get-tuple-element.50._), channel_id=1, source_target_pairs={{16,0},{32,16},{48,32},{64,48},{80,64},{96,80},{112,96},{17,1},{33... | collective-permute-start | bytes 589832 | tf_op jit(solution)/shard_map/ppermute | solution.py:600
  118.7 2.1 %copy-start.40 = (bf16[288,192]{1,0:T(8,128)(2,1)S(1)}, bf16[288,192]{1,0:T(8,128)(2,1)}, u32[]{:S(2)}) copy-start(bf16[288,192]{1,0:T(8,128)(2,1)} %constant.30.clone.sel_ref) | copy-start | bytes 331780
  118.8 5.1 %copy-start.12 = (bf16[1024,1024]{1,0:T(8,128)(2,1)S(1)}, bf16[1024,1024]{1,0:T(8,128)(2,1)}, u32[]{:S(2)}) copy-start(bf16[1024,1024]{1,0:T(8,128)(2,1)} %wo_hbm.5) | copy-start | bytes 6291460
  118.8 5.1 %copy-start.14 = (bf16[512,2048]{1,0:T(8,128)(2,1)S(1)}, bf16[512,2048]{1,0:T(8,128)(2,1)}, u32[]{:S(2)}) copy-start(bf16[512,2048]{1,0:T(8,128)(2,1)} %copy-done.13) | copy-start | bytes 6291460
  120.9 3.0 %copy-start.4 = (bf16[1024,2048]{1,0:T(8,128)(2,1)S(1)}, bf16[1024,2048]{1,0:T(8,128)(2,1)}, u32[]{:S(2)}) copy-start(bf16[1024,2048]{1,0:T(8,128)(2,1)} %wp_hbm.7) | copy-start | bytes 12582916
  120.9 3.1 %copy-start.10 = (bf16[8,384,512]{2,1,0:T(8,128)(2,1)S(1)}, bf16[8,384,512]{2,1,0:T(8,128)(2,1)}, u32[]{:S(2)}) copy-start(bf16[8,384,512]{2,1,0:T(8,128)(2,1)} %copy-done.9) | copy-start | bytes 9437188
  120.9 3.1 %copy-start.16 = (bf16[192,1024]{1,0:T(8,128)(2,1)S(1)}, bf16[192,1024]{1,0:T(8,128)(2,1)}, u32[]{:S(2)}) copy-start(bf16[192,1024]{1,0:T(8,128)(2,1)} %encode.1._) | copy-start | bytes 1179652
  120.9 3.2 %copy-start.30 = (bf16[192,1024]{1,0:T(8,128)(2,1)S(1)}, bf16[192,1024]{1,0:T(8,128)(2,1)}, u32[]{:S(2)}) copy-start(bf16[192,1024]{1,0:T(8,128)(2,1)} %copy-done.28) | copy-start | bytes 1179652
  120.9 3.3 %copy-start.32 = (bf16[192,1024]{1,0:T(8,128)(2,1)S(1)}, bf16[192,1024]{1,0:T(8,128)(2,1)}, u32[]{:S(2)}) copy-start(bf16[192,1024]{1,0:T(8,128)(2,1)} %copy-done.31) | copy-start | bytes 1179652
  120.9 3.4 %copy-start.34 = (bf16[192,1024]{1,0:T(8,128)(2,1)S(1)}, bf16[192,1024]{1,0:T(8,128)(2,1)}, u32[]{:S(2)}) copy-start(bf16[192,1024]{1,0:T(8,128)(2,1)} %copy-done.33) | copy-start | bytes 1179652
  134.8 0.9 copy-start.20
  135.7 0.9 copy-start.22
  136.6 0.7 copy-start.26
  137.4 15.1 %copy-start.21 = (f32[192,1024]{1,0:T(8,128)S(1)}, f32[192,1024]{1,0:T(8,128)}, u32[]{:S(2)}) copy-start(f32[192,1024]{1,0:T(8,128)} %copy-done.20) | copy-start | bytes 2359300
  137.4 33.6 %all-to-all-start.1 = ((bf16[128,4,1024]{2,1,0:T(4,128)(2,1)}), bf16[128,4,1024]{2,1,0:T(4,128)(2,1)}, u32[]{:S(2)}, u32[]{:S(2)}) async-start(bf16[128,4,1024]{2,1,0:T(4,128)(2,1)} %get-tuple-element.60), calls=%async_computation.1 | async-start | bytes 2097152 | tf_op jit(solution)/shard_map/all_to_all | solution.py:756
  152.4 2.2 %copy-start.5 = (bf16[1024,2048]{1,0:T(8,128)(2,1)S(1)}, bf16[1024,2048]{1,0:T(8,128)(2,1)}, u32[]{:S(2)}) copy-start(bf16[1024,2048]{1,0:T(8,128)(2,1)} %wp_hbm.7) | copy-start | bytes 12582916
  154.6 1.1 copy-start.23
  155.7 1.0 copy-start.27
  160.4 11.9 %copy-start.36 = (bf16[512,256]{1,0:T(8,128)(2,1)S(1)}, bf16[512,256]{1,0:T(8,128)(2,1)}, u32[]{:S(2)}) copy-start(bf16[512,256]{1,0:T(8,128)(2,1)} %copy-done.35) | copy-start | bytes 786436

commit v3 on v2

--- a/solution.py
+++ b/solution.py
@@ -101,20 +101,27 @@
     any_spec = pl.BlockSpec(memory_space=pl.ANY)
     vmem_spec = pl.BlockSpec(memory_space=pltpu.VMEM)
     moved = sum(x.size * x.dtype.itemsize for x in ins)
-    moved += sum(int(np.prod(s)) * jnp.dtype(t).itemsize for s, t in outs)
+    moved += sum(int(np.prod(o[0])) * jnp.dtype(o[1]).itemsize for o in outs)
     held = sum(x.size * x.dtype.itemsize for x, k in zip(ins, kinds) if k == "v")
-    held += sum(int(np.prod(s)) * jnp.dtype(t).itemsize for s, t in outs)
+    held += sum(int(np.prod(o[0])) * jnp.dtype(o[1]).itemsize for o in outs if len(o) == 2)
     for item in scratch:
         if jnp.issubdtype(item.dtype, jnp.floating):
             held += int(np.prod(item.shape)) * jnp.dtype(item.dtype).itemsize
     single = len(outs) == 1
-    shapes = [jax.ShapeDtypeStruct(s, t) for s, t in outs]
+    shapes = [
+        jax.ShapeDtypeStruct(*o) if len(o) == 2 else pltpu.HBM(o[0], o[1]) for o in outs
+    ]
+    specs = [vmem_spec if len(o) == 2 else any_spec for o in outs]
+    ins = [
+        pltpu.with_memory_space_constraint(x, pltpu.HBM) if k == "h" else x
+        for x, k in zip(ins, kinds)
+    ]
     return pl.pallas_call(
         body,
         name=name,
         out_shape=shapes[0] if single else shapes,
-        in_specs=[any_spec if k == "h" else vmem_spec for k in kinds],
-        out_specs=vmem_spec if single else [vmem_spec] * len(outs),
+        in_specs=[vmem_spec if k == "v" else any_spec for k in kinds],
+        out_specs=specs[0] if single else specs,
         scratch_shapes=scratch,
         compiler_params=pltpu.CompilerParams(vmem_limit_bytes=held + SLACK_BYTES),
         cost_estimate=pl.CostEstimate(
@@ -123,7 +130,12 @@
     )(*ins)
 
 
-def place_kernel(tile_ref, cell_ref, obs_ref, pay_ref, place_ref, *, devices, cap, wide):
+def place_kernel(
+    tile_hbm, cell_hbm, obs_hbm, pay_hbm, place_hbm,
+    tile_ref, cell_ref, obs_ref, pay_ref, place_ref, sems, *, devices, cap, wide,
+):
+    copies = fetch([tile_hbm, cell_hbm, obs_hbm], [tile_ref, cell_ref, obs_ref], sems)
+    copies[0].wait()
     rows, model = obs_ref.shape
     slots = devices * cap
     tile = tile_ref[...]
@@ -134,6 +146,8 @@
     slot = tile * cap + rank
     placing = (slot == iota((slots, rows), 0)).astype(F32).astype(BF)
     place_ref[...] = placing
+    copies[1].wait()
+    copies[2].wait()
     cell = cell_ref[...]
     shift = wide.bit_length() - 1
     line_no = iota((128, rows), 0)
@@ -144,14 +158,19 @@
     pay_ref[:, :, model:] = code_rows.reshape(devices, cap, 128)
     moved = dot(placing, obs_ref[...]).astype(BF)
     pay_ref[:, :, :model] = moved.reshape(devices, cap, model)
+    for copy in fetch([pay_ref, place_ref], [pay_hbm, place_hbm], sems):
+        copy.wait()
 
 
 def grid_kernel(
-    grid_ref, cot_ref, gain_ref, wq_hbm, wp_hbm, wd_hbm, q_ref, own_ref, dh_ref,
-    nrm, wq, wp, wd, sems,
+    grid_hbm, cot_hbm, gain_ref, wq_hbm, wp_hbm, wd_hbm, q_hbm, own_hbm, dh_hbm,
+    grid_ref, cot_ref, q_ref, own_ref, dh_ref, nrm, wq, wp, wd, sems, out_sems,
 ):
-    copies = fetch([wq_hbm, wp_hbm, wd_hbm], [wq, wp, wd], sems)
+    first, *copies = fetch(
+        [grid_hbm, wq_hbm, wp_hbm, wd_hbm, cot_hbm], [grid_ref, wq, wp, wd, cot_ref], sems
+    )
     cells, model = grid_ref.shape
+    first.wait()
     for rows in row_chunks(cells):
         normed, _ = unit(grid_ref[rows, :].astype(F32))
         nrm[rows, :] = (normed * gain_ref[0:1, :]).astype(BF)
@@ -170,19 +189,25 @@
 
     tiles_of(2 * model, own)
     copies[2].wait()
+    copies[3].wait()
 
     def hidden(j):
         dh_ref[:, pl.ds(j, TILE)] = dot(cot_ref[...], wd[pl.ds(j, TILE), :], NT).astype(BF)
 
     tiles_of(dh_ref.shape[1], hidden)
+    for copy in fetch([q_ref, own_ref, dh_ref], [q_hbm, own_hbm, dh_hbm], out_sems):
+        copy.wait()
 
 
 def cross_kernel(
-    arr_ref, grid_ref, q_ref, own_ref, gain_ref, wp_hbm, wo_hbm,
-    state_ref, top_ref, bottom_ref, pairs_ref, wts_ref, mix_ref, ow_ref,
-    arr, wp, wo, scores, bias, sems, *, wide,
+    arr_ref, grid_hbm, q_hbm, own_hbm, gain_ref, wp_hbm, wo_hbm,
+    state_hbm, top_ref, bottom_ref, pairs_hbm, wts_hbm, mix_hbm, ow_hbm,
+    arr, wp, wo, scores, bias, grid_ref, q_ref, own_ref, state_ref, pairs_ref, wts_ref,
+    mix_ref, ow_ref, sems, out_sems, *, wide,
 ):
-    copies = fetch([wp_hbm, wo_hbm], [wp, wo], sems)
+    copies = fetch(
+        [wp_hbm, wo_hbm, q_hbm, own_hbm, grid_hbm], [wp, wo, q_ref, own_ref, grid_ref], sems
+    )
     cells, model = grid_ref.shape
     rim = top_ref.shape[0]
     slots = arr.shape[0]
@@ -203,6 +228,9 @@
         ).astype(BF)
 
     tiles_of(2 * model, project)
+    leaving = fetch([pairs_ref], [pairs_hbm], out_sems.at[pl.ds(0, 1)])
+    copies[2].wait()
+    copies[3].wait()
 
     def soften(h, k, own_scores):
         own_weights = []
@@ -241,7 +269,11 @@
                 mix + weights[k].astype(F32) * own_ref[:, vals].astype(F32)
             ).astype(BF)
 
+    leaving += fetch(
+        [wts_ref, mix_ref, ow_ref], [wts_hbm, mix_hbm, ow_hbm], out_sems.at[pl.ds(1, 3)]
+    )
     copies[1].wait()
+    copies[4].wait()
 
     def project_out(j):
         state_ref[:, pl.ds(j, TILE)] = grid_ref[:, pl.ds(j, TILE)].astype(F32) + dot(
@@ -249,6 +281,7 @@
         )
 
     tiles_of(model, project_out)
+    leaving += fetch([state_ref], [state_hbm], out_sems.at[pl.ds(4, 1)])
     for i in range(0, cells, CHUNK):
         normed, _ = unit(state_ref[pl.ds(i, CHUNK), :])
         normed = (normed * gain_ref[1:2, :]).astype(BF)
@@ -256,6 +289,8 @@
             top_ref[pl.ds(i, CHUNK), :] = normed
         else:
             bottom_ref[pl.ds(i - rim, CHUNK), :] = normed
+    for copy in leaving:
+        copy.wait()
 
 
 def near_own_kernel(top_ref, bottom_ref, w_hbm, q_ref, kv_ref, nrm, w, sems):
@@ -501,8 +536,8 @@
 def cross_back_kernel(
     dn_ref, north_ref, south_ref, state_ref, dafter_ref, gain_ref, q_ref, own_ref, pairs_ref,
     wts_ref, mix_ref, ow_ref, wp_hbm, wo_hbm, _,
-    dstate_ref, slot_ref, dq_ref, down_ref,
-    wp, wo, dsb, dmix, dpairs, scores, ds, sems,
+    dstate_hbm, slot_ref, dq_hbm, down_hbm,
+    wp, wo, dsb, dmix, dpairs, scores, ds, dstate_ref, dq_ref, down_ref, sems, out_sems,
 ):
     copies = fetch([wo_hbm, wp_hbm], [wo, wp], sems)
     cells, model = state_ref.shape
@@ -558,6 +593,9 @@
             dpairs[:, keys] = dot(stacked(q), ds[k], TN).T.astype(BF)
             dpairs[:, vals] = dot(stacked(grad), wts_ref[h], TN).T.astype(BF)
 
+    leaving = fetch(
+        [dstate_ref, dq_ref, down_ref], [dstate_hbm, dq_hbm, down_hbm], out_sems
+    )
     copies[1].wait()
 
     def slot_back(j):
@@ -565,6 +603,13 @@
         slot_ref[:, :, pl.ds(j, TILE)] = grads.reshape(slot_ref.shape[:2] + (TILE,))
 
     tiles_of(model, slot_back)
+    for copy in leaving:
+        copy.wait()
+
+
+def gather_kernel(place_ref, ret_ref, out_ref, ret):
+    ret[...] = ret_ref[...].reshape(ret.shape)
+    out_ref[...] = dot(place_ref[...], ret[...], TN).astype(BF)
 
 
 def grid_back_kernel(
@@ -657,38 +702,46 @@
 
     payload, placing = call(
         functools.partial(place_kernel, devices=devices, cap=cap, wide=rows_lon),
-        (obs_tile.reshape(1, rows_obs), obs_cell.reshape(1, rows_obs), observations), "vvv",
-        [((devices, cap, model + 128), BF), ((slots, rows_obs), BF)], [],
+        (obs_tile.reshape(1, rows_obs), obs_cell.reshape(1, rows_obs), observations), "hhh",
+        [((devices, cap, model + 128), BF, "h"), ((slots, rows_obs), BF, "h")],
+        [vm((1, rows_obs), jnp.int32), vm((1, rows_obs), jnp.int32), vm((rows_obs, model), BF),
+         vm((devices, cap, model + 128), BF), vm((slots, rows_obs), BF), dma((3,))],
         2 * rows_obs * slots * model, "place",
     )
     arrived = lax.all_to_all(payload, ("lat", "lon"), 0, 0, tiled=True)
     q_c, own_pairs, dhid = call(
         grid_kernel,
-        (flat, cot, norm_gains, w_cross_query, w_cross_pairs, w_down), "vvvhhh",
-        [((cells, model), BF), ((cells, 2 * model), BF), ((cells, ff), BF)],
-        [vm((cells, model), BF), vm((model, model), BF), vm((model, 2 * model), BF),
-         vm((ff, model), BF), dma((3,))],
+        (flat, cot, norm_gains, w_cross_query, w_cross_pairs, w_down), "hhvhhh",
+        [((cells, model), BF, "h"), ((cells, 2 * model), BF, "h"), ((cells, ff), BF, "h")],
+        [vm((cells, model), BF), vm((cells, model), BF), vm((cells, model), BF),
+         vm((cells, 2 * model), BF), vm((cells, ff), BF),
+         vm((cells, model), BF), vm((model, model), BF), vm((model, 2 * model), BF),
+         vm((ff, model), BF), dma((5,)), dma((3,))],
         2 * cells * model * (3 * model + ff), "grid_proj",
     )
     state, top, bottom, slot_pairs, cross_w, cross_mix, own_w = call(
         functools.partial(cross_kernel, wide=rows_lon),
-        (arrived, flat, q_c, own_pairs, norm_gains, w_cross_pairs, w_cross_out), "vvvvvhh",
-        [((cells, model), F32), ((rim, model), BF), ((rim, model), BF), ((slots, 2 * model), BF),
-         ((pairs_n, 2 * cells, slots), BF), ((cells, model), BF), ((cells, model), BF)],
+        (arrived, flat, q_c, own_pairs, norm_gains, w_cross_pairs, w_cross_out), "vhhhvhh",
+        [((cells, model), F32, "h"), ((rim, model), BF), ((rim, model), BF),
+         ((slots, 2 * model), BF, "h"), ((pairs_n, 2 * cells, slots), BF, "h"),
+         ((cells, model), BF, "h"), ((cells, model), BF, "h")],
         [vm((slots, model + 128), BF), vm((model, 2 * model), BF), vm((model, model), BF),
-         vm((GROUP, 2 * cells, slots), F32), vm((cells, slots), F32), dma((2,))],
+         vm((GROUP, 2 * cells, slots), F32), vm((cells, slots), F32), vm((cells, model), BF),
+         vm((cells, model), BF), vm((cells, 2 * model), BF), vm((cells, model), F32),
+         vm((slots, 2 * model), BF), vm((pairs_n, 2 * cells, slots), BF), vm((cells, model), BF),
+         vm((cells, model), BF), dma((5,)), dma((5,))],
         2 * slots * model * 2 * model * 2, "cross",
     )
     south = line(top, -1)
     north = line(bottom, 1)
     q_n, kv_own = call(
-        near_own_kernel, (top, bottom, w_near_proj), "vvh",
+        near_own_kernel, (top, bottom, w_near_proj), "vva",
         [((cells, model), BF), ((cells, 2 * model), BF)],
         [vm((cells, model), BF), vm((model, 3 * model), BF), dma((2,))],
         2 * cells * model * 3 * model, "near_own",
     )
     west_send, east_send = call(
-        rim_kernel, (top, bottom, north, south, jnp.asarray(select), kv_own), "vvvvvh",
+        rim_kernel, (top, bottom, north, south, jnp.asarray(select), kv_own), "vvvvva",
         [((side, model), BF), ((side, model), BF)],
         [vm((cells + 2 * rim, model), BF)],
         2 * 2 * side * 2 * cells * model, "rim",
@@ -696,7 +749,7 @@
     east = ring(west_send, -1)
     west = ring(east_send, 1)
     kv_rows = call(
-        near_rows_kernel, (north, south, w_near_proj), "vvh",
+        near_rows_kernel, (north, south, w_near_proj), "vva",
         [((2 * rim, 2 * model), BF)],
         [vm((2 * rim, model), BF), vm((model, 2 * model), BF), dma((1,))],
         2 * 2 * rim * model * 2 * model, "near_rows",
@@ -704,7 +757,7 @@
     after, hidden, dwest, deast, dqkv, drows, dafter = call(
         near_kernel,
         (q_n, west, east, base, inside, state, cot, dhid, norm_gains, kv_own, kv_rows,
-         w_near_proj, w_near_out, w_up), "vvvvvvvvvhhhhh",
+         w_near_proj, w_near_out, w_up), "vvvvvvvvvaaaaa",
         [((cells, model), F32), ((cells, ff), BF), ((side, model), BF), ((side, model), BF),
          ((cells, 3 * model), BF), ((2 * rim, 2 * model), BF), ((cells, model), F32)],
         [vm((model, 2 * model), BF), vm((model, model), BF), vm((model, ff), BF),
@@ -719,7 +772,7 @@
     from_east = ring(dwest, -1)
     from_west = ring(deast, 1)
     dn_rows = call(
-        rows_back_kernel, (drows, w_near_proj), "vh", [((2 * rim, model), F32)],
+        rows_back_kernel, (drows, w_near_proj), "va", [((2 * rim, model), F32)],
         [vm((model, 2 * model), BF), dma((1,))],
         2 * 2 * rim * model * 2 * model, "rows_back",
     )
@@ -733,37 +786,39 @@
     from_north = line(dsouth, 1)
     dn_own = call(
         own_back_kernel,
-        (dqkv, from_east, from_west, jnp.asarray(select[:, :cells]), w_near_proj, dnorth), "vvvvhh",
+        (dqkv, from_east, from_west, jnp.asarray(select[:, :cells]), w_near_proj, dnorth), "vvvvaa",
         [((cells, model), F32)],
         [vm((2 * side, model), BF), vm((model, 3 * model), BF), dma((1,))],
         2 * cells * model * 3 * model, "own_back",
     )
     encoded = call(
-        encode_kernel, (after, hidden, w_down, dsouth), "vvhh", [((cells, model), BF)],
+        encode_kernel, (after, hidden, w_down, dsouth), "vvaa", [((cells, model), BF)],
         [vm((ff, model), BF), dma((1,))], 2 * cells * model * ff, "encode",
     )
     dstate, slot_grads, dq, down = call(
         cross_back_kernel,
         (dn_own, from_north, from_south, state, dafter, norm_gains, q_c, own_pairs, slot_pairs,
-         cross_w, cross_mix, own_w, w_cross_pairs, w_cross_out, encoded), "vvvvvvvvvvvvhhh",
-        [((cells, model), F32), ((devices, cap, model), BF), ((cells, model), BF),
-         ((cells, 2 * model), BF)],
+         cross_w, cross_mix, own_w, w_cross_pairs, w_cross_out, encoded), "vvvvvvvvvvvvaaa",
+        [((cells, model), F32, "h"), ((devices, cap, model), BF), ((cells, model), BF, "h"),
+         ((cells, 2 * model), BF, "h")],
         [vm((model, 2 * model), BF), vm((model, model), BF), vm((cells, model), BF),
          vm((cells, model), BF), vm((slots, 2 * model), BF), vm((GROUP, 2 * cells, slots), F32),
-         vm((GROUP, 2 * cells, slots), BF), dma((2,))],
+         vm((GROUP, 2 * cells, slots), BF), vm((cells, model), F32), vm((cells, model), BF),
+         vm((cells, 2 * model), BF), dma((2,)), dma((3,))],
         2 * slots * model * 2 * model * 2, "cross_back",
     )
-    returned = lax.all_to_all(
-        slot_grads, ("lat", "lon"), 0, 0, tiled=True
-    ).reshape(slots, model)
+    returned = lax.all_to_all(slot_grads, ("lat", "lon"), 0, 0, tiled=True)
     grid_grad = call(
         grid_back_kernel,
-        (flat, dstate, norm_gains, dq, down, w_cross_query, w_cross_pairs), "vvvvvhh",
+        (flat, dstate, norm_gains, dq, down, w_cross_query, w_cross_pairs), "vvvvvaa",
         [((cells, model), BF)],
         [vm((model, model), BF), vm((model, 2 * model), BF), vm((cells, model), F32), dma((2,))],
         2 * cells * model * 3 * model, "grid_back",
     )
-    obs_grad = dot(placing, returned, TN).astype(BF)
+    obs_grad = call(
+        gather_kernel, (placing, returned), "vv", [((rows_obs, model), BF)],
+        [vm((slots, model), BF)], 2 * rows_obs * slots * model, "gather",
+    )
     shape = (rows_lat, rows_lon, model)
     return encoded.reshape(shape), grid_grad.reshape(shape), obs_grad
 

time: 174 us -> 158 us (0.908)
  local copies, waits for them, and re-layouts: 35.7 us -> 13.6 us
  waiting for transfers between devices: 25.6 us -> 31.2 us
  Pallas kernels: 68 us -> 70.1 us
    unnamed x100 -> x62, local copies, waits for them, and re-layouts: 34.3 us -> 13.6 us
    all_to_all x1, waiting for transfers between devices: 8.48 us -> 13.5 us  [per_device(): arrived = lax.all_to_all(payload, ('lat', 'lon'), 0, 0, tiled=True)]
    pallas_call x13 -> x14, Pallas kernels: 68 us -> 70.1 us  [call(): pl.pallas_call(body, name=name, out_shape=shapes[0] if single else shapes...]
  transfers between devices with their start and end apart: 10 -> 10, of which waited for: 6 -> 6; matrix products, arithmetic and copies ran while one was open for 0% -> 0% of each run, Pallas kernels for 13% -> 14%
where the time goes in v3:
time: 158 us
  Pallas kernels  70.1 us (44%)
  starting transfers between devices  41.7 us (26%)
  waiting for transfers between devices  31.2 us (20%)
  local copies, waits for them, and re-layouts  13.6 us (9%)
    pallas_call x14, Pallas kernels, call(): pl.pallas_call(body, name=name, out_shape=shapes[0] if single else shapes...  70.1 us
    all_to_all x1, starting transfers between devices, per_device(): returned = lax.all_to_all(slot_grads, ('lat', 'lon'), 0, 0, tiled=True)  14.7 us
    unnamed x62, local copies, waits for them, and re-layouts  13.6 us
    all_to_all x1, waiting for transfers between devices, per_device(): arrived = lax.all_to_all(payload, ('lat', 'lon'), 0, 0, tiled=True)  13.5 us
    all_to_all x1, starting transfers between devices, per_device(): arrived = lax.all_to_all(payload, ('lat', 'lon'), 0, 0, tiled=True)  11.5 us
    all_to_all x1, waiting for transfers between devices, per_device(): returned = lax.all_to_all(slot_grads, ('lat', 'lon'), 0, 0, tiled=True)  9.74 us
    ppermute x4, starting transfers between devices, line(): return lax.ppermute(value, 'lat', pairs)  9.62 us
    ppermute x4, waiting for transfers between devices, ring(): lax.ppermute(value, 'lon', [(i, (i + by) % size) for i in range(size)])  7.92 us
  transfers between devices with their start and end apart: 10, of which 6 were waited for; matrix products, arithmetic and copies ran while one was open for 0% of the time, Pallas kernels for 14%

profile of v3, /device:TPU:1, one launch (start us, length us, event | category | flops | bytes accessed | tf_op | source)
XLA Modules:
  0.0 157.6 jit_solution(16541456287527707286)
XLA Ops:
  0.6 0.0 copy-start.23
  0.6 2.8 %place.1 = (bf16[128,4,1152]{2,1,0:T(4,128)(2,1)}, bf16[512,256]{1,0:T(8,128)(2,1)}) custom-call(s32[1,256]{1,0:T(1,128)} %bitcast.15, s32[1,256]{1,0:T(1,128)} %bitcast.16, bf16[256,1024]{1,0:T(8,128)(2,1)} %obs_hbm.1), custom_call_target="tpu_custom_call" | custom-call | flops 268435456 | bytes 1968128 | tf_op jit(solution)/shard_map/place/pallas_call | solution.py:119
  3.4 11.5 %all-to-all-start = ((bf16[128,4,1152]{2,1,0:T(4,128)(2,1)}), bf16[128,4,1152]{2,1,0:T(4,128)(2,1)S(1)}, u32[]{:S(2)}, u32[]{:S(2)}) async-start(bf16[128,4,1152]{2,1,0:T(4,128)(2,1)} %get-tuple-element.32), calls=%async_computation | async-start | bytes 2359296 | tf_op jit(solution)/shard_map/all_to_all | solution.py:711
  14.9 0.0 copy-done.23
  15.0 6.8 %grid_proj.1 = (bf16[192,1024]{1,0:T(8,128)(2,1)}, bf16[192,2048]{1,0:T(8,128)(2,1)}, bf16[192,2048]{1,0:T(8,128)(2,1)}) custom-call(bf16[192,1024]{1,0:T(8,128)(2,1)} %bitcast.8, bf16[192,1024]{1,0:T(8,128)(2,1)} %bitcast.12, f32[3,1024]{1,0:T(4,128)S(1)} %copy-done.23, bf16[1024,1024]{1,0:T(8,128)(2,1)} %wq_hbm.3, bf16[1024,2048]{1,0:T(8,128)(2,1)} %wp_hbm.7, ...), custom_call_target="tpu_custom_call" | custom-call | flops 2013265920 | bytes 13250560 | tf_op jit(solution)/shard_map/grid_proj/pallas_call | solution.py:119
  21.8 13.5 %all-to-all-done.arr_ref = bf16[128,4,1152]{2,1,0:T(4,128)(2,1)S(1)} async-done(((bf16[128,4,1152]{2,1,0:T(4,128)(2,1)}), bf16[128,4,1152]{2,1,0:T(4,128)(2,1)S(1)}, u32[]{:S(2)}, u32[]{:S(2)}) %all-to-all-start) | async-done | bytes 1179680 | tf_op jit(solution)/shard_map/all_to_all | solution.py:711
  35.3 11.2 %cross.1 = (f32[192,1024]{1,0:T(8,128)}, bf16[96,1024]{1,0:T(8,128)(2,1)S(1)}, bf16[96,1024]{1,0:T(8,128)(2,1)S(1)}, bf16[512,2048]{1,0:T(8,128)(2,1)}, bf16[8,3...) custom-call(bf16[128,4,1152]{2,1,0:T(4,128)(2,1)S(1)} %all-to-all-done.arr_ref, ...), custom_call_target="tpu_custom_call" | custom-call | flops 4294967296 | bytes 16265216 | tf_op jit(solution)/shard_map/cross/pallas_call | solution.py:119
  46.5 1.3 collective-permute-start.1
  47.8 4.0 %collective-permute-start = (bf16[96,1024]{1,0:T(8,128)(2,1)S(1)}, bf16[96,1024]{1,0:T(8,128)(2,1)S(1)}, u32[]{:S(2)}, u32[]{:S(2)}) collective-permute-start(bf16[96,1024]{1,0:T(8,128)(2,1)S(1)} %get-tuple-element.36.bottom_ref), channel_id=1, source_target_pairs={{0,16},{16,32},{32,48},{48,64},{64,80},{80,96},{96,112},{1,17},{17... | collective-permute-start | bytes 589832 | tf_op jit(solution)/shard_map/ppermute | solution.py:645
  51.8 0.0 copy-start
  51.8 2.8 %copy-done = bf16[1024,3072]{1,0:T(8,128)(2,1)S(1)} copy-done((bf16[1024,3072]{1,0:T(8,128)(2,1)S(1)}, bf16[1024,3072]{1,0:T(8,128)(2,1)}, u32[]{:S(2)}) %copy-start) | copy-done | bytes 6291480
  54.6 2.6 %near_own.1 = (bf16[192,1024]{1,0:T(8,128)(2,1)S(1)}, bf16[192,2048]{1,0:T(8,128)(2,1)S(1)}) custom-call(bf16[96,1024]{1,0:T(8,128)(2,1)S(1)} %get-tuple-element.35.top_ref, bf16[96,1024]{1,0:T(8,128)(2,1)S(1)} %get-tuple-element.36.bottom_ref, bf16[1024,3072]{1,0:T(8,128)(2,1)S(1)} %copy-done), custom_call_target="tpu_custom_call" | custom-call | flops 1207959552 | bytes 7864320 | tf_op jit(solution)/shard_map/near_own/pallas_call | solution.py:119
  57.2 0.0 collective-permute-done.1.south_ref
  57.2 0.0 collective-permute-done.north_ref
  57.3 0.0 copy-done.22
  57.3 0.5 rim.1
  57.7 2.6 %collective-permute-start.2 = (bf16[144,1024]{1,0:T(8,128)(2,1)S(1)}, bf16[144,1024]{1,0:T(8,128)(2,1)S(1)}, u32[]{:S(2)}, u32[]{:S(2)}) collective-permute-start(bf16[144,1024]{1,0:T(8,128)(2,1)S(1)} %get-tuple-element.39), channel_id=1, source_target_pairs={{0,1},{1,2},{2,3},{3,4},{4,5},{5,6},{6,7},{7,8},{8,9},{9,10},{10,1... | collective-permute-start | bytes 884744 | tf_op jit(solution)/shard_map/ppermute | solution.py:639
  60.3 0.0 collective-permute-start.3
  60.3 0.0 copy-done.28
  60.3 0.0 copy-start.1
  60.3 2.8 %copy-done.1 = bf16[1024,3072]{1,0:T(8,128)(2,1)S(1)} copy-done((bf16[1024,3072]{1,0:T(8,128)(2,1)S(1)}, bf16[1024,3072]{1,0:T(8,128)(2,1)}, u32[]{:S(2)}) %copy-start.1) | copy-done | bytes 6291480
  63.1 1.8 %near_rows.1.kvr_hbm = bf16[192,2048]{1,0:T(8,128)(2,1)S(1)} custom-call(bf16[96,1024]{1,0:T(8,128)(2,1)S(1)} %collective-permute-done.north_ref, bf16[96,1024]{1,0:T(8,128)(2,1)S(1)} %collective-permute-done.1.south_ref, bf16[1024,3072]{1,0:T(8,128)(2,1)S(1)} %copy-done.1), custom_call_target="tpu_custom_call" | custom-call | flops 805306368 | bytes 7471104 | tf_op jit(solution)/shard_map/near_rows/pallas_call | solution.py:119
  64.9 2.2 %collective-permute-done.2.west_ref = bf16[144,1024]{1,0:T(8,128)(2,1)S(1)} collective-permute-done((bf16[144,1024]{1,0:T(8,128)(2,1)S(1)}, bf16[144,1024]{1,0:T(8,128)(2,1)S(1)}, u32[]{:S(2)}, u32[]{:S(2)}) %collective-permute-start.2) | collective-permute-done | bytes 294944 | tf_op jit(solution)/shard_map/ppermute | solution.py:639
  67.1 3.2 %collective-permute-done.3.east_ref = bf16[144,1024]{1,0:T(8,128)(2,1)S(1)} collective-permute-done((bf16[144,1024]{1,0:T(8,128)(2,1)S(1)}, bf16[144,1024]{1,0:T(8,128)(2,1)S(1)}, u32[]{:S(2)}, u32[]{:S(2)}) %collective-permute-start.3) | collective-permute-done | bytes 294944 | tf_op jit(solution)/shard_map/ppermute | solution.py:639
  70.4 0.0 copy-done.13
  70.4 0.0 slice-start.1
  70.4 22.5 %near.1 = (f32[192,1024]{1,0:T(8,128)S(1)}, bf16[192,2048]{1,0:T(8,128)(2,1)S(1)}, bf16[144,1024]{1,0:T(8,128)(2,1)S(1)}, bf16[144,1024]{1,0:T(8,128)(2,1)S(1)},...) custom-call(bf16[192,1024]{1,0:T(8,128)(2,1)S(1)} %get-tuple-element.37.q_ref, ...), custom_call_target="tpu_custom_call" | custom-call | flops 20000000000 | bytes 22351872 | tf_op jit(solution)/shard_map/near/pallas_call | solution.py:119
  92.9 0.1 collective-permute-start.4
  93.0 3.2 %collective-permute-start.5 = (bf16[144,1024]{1,0:T(8,128)(2,1)S(1)}, bf16[144,1024]{1,0:T(8,128)(2,1)S(1)}, u32[]{:S(2)}, u32[]{:S(2)}) collective-permute-start(bf16[144,1024]{1,0:T(8,128)(2,1)S(1)} %get-tuple-element.47), channel_id=1, source_target_pairs={{0,1},{1,2},{2,3},{3,4},{4,5},{5,6},{6,7},{7,8},{8,9},{9,10},{10,1... | collective-permute-start | bytes 884744 | tf_op jit(solution)/shard_map/ppermute | solution.py:639
  96.2 0.0 copy-start.4
  96.2 2.1 %rows_back.1.dn_ref = f32[192,1024]{1,0:T(8,128)S(1)} custom-call(bf16[192,2048]{1,0:T(8,128)(2,1)S(1)} %get-tuple-element.45.drows_ref, bf16[1024,3072]{1,0:T(8,128)(2,1)S(1)} %bitcast.7), custom_call_target="tpu_custom_call" | custom-call | flops 805306368 | bytes 7864320 | tf_op jit(solution)/shard_map/rows_back/pallas_call | solution.py:119
  98.3 2.3 %collective-permute-done.4.from_east_ref = bf16[144,1024]{1,0:T(8,128)(2,1)S(1)} collective-permute-done((bf16[144,1024]{1,0:T(8,128)(2,1)S(1)}, bf16[144,1024]{1,0:T(8,128)(2,1)S(1)}, u32[]{:S(2)}, u32[]{:S(2)}) %collective-permute-start.4) | collective-permute-done | bytes 294944 | tf_op jit(solution)/shard_map/ppermute | solution.py:639
  100.6 0.2 collective-permute-done.5.from_west_ref
  100.8 0.4 fold.1
  101.2 2.8 %collective-permute-start.6 = (bf16[96,1024]{1,0:T(8,128)(2,1)S(1)}, bf16[96,1024]{1,0:T(8,128)(2,1)S(1)}, u32[]{:S(2)}, u32[]{:S(2)}) collective-permute-start(bf16[96,1024]{1,0:T(8,128)(2,1)S(1)} %get-tuple-element.48._), channel_id=1, source_target_pairs={{0,16},{16,32},{32,48},{48,64},{64,80},{80,96},{96,112},{1,17},{17... | collective-permute-start | bytes 589832 | tf_op jit(solution)/shard_map/ppermute | solution.py:645
  104.0 1.5 collective-permute-start.7
  105.5 0.0 copy-done.4
  105.5 0.0 copy-start.25
  105.5 0.0 copy-start.7
  105.6 0.0 copy-start.8
  105.6 0.0 copy-start.19
  105.6 2.1 %encode.1._ = bf16[192,1024]{1,0:T(8,128)(2,1)} custom-call(f32[192,1024]{1,0:T(8,128)S(1)} %get-tuple-element.43.after_ref, bf16[192,2048]{1,0:T(8,128)(2,1)S(1)} %get-tuple-element.44.hid_ref, bf16[2048,1024]{1,0:T(8,128)(2,1)S(1)} %copy-done.4, bf16[96,1024]{1,0:T(8,128)(2,1)S(1)} %get-tuple-element.48._), custom_call_target="tpu_custom_call" | custom-call | flops 805306368 | bytes 6356992 | tf_op jit(solution)/shard_map/encode/pallas_call | solution.py:119
  107.7 0.0 copy-start.2
  107.7 0.0 copy-start.10
  107.7 0.0 copy-start.18
  107.7 2.9 %own_back.1.dn_ref = f32[192,1024]{1,0:T(8,128)S(1)} custom-call(bf16[192,3072]{1,0:T(8,128)(2,1)S(1)} %get-tuple-element.49.dqkv_ref, bf16[144,1024]{1,0:T(8,128)(2,1)S(1)} %collective-permute-done.4.from_east_ref, bf16[144,1024]{1,0:T(8,128)(2,1)S(1)} %collective-permute-done.5.from_west_ref, bf16[288,192]{1,0:T(8,128)(2,1)S(1)} %copy-done.25, ...), custom_call_target="tpu_custom_call" | custom-call | flops 1207959552 | bytes 9154560 | tf_op jit(solution)/shard_map/own_back/pallas_call | solution.py:119
  110.6 0.0 collective-permute-done.6.north_ref
  110.6 0.0 collective-permute-done.7.south_ref
  110.7 0.2 copy-done.6
  110.9 0.2 copy-done.12
  111.1 0.1 copy-done.18
  111.2 9.5 %cross_back.1 = (f32[192,1024]{1,0:T(8,128)}, bf16[128,4,1024]{2,1,0:T(4,128)(2,1)S(1)}, bf16[192,1024]{1,0:T(8,128)(2,1)}, bf16[192,2048]{1,0:T(8,128)(2,1)}) custom-call(f32[192,1024]{1,0:T(8,128)S(1)} %own_back.1.dn_ref, bf16[96,1024]{1,0:T(8,128)(2,1)S(1)} %collective-permute-done.6.north_ref, bf16[96,1024]{1,0:T(8,128)(2,1)S(1)} %collective-permute-done.7.south_ref, ...), custom_call_target="tpu_custom_call" | custom-call | flops 4294967296 | bytes 19673088 | tf_op jit(solution)/shard_map/cross_back/pallas_call | solution.py:119
  120.7 0.0 copy-start.11
  120.7 1.0 copy-done.11
  121.7 14.7 %all-to-all-start.1 = ((bf16[128,4,1024]{2,1,0:T(4,128)(2,1)}), bf16[128,4,1024]{2,1,0:T(4,128)(2,1)S(1)}, u32[]{:S(2)}, u32[]{:S(2)}) async-start(bf16[128,4,1024]{2,1,0:T(4,128)(2,1)} %copy-done.11), calls=%async_computation.1 | async-start | bytes 2097152 | tf_op jit(solution)/shard_map/all_to_all | solution.py:810
  136.4 0.0 copy-start.3
  136.4 2.2 %copy-done.3 = bf16[1024,2048]{1,0:T(8,128)(2,1)S(1)} copy-done((bf16[1024,2048]{1,0:T(8,128)(2,1)S(1)}, bf16[1024,2048]{1,0:T(8,128)(2,1)}, u32[]{:S(2)}) %copy-start.3) | copy-done | bytes 4194328
  138.6 1.1 copy-done.14
  139.7 1.1 copy-done.15
  140.8 1.0 copy-done.17
  141.8 3.7 %grid_back.1 = bf16[192,1024]{1,0:T(8,128)(2,1)} custom-call(bf16[192,1024]{1,0:T(8,128)(2,1)S(1)} %bitcast.10, f32[192,1024]{1,0:T(8,128)S(1)} %copy-done.14, f32[3,1024]{1,0:T(4,128)S(1)} %copy-done.23, bf16[192,1024]{1,0:T(8,128)(2,1)S(1)} %copy-done.17, bf16[192,2048]{1,0:T(8,128)(2,1)S(1)} %copy-done.15, bf16[1024,1024]{1,0:T(8,128)(2,1)S(1)} %copy-done.5, ...), custom_call_target="tpu_custom_call" | custom-call | flops 1207959552 | bytes 9056256 | tf_op jit(solution)/shard_map/grid_back/pallas_call | solution.py:119
  145.5 9.7 %all-to-all-done.1.ret_ref = bf16[128,4,1024]{2,1,0:T(4,128)(2,1)S(1)} async-done(((bf16[128,4,1024]{2,1,0:T(4,128)(2,1)}), bf16[128,4,1024]{2,1,0:T(4,128)(2,1)S(1)}, u32[]{:S(2)}, u32[]{:S(2)}) %all-to-all-start.1) | async-done | bytes 1048608 | tf_op jit(solution)/shard_map/all_to_all | solution.py:810
  155.3 0.9 copy-done.21
  156.2 1.3 gather.1
  (34 shorter events, 0.1 us)
Async XLA Ops:
  0.6 14.3 %copy-start.23 = (f32[3,1024]{1,0:T(4,128)S(1)}, f32[3,1024]{1,0:T(4,128)}, u32[]{:S(2)}) copy-start(f32[3,1024]{1,0:T(4,128)} %gain_ref.9) | copy-start | bytes 36868
  3.4 31.8 %all-to-all-start = ((bf16[128,4,1152]{2,1,0:T(4,128)(2,1)}), bf16[128,4,1152]{2,1,0:T(4,128)(2,1)S(1)}, u32[]{:S(2)}, u32[]{:S(2)}) async-start(bf16[128,4,1152]{2,1,0:T(4,128)(2,1)} %get-tuple-element.32), calls=%async_computation | async-start | bytes 2359296 | tf_op jit(solution)/shard_map/all_to_all | solution.py:711
  46.5 10.8 %collective-permute-start.1 = (bf16[96,1024]{1,0:T(8,128)(2,1)S(1)}, bf16[96,1024]{1,0:T(8,128)(2,1)S(1)}, u32[]{:S(2)}, u32[]{:S(2)}) collective-permute-start(bf16[96,1024]{1,0:T(8,128)(2,1)S(1)} %get-tuple-element.35.top_ref), channel_id=1, source_target_pairs={{16,0},{32,16},{48,32},{64,48},{80,64},{96,80},{112,96},{17,1},{33... | collective-permute-start | bytes 589832 | tf_op jit(solution)/shard_map/ppermute | solution.py:645
  47.8 9.5 %collective-permute-start = (bf16[96,1024]{1,0:T(8,128)(2,1)S(1)}, bf16[96,1024]{1,0:T(8,128)(2,1)S(1)}, u32[]{:S(2)}, u32[]{:S(2)}) collective-permute-start(bf16[96,1024]{1,0:T(8,128)(2,1)S(1)} %get-tuple-element.36.bottom_ref), channel_id=1, source_target_pairs={{0,16},{16,32},{32,48},{48,64},{64,80},{80,96},{96,112},{1,17},{17... | collective-permute-start | bytes 589832 | tf_op jit(solution)/shard_map/ppermute | solution.py:645
  51.8 2.8 %copy-start = (bf16[1024,3072]{1,0:T(8,128)(2,1)S(1)}, bf16[1024,3072]{1,0:T(8,128)(2,1)}, u32[]{:S(2)}) copy-start(bf16[1024,3072]{1,0:T(8,128)(2,1)} %w_hbm.7) | copy-start | bytes 18874372
  54.6 2.7 %copy-start.22 = (bf16[288,384]{1,0:T(8,128)(2,1)S(1)}, bf16[288,384]{1,0:T(8,128)(2,1)}, u32[]{:S(2)}) copy-start(bf16[288,384]{1,0:T(8,128)(2,1)} %constant.28.clone.sel_ref) | copy-start | bytes 663556
  54.6 5.7 %copy-start.28 = (s32[8,768]{1,0:T(8,128)S(1)}, s32[8,768]{1,0:T(8,128)}, u32[]{:S(2)}) copy-start(s32[8,768]{1,0:T(8,128)} %constant.27.clone) | copy-start | bytes 73732
  57.7 9.4 %collective-permute-start.2 = (bf16[144,1024]{1,0:T(8,128)(2,1)S(1)}, bf16[144,1024]{1,0:T(8,128)(2,1)S(1)}, u32[]{:S(2)}, u32[]{:S(2)}) collective-permute-start(bf16[144,1024]{1,0:T(8,128)(2,1)S(1)} %get-tuple-element.39), channel_id=1, source_target_pairs={{0,1},{1,2},{2,3},{3,4},{4,5},{5,6},{6,7},{7,8},{8,9},{9,10},{10,1... | collective-permute-start | bytes 884744 | tf_op jit(solution)/shard_map/ppermute | solution.py:639
  60.3 10.1 %collective-permute-start.3 = (bf16[144,1024]{1,0:T(8,128)(2,1)S(1)}, bf16[144,1024]{1,0:T(8,128)(2,1)S(1)}, u32[]{:S(2)}, u32[]{:S(2)}) collective-permute-start(bf16[144,1024]{1,0:T(8,128)(2,1)S(1)} %get-tuple-element.40), channel_id=1, source_target_pairs={{0,15},{1,0},{2,1},{3,2},{4,3},{5,4},{6,5},{7,6},{8,7},{9,8},{10,9... | collective-permute-start | bytes 884744 | tf_op jit(solution)/shard_map/ppermute | solution.py:639
  60.3 2.8 %copy-start.1 = (bf16[1024,3072]{1,0:T(8,128)(2,1)S(1)}, bf16[1024,3072]{1,0:T(8,128)(2,1)}, u32[]{:S(2)}) copy-start(bf16[1024,3072]{1,0:T(8,128)(2,1)} %w_hbm.7) | copy-start | bytes 18874372
  63.1 7.3 %copy-start.13 = (f32[192,1024]{1,0:T(8,128)S(1)}, f32[192,1024]{1,0:T(8,128)}, u32[]{:S(2)}) copy-start(f32[192,1024]{1,0:T(8,128)} %get-tuple-element.41.state_ref) | copy-start | bytes 2359300
  63.1 7.3 %copy-start.16 = (bf16[12,16,1024]{2,1,0:T(8,128)(2,1)S(1)}, bf16[12,16,1024]{2,1,0:T(8,128)(2,1)}, u32[]{:S(2)}) copy-start(bf16[12,16,1024]{2,1,0:T(8,128)(2,1)} %param.22) | copy-start | bytes 1179652
  63.1 7.3 %copy-start.26 = (bf16[192,2048]{1,0:T(8,128)(2,1)S(1)}, bf16[192,2048]{1,0:T(8,128)(2,1)}, u32[]{:S(2)}) copy-start(bf16[192,2048]{1,0:T(8,128)(2,1)} %get-tuple-element.42.dh_ref) | copy-start | bytes 2359300
  63.1 7.3 %copy-start.27 = (bf16[192,768]{1,0:T(8,128)(2,1)S(1)}, bf16[192,768]{1,0:T(8,128)(2,1)}, u32[]{:S(2)}) copy-start(bf16[192,768]{1,0:T(8,128)(2,1)} %constant.26.clone.base_ref) | copy-start | bytes 884740
  70.4 25.8 %slice-start = ((s8[6291456]{0:T(1024)(128)(4,1)}), s8[4194304]{0:T(1024)(128)(4,1)S(1)}, s32[]{:S(2)}) async-start(s8[6291456]{0:T(1024)(128)(4,1)} %bitcast.6), calls=%async_computation.2 | async-start | bytes 8388608
  70.4 25.8 %slice-start.1 = ((s8[6291456]{0:T(1024)(128)(4,1)}), s8[2097152]{0:T(1024)(128)(4,1)S(1)}, s32[]{:S(2)}) async-start(s8[6291456]{0:T(1024)(128)(4,1)} %bitcast.6), calls=%async_computation.3 | async-start | bytes 4194304
  92.9 7.7 %collective-permute-start.4 = (bf16[144,1024]{1,0:T(8,128)(2,1)S(1)}, bf16[144,1024]{1,0:T(8,128)(2,1)S(1)}, u32[]{:S(2)}, u32[]{:S(2)}) collective-permute-start(bf16[144,1024]{1,0:T(8,128)(2,1)S(1)} %get-tuple-element.46), channel_id=1, source_target_pairs={{0,15},{1,0},{2,1},{3,2},{4,3},{5,4},{6,5},{7,6},{8,7},{9,8},{10,9... | collective-permute-start | bytes 884744 | tf_op jit(solution)/shard_map/ppermute | solution.py:639
  93.0 7.8 %collective-permute-start.5 = (bf16[144,1024]{1,0:T(8,128)(2,1)S(1)}, bf16[144,1024]{1,0:T(8,128)(2,1)S(1)}, u32[]{:S(2)}, u32[]{:S(2)}) collective-permute-start(bf16[144,1024]{1,0:T(8,128)(2,1)S(1)} %get-tuple-element.47), channel_id=1, source_target_pairs={{0,1},{1,2},{2,3},{3,4},{4,5},{5,6},{6,7},{7,8},{8,9},{9,10},{10,1... | collective-permute-start | bytes 884744 | tf_op jit(solution)/shard_map/ppermute | solution.py:639
  96.2 4.6 %copy-start.24 = (bf16[288,192]{1,0:T(8,128)(2,1)S(1)}, bf16[288,192]{1,0:T(8,128)(2,1)}, u32[]{:S(2)}) copy-start(bf16[288,192]{1,0:T(8,128)(2,1)} %constant.29.clone.sel_ref) | copy-start | bytes 331780
  96.2 9.3 %copy-start.4 = (bf16[2048,1024]{1,0:T(8,128)(2,1)S(1)}, bf16[2048,1024]{1,0:T(8,128)(2,1)}, u32[]{:S(2)}) copy-start(bf16[2048,1024]{1,0:T(8,128)(2,1)} %wd_hbm.3) | copy-start | bytes 12582916
  101.2 9.4 %collective-permute-start.6 = (bf16[96,1024]{1,0:T(8,128)(2,1)S(1)}, bf16[96,1024]{1,0:T(8,128)(2,1)S(1)}, u32[]{:S(2)}, u32[]{:S(2)}) collective-permute-start(bf16[96,1024]{1,0:T(8,128)(2,1)S(1)} %get-tuple-element.48._), channel_id=1, source_target_pairs={{0,16},{16,32},{32,48},{48,64},{64,80},{80,96},{96,112},{1,17},{17... | collective-permute-start | bytes 589832 | tf_op jit(solution)/shard_map/ppermute | solution.py:645
  104.0 6.6 %collective-permute-start.7 = (bf16[96,1024]{1,0:T(8,128)(2,1)S(1)}, bf16[96,1024]{1,0:T(8,128)(2,1)S(1)}, u32[]{:S(2)}, u32[]{:S(2)}) collective-permute-start(bf16[96,1024]{1,0:T(8,128)(2,1)S(1)} %get-tuple-element.50._), channel_id=1, source_target_pairs={{16,0},{32,16},{48,32},{64,48},{80,64},{96,80},{112,96},{17,1},{33... | collective-permute-start | bytes 589832 | tf_op jit(solution)/shard_map/ppermute | solution.py:645
  105.5 2.1 %copy-start.25 = (bf16[288,192]{1,0:T(8,128)(2,1)S(1)}, bf16[288,192]{1,0:T(8,128)(2,1)}, u32[]{:S(2)}) copy-start(bf16[288,192]{1,0:T(8,128)(2,1)} %constant.30.clone.sel_ref) | copy-start | bytes 331780
  105.5 5.1 %copy-start.7 = (bf16[1024,1024]{1,0:T(8,128)(2,1)S(1)}, bf16[1024,1024]{1,0:T(8,128)(2,1)}, u32[]{:S(2)}) copy-start(bf16[1024,1024]{1,0:T(8,128)(2,1)} %wo_hbm.5) | copy-start | bytes 6291460
  105.6 5.1 %copy-start.8 = (bf16[512,2048]{1,0:T(8,128)(2,1)S(1)}, bf16[512,2048]{1,0:T(8,128)(2,1)}, u32[]{:S(2)}) copy-start(bf16[512,2048]{1,0:T(8,128)(2,1)} %get-tuple-element.52.pairs_ref) | copy-start | bytes 6291460
  105.6 5.1 %copy-start.19 = (bf16[192,1024]{1,0:T(8,128)(2,1)S(1)}, bf16[192,1024]{1,0:T(8,128)(2,1)}, u32[]{:S(2)}) copy-start(bf16[192,1024]{1,0:T(8,128)(2,1)} %get-tuple-element.54.mix_ref) | copy-start | bytes 1179652
  105.6 5.1 %copy-start.20 = (bf16[192,1024]{1,0:T(8,128)(2,1)S(1)}, bf16[192,1024]{1,0:T(8,128)(2,1)}, u32[]{:S(2)}) copy-start(bf16[192,1024]{1,0:T(8,128)(2,1)} %get-tuple-element.55.ow_ref) | copy-start | bytes 1179652
  107.7 3.0 %copy-start.2 = (bf16[1024,2048]{1,0:T(8,128)(2,1)S(1)}, bf16[1024,2048]{1,0:T(8,128)(2,1)}, u32[]{:S(2)}) copy-start(bf16[1024,2048]{1,0:T(8,128)(2,1)} %wp_hbm.7) | copy-start | bytes 12582916
  107.7 3.2 %copy-start.6 = (bf16[8,384,512]{2,1,0:T(8,128)(2,1)S(1)}, bf16[8,384,512]{2,1,0:T(8,128)(2,1)}, u32[]{:S(2)}) copy-start(bf16[8,384,512]{2,1,0:T(8,128)(2,1)} %get-tuple-element.53.wts_ref) | copy-start | bytes 9437188
  107.7 3.2 %copy-start.10 = (bf16[192,1024]{1,0:T(8,128)(2,1)S(1)}, bf16[192,1024]{1,0:T(8,128)(2,1)}, u32[]{:S(2)}) copy-start(bf16[192,1024]{1,0:T(8,128)(2,1)} %encode.1._) | copy-start | bytes 1179652
  107.7 3.4 %copy-start.12 = (bf16[192,2048]{1,0:T(8,128)(2,1)S(1)}, bf16[192,2048]{1,0:T(8,128)(2,1)}, u32[]{:S(2)}) copy-start(bf16[192,2048]{1,0:T(8,128)(2,1)} %get-tuple-element.34.own_hbm.own_ref) | copy-start | bytes 2359300
  107.7 3.5 %copy-start.18 = (bf16[192,1024]{1,0:T(8,128)(2,1)S(1)}, bf16[192,1024]{1,0:T(8,128)(2,1)}, u32[]{:S(2)}) copy-start(bf16[192,1024]{1,0:T(8,128)(2,1)} %get-tuple-element.33.q_hbm.q_ref) | copy-start | bytes 1179652
  111.2 25.2 %copy-start.9 = (bf16[12,16,1024]{2,1,0:T(8,128)(2,1)S(1)}, bf16[12,16,1024]{2,1,0:T(8,128)(2,1)}, u32[]{:S(2)}) copy-start(bf16[12,16,1024]{2,1,0:T(8,128)(2,1)} %param.18) | copy-start | bytes 1179652
  120.7 1.0 copy-start.11
  121.7 14.7 %copy-start.5 = (bf16[1024,1024]{1,0:T(8,128)(2,1)S(1)}, bf16[1024,1024]{1,0:T(8,128)(2,1)}, u32[]{:S(2)}) copy-start(bf16[1024,1024]{1,0:T(8,128)(2,1)} %wq_hbm.3) | copy-start | bytes 6291460
  121.7 33.6 %all-to-all-start.1 = ((bf16[128,4,1024]{2,1,0:T(4,128)(2,1)}), bf16[128,4,1024]{2,1,0:T(4,128)(2,1)S(1)}, u32[]{:S(2)}, u32[]{:S(2)}) async-start(bf16[128,4,1024]{2,1,0:T(4,128)(2,1)} %copy-done.11), calls=%async_computation.1 | async-start | bytes 2097152 | tf_op jit(solution)/shard_map/all_to_all | solution.py:810
  136.4 2.2 %copy-start.3 = (bf16[1024,2048]{1,0:T(8,128)(2,1)S(1)}, bf16[1024,2048]{1,0:T(8,128)(2,1)}, u32[]{:S(2)}) copy-start(bf16[1024,2048]{1,0:T(8,128)(2,1)} %wp_hbm.7) | copy-start | bytes 12582916
  138.6 1.1 copy-start.14
  139.7 1.1 copy-start.15
  140.8 1.0 copy-start.17
  155.3 1.0 copy-start.21

commit v4 on v3

--- a/solution.py
+++ b/solution.py
@@ -205,10 +205,10 @@
     arr, wp, wo, scores, bias, grid_ref, q_ref, own_ref, state_ref, pairs_ref, wts_ref,
     mix_ref, ow_ref, sems, out_sems, *, wide,
 ):
-    copies = fetch(
-        [wp_hbm, wo_hbm, q_hbm, own_hbm, grid_hbm], [wp, wo, q_ref, own_ref, grid_ref], sems
-    )
     cells, model = grid_ref.shape
+    parts = [pl.ds(j, TILE) for j in range(0, 2 * model, TILE)]
+    copies = fetch([wp_hbm.at[:, c] for c in parts], [wp.at[:, c] for c in parts], sems)
+    lates = out_sems.at[pl.ds(5, 4)]
     rim = top_ref.shape[0]
     slots = arr.shape[0]
     arr[...] = arr_ref[...].reshape(arr.shape)
@@ -220,17 +220,16 @@
     col_gap = (cell & (wide - 1)).astype(F32) - (codes[1:2] - 1.0)
     near = -(row_gap * row_gap + col_gap * col_gap) * (1.0 / SPREAD)
     bias[...] = jnp.where(codes[0:1] > 0.5, near, LOW_SCORE)
-    copies[0].wait()
-
-    def project(j):
-        pairs_ref[:, pl.ds(j, TILE)] = dot(
-            arr[:, :model], wp[:, pl.ds(j, TILE)]
-        ).astype(BF)
-
-    tiles_of(2 * model, project)
+    for i, cols in enumerate(parts):
+        copies[i].wait()
+        if i == 0:
+            late = fetch(
+                [q_hbm, own_hbm, wo_hbm, grid_hbm], [q_ref, own_ref, wo, grid_ref], lates
+            )
+        pairs_ref[:, cols] = dot(arr[:, :model], wp[:, cols]).astype(BF)
     leaving = fetch([pairs_ref], [pairs_hbm], out_sems.at[pl.ds(0, 1)])
-    copies[2].wait()
-    copies[3].wait()
+    late[0].wait()
+    late[1].wait()
 
     def soften(h, k, own_scores):
         own_weights = []
@@ -272,8 +271,8 @@
     leaving += fetch(
         [wts_ref, mix_ref, ow_ref], [wts_hbm, mix_hbm, ow_hbm], out_sems.at[pl.ds(1, 3)]
     )
-    copies[1].wait()
-    copies[4].wait()
+    late[2].wait()
+    late[3].wait()
 
     def project_out(j):
         state_ref[:, pl.ds(j, TILE)] = grid_ref[:, pl.ds(j, TILE)].astype(F32) + dot(
@@ -350,11 +349,39 @@
     tiles_of(2 * model, pairs)
 
 
+def near_back_loop(q_ref, kv, kv_rows, wts, cols, mix, dmix, dkv, scores, ds, put):
+    cells, model = q_ref.shape
+
+    @pl.loop(0, model // (PAIR * GROUP))
+    def _(g):
+        heads, deltas = [], []
+        for k in range(GROUP):
+            h = g * GROUP + k
+            keys = pl.ds(pl.multiple_of(h * PAIR, PAIR), PAIR)
+            vals = pl.ds(pl.multiple_of(model + h * PAIR, PAIR), PAIR)
+            heads.append((h, keys, vals))
+            grad = dmix[:, keys]
+            scores[k, :, pl.ds(0, cols.size)] = dot(stacked(grad), kv[kv_rows, vals], NT)
+            deltas.append(lane_sums(grad.astype(F32) * mix[:, keys].astype(F32)))
+        for k, (h, keys, vals) in enumerate(heads):
+            for s in range(2):
+                for i in range(0, cells, CHUNK):
+                    rows = pl.ds(s * cells + i, CHUNK)
+                    ds[k, rows, :] = (
+                        wts[h, rows, cols].astype(F32)
+                        * (scores[k, rows, pl.ds(0, cols.size)] - deltas[k][s][i : i + CHUNK])
+                    ).astype(BF)
+        for k, (h, keys, vals) in enumerate(heads):
+            put(keys, merged(dot(ds[k], kv[kv_rows, keys])))
+            dkv[:, keys] = dot(stacked(q_ref[:, keys]), ds[k], TN).T.astype(BF)
+            dkv[:, vals] = dot(stacked(dmix[:, keys]), wts[h, :, cols], TN).T.astype(BF)
+
+
 def near_kernel(
     q_ref, west_ref, east_ref, base_ref, inside_ref, state_ref, cot_ref, dh_ref, gain_ref,
     kvo_hbm, kvr_hbm, wn_hbm, wo_hbm, wu_hbm,
-    after_ref, hid_ref, dwest_ref, deast_ref, dqkv_ref, drows_ref, dafter_ref,
-    wkv, wo, wu, kv, dkv, x, wts, scores, ds, bias, mix, nrm, du, acc, dab, dmix, sems,
+    after_ref, hid_ref, dwest_ref, deast_ref, dq_ref, wts_hbm, mix, dmix, dafter_ref,
+    wkv, wo, wu, kv, dkv, x, wts, scores, ds, bias, nrm, du, acc, dab, sems, out_sems,
 ):
     cells, model = state_ref.shape
     keys_all = kv.shape[0]
@@ -400,6 +427,7 @@
         for k, (h, keys, vals) in enumerate(heads):
             mix[:, keys] = merged(dot(wts[h], kv[:, vals])).astype(BF)
 
+    leaving = fetch([wts.at[:, :, pl.ds(0, ext)]], [wts_hbm], out_sems)
     copies[3].wait()
 
     def project_out(j):
@@ -442,39 +470,52 @@
 
     tiles_of(model, mix_back)
 
-    @pl.loop(0, model // (PAIR * GROUP))
-    def _(g):
-        heads, deltas = [], []
-        for k in range(GROUP):
-            h = g * GROUP + k
-            keys = pl.ds(pl.multiple_of(h * PAIR, PAIR), PAIR)
-            vals = pl.ds(pl.multiple_of(model + h * PAIR, PAIR), PAIR)
-            heads.append((h, keys, vals))
-            grad = dmix[:, keys]
-            scores[k] = dot(stacked(grad), kv[:, vals], NT)
-            deltas.append(lane_sums(grad.astype(F32) * mix[:, keys].astype(F32)))
-        for k, (h, keys, vals) in enumerate(heads):
-            for s in range(2):
-                for i in range(0, cells, CHUNK):
-                    rows = pl.ds(s * cells + i, CHUNK)
-                    ds[k, rows, :] = (
-                        wts[h, rows, :].astype(F32)
-                        * (scores[k, rows, :] - deltas[k][s][i : i + CHUNK])
-                    ).astype(BF)
-        for k, (h, keys, vals) in enumerate(heads):
-            dq = merged(dot(ds[k], kv[:, keys])) * HALF ** (-0.5)
-            dqkv_ref[:, keys] = dq.astype(BF)
-            dkv[:, keys] = dot(stacked(q_ref[:, keys]), ds[k], TN).T.astype(BF)
-            dkv[:, vals] = dot(stacked(dmix[:, keys]), wts[h], TN).T.astype(BF)
+    outer = pl.ds(ext, keys_all - ext)
+
+    def put(keys, dq):
+        dq_ref[:, keys] = dq
+
+    near_back_loop(q_ref, kv, outer, wts, outer, mix, dmix, dkv, scores, ds, put)
 
     def rim_back(j):
-        both = dot(dkv[pl.ds(ext, 2 * side), :], wkv[pl.ds(j, TILE), :], NT).astype(BF)
+        both = dot(dkv[pl.ds(0, 2 * side), :], wkv[pl.ds(j, TILE), :], NT).astype(BF)
         dwest_ref[:, pl.ds(j, TILE)] = both[:side]
         deast_ref[:, pl.ds(j, TILE)] = both[side:]
 
     tiles_of(model, rim_back)
-    dqkv_ref[:, pl.ds(model, 2 * model)] = dkv[pl.ds(0, cells), :]
-    drows_ref[...] = dkv[pl.ds(cells, cells), :]
+    for copy in leaving:
+        copy.wait()
+
+
+def middle_back_kernel(
+    q_ref, kvo_ref, kvr_ref, mix, dmix, dq_in_ref, wts_hbm, wn_hbm,
+    dq_ref, down_ref, dn_ref, wkv, kv, dkv, wts, scores, ds, sems,
+):
+    cells, model = q_ref.shape
+    part = cells - PAIR
+    copies = fetch(
+        [wts_hbm.at[:, :, pl.ds(PAIR, kv.shape[0])], wn_hbm.at[:, pl.ds(model, 2 * model)]],
+        [wts, wkv],
+        sems,
+    )
+    kv[pl.ds(0, part), :] = kvo_ref[pl.ds(PAIR, part), :]
+    kv[pl.ds(part, cells), :] = kvr_ref[...]
+    copies[0].wait()
+
+    def put(keys, dq):
+        dq_ref[:, keys] = dq + dq_in_ref[:, keys]
+
+    whole = pl.ds(0, kv.shape[0])
+    near_back_loop(q_ref, kv, whole, wts, whole, mix, dmix, dkv, scores, ds, put)
+    down_ref[...] = dkv[pl.ds(0, part), :]
+    copies[1].wait()
+
+    def back(j):
+        dn_ref[:, pl.ds(j, TILE)] = dot(
+            dkv[pl.ds(part, cells), :], wkv[pl.ds(j, TILE), :], NT
+        )
+
+    tiles_of(model, back)
 
 
 def encode_kernel(after_ref, hid_ref, wd_hbm, _, enc_ref, wd, sems):
@@ -487,17 +528,6 @@
         ).astype(BF)
 
     tiles_of(after_ref.shape[1], down)
-
-
-def rows_back_kernel(drows_ref, w_hbm, dn_ref, w, sems):
-    model = dn_ref.shape[1]
-    copies = fetch([w_hbm.at[:, pl.ds(model, 2 * model)]], [w], sems)
-    copies[0].wait()
-
-    def back(j):
-        dn_ref[:, pl.ds(j, TILE)] = dot(drows_ref[...], w[pl.ds(j, TILE), :], NT)
-
-    tiles_of(model, back)
 
 
 def fold_kernel(dn_ref, from_east_ref, from_west_ref, sel_ref, north_ref, south_ref, x):
@@ -516,28 +546,39 @@
 
 
 def own_back_kernel(
-    dqkv_ref, from_east_ref, from_west_ref, sel_ref, w_hbm, _, dn_ref, x, w, sems
-):
-    copies = fetch([w_hbm], [w], sems)
+    q_ref, kvo_ref, mix, dmix, dq_in_ref, down_ref, from_east_ref, from_west_ref, sel_ref,
+    wts_hbm, w_hbm, _, dn_ref, dqkv, dkv, wts, scores, ds, x, w, sems,
+):
+    copies = fetch([wts_hbm.at[:, :, pl.ds(0, PAIR)], w_hbm], [wts, w], sems)
+    cells, model = q_ref.shape
     side = from_east_ref.shape[0]
     x[pl.ds(0, side), :] = from_west_ref[...]
     x[pl.ds(side, side), :] = from_east_ref[...]
     copies[0].wait()
 
+    def put(keys, dq):
+        dqkv[:, keys] = ((dq + dq_in_ref[:, keys]) * HALF ** (-0.5)).astype(BF)
+
+    whole = pl.ds(0, PAIR)
+    near_back_loop(q_ref, kvo_ref, whole, wts, whole, mix, dmix, dkv, scores, ds, put)
+    dqkv[pl.ds(0, PAIR), pl.ds(model, 2 * model)] = dkv[...]
+    dqkv[pl.ds(PAIR, cells - PAIR), pl.ds(model, 2 * model)] = down_ref[...]
+    copies[1].wait()
+
     def back(j):
         cols = pl.ds(j, TILE)
-        dn_ref[:, cols] = dot(dqkv_ref[...], w[cols, :], NT) + dot(
+        dn_ref[:, cols] = dot(dqkv[...], w[cols, :], NT) + dot(
             sel_ref[...], x[:, cols], TN
         )
 
-    tiles_of(dn_ref.shape[1], back)
+    tiles_of(model, back)
 
 
 def cross_back_kernel(
     dn_ref, north_ref, south_ref, state_ref, dafter_ref, gain_ref, q_ref, own_ref, pairs_ref,
-    wts_ref, mix_ref, ow_ref, wp_hbm, wo_hbm, _,
-    dstate_hbm, slot_ref, dq_hbm, down_hbm,
-    wp, wo, dsb, dmix, dpairs, scores, ds, dstate_ref, dq_ref, down_ref, sems, out_sems,
+    wts_ref, mix_ref, ow_ref, wp_hbm, wo_hbm,
+    dstate_hbm, slot_hbm, dq_hbm, down_hbm,
+    wp, wo, dsb, dmix, dpairs, scores, ds, dstate_ref, dq_ref, down_ref, slot_ref, sems, out_sems,
 ):
     copies = fetch([wo_hbm, wp_hbm], [wo, wp], sems)
     cells, model = state_ref.shape
@@ -594,21 +635,26 @@
             dpairs[:, vals] = dot(stacked(grad), wts_ref[h], TN).T.astype(BF)
 
     leaving = fetch(
-        [dstate_ref, dq_ref, down_ref], [dstate_hbm, dq_hbm, down_hbm], out_sems
+        [dstate_ref, dq_ref, down_ref], [dstate_hbm, dq_hbm, down_hbm],
+        out_sems.at[pl.ds(0, 3)],
     )
     copies[1].wait()
-
-    def slot_back(j):
-        grads = dot(dpairs[...], wp[pl.ds(j, TILE), :], NT).astype(BF)
-        slot_ref[:, :, pl.ds(j, TILE)] = grads.reshape(slot_ref.shape[:2] + (TILE,))
-
-    tiles_of(model, slot_back)
+    half = model // 2
+    for i in range(2):
+        cols = pl.ds(i * half, half)
+        grads = dot(dpairs[...], wp[cols, :], NT).astype(BF)
+        slot_ref[:, :, cols] = grads.reshape(slot_ref.shape[:2] + (half,))
+        leaving += fetch(
+            [slot_ref.at[:, :, cols]], [slot_hbm.at[:, :, cols]], out_sems.at[pl.ds(3 + i, 1)]
+        )
     for copy in leaving:
         copy.wait()
 
 
-def gather_kernel(place_ref, ret_ref, out_ref, ret):
+def gather_kernel(place_hbm, ret_ref, out_ref, place_ref, ret, sems):
+    copies = fetch([place_hbm], [place_ref], sems)
     ret[...] = ret_ref[...].reshape(ret.shape)
+    copies[0].wait()
     out_ref[...] = dot(place_ref[...], ret[...], TN).astype(BF)
 
 
@@ -729,7 +775,7 @@
          vm((GROUP, 2 * cells, slots), F32), vm((cells, slots), F32), vm((cells, model), BF),
          vm((cells, model), BF), vm((cells, 2 * model), BF), vm((cells, model), F32),
          vm((slots, 2 * model), BF), vm((pairs_n, 2 * cells, slots), BF), vm((cells, model), BF),
-         vm((cells, model), BF), dma((5,)), dma((5,))],
+         vm((cells, model), BF), dma((2 * model // TILE,)), dma((9,))],
         2 * slots * model * 2 * model * 2, "cross",
     )
     south = line(top, -1)
@@ -754,27 +800,34 @@
         [vm((2 * rim, model), BF), vm((model, 2 * model), BF), dma((1,))],
         2 * 2 * rim * model * 2 * model, "near_rows",
     )
-    after, hidden, dwest, deast, dqkv, drows, dafter = call(
+    after, hidden, dwest, deast, dq_rim, near_w, near_mix, dmix, dafter = call(
         near_kernel,
         (q_n, west, east, base, inside, state, cot, dhid, norm_gains, kv_own, kv_rows,
          w_near_proj, w_near_out, w_up), "vvvvvvvvvaaaaa",
         [((cells, model), F32), ((cells, ff), BF), ((side, model), BF), ((side, model), BF),
-         ((cells, 3 * model), BF), ((2 * rim, 2 * model), BF), ((cells, model), F32)],
+         ((cells, model), F32), ((pairs_n, 2 * cells, 2 * cells), BF, "h"), ((cells, model), BF),
+         ((cells, model), BF), ((cells, model), F32)],
         [vm((model, 2 * model), BF), vm((model, model), BF), vm((model, ff), BF),
-         vm((keys_all, 2 * model), BF), vm((keys_all, 2 * model), BF),
+         vm((keys_all, 2 * model), BF), vm((keys_all - 2 * cells, 2 * model), BF),
          vm((2 * side, model), BF), vm((pairs_n, 2 * cells, keys_all), BF),
-         vm((GROUP, 2 * cells, keys_all), F32), vm((GROUP, 2 * cells, keys_all), BF),
-         vm((cells, keys_all), F32), vm((cells, model), BF), vm((cells, model), BF),
+         vm((GROUP, 2 * cells, keys_all), F32),
+         vm((GROUP, 2 * cells, keys_all - 2 * cells), BF),
+         vm((cells, keys_all), F32), vm((cells, model), BF),
          vm((cells, ff), BF), vm((cells, model), F32), vm((cells, model), BF),
-         vm((cells, model), BF), dma((5,))],
+         dma((5,)), dma((1,))],
         2e10, "near",
     )
     from_east = ring(dwest, -1)
     from_west = ring(deast, 1)
-    dn_rows = call(
-        rows_back_kernel, (drows, w_near_proj), "va", [((2 * rim, model), F32)],
-        [vm((model, 2 * model), BF), dma((1,))],
-        2 * 2 * rim * model * 2 * model, "rows_back",
+    middle = 2 * cells - PAIR
+    dq_most, down_part, dn_rows = call(
+        middle_back_kernel,
+        (q_n, kv_own, kv_rows, near_mix, dmix, dq_rim, near_w, w_near_proj), "vvvvvvha",
+        [((cells, model), F32), ((cells - PAIR, 2 * model), BF), ((2 * rim, model), F32)],
+        [vm((model, 2 * model), BF), vm((middle, 2 * model), BF), vm((middle, 2 * model), BF),
+         vm((pairs_n, 2 * cells, middle), BF), vm((GROUP, 2 * cells, middle), F32),
+         vm((GROUP, 2 * cells, middle), BF), dma((2,))],
+        4 * cells * model * 2 * model, "middle_back",
     )
     dnorth, dsouth = call(
         fold_kernel, (dn_rows, from_east, from_west, jnp.asarray(select[:, cells:])), "vvvv",
@@ -786,28 +839,32 @@
     from_north = line(dsouth, 1)
     dn_own = call(
         own_back_kernel,
-        (dqkv, from_east, from_west, jnp.asarray(select[:, :cells]), w_near_proj, dnorth), "vvvvaa",
+        (q_n, kv_own, near_mix, dmix, dq_most, down_part, from_east, from_west,
+         jnp.asarray(select[:, :cells]), near_w, w_near_proj, dnorth), "vvvvvvvvvhaa",
         [((cells, model), F32)],
-        [vm((2 * side, model), BF), vm((model, 3 * model), BF), dma((1,))],
-        2 * cells * model * 3 * model, "own_back",
-    )
-    encoded = call(
-        encode_kernel, (after, hidden, w_down, dsouth), "vvaa", [((cells, model), BF)],
-        [vm((ff, model), BF), dma((1,))], 2 * cells * model * ff, "encode",
+        [vm((cells, 3 * model), BF), vm((PAIR, 2 * model), BF),
+         vm((pairs_n, 2 * cells, PAIR), BF), vm((GROUP, 2 * cells, PAIR), F32),
+         vm((GROUP, 2 * cells, PAIR), BF), vm((2 * side, model), BF),
+         vm((model, 3 * model), BF), dma((2,))],
+        2 * cells * model * 4 * model, "own_back",
     )
     dstate, slot_grads, dq, down = call(
         cross_back_kernel,
         (dn_own, from_north, from_south, state, dafter, norm_gains, q_c, own_pairs, slot_pairs,
-         cross_w, cross_mix, own_w, w_cross_pairs, w_cross_out, encoded), "vvvvvvvvvvvvaaa",
-        [((cells, model), F32, "h"), ((devices, cap, model), BF), ((cells, model), BF, "h"),
-         ((cells, 2 * model), BF, "h")],
+         cross_w, cross_mix, own_w, w_cross_pairs, w_cross_out), "vvvvvvvvvvvvaa",
+        [((cells, model), F32, "h"), ((devices, cap, model), BF, "h"),
+         ((cells, model), BF, "h"), ((cells, 2 * model), BF, "h")],
         [vm((model, 2 * model), BF), vm((model, model), BF), vm((cells, model), BF),
          vm((cells, model), BF), vm((slots, 2 * model), BF), vm((GROUP, 2 * cells, slots), F32),
          vm((GROUP, 2 * cells, slots), BF), vm((cells, model), F32), vm((cells, model), BF),
-         vm((cells, 2 * model), BF), dma((2,)), dma((3,))],
+         vm((cells, 2 * model), BF), vm((devices, cap, model), BF), dma((2,)), dma((5,))],
         2 * slots * model * 2 * model * 2, "cross_back",
     )
     returned = lax.all_to_all(slot_grads, ("lat", "lon"), 0, 0, tiled=True)
+    encoded = call(
+        encode_kernel, (after, hidden, w_down, dq), "vvaa", [((cells, model), BF)],
+        [vm((ff, model), BF), dma((1,))], 2 * cells * model * ff, "encode",
+    )
     grid_grad = call(
         grid_back_kernel,
         (flat, dstate, norm_gains, dq, down, w_cross_query, w_cross_pairs), "vvvvvaa",
@@ -816,8 +873,8 @@
         2 * cells * model * 3 * model, "grid_back",
     )
     obs_grad = call(
-        gather_kernel, (placing, returned), "vv", [((rows_obs, model), BF)],
-        [vm((slots, model), BF)], 2 * rows_obs * slots * model, "gather",
+        gather_kernel, (placing, returned), "hv", [((rows_obs, model), BF)],
+        [vm((slots, rows_obs), BF), vm((slots, model), BF), dma((1,))], 2 * rows_obs * slots * model, "gather",
     )
     shape = (rows_lat, rows_lon, model)
     return encoded.reshape(shape), grid_grad.reshape(shape), obs_grad

time: 158 us -> 155 us (0.981)
  Pallas kernels: 70.1 us -> 75.9 us
  waiting for transfers between devices: 31.2 us -> 26.7 us
  local copies, waits for them, and re-layouts: 13.6 us -> 11.1 us
  starting transfers between devices: 41.7 us -> 39.8 us
    pallas_call x14, Pallas kernels: 70.1 us -> 75.9 us  [call(): pl.pallas_call(body, name=name, out_shape=shapes[0] if single else shapes...]
    unnamed x62 -> x58, local copies, waits for them, and re-layouts: 13.6 us -> 11.1 us
    ppermute x4, waiting for transfers between devices: 7.92 us -> 5.44 us  [ring(): lax.ppermute(value, 'lon', [(i, (i + by) % size) for i in range(size)])]
    all_to_all x1, waiting for transfers between devices: 9.74 us -> 7.74 us  [per_device(): returned = lax.all_to_all(slot_grads, ('lat', 'lon'), 0, 0, tiled=True)]
    all_to_all x1, starting transfers between devices: 14.7 us -> 12.8 us  [per_device(): returned = lax.all_to_all(slot_grads, ('lat', 'lon'), 0, 0, tiled=True)]
  transfers between devices with their start and end apart: 10 -> 10, of which waited for: 6 -> 4; matrix products, arithmetic and copies ran while one was open for 0% -> 0% of each run, Pallas kernels for 14% -> 19%
where the time goes in v4:
time: 155 us
  Pallas kernels  75.9 us (49%)
  starting transfers between devices  39.8 us (26%)
  waiting for transfers between devices  26.7 us (17%)
  local copies, waits for them, and re-layouts  11.1 us (7%)
    pallas_call x14, Pallas kernels, call(): pl.pallas_call(body, name=name, out_shape=shapes[0] if single else shapes...  75.9 us
    all_to_all x1, waiting for transfers between devices, per_device(): arrived = lax.all_to_all(payload, ('lat', 'lon'), 0, 0, tiled=True)  13.5 us
    all_to_all x1, starting transfers between devices, per_device(): returned = lax.all_to_all(slot_grads, ('lat', 'lon'), 0, 0, tiled=True)  12.8 us
    all_to_all x1, starting transfers between devices, per_device(): arrived = lax.all_to_all(payload, ('lat', 'lon'), 0, 0, tiled=True)  11.5 us
    unnamed x58, local copies, waits for them, and re-layouts  11.1 us
    ppermute x4, starting transfers between devices, line(): return lax.ppermute(value, 'lat', pairs)  9.57 us
    all_to_all x1, waiting for transfers between devices, per_device(): returned = lax.all_to_all(slot_grads, ('lat', 'lon'), 0, 0, tiled=True)  7.74 us
    ppermute x4, starting transfers between devices, ring(): lax.ppermute(value, 'lon', [(i, (i + by) % size) for i in range(size)])  5.92 us
  transfers between devices with their start and end apart: 10, of which 4 were waited for; matrix products, arithmetic and copies ran while one was open for 0% of the time, Pallas kernels for 19%

profile of v4, /device:TPU:1, one launch (start us, length us, event | category | flops | bytes accessed | tf_op | source)
XLA Modules:
  0.0 154.8 jit_solution(4870628251248641018)
XLA Ops:
  0.6 0.0 copy-start.20
  0.6 2.8 %place.1 = (bf16[128,4,1152]{2,1,0:T(4,128)(2,1)}, bf16[512,256]{1,0:T(8,128)(2,1)}) custom-call(s32[1,256]{1,0:T(1,128)} %bitcast.15, s32[1,256]{1,0:T(1,128)} %bitcast.16, bf16[256,1024]{1,0:T(8,128)(2,1)} %obs_hbm.1), custom_call_target="tpu_custom_call" | custom-call | flops 268435456 | bytes 1968128 | tf_op jit(solution)/shard_map/place/pallas_call | solution.py:119
  3.5 11.5 %all-to-all-start = ((bf16[128,4,1152]{2,1,0:T(4,128)(2,1)}), bf16[128,4,1152]{2,1,0:T(4,128)(2,1)S(1)}, u32[]{:S(2)}, u32[]{:S(2)}) async-start(bf16[128,4,1152]{2,1,0:T(4,128)(2,1)} %get-tuple-element.37), calls=%async_computation | async-start | bytes 2359296 | tf_op jit(solution)/shard_map/all_to_all | solution.py:757
  15.0 0.0 copy-done.20
  15.0 6.8 %grid_proj.1 = (bf16[192,1024]{1,0:T(8,128)(2,1)}, bf16[192,2048]{1,0:T(8,128)(2,1)}, bf16[192,2048]{1,0:T(8,128)(2,1)}) custom-call(bf16[192,1024]{1,0:T(8,128)(2,1)} %bitcast.8, bf16[192,1024]{1,0:T(8,128)(2,1)} %bitcast.11, f32[3,1024]{1,0:T(4,128)S(1)} %copy-done.20, bf16[1024,1024]{1,0:T(8,128)(2,1)} %wq_hbm.3, bf16[1024,2048]{1,0:T(8,128)(2,1)} %wp_hbm.7, ...), custom_call_target="tpu_custom_call" | custom-call | flops 2013265920 | bytes 13250560 | tf_op jit(solution)/shard_map/grid_proj/pallas_call | solution.py:119
  21.8 13.5 %all-to-all-done.arr_ref = bf16[128,4,1152]{2,1,0:T(4,128)(2,1)S(1)} async-done(((bf16[128,4,1152]{2,1,0:T(4,128)(2,1)}), bf16[128,4,1152]{2,1,0:T(4,128)(2,1)S(1)}, u32[]{:S(2)}, u32[]{:S(2)}) %all-to-all-start) | async-done | bytes 1179680 | tf_op jit(solution)/shard_map/all_to_all | solution.py:757
  35.3 10.6 %cross.1 = (f32[192,1024]{1,0:T(8,128)}, bf16[96,1024]{1,0:T(8,128)(2,1)S(1)}, bf16[96,1024]{1,0:T(8,128)(2,1)S(1)}, bf16[512,2048]{1,0:T(8,128)(2,1)}, bf16[8,3...) custom-call(bf16[128,4,1152]{2,1,0:T(4,128)(2,1)S(1)} %all-to-all-done.arr_ref, ...), custom_call_target="tpu_custom_call" | custom-call | flops 4294967296 | bytes 16265216 | tf_op jit(solution)/shard_map/cross/pallas_call | solution.py:119
  45.9 1.3 collective-permute-start.1
  47.2 4.0 %collective-permute-start = (bf16[96,1024]{1,0:T(8,128)(2,1)S(1)}, bf16[96,1024]{1,0:T(8,128)(2,1)S(1)}, u32[]{:S(2)}, u32[]{:S(2)}) collective-permute-start(bf16[96,1024]{1,0:T(8,128)(2,1)S(1)} %get-tuple-element.41.bottom_ref), channel_id=1, source_target_pairs={{0,16},{16,32},{32,48},{48,64},{64,80},{80,96},{96,112},{1,17},{17... | collective-permute-start | bytes 589832 | tf_op jit(solution)/shard_map/ppermute | solution.py:691
  51.2 0.0 copy-start
  51.2 2.8 %copy-done = bf16[1024,3072]{1,0:T(8,128)(2,1)S(1)} copy-done((bf16[1024,3072]{1,0:T(8,128)(2,1)S(1)}, bf16[1024,3072]{1,0:T(8,128)(2,1)}, u32[]{:S(2)}) %copy-start) | copy-done | bytes 6291480
  54.0 2.6 %near_own.1 = (bf16[192,1024]{1,0:T(8,128)(2,1)S(1)}, bf16[192,2048]{1,0:T(8,128)(2,1)S(1)}) custom-call(bf16[96,1024]{1,0:T(8,128)(2,1)S(1)} %get-tuple-element.40.top_ref, bf16[96,1024]{1,0:T(8,128)(2,1)S(1)} %get-tuple-element.41.bottom_ref, bf16[1024,3072]{1,0:T(8,128)(2,1)S(1)} %copy-done), custom_call_target="tpu_custom_call" | custom-call | flops 1207959552 | bytes 7864320 | tf_op jit(solution)/shard_map/near_own/pallas_call | solution.py:119
  56.6 0.0 collective-permute-done.1.south_ref
  56.6 0.0 collective-permute-done.north_ref
  56.6 0.0 copy-done.19
  56.7 0.5 rim.1
  57.1 2.6 %collective-permute-start.2 = (bf16[144,1024]{1,0:T(8,128)(2,1)S(1)}, bf16[144,1024]{1,0:T(8,128)(2,1)S(1)}, u32[]{:S(2)}, u32[]{:S(2)}) collective-permute-start(bf16[144,1024]{1,0:T(8,128)(2,1)S(1)} %get-tuple-element.44), channel_id=1, source_target_pairs={{0,1},{1,2},{2,3},{3,4},{4,5},{5,6},{6,7},{7,8},{8,9},{9,10},{10,1... | collective-permute-start | bytes 884744 | tf_op jit(solution)/shard_map/ppermute | solution.py:685
  59.7 0.0 collective-permute-start.3
  59.7 0.0 copy-done.26
  59.8 0.0 copy-start.1
  59.8 2.8 %copy-done.1 = bf16[1024,3072]{1,0:T(8,128)(2,1)S(1)} copy-done((bf16[1024,3072]{1,0:T(8,128)(2,1)S(1)}, bf16[1024,3072]{1,0:T(8,128)(2,1)}, u32[]{:S(2)}) %copy-start.1) | copy-done | bytes 6291480
  62.6 0.0 copy-start.25
  62.6 1.8 %near_rows.1.kvr_hbm.kvr_ref = bf16[192,2048]{1,0:T(8,128)(2,1)S(1)} custom-call(bf16[96,1024]{1,0:T(8,128)(2,1)S(1)} %collective-permute-done.north_ref, bf16[96,1024]{1,0:T(8,128)(2,1)S(1)} %collective-permute-done.1.south_ref, bf16[1024,3072]{1,0:T(8,128)(2,1)S(1)} %copy-done.1), custom_call_target="tpu_custom_call" | custom-call | flops 805306368 | bytes 7471104 | tf_op jit(solution)/shard_map/near_rows/pallas_call | solution.py:119
  64.4 2.2 %collective-permute-done.2.west_ref = bf16[144,1024]{1,0:T(8,128)(2,1)S(1)} collective-permute-done((bf16[144,1024]{1,0:T(8,128)(2,1)S(1)}, bf16[144,1024]{1,0:T(8,128)(2,1)S(1)}, u32[]{:S(2)}, u32[]{:S(2)}) %collective-permute-start.2) | collective-permute-done | bytes 294944 | tf_op jit(solution)/shard_map/ppermute | solution.py:685
  66.6 3.2 %collective-permute-done.3.east_ref = bf16[144,1024]{1,0:T(8,128)(2,1)S(1)} collective-permute-done((bf16[144,1024]{1,0:T(8,128)(2,1)S(1)}, bf16[144,1024]{1,0:T(8,128)(2,1)S(1)}, u32[]{:S(2)}, u32[]{:S(2)}) %collective-permute-start.3) | collective-permute-done | bytes 294944 | tf_op jit(solution)/shard_map/ppermute | solution.py:685
  69.8 0.0 copy-done.12
  69.8 0.0 copy-done.15
  69.8 0.0 copy-done.23
  69.8 0.0 copy-done.24
  69.8 0.0 copy-done.25
  69.8 0.0 slice-start.1
  69.8 20.2 %near.1 = (f32[192,1024]{1,0:T(8,128)S(1)}, bf16[192,2048]{1,0:T(8,128)(2,1)S(1)}, bf16[144,1024]{1,0:T(8,128)(2,1)S(1)}, bf16[144,1024]{1,0:T(8,128)(2,1)S(1)},...) custom-call(bf16[192,1024]{1,0:T(8,128)(2,1)S(1)} %get-tuple-element, ...), custom_call_target="tpu_custom_call" | custom-call | flops 20000000000 | bytes 24317952 | tf_op jit(solution)/shard_map/near/pallas_call | solution.py:119
  90.1 0.1 collective-permute-start.4
  90.2 3.2 %collective-permute-start.5 = (bf16[144,1024]{1,0:T(8,128)(2,1)S(1)}, bf16[144,1024]{1,0:T(8,128)(2,1)S(1)}, u32[]{:S(2)}, u32[]{:S(2)}) collective-permute-start(bf16[144,1024]{1,0:T(8,128)(2,1)S(1)} %get-tuple-element.57), channel_id=1, source_target_pairs={{0,1},{1,2},{2,3},{3,4},{4,5},{5,6},{6,7},{7,8},{8,9},{9,10},{10,1... | collective-permute-start | bytes 884744 | tf_op jit(solution)/shard_map/ppermute | solution.py:685
  93.4 0.0 copy-start.22
  93.4 5.7 %middle_back.1 = (f32[192,1024]{1,0:T(8,128)S(1)}, bf16[64,2048]{1,0:T(8,128)(2,1)S(1)}, f32[192,1024]{1,0:T(8,128)S(1)}) custom-call(bf16[192,1024]{1,0:T(8,128)(2,1)S(1)} %get-tuple-element.42.q_ref, bf16[192,2048]{1,0:T(8,128)(2,1)S(1)} %get-tuple-element.43._.kvo_hbm.kvo_ref, bf16[192,2048]{1,0:T(8,128)(2,1)S(1)} %near_rows.1.kvr_hbm.kvr_ref, ...), custom_call_target="tpu_custom_call" | custom-call | flops 1610612736 | bytes 14024704 | tf_op jit(solution)/shard_map/middle_back/pallas_call | solution.py:119
  99.2 0.0 collective-permute-done.4.from_east_ref
  99.2 0.0 collective-permute-done.5.from_west_ref
  99.2 0.0 copy-start.18
  99.2 0.4 fold.1
  99.6 2.8 %collective-permute-start.6 = (bf16[96,1024]{1,0:T(8,128)(2,1)S(1)}, bf16[96,1024]{1,0:T(8,128)(2,1)S(1)}, u32[]{:S(2)}, u32[]{:S(2)}) collective-permute-start(bf16[96,1024]{1,0:T(8,128)(2,1)S(1)} %get-tuple-element.60), channel_id=1, source_target_pairs={{0,16},{16,32},{32,48},{48,64},{64,80},{80,96},{96,112},{1,17},{17... | collective-permute-start | bytes 589832 | tf_op jit(solution)/shard_map/ppermute | solution.py:691
  102.4 1.5 collective-permute-start.7
  103.9 0.0 copy-done.22
  103.9 0.0 copy-start.2
  103.9 0.0 copy-start.7
  103.9 0.0 copy-start.16
  104.0 0.0 copy-start.17
  104.0 6.3 %own_back.1.dn_ref = f32[192,1024]{1,0:T(8,128)S(1)} custom-call(bf16[192,1024]{1,0:T(8,128)(2,1)S(1)} %get-tuple-element.42.q_ref, bf16[192,2048]{1,0:T(8,128)(2,1)S(1)} %get-tuple-element.43._.kvo_hbm.kvo_ref, bf16[192,1024]{1,0:T(8,128)(2,1)S(1)} %get-tuple-element.50.mix, bf16[192,1024]{1,0:T(8,128)(2,1)S(1)} %get-tuple-element.51.dmix, ...), custom_call_target="tpu_custom_call" | custom-call | flops 1610612736 | bytes 13348864 | tf_op jit(solution)/shard_map/own_back/pallas_call | solution.py:119
  110.3 0.0 collective-permute-done.6.north_ref
  110.3 0.0 collective-permute-done.7.south_ref
  110.4 10.3 %cross_back.1 = (f32[192,1024]{1,0:T(8,128)}, bf16[128,4,1024]{2,1,0:T(4,128)(2,1)}, bf16[192,1024]{1,0:T(8,128)(2,1)}, bf16[192,2048]{1,0:T(8,128)(2,1)}) custom-call(f32[192,1024]{1,0:T(8,128)S(1)} %own_back.1.dn_ref, bf16[96,1024]{1,0:T(8,128)(2,1)S(1)} %collective-permute-done.6.north_ref, bf16[96,1024]{1,0:T(8,128)(2,1)S(1)} %collective-permute-done.7.south_ref, ...), custom_call_target="tpu_custom_call" | custom-call | flops 4294967296 | bytes 19279872 | tf_op jit(solution)/shard_map/cross_back/pallas_call | solution.py:119
  120.7 0.0 copy-start.10
  120.7 0.0 copy-start.9
  120.7 12.8 %all-to-all-start.1 = ((bf16[128,4,1024]{2,1,0:T(4,128)(2,1)}), bf16[128,4,1024]{2,1,0:T(4,128)(2,1)S(1)}, u32[]{:S(2)}, u32[]{:S(2)}) async-start(bf16[128,4,1024]{2,1,0:T(4,128)(2,1)} %get-tuple-element.70), calls=%async_computation.1 | async-start | bytes 2097152 | tf_op jit(solution)/shard_map/all_to_all | solution.py:863
  133.5 0.0 copy-start.4
  133.5 2.2 %copy-done.4 = bf16[2048,1024]{1,0:T(8,128)(2,1)S(1)} copy-done((bf16[2048,1024]{1,0:T(8,128)(2,1)S(1)}, bf16[2048,1024]{1,0:T(8,128)(2,1)}, u32[]{:S(2)}) %copy-start.4) | copy-done | bytes 4194328
  135.7 2.0 %encode.1 = bf16[192,1024]{1,0:T(8,128)(2,1)} custom-call(f32[192,1024]{1,0:T(8,128)S(1)} %get-tuple-element.48.after_ref, bf16[192,2048]{1,0:T(8,128)(2,1)S(1)} %get-tuple-element.49.hid_ref, bf16[2048,1024]{1,0:T(8,128)(2,1)S(1)} %copy-done.4, bf16[192,1024]{1,0:T(8,128)(2,1)S(1)} %copy-done.10), custom_call_target="tpu_custom_call" | custom-call | flops 805306368 | bytes 6553600 | tf_op jit(solution)/shard_map/encode/pallas_call | solution.py:119
  137.8 0.1 copy-done.3
  137.9 0.8 copy-done.5
  138.7 1.1 copy-done.13
  139.8 1.1 copy-done.14
  141.0 3.7 %grid_back.1 = bf16[192,1024]{1,0:T(8,128)(2,1)} custom-call(bf16[192,1024]{1,0:T(8,128)(2,1)S(1)} %bitcast.10, f32[192,1024]{1,0:T(8,128)S(1)} %copy-done.13, f32[3,1024]{1,0:T(4,128)S(1)} %copy-done.20, bf16[192,1024]{1,0:T(8,128)(2,1)S(1)} %copy-done.10, bf16[192,2048]{1,0:T(8,128)(2,1)S(1)} %copy-done.14, bf16[1024,1024]{1,0:T(8,128)(2,1)S(1)} %copy-done.5, ...), custom_call_target="tpu_custom_call" | custom-call | flops 1207959552 | bytes 9056256 | tf_op jit(solution)/shard_map/grid_back/pallas_call | solution.py:119
  144.7 7.7 %all-to-all-done.1.ret_ref = bf16[128,4,1024]{2,1,0:T(4,128)(2,1)S(1)} async-done(((bf16[128,4,1024]{2,1,0:T(4,128)(2,1)}), bf16[128,4,1024]{2,1,0:T(4,128)(2,1)S(1)}, u32[]{:S(2)}, u32[]{:S(2)}) %all-to-all-start.1) | async-done | bytes 1048608 | tf_op jit(solution)/shard_map/all_to_all | solution.py:863
  152.4 2.2 %gather.1 = bf16[256,1024]{1,0:T(8,128)(2,1)} custom-call(bf16[512,256]{1,0:T(8,128)(2,1)} %get-tuple-element.69.place_hbm, bf16[128,4,1024]{2,1,0:T(4,128)(2,1)S(1)} %all-to-all-done.1.ret_ref), custom_call_target="tpu_custom_call" | custom-call | flops 268435456 | bytes 1835008 | tf_op jit(solution)/shard_map/gather/pallas_call | solution.py:119
  (30 shorter events, 0.1 us)
Async XLA Ops:
  0.6 14.3 %copy-start.20 = (f32[3,1024]{1,0:T(4,128)S(1)}, f32[3,1024]{1,0:T(4,128)}, u32[]{:S(2)}) copy-start(f32[3,1024]{1,0:T(4,128)} %gain_ref.9) | copy-start | bytes 36868
  3.5 31.8 %all-to-all-start = ((bf16[128,4,1152]{2,1,0:T(4,128)(2,1)}), bf16[128,4,1152]{2,1,0:T(4,128)(2,1)S(1)}, u32[]{:S(2)}, u32[]{:S(2)}) async-start(bf16[128,4,1152]{2,1,0:T(4,128)(2,1)} %get-tuple-element.37), calls=%async_computation | async-start | bytes 2359296 | tf_op jit(solution)/shard_map/all_to_all | solution.py:757
  45.9 10.8 %collective-permute-start.1 = (bf16[96,1024]{1,0:T(8,128)(2,1)S(1)}, bf16[96,1024]{1,0:T(8,128)(2,1)S(1)}, u32[]{:S(2)}, u32[]{:S(2)}) collective-permute-start(bf16[96,1024]{1,0:T(8,128)(2,1)S(1)} %get-tuple-element.40.top_ref), channel_id=1, source_target_pairs={{16,0},{32,16},{48,32},{64,48},{80,64},{96,80},{112,96},{17,1},{33... | collective-permute-start | bytes 589832 | tf_op jit(solution)/shard_map/ppermute | solution.py:691
  47.2 9.5 %collective-permute-start = (bf16[96,1024]{1,0:T(8,128)(2,1)S(1)}, bf16[96,1024]{1,0:T(8,128)(2,1)S(1)}, u32[]{:S(2)}, u32[]{:S(2)}) collective-permute-start(bf16[96,1024]{1,0:T(8,128)(2,1)S(1)} %get-tuple-element.41.bottom_ref), channel_id=1, source_target_pairs={{0,16},{16,32},{32,48},{48,64},{64,80},{80,96},{96,112},{1,17},{17... | collective-permute-start | bytes 589832 | tf_op jit(solution)/shard_map/ppermute | solution.py:691
  51.2 2.8 %copy-start = (bf16[1024,3072]{1,0:T(8,128)(2,1)S(1)}, bf16[1024,3072]{1,0:T(8,128)(2,1)}, u32[]{:S(2)}) copy-start(bf16[1024,3072]{1,0:T(8,128)(2,1)} %w_hbm.5) | copy-start | bytes 18874372
  54.0 2.7 %copy-start.19 = (bf16[288,384]{1,0:T(8,128)(2,1)S(1)}, bf16[288,384]{1,0:T(8,128)(2,1)}, u32[]{:S(2)}) copy-start(bf16[288,384]{1,0:T(8,128)(2,1)} %constant.28.clone.sel_ref) | copy-start | bytes 663556
  54.0 5.8 %copy-start.26 = (s32[8,768]{1,0:T(8,128)S(1)}, s32[8,768]{1,0:T(8,128)}, u32[]{:S(2)}) copy-start(s32[8,768]{1,0:T(8,128)} %constant.27.clone) | copy-start | bytes 73732
  57.1 9.4 %collective-permute-start.2 = (bf16[144,1024]{1,0:T(8,128)(2,1)S(1)}, bf16[144,1024]{1,0:T(8,128)(2,1)S(1)}, u32[]{:S(2)}, u32[]{:S(2)}) collective-permute-start(bf16[144,1024]{1,0:T(8,128)(2,1)S(1)} %get-tuple-element.44), channel_id=1, source_target_pairs={{0,1},{1,2},{2,3},{3,4},{4,5},{5,6},{6,7},{7,8},{8,9},{9,10},{10,1... | collective-permute-start | bytes 884744 | tf_op jit(solution)/shard_map/ppermute | solution.py:685
  59.7 10.1 %collective-permute-start.3 = (bf16[144,1024]{1,0:T(8,128)(2,1)S(1)}, bf16[144,1024]{1,0:T(8,128)(2,1)S(1)}, u32[]{:S(2)}, u32[]{:S(2)}) collective-permute-start(bf16[144,1024]{1,0:T(8,128)(2,1)S(1)} %get-tuple-element.45), channel_id=1, source_target_pairs={{0,15},{1,0},{2,1},{3,2},{4,3},{5,4},{6,5},{7,6},{8,7},{9,8},{10,9... | collective-permute-start | bytes 884744 | tf_op jit(solution)/shard_map/ppermute | solution.py:685
  59.8 2.8 %copy-start.1 = (bf16[1024,3072]{1,0:T(8,128)(2,1)S(1)}, bf16[1024,3072]{1,0:T(8,128)(2,1)}, u32[]{:S(2)}) copy-start(bf16[1024,3072]{1,0:T(8,128)(2,1)} %w_hbm.5) | copy-start | bytes 18874372
  62.5 7.3 %copy-start.12 = (f32[192,1024]{1,0:T(8,128)S(1)}, f32[192,1024]{1,0:T(8,128)}, u32[]{:S(2)}) copy-start(f32[192,1024]{1,0:T(8,128)} %get-tuple-element.46.state_ref) | copy-start | bytes 2359300
  62.6 7.3 %copy-start.15 = (bf16[12,16,1024]{2,1,0:T(8,128)(2,1)S(1)}, bf16[12,16,1024]{2,1,0:T(8,128)(2,1)}, u32[]{:S(2)}) copy-start(bf16[12,16,1024]{2,1,0:T(8,128)(2,1)} %param.22) | copy-start | bytes 1179652
  62.6 7.3 %copy-start.23 = (bf16[1024,1024]{1,0:T(8,128)(2,1)S(1)}, bf16[1024,1024]{1,0:T(8,128)(2,1)}, u32[]{:S(2)}) copy-start(bf16[1024,1024]{1,0:T(8,128)(2,1)} %wo_hbm.4) | copy-start | bytes 6291460
  62.6 7.3 %copy-start.24 = (bf16[192,2048]{1,0:T(8,128)(2,1)S(1)}, bf16[192,2048]{1,0:T(8,128)(2,1)}, u32[]{:S(2)}) copy-start(bf16[192,2048]{1,0:T(8,128)(2,1)} %get-tuple-element.47.dh_ref) | copy-start | bytes 2359300
  62.6 7.3 %copy-start.25 = (bf16[192,768]{1,0:T(8,128)(2,1)S(1)}, bf16[192,768]{1,0:T(8,128)(2,1)}, u32[]{:S(2)}) copy-start(bf16[192,768]{1,0:T(8,128)(2,1)} %constant.26.clone.base_ref) | copy-start | bytes 884740
  69.8 23.6 %slice-start = ((s8[6291456]{0:T(1024)(128)(4,1)}), s8[4194304]{0:T(1024)(128)(4,1)S(1)}, s32[]{:S(2)}) async-start(s8[6291456]{0:T(1024)(128)(4,1)} %bitcast.6), calls=%async_computation.2 | async-start | bytes 8388608
  69.8 23.6 %slice-start.1 = ((s8[6291456]{0:T(1024)(128)(4,1)}), s8[2097152]{0:T(1024)(128)(4,1)S(1)}, s32[]{:S(2)}) async-start(s8[6291456]{0:T(1024)(128)(4,1)} %bitcast.6), calls=%async_computation.3 | async-start | bytes 4194304
  90.1 9.1 %collective-permute-start.4 = (bf16[144,1024]{1,0:T(8,128)(2,1)S(1)}, bf16[144,1024]{1,0:T(8,128)(2,1)S(1)}, u32[]{:S(2)}, u32[]{:S(2)}) collective-permute-start(bf16[144,1024]{1,0:T(8,128)(2,1)S(1)} %get-tuple-element.56), channel_id=1, source_target_pairs={{0,15},{1,0},{2,1},{3,2},{4,3},{5,4},{6,5},{7,6},{8,7},{9,8},{10,9... | collective-permute-start | bytes 884744 | tf_op jit(solution)/shard_map/ppermute | solution.py:685
  90.2 9.0 %collective-permute-start.5 = (bf16[144,1024]{1,0:T(8,128)(2,1)S(1)}, bf16[144,1024]{1,0:T(8,128)(2,1)S(1)}, u32[]{:S(2)}, u32[]{:S(2)}) collective-permute-start(bf16[144,1024]{1,0:T(8,128)(2,1)S(1)} %get-tuple-element.57), channel_id=1, source_target_pairs={{0,1},{1,2},{2,3},{3,4},{4,5},{5,6},{6,7},{7,8},{8,9},{9,10},{10,1... | collective-permute-start | bytes 884744 | tf_op jit(solution)/shard_map/ppermute | solution.py:685
  93.4 5.8 %copy-start.21 = (bf16[288,192]{1,0:T(8,128)(2,1)S(1)}, bf16[288,192]{1,0:T(8,128)(2,1)}, u32[]{:S(2)}) copy-start(bf16[288,192]{1,0:T(8,128)(2,1)} %constant.29.clone.sel_ref) | copy-start | bytes 331780
  93.4 10.5 %copy-start.22 = (bf16[288,192]{1,0:T(8,128)(2,1)S(1)}, bf16[288,192]{1,0:T(8,128)(2,1)}, u32[]{:S(2)}) copy-start(bf16[288,192]{1,0:T(8,128)(2,1)} %constant.30.clone.sel_ref) | copy-start | bytes 331780
  99.2 11.1 %copy-start.18 = (bf16[192,1024]{1,0:T(8,128)(2,1)S(1)}, bf16[192,1024]{1,0:T(8,128)(2,1)}, u32[]{:S(2)}) copy-start(bf16[192,1024]{1,0:T(8,128)(2,1)} %get-tuple-element.65.ow_ref) | copy-start | bytes 1179652
  99.6 10.7 %collective-permute-start.6 = (bf16[96,1024]{1,0:T(8,128)(2,1)S(1)}, bf16[96,1024]{1,0:T(8,128)(2,1)S(1)}, u32[]{:S(2)}, u32[]{:S(2)}) collective-permute-start(bf16[96,1024]{1,0:T(8,128)(2,1)S(1)} %get-tuple-element.60), channel_id=1, source_target_pairs={{0,16},{16,32},{32,48},{48,64},{64,80},{80,96},{96,112},{1,17},{17... | collective-permute-start | bytes 589832 | tf_op jit(solution)/shard_map/ppermute | solution.py:691
  102.4 7.9 %collective-permute-start.7 = (bf16[96,1024]{1,0:T(8,128)(2,1)S(1)}, bf16[96,1024]{1,0:T(8,128)(2,1)S(1)}, u32[]{:S(2)}, u32[]{:S(2)}) collective-permute-start(bf16[96,1024]{1,0:T(8,128)(2,1)S(1)} %get-tuple-element.59._), channel_id=1, source_target_pairs={{16,0},{32,16},{48,32},{64,48},{80,64},{96,80},{112,96},{17,1},{33... | collective-permute-start | bytes 589832 | tf_op jit(solution)/shard_map/ppermute | solution.py:691
  103.9 6.4 %copy-start.2 = (bf16[1024,2048]{1,0:T(8,128)(2,1)S(1)}, bf16[1024,2048]{1,0:T(8,128)(2,1)}, u32[]{:S(2)}) copy-start(bf16[1024,2048]{1,0:T(8,128)(2,1)} %wp_hbm.7) | copy-start | bytes 12582916
  103.9 6.4 %copy-start.6 = (bf16[8,384,512]{2,1,0:T(8,128)(2,1)S(1)}, bf16[8,384,512]{2,1,0:T(8,128)(2,1)}, u32[]{:S(2)}) copy-start(bf16[8,384,512]{2,1,0:T(8,128)(2,1)} %get-tuple-element.63.wts_ref) | copy-start | bytes 9437188
  103.9 6.4 %copy-start.7 = (bf16[1024,1024]{1,0:T(8,128)(2,1)S(1)}, bf16[1024,1024]{1,0:T(8,128)(2,1)}, u32[]{:S(2)}) copy-start(bf16[1024,1024]{1,0:T(8,128)(2,1)} %wo_hbm.5) | copy-start | bytes 6291460
  103.9 6.4 %copy-start.8 = (bf16[512,2048]{1,0:T(8,128)(2,1)S(1)}, bf16[512,2048]{1,0:T(8,128)(2,1)}, u32[]{:S(2)}) copy-start(bf16[512,2048]{1,0:T(8,128)(2,1)} %get-tuple-element.62.pairs_ref) | copy-start | bytes 6291460
  103.9 6.4 %copy-start.11 = (bf16[192,2048]{1,0:T(8,128)(2,1)S(1)}, bf16[192,2048]{1,0:T(8,128)(2,1)}, u32[]{:S(2)}) copy-start(bf16[192,2048]{1,0:T(8,128)(2,1)} %get-tuple-element.39.own_hbm.own_ref) | copy-start | bytes 2359300
  103.9 6.4 %copy-start.16 = (bf16[192,1024]{1,0:T(8,128)(2,1)S(1)}, bf16[192,1024]{1,0:T(8,128)(2,1)}, u32[]{:S(2)}) copy-start(bf16[192,1024]{1,0:T(8,128)(2,1)} %get-tuple-element.38.q_hbm.q_ref) | copy-start | bytes 1179652
  104.0 6.4 %copy-start.17 = (bf16[192,1024]{1,0:T(8,128)(2,1)S(1)}, bf16[192,1024]{1,0:T(8,128)(2,1)}, u32[]{:S(2)}) copy-start(bf16[192,1024]{1,0:T(8,128)(2,1)} %get-tuple-element.64.mix_ref) | copy-start | bytes 1179652
  120.7 12.8 %copy-start.10 = (bf16[192,1024]{1,0:T(8,128)(2,1)S(1)}, bf16[192,1024]{1,0:T(8,128)(2,1)}, u32[]{:S(2)}) copy-start(bf16[192,1024]{1,0:T(8,128)(2,1)} %get-tuple-element.66._.dq_ref) | copy-start | bytes 1179652
  120.7 17.1 %copy-start.9 = (bf16[12,16,1024]{2,1,0:T(8,128)(2,1)S(1)}, bf16[12,16,1024]{2,1,0:T(8,128)(2,1)}, u32[]{:S(2)}) copy-start(bf16[12,16,1024]{2,1,0:T(8,128)(2,1)} %param.18) | copy-start | bytes 1179652
  120.7 31.7 %all-to-all-start.1 = ((bf16[128,4,1024]{2,1,0:T(4,128)(2,1)}), bf16[128,4,1024]{2,1,0:T(4,128)(2,1)S(1)}, u32[]{:S(2)}, u32[]{:S(2)}) async-start(bf16[128,4,1024]{2,1,0:T(4,128)(2,1)} %get-tuple-element.70), calls=%async_computation.1 | async-start | bytes 2097152 | tf_op jit(solution)/shard_map/all_to_all | solution.py:863
  133.5 2.2 %copy-start.4 = (bf16[2048,1024]{1,0:T(8,128)(2,1)S(1)}, bf16[2048,1024]{1,0:T(8,128)(2,1)}, u32[]{:S(2)}) copy-start(bf16[2048,1024]{1,0:T(8,128)(2,1)} %wd_hbm.3) | copy-start | bytes 12582916
  135.7 2.2 %copy-start.3 = (bf16[1024,2048]{1,0:T(8,128)(2,1)S(1)}, bf16[1024,2048]{1,0:T(8,128)(2,1)}, u32[]{:S(2)}) copy-start(bf16[1024,2048]{1,0:T(8,128)(2,1)} %wp_hbm.7) | copy-start | bytes 12582916
  135.7 3.0 %copy-start.5 = (bf16[1024,1024]{1,0:T(8,128)(2,1)S(1)}, bf16[1024,1024]{1,0:T(8,128)(2,1)}, u32[]{:S(2)}) copy-start(bf16[1024,1024]{1,0:T(8,128)(2,1)} %wq_hbm.3) | copy-start | bytes 6291460
  138.7 1.1 copy-start.13
  139.8 1.1 copy-start.14

commit v5 on v4

--- a/solution.py
+++ b/solution.py
@@ -20,11 +20,12 @@
 NT = (((1,), (1,)), ((), ()))
 TN = (((0,), (0,)), ((), ()))
 CHUNK = 32
+SOFT = 32
 TILE = 1024
 PAIR = 128
 HALF = 64
 SLACK_BYTES = 8 * 2**20
-FEED_TILE = 512
+FEED_TILE = 1024
 GROUP = 2
 GELU_C = 0.7978845608028654
 GELU_A = 0.044715
@@ -235,14 +236,14 @@
         own_weights = []
         for side in range(2):
             parts = []
-            for i in range(0, cells, CHUNK):
-                own_score = own_scores[side][i : i + CHUNK]
-                x = scores[k, pl.ds(side * cells + i, CHUNK), :] + bias[pl.ds(i, CHUNK), :]
+            for i in range(0, cells, SOFT):
+                own_score = own_scores[side][i : i + SOFT]
+                x = scores[k, pl.ds(side * cells + i, SOFT), :] + bias[pl.ds(i, SOFT), :]
                 peak = jnp.maximum(jnp.max(x, -1, keepdims=True), own_score)
                 x = jnp.exp(x - peak)
                 own_weight = jnp.exp(own_score - peak)
                 inverse = 1.0 / (jnp.sum(x, -1, keepdims=True) + own_weight)
-                wts_ref[h, pl.ds(side * cells + i, CHUNK), :] = (x * inverse).astype(BF)
+                wts_ref[h, pl.ds(side * cells + i, SOFT), :] = (x * inverse).astype(BF)
                 parts.append(own_weight * inverse)
             own_weights.append(jnp.concatenate(parts, axis=0))
         lanes = iota((cells, PAIR), 1) < HALF
@@ -336,17 +337,59 @@
     tiles_of(model, pick)
 
 
-def near_rows_kernel(north_ref, south_ref, w_hbm, kv_ref, x, w, sems):
+def spread(first, second):
+    lanes = iota((first.shape[0], PAIR), 1) < HALF
+    return jnp.where(lanes, first, second)
+
+
+def inner_kernel(
+    north_ref, south_ref, q_ref, kvo_ref, base_ref, inside_ref, w_hbm,
+    kvr_ref, wts_hbm, mix_ref, peak_ref, sum_ref,
+    x, w, kv, bias, scores, wts, sems, out_sems,
+):
     rim, model = north_ref.shape
+    cells = q_ref.shape[0]
     copies = fetch([w_hbm.at[:, pl.ds(model, 2 * model)]], [w], sems)
     x[pl.ds(0, rim), :] = north_ref[...]
     x[pl.ds(rim, rim), :] = south_ref[...]
+    kv[pl.ds(0, cells), :] = kvo_ref[...]
+    bias[...] = base_ref[...].astype(F32) + inside_ref[0:1, :]
     copies[0].wait()
 
     def pairs(j):
-        kv_ref[:, pl.ds(j, TILE)] = dot(x[...], w[:, pl.ds(j, TILE)]).astype(BF)
+        part = dot(x[...], w[:, pl.ds(j, TILE)]).astype(BF)
+        kvr_ref[:, pl.ds(j, TILE)] = part
+        kv[pl.ds(cells, cells), pl.ds(j, TILE)] = part
 
     tiles_of(2 * model, pairs)
+
+    @pl.loop(0, model // (PAIR * GROUP))
+    def _(g):
+        heads = []
+        for k in range(GROUP):
+            h = g * GROUP + k
+            keys = pl.ds(pl.multiple_of(h * PAIR, PAIR), PAIR)
+            vals = pl.ds(pl.multiple_of(model + h * PAIR, PAIR), PAIR)
+            heads.append((h, keys, vals))
+            scores[k] = dot(stacked(q_ref[:, keys]), kv[:, keys], NT)
+        for k, (h, keys, vals) in enumerate(heads):
+            for i in range(0, cells, SOFT):
+                peaks, sums = [], []
+                for side in range(2):
+                    rows = pl.ds(side * cells + i, SOFT)
+                    v = scores[k, rows, :] + bias[pl.ds(i, SOFT), :]
+                    peak = jnp.max(v, -1, keepdims=True)
+                    v = jnp.exp(v - peak)
+                    wts[h, rows, :] = v.astype(BF)
+                    peaks.append(peak)
+                    sums.append(jnp.sum(v, -1, keepdims=True))
+                peak_ref[pl.ds(i, SOFT), keys] = spread(*peaks)
+                sum_ref[pl.ds(i, SOFT), keys] = spread(*sums)
+        for k, (h, keys, vals) in enumerate(heads):
+            mix_ref[:, keys] = merged(dot(wts[h], kv[:, vals]))
+
+    for copy in fetch([wts], [wts_hbm], out_sems):
+        copy.wait()
 
 
 def near_back_loop(q_ref, kv, kv_rows, wts, cols, mix, dmix, dkv, scores, ds, put):
@@ -365,11 +408,11 @@
             deltas.append(lane_sums(grad.astype(F32) * mix[:, keys].astype(F32)))
         for k, (h, keys, vals) in enumerate(heads):
             for s in range(2):
-                for i in range(0, cells, CHUNK):
-                    rows = pl.ds(s * cells + i, CHUNK)
+                for i in range(0, cells, SOFT):
+                    rows = pl.ds(s * cells + i, SOFT)
                     ds[k, rows, :] = (
                         wts[h, rows, cols].astype(F32)
-                        * (scores[k, rows, pl.ds(0, cols.size)] - deltas[k][s][i : i + CHUNK])
+                        * (scores[k, rows, pl.ds(0, cols.size)] - deltas[k][s][i : i + SOFT])
                     ).astype(BF)
         for k, (h, keys, vals) in enumerate(heads):
             put(keys, merged(dot(ds[k], kv[kv_rows, keys])))
@@ -379,32 +422,25 @@
 
 def near_kernel(
     q_ref, west_ref, east_ref, base_ref, inside_ref, state_ref, cot_ref, dh_ref, gain_ref,
-    kvo_hbm, kvr_hbm, wn_hbm, wo_hbm, wu_hbm,
-    after_ref, hid_ref, dwest_ref, deast_ref, dq_ref, wts_hbm, mix, dmix, dafter_ref,
-    wkv, wo, wu, kv, dkv, x, wts, scores, ds, bias, nrm, du, acc, dab, sems, out_sems,
+    mix_in_ref, peak_ref, sum_ref, wn_hbm, wo_hbm, wu_hbm,
+    after_ref, hid_ref, dwest_ref, deast_ref, dq_ref, mix, dscaled_ref, dafter_ref,
+    wkv, wo, wu, kv, dkv, x, wts, scores, ds, bias, share, nrm, du, acc, dab, dmix, sems,
 ):
     cells, model = state_ref.shape
     keys_all = kv.shape[0]
-    ext = 2 * cells
     side = west_ref.shape[0]
-    ends = ext + 2 * side
+    ends = 2 * side
     copies = fetch(
-        [kvo_hbm, kvr_hbm, wn_hbm.at[:, pl.ds(model, 2 * model)], wo_hbm, wu_hbm],
-        [kv.at[pl.ds(0, cells), :], kv.at[pl.ds(cells, cells), :], wkv, wo, wu],
-        sems,
+        [wn_hbm.at[:, pl.ds(model, 2 * model)], wo_hbm, wu_hbm], [wkv, wo, wu], sems
     )
     x[pl.ds(0, side), :] = west_ref[...]
     x[pl.ds(side, side), :] = east_ref[...]
     kv[pl.ds(ends, keys_all - ends), :] = jnp.zeros((keys_all - ends, 2 * model), BF)
     bias[...] = base_ref[...].astype(F32) + inside_ref[0:1, :]
     copies[0].wait()
-    copies[1].wait()
-    copies[2].wait()
 
     def project(j):
-        kv[pl.ds(ext, 2 * side), pl.ds(j, TILE)] = dot(
-            x[...], wkv[:, pl.ds(j, TILE)]
-        ).astype(BF)
+        kv[pl.ds(0, ends), pl.ds(j, TILE)] = dot(x[...], wkv[:, pl.ds(j, TILE)]).astype(BF)
 
     tiles_of(2 * model, project)
 
@@ -418,17 +454,28 @@
             heads.append((h, keys, vals))
             scores[k] = dot(stacked(q_ref[:, keys]), kv[:, keys], NT)
         for k, (h, keys, vals) in enumerate(heads):
-            for start in range(0, 2 * cells, CHUNK):
-                rows = pl.ds(start, CHUNK)
-                v = scores[k, rows, :] + bias[pl.ds(start % cells, CHUNK), :]
-                v = jnp.exp(v - jnp.max(v, -1, keepdims=True))
-                inverse = 1.0 / jnp.sum(v, -1, keepdims=True)
-                wts[h, rows, :] = (v * inverse).astype(BF)
+            for i in range(0, cells, SOFT):
+                here = pl.ds(i, SOFT)
+                peaks, sums = peak_ref[here, keys], sum_ref[here, keys]
+                shares = []
+                for s in range(2):
+                    rows = pl.ds(s * cells + i, SOFT)
+                    before = peaks[:, s * HALF : s * HALF + 1]
+                    v = scores[k, rows, :] + bias[here, :]
+                    peak = jnp.maximum(jnp.max(v, -1, keepdims=True), before)
+                    v = jnp.exp(v - peak)
+                    part = jnp.exp(before - peak)
+                    total = jnp.sum(v, -1, keepdims=True)
+                    total = total + part * sums[:, s * HALF : s * HALF + 1]
+                    inverse = 1.0 / total
+                    wts[h, rows, :] = (v * inverse).astype(BF)
+                    shares.append(part * inverse)
+                share[here, keys] = spread(*shares)
         for k, (h, keys, vals) in enumerate(heads):
-            mix[:, keys] = merged(dot(wts[h], kv[:, vals])).astype(BF)
-
-    leaving = fetch([wts.at[:, :, pl.ds(0, ext)]], [wts_hbm], out_sems)
-    copies[3].wait()
+            rims = merged(dot(wts[h], kv[:, vals]))
+            mix[:, keys] = (rims + mix_in_ref[:, keys] * share[:, keys]).astype(BF)
+
+    copies[1].wait()
 
     def project_out(j):
         after_ref[:, pl.ds(j, TILE)] = state_ref[:, pl.ds(j, TILE)] + dot(
@@ -439,7 +486,7 @@
     for rows in row_chunks(cells):
         normed, _ = unit(after_ref[rows, :])
         nrm[rows, :] = (normed * gain_ref[2:3, :]).astype(BF)
-    copies[4].wait()
+    copies[2].wait()
 
     def feed(j):
         cols = pl.ds(j, FEED_TILE)
@@ -466,11 +513,13 @@
         dab[rows, :] = total.astype(BF)
 
     def mix_back(j):
-        dmix[:, pl.ds(j, TILE)] = dot(dab[...], wo[pl.ds(j, TILE), :], NT).astype(BF)
+        cols = pl.ds(j, TILE)
+        grad = dot(dab[...], wo[cols, :], NT)
+        dmix[:, cols] = grad.astype(BF)
+        dscaled_ref[:, cols] = (grad * share[:, cols]).astype(BF)
 
     tiles_of(model, mix_back)
-
-    outer = pl.ds(ext, keys_all - ext)
+    outer = pl.ds(0, keys_all)
 
     def put(keys, dq):
         dq_ref[:, keys] = dq
@@ -483,8 +532,6 @@
         deast_ref[:, pl.ds(j, TILE)] = both[side:]
 
     tiles_of(model, rim_back)
-    for copy in leaving:
-        copy.wait()
 
 
 def middle_back_kernel(
@@ -612,11 +659,11 @@
             own_dots.append(lane_sums(grad_f * own_ref[:, vals].astype(F32)))
         for k, (h, keys, vals) in enumerate(heads):
             for s in range(2):
-                for i in range(0, cells, CHUNK):
-                    rows = pl.ds(s * cells + i, CHUNK)
+                for i in range(0, cells, SOFT):
+                    rows = pl.ds(s * cells + i, SOFT)
                     ds[k, rows, :] = (
                         wts_ref[h, rows, :].astype(F32)
-                        * (scores[k, rows, :] - deltas[k][s][i : i + CHUNK])
+                        * (scores[k, rows, :] - deltas[k][s][i : i + SOFT])
                     ).astype(BF)
         for k, (h, keys, vals) in enumerate(heads):
             lanes = iota((cells, PAIR), 1) < HALF
@@ -734,7 +781,7 @@
         np.abs(places[None, :, 1] - own_cols[:, None]) <= RADIUS
     )
     base[:, :keys_n][allowed] = 0.0
-    base = jnp.asarray(base.astype(jnp.bfloat16))
+    base = base.astype(jnp.bfloat16)
     key_rows = np.zeros((8, keys_all), np.int32)
     key_rows[:, :keys_n] = places[None, :, 0]
     key_lat = jnp.asarray(key_rows) + lax.axis_index("lat") * rows_lat
@@ -794,27 +841,32 @@
     )
     east = ring(west_send, -1)
     west = ring(east_send, 1)
-    kv_rows = call(
-        near_rows_kernel, (north, south, w_near_proj), "vva",
-        [((2 * rim, 2 * model), BF)],
-        [vm((2 * rim, model), BF), vm((model, 2 * model), BF), dma((1,))],
-        2 * 2 * rim * model * 2 * model, "near_rows",
-    )
-    after, hidden, dwest, deast, dq_rim, near_w, near_mix, dmix, dafter = call(
+    kv_rows, near_w, inner_mix, inner_peak, inner_sum = call(
+        inner_kernel,
+        (north, south, q_n, kv_own, jnp.asarray(base[:, : 2 * cells]), inside[:, : 2 * cells],
+         w_near_proj), "vvvvvva",
+        [((2 * rim, 2 * model), BF), ((pairs_n, 2 * cells, 2 * cells), BF, "h"),
+         ((cells, model), F32), ((cells, model), F32), ((cells, model), F32)],
+        [vm((2 * rim, model), BF), vm((model, 2 * model), BF), vm((2 * cells, 2 * model), BF),
+         vm((cells, 2 * cells), F32), vm((GROUP, 2 * cells, 2 * cells), F32),
+         vm((pairs_n, 2 * cells, 2 * cells), BF), dma((1,)), dma((1,))],
+        4 * rim * model * 2 * model * 2, "inner",
+    )
+    outer = keys_all - 2 * cells
+    after, hidden, dwest, deast, dq_rim, near_mix, dmix, dafter = call(
         near_kernel,
-        (q_n, west, east, base, inside, state, cot, dhid, norm_gains, kv_own, kv_rows,
-         w_near_proj, w_near_out, w_up), "vvvvvvvvvaaaaa",
+        (q_n, west, east, jnp.asarray(base[:, 2 * cells :]), inside[:, 2 * cells :], state, cot,
+         dhid, norm_gains, inner_mix, inner_peak, inner_sum, w_near_proj, w_near_out, w_up),
+        "vvvvvvvvvvvvaaa",
         [((cells, model), F32), ((cells, ff), BF), ((side, model), BF), ((side, model), BF),
-         ((cells, model), F32), ((pairs_n, 2 * cells, 2 * cells), BF, "h"), ((cells, model), BF),
-         ((cells, model), BF), ((cells, model), F32)],
+         ((cells, model), F32), ((cells, model), BF), ((cells, model), BF),
+         ((cells, model), F32)],
         [vm((model, 2 * model), BF), vm((model, model), BF), vm((model, ff), BF),
-         vm((keys_all, 2 * model), BF), vm((keys_all - 2 * cells, 2 * model), BF),
-         vm((2 * side, model), BF), vm((pairs_n, 2 * cells, keys_all), BF),
-         vm((GROUP, 2 * cells, keys_all), F32),
-         vm((GROUP, 2 * cells, keys_all - 2 * cells), BF),
-         vm((cells, keys_all), F32), vm((cells, model), BF),
-         vm((cells, ff), BF), vm((cells, model), F32), vm((cells, model), BF),
-         dma((5,)), dma((1,))],
+         vm((outer, 2 * model), BF), vm((outer, 2 * model), BF), vm((2 * side, model), BF),
+         vm((pairs_n, 2 * cells, outer), BF), vm((GROUP, 2 * cells, outer), F32),
+         vm((GROUP, 2 * cells, outer), BF), vm((cells, outer), F32), vm((cells, model), F32),
+         vm((cells, model), BF), vm((cells, ff), BF), vm((cells, model), F32),
+         vm((cells, model), BF), vm((cells, model), BF), dma((3,))],
         2e10, "near",
     )
     from_east = ring(dwest, -1)

time: 155 us -> 162 us (1.045)
  Pallas kernels: 75.9 us -> 87.3 us
  local copies, waits for them, and re-layouts: 11.1 us -> 5.57 us
    pallas_call x14, Pallas kernels: 75.9 us -> 87.3 us  [call(): pl.pallas_call(body, name=name, out_shape=shapes[0] if single else shapes...]
    unnamed x58 -> x70, local copies, waits for them, and re-layouts: 11.1 us -> 5.57 us
  transfers between devices with their start and end apart: 10 -> 10, of which waited for: 4 -> 5; matrix products, arithmetic and copies ran while one was open for 0% -> 0% of each run, Pallas kernels for 19% -> 21%
where the time goes in v5:
time: 162 us
  Pallas kernels  87.3 us (54%)
  starting transfers between devices  40.3 us (25%)
  waiting for transfers between devices  27.1 us (17%)
  local copies, waits for them, and re-layouts  5.57 us (3%)
    pallas_call x14, Pallas kernels, call(): pl.pallas_call(body, name=name, out_shape=shapes[0] if single else shapes...  87.3 us
    all_to_all x1, waiting for transfers between devices, per_device(): arrived = lax.all_to_all(payload, ('lat', 'lon'), 0, 0, tiled=True)  13.3 us
    all_to_all x1, starting transfers between devices, per_device(): returned = lax.all_to_all(slot_grads, ('lat', 'lon'), 0, 0, tiled=True)  12.8 us
    all_to_all x1, starting transfers between devices, per_device(): arrived = lax.all_to_all(payload, ('lat', 'lon'), 0, 0, tiled=True)  11.5 us
    ppermute x4, starting transfers between devices, line(): return lax.ppermute(value, 'lat', pairs)  10.9 us
    all_to_all x1, waiting for transfers between devices, per_device(): returned = lax.all_to_all(slot_grads, ('lat', 'lon'), 0, 0, tiled=True)  7.72 us
    unnamed x70, local copies, waits for them, and re-layouts  5.57 us
    ppermute x4, starting transfers between devices, ring(): lax.ppermute(value, 'lon', [(i, (i + by) % size) for i in range(size)])  5.1 us
  transfers between devices with their start and end apart: 10, of which 5 were waited for; matrix products, arithmetic and copies ran while one was open for 0% of the time, Pallas kernels for 21%

profile of v5, /device:TPU:1, one launch (start us, length us, event | category | flops | bytes accessed | tf_op | source)
XLA Modules:
  0.0 161.7 jit_solution(7800337812172538290)
XLA Ops:
  0.6 0.0 copy-start.23
  0.6 2.8 %place.1 = (bf16[128,4,1152]{2,1,0:T(4,128)(2,1)}, bf16[512,256]{1,0:T(8,128)(2,1)}) custom-call(s32[1,256]{1,0:T(1,128)} %bitcast.17, s32[1,256]{1,0:T(1,128)} %bitcast.18, bf16[256,1024]{1,0:T(8,128)(2,1)} %obs_hbm.1), custom_call_target="tpu_custom_call" | custom-call | flops 268435456 | bytes 1968128 | tf_op jit(solution)/shard_map/place/pallas_call | solution.py:120
  3.4 11.5 %all-to-all-start = ((bf16[128,4,1152]{2,1,0:T(4,128)(2,1)}), bf16[128,4,1152]{2,1,0:T(4,128)(2,1)S(1)}, u32[]{:S(2)}, u32[]{:S(2)}) async-start(bf16[128,4,1152]{2,1,0:T(4,128)(2,1)} %get-tuple-element.41), calls=%async_computation | async-start | bytes 2359296 | tf_op jit(solution)/shard_map/all_to_all | solution.py:804
  15.0 0.0 copy-done.23
  15.0 0.0 slice-start
  15.0 6.9 %grid_proj.1 = (bf16[192,1024]{1,0:T(8,128)(2,1)}, bf16[192,2048]{1,0:T(8,128)(2,1)}, bf16[192,2048]{1,0:T(8,128)(2,1)}) custom-call(bf16[192,1024]{1,0:T(8,128)(2,1)} %bitcast.10, bf16[192,1024]{1,0:T(8,128)(2,1)} %bitcast.13, f32[3,1024]{1,0:T(4,128)S(1)} %copy-done.23, bf16[1024,1024]{1,0:T(8,128)(2,1)} %wq_hbm.3, bf16[1024,2048]{1,0:T(8,128)(2,1)} %wp_hbm.7, ...), custom_call_target="tpu_custom_call" | custom-call | flops 2013265920 | bytes 13250560 | tf_op jit(solution)/shard_map/grid_proj/pallas_call | solution.py:120
  21.9 13.3 %all-to-all-done.arr_ref = bf16[128,4,1152]{2,1,0:T(4,128)(2,1)S(1)} async-done(((bf16[128,4,1152]{2,1,0:T(4,128)(2,1)}), bf16[128,4,1152]{2,1,0:T(4,128)(2,1)S(1)}, u32[]{:S(2)}, u32[]{:S(2)}) %all-to-all-start) | async-done | bytes 1179680 | tf_op jit(solution)/shard_map/all_to_all | solution.py:804
  35.3 10.8 %cross.1 = (f32[192,1024]{1,0:T(8,128)}, bf16[96,1024]{1,0:T(8,128)(2,1)S(1)}, bf16[96,1024]{1,0:T(8,128)(2,1)S(1)}, bf16[512,2048]{1,0:T(8,128)(2,1)}, bf16[8,3...) custom-call(bf16[128,4,1152]{2,1,0:T(4,128)(2,1)S(1)} %all-to-all-done.arr_ref, ...), custom_call_target="tpu_custom_call" | custom-call | flops 4294967296 | bytes 16265216 | tf_op jit(solution)/shard_map/cross/pallas_call | solution.py:120
  46.0 1.3 collective-permute-start.1
  47.3 4.0 %collective-permute-start = (bf16[96,1024]{1,0:T(8,128)(2,1)S(1)}, bf16[96,1024]{1,0:T(8,128)(2,1)S(1)}, u32[]{:S(2)}, u32[]{:S(2)}) collective-permute-start(bf16[96,1024]{1,0:T(8,128)(2,1)S(1)} %get-tuple-element.45.bottom_ref), channel_id=1, source_target_pairs={{0,16},{16,32},{32,48},{48,64},{64,80},{80,96},{96,112},{1,17},{17... | collective-permute-start | bytes 589832 | tf_op jit(solution)/shard_map/ppermute | solution.py:738
  51.4 0.0 copy-done.30
  51.4 0.0 slice-done
  51.4 0.0 copy-start.22
  51.4 0.0 copy-start.26
  51.4 2.7 %near_own.1 = (bf16[192,1024]{1,0:T(8,128)(2,1)S(1)}, bf16[192,2048]{1,0:T(8,128)(2,1)S(1)}) custom-call(bf16[96,1024]{1,0:T(8,128)(2,1)S(1)} %get-tuple-element.44.top_ref, bf16[96,1024]{1,0:T(8,128)(2,1)S(1)} %get-tuple-element.45.bottom_ref, bf16[1024,3072]{1,0:T(8,128)(2,1)S(1)} %bitcast.7), custom_call_target="tpu_custom_call" | custom-call | flops 1207959552 | bytes 7864320 | tf_op jit(solution)/shard_map/near_own/pallas_call | solution.py:120
  54.1 0.5 collective-permute-done.1.south_ref
  54.6 1.0 collective-permute-done.north_ref
  55.6 0.5 rim.1
  56.1 1.8 %collective-permute-start.2 = (bf16[144,1024]{1,0:T(8,128)(2,1)S(1)}, bf16[144,1024]{1,0:T(8,128)(2,1)S(1)}, u32[]{:S(2)}, u32[]{:S(2)}) collective-permute-start(bf16[144,1024]{1,0:T(8,128)(2,1)S(1)} %get-tuple-element.48), channel_id=1, source_target_pairs={{0,1},{1,2},{2,3},{3,4},{4,5},{5,6},{6,7},{7,8},{8,9},{9,10},{10,1... | collective-permute-start | bytes 884744 | tf_op jit(solution)/shard_map/ppermute | solution.py:732
  57.9 0.0 collective-permute-start.3
  57.9 0.0 copy-done.26
  57.9 0.0 copy-start.18
  57.9 0.0 copy-start.27
  57.9 0.0 copy-start.29
  57.9 6.2 %inner.1 = (bf16[192,2048]{1,0:T(8,128)(2,1)S(1)}, bf16[8,384,384]{2,1,0:T(8,128)(2,1)}, f32[192,1024]{1,0:T(8,128)S(1)}, f32[192,1024]{1,0:T(8,128)S(1)}, f32[192,1024]{1,0:T(8,128)S(1)}) custom-call(bf16[96,1024]{1,0:T(8,128)(2,1)S(1)} %collective-permute-done.north_ref, bf16[96,1024]{1,0:T(8,128)(2,1)S(1)} %collective-permute-done.1.south_ref, ...), custom_call_target="tpu_custom_call" | custom-call | flops 1610612736 | bytes 13529088 | tf_op jit(solution)/shard_map/inner/pallas_call | solution.py:120
  64.2 0.0 collective-permute-done.2.west_ref
  64.2 4.5 %collective-permute-done.3.east_ref = bf16[144,1024]{1,0:T(8,128)(2,1)S(1)} collective-permute-done((bf16[144,1024]{1,0:T(8,128)(2,1)S(1)}, bf16[144,1024]{1,0:T(8,128)(2,1)S(1)}, u32[]{:S(2)}, u32[]{:S(2)}) %collective-permute-start.3) | collective-permute-done | bytes 294944 | tf_op jit(solution)/shard_map/ppermute | solution.py:732
  68.7 0.0 copy-done.18
  68.7 0.0 copy-done.28
  68.7 0.0 copy-done.29
  68.7 0.0 slice-start.3
  68.7 26.9 %near.1 = (f32[192,1024]{1,0:T(8,128)S(1)}, bf16[192,2048]{1,0:T(8,128)(2,1)S(1)}, bf16[144,1024]{1,0:T(8,128)(2,1)S(1)}, bf16[144,1024]{1,0:T(8,128)(2,1)S(1)},...) custom-call(bf16[192,1024]{1,0:T(8,128)(2,1)S(1)} %get-tuple-element, ...), custom_call_target="tpu_custom_call" | custom-call | flops 20000000000 | bytes 22585344 | tf_op jit(solution)/shard_map/near/pallas_call | solution.py:120
  95.7 0.1 collective-permute-start.4
  95.8 3.2 %collective-permute-start.5 = (bf16[144,1024]{1,0:T(8,128)(2,1)S(1)}, bf16[144,1024]{1,0:T(8,128)(2,1)S(1)}, u32[]{:S(2)}, u32[]{:S(2)}) collective-permute-start(bf16[144,1024]{1,0:T(8,128)(2,1)S(1)} %get-tuple-element.65), channel_id=1, source_target_pairs={{0,1},{1,2},{2,3},{3,4},{4,5},{5,6},{6,7},{7,8},{8,9},{9,10},{10,1... | collective-permute-start | bytes 884744 | tf_op jit(solution)/shard_map/ppermute | solution.py:732
  99.0 0.0 copy-start.25
  99.0 5.7 %middle_back.1 = (f32[192,1024]{1,0:T(8,128)S(1)}, bf16[64,2048]{1,0:T(8,128)(2,1)S(1)}, f32[192,1024]{1,0:T(8,128)S(1)}) custom-call(bf16[192,1024]{1,0:T(8,128)(2,1)S(1)} %get-tuple-element.46.q_ref, bf16[192,2048]{1,0:T(8,128)(2,1)S(1)} %get-tuple-element.47._.kvo_ref, bf16[192,2048]{1,0:T(8,128)(2,1)S(1)} %get-tuple-element.59.kvr_ref, ...), custom_call_target="tpu_custom_call" | custom-call | flops 1610612736 | bytes 14024704 | tf_op jit(solution)/shard_map/middle_back/pallas_call | solution.py:120
  104.8 0.0 collective-permute-done.4.from_east_ref
  104.8 0.0 collective-permute-done.5.from_west_ref
  104.8 0.0 copy-start.19
  104.8 0.0 copy-start.20
  104.8 0.0 copy-start.21
  104.8 0.4 fold.1
  105.2 4.1 %collective-permute-start.6 = (bf16[96,1024]{1,0:T(8,128)(2,1)S(1)}, bf16[96,1024]{1,0:T(8,128)(2,1)S(1)}, u32[]{:S(2)}, u32[]{:S(2)}) collective-permute-start(bf16[96,1024]{1,0:T(8,128)(2,1)S(1)} %get-tuple-element.68), channel_id=1, source_target_pairs={{0,16},{16,32},{32,48},{48,64},{64,80},{80,96},{96,112},{1,17},{17... | collective-permute-start | bytes 589832 | tf_op jit(solution)/shard_map/ppermute | solution.py:738
  109.3 1.5 collective-permute-start.7
  110.9 0.0 copy-start
  110.9 0.0 copy-start.4
  110.9 0.0 copy-start.5
  110.9 6.3 %own_back.1.dn_ref = f32[192,1024]{1,0:T(8,128)S(1)} custom-call(bf16[192,1024]{1,0:T(8,128)(2,1)S(1)} %get-tuple-element.46.q_ref, bf16[192,2048]{1,0:T(8,128)(2,1)S(1)} %get-tuple-element.47._.kvo_ref, bf16[192,1024]{1,0:T(8,128)(2,1)S(1)} %get-tuple-element.57.mix, bf16[192,1024]{1,0:T(8,128)(2,1)S(1)} %get-tuple-element.58.dmix, ...), custom_call_target="tpu_custom_call" | custom-call | flops 1610612736 | bytes 13348864 | tf_op jit(solution)/shard_map/own_back/pallas_call | solution.py:120
  117.2 0.0 collective-permute-done.6.north_ref
  117.2 0.0 collective-permute-done.7.south_ref
  117.3 10.2 %cross_back.1 = (f32[192,1024]{1,0:T(8,128)}, bf16[128,4,1024]{2,1,0:T(4,128)(2,1)}, bf16[192,1024]{1,0:T(8,128)(2,1)}, bf16[192,2048]{1,0:T(8,128)(2,1)}) custom-call(f32[192,1024]{1,0:T(8,128)S(1)} %own_back.1.dn_ref, bf16[96,1024]{1,0:T(8,128)(2,1)S(1)} %collective-permute-done.6.north_ref, bf16[96,1024]{1,0:T(8,128)(2,1)S(1)} %collective-permute-done.7.south_ref, ...), custom_call_target="tpu_custom_call" | custom-call | flops 4294967296 | bytes 19279872 | tf_op jit(solution)/shard_map/cross_back/pallas_call | solution.py:120
  127.6 0.0 copy-start.8
  127.6 0.0 copy-start.7
  127.6 12.8 %all-to-all-start.1 = ((bf16[128,4,1024]{2,1,0:T(4,128)(2,1)}), bf16[128,4,1024]{2,1,0:T(4,128)(2,1)S(1)}, u32[]{:S(2)}, u32[]{:S(2)}) async-start(bf16[128,4,1024]{2,1,0:T(4,128)(2,1)} %get-tuple-element.78), calls=%async_computation.1 | async-start | bytes 2097152 | tf_op jit(solution)/shard_map/all_to_all | solution.py:915
  140.4 0.0 copy-start.2
  140.4 2.2 %copy-done.2 = bf16[2048,1024]{1,0:T(8,128)(2,1)S(1)} copy-done((bf16[2048,1024]{1,0:T(8,128)(2,1)S(1)}, bf16[2048,1024]{1,0:T(8,128)(2,1)}, u32[]{:S(2)}) %copy-start.2) | copy-done | bytes 4194328
  142.6 2.0 %encode.1 = bf16[192,1024]{1,0:T(8,128)(2,1)} custom-call(f32[192,1024]{1,0:T(8,128)S(1)} %copy-done.13, bf16[192,2048]{1,0:T(8,128)(2,1)S(1)} %copy-done.15, bf16[2048,1024]{1,0:T(8,128)(2,1)S(1)} %copy-done.2, bf16[192,1024]{1,0:T(8,128)(2,1)S(1)} %copy-done.8), custom_call_target="tpu_custom_call" | custom-call | flops 805306368 | bytes 6553600 | tf_op jit(solution)/shard_map/encode/pallas_call | solution.py:120
  144.7 0.1 copy-done.1
  144.8 0.8 copy-done.3
  145.6 1.1 copy-done.16
  146.7 1.1 copy-done.17
  147.9 3.7 %grid_back.1 = bf16[192,1024]{1,0:T(8,128)(2,1)} custom-call(bf16[192,1024]{1,0:T(8,128)(2,1)S(1)} %bitcast.12, f32[192,1024]{1,0:T(8,128)S(1)} %copy-done.16, f32[3,1024]{1,0:T(4,128)S(1)} %copy-done.23, bf16[192,1024]{1,0:T(8,128)(2,1)S(1)} %copy-done.8, bf16[192,2048]{1,0:T(8,128)(2,1)S(1)} %copy-done.17, bf16[1024,1024]{1,0:T(8,128)(2,1)S(1)} %copy-done.3, ...), custom_call_target="tpu_custom_call" | custom-call | flops 1207959552 | bytes 9056256 | tf_op jit(solution)/shard_map/grid_back/pallas_call | solution.py:120
  151.6 7.7 %all-to-all-done.1.ret_ref = bf16[128,4,1024]{2,1,0:T(4,128)(2,1)S(1)} async-done(((bf16[128,4,1024]{2,1,0:T(4,128)(2,1)}), bf16[128,4,1024]{2,1,0:T(4,128)(2,1)S(1)}, u32[]{:S(2)}, u32[]{:S(2)}) %all-to-all-start.1) | async-done | bytes 1048608 | tf_op jit(solution)/shard_map/all_to_all | solution.py:915
  159.3 2.2 %gather.1 = bf16[256,1024]{1,0:T(8,128)(2,1)} custom-call(bf16[512,256]{1,0:T(8,128)(2,1)} %get-tuple-element.77.place_hbm, bf16[128,4,1024]{2,1,0:T(4,128)(2,1)S(1)} %all-to-all-done.1.ret_ref), custom_call_target="tpu_custom_call" | custom-call | flops 268435456 | bytes 1835008 | tf_op jit(solution)/shard_map/gather/pallas_call | solution.py:120
  (44 shorter events, 0.1 us)
Async XLA Ops:
  0.6 14.3 %copy-start.23 = (f32[3,1024]{1,0:T(4,128)S(1)}, f32[3,1024]{1,0:T(4,128)}, u32[]{:S(2)}) copy-start(f32[3,1024]{1,0:T(4,128)} %gain_ref.9) | copy-start | bytes 36868
  3.4 31.8 %all-to-all-start = ((bf16[128,4,1152]{2,1,0:T(4,128)(2,1)}), bf16[128,4,1152]{2,1,0:T(4,128)(2,1)S(1)}, u32[]{:S(2)}, u32[]{:S(2)}) async-start(bf16[128,4,1152]{2,1,0:T(4,128)(2,1)} %get-tuple-element.41), calls=%async_computation | async-start | bytes 2359296 | tf_op jit(solution)/shard_map/all_to_all | solution.py:804
  15.0 36.4 %slice-start = ((s8[6291456]{0:T(1024)(128)(4,1)}), s8[2097152]{0:T(1024)(128)(4,1)S(1)}, s32[]{:S(2)}) async-start(s8[6291456]{0:T(1024)(128)(4,1)} %bitcast.6), calls=%async_computation.2 | async-start | bytes 4194304
  35.3 16.1 %copy-start.30 = (s32[8,768]{1,0:T(8,128)S(1)}, s32[8,768]{1,0:T(8,128)}, u32[]{:S(2)}) copy-start(s32[8,768]{1,0:T(8,128)} %constant.28.clone) | copy-start | bytes 73732
  35.3 16.1 %slice-start.1 = ((s8[6291456]{0:T(1024)(128)(4,1)}), s8[4194304]{0:T(1024)(128)(4,1)S(1)}, s32[]{:S(2)}) async-start(s8[6291456]{0:T(1024)(128)(4,1)} %bitcast.6), calls=%async_computation.3 | async-start | bytes 8388608
  46.0 8.5 %collective-permute-start.1 = (bf16[96,1024]{1,0:T(8,128)(2,1)S(1)}, bf16[96,1024]{1,0:T(8,128)(2,1)S(1)}, u32[]{:S(2)}, u32[]{:S(2)}) collective-permute-start(bf16[96,1024]{1,0:T(8,128)(2,1)S(1)} %get-tuple-element.44.top_ref), channel_id=1, source_target_pairs={{16,0},{32,16},{48,32},{64,48},{80,64},{96,80},{112,96},{17,1},{33... | collective-permute-start | bytes 589832 | tf_op jit(solution)/shard_map/ppermute | solution.py:738
  47.3 8.2 %collective-permute-start = (bf16[96,1024]{1,0:T(8,128)(2,1)S(1)}, bf16[96,1024]{1,0:T(8,128)(2,1)S(1)}, u32[]{:S(2)}, u32[]{:S(2)}) collective-permute-start(bf16[96,1024]{1,0:T(8,128)(2,1)S(1)} %get-tuple-element.45.bottom_ref), channel_id=1, source_target_pairs={{0,16},{16,32},{32,48},{48,64},{64,80},{80,96},{96,112},{1,17},{17... | collective-permute-start | bytes 589832 | tf_op jit(solution)/shard_map/ppermute | solution.py:738
  51.4 4.2 %copy-start.22 = (bf16[288,384]{1,0:T(8,128)(2,1)S(1)}, bf16[288,384]{1,0:T(8,128)(2,1)}, u32[]{:S(2)}) copy-start(bf16[288,384]{1,0:T(8,128)(2,1)} %constant.29.clone.sel_ref) | copy-start | bytes 663556
  51.4 6.4 %copy-start.26 = (bf16[192,384]{1,0:T(8,128)(2,1)S(1)}, bf16[192,384]{1,0:T(8,128)(2,1)}, u32[]{:S(2)}) copy-start(bf16[192,384]{1,0:T(8,128)(2,1)} %constant.30.clone.base_ref) | copy-start | bytes 442372
  56.1 8.1 %collective-permute-start.2 = (bf16[144,1024]{1,0:T(8,128)(2,1)S(1)}, bf16[144,1024]{1,0:T(8,128)(2,1)S(1)}, u32[]{:S(2)}, u32[]{:S(2)}) collective-permute-start(bf16[144,1024]{1,0:T(8,128)(2,1)S(1)} %get-tuple-element.48), channel_id=1, source_target_pairs={{0,1},{1,2},{2,3},{3,4},{4,5},{5,6},{6,7},{7,8},{8,9},{9,10},{10,1... | collective-permute-start | bytes 884744 | tf_op jit(solution)/shard_map/ppermute | solution.py:732
  57.9 10.8 %collective-permute-start.3 = (bf16[144,1024]{1,0:T(8,128)(2,1)S(1)}, bf16[144,1024]{1,0:T(8,128)(2,1)S(1)}, u32[]{:S(2)}, u32[]{:S(2)}) collective-permute-start(bf16[144,1024]{1,0:T(8,128)(2,1)S(1)} %get-tuple-element.49), channel_id=1, source_target_pairs={{0,15},{1,0},{2,1},{3,2},{4,3},{5,4},{6,5},{7,6},{8,7},{9,8},{10,9... | collective-permute-start | bytes 884744 | tf_op jit(solution)/shard_map/ppermute | solution.py:732
  57.9 10.8 %copy-start.10 = (f32[192,1024]{1,0:T(8,128)S(1)}, f32[192,1024]{1,0:T(8,128)}, u32[]{:S(2)}) copy-start(f32[192,1024]{1,0:T(8,128)} %get-tuple-element.50.state_ref) | copy-start | bytes 2359300
  57.9 10.8 %copy-start.18 = (bf16[12,16,1024]{2,1,0:T(8,128)(2,1)S(1)}, bf16[12,16,1024]{2,1,0:T(8,128)(2,1)}, u32[]{:S(2)}) copy-start(bf16[12,16,1024]{2,1,0:T(8,128)(2,1)} %param.23) | copy-start | bytes 1179652
  57.9 10.8 %copy-start.27 = (bf16[1024,1024]{1,0:T(8,128)(2,1)S(1)}, bf16[1024,1024]{1,0:T(8,128)(2,1)}, u32[]{:S(2)}) copy-start(bf16[1024,1024]{1,0:T(8,128)(2,1)} %wo_hbm.4) | copy-start | bytes 6291460
  57.9 10.8 %copy-start.28 = (bf16[192,2048]{1,0:T(8,128)(2,1)S(1)}, bf16[192,2048]{1,0:T(8,128)(2,1)}, u32[]{:S(2)}) copy-start(bf16[192,2048]{1,0:T(8,128)(2,1)} %get-tuple-element.51.dh_ref) | copy-start | bytes 2359300
  57.9 10.8 %copy-start.29 = (bf16[192,384]{1,0:T(8,128)(2,1)S(1)}, bf16[192,384]{1,0:T(8,128)(2,1)}, u32[]{:S(2)}) copy-start(bf16[192,384]{1,0:T(8,128)(2,1)} %constant.31.clone.base_ref) | copy-start | bytes 442372
  68.7 30.3 %slice-start.2 = ((s8[6291456]{0:T(1024)(128)(4,1)}), s8[4194304]{0:T(1024)(128)(4,1)S(1)}, s32[]{:S(2)}) async-start(s8[6291456]{0:T(1024)(128)(4,1)} %bitcast.8), calls=%async_computation.4 | async-start | bytes 8388608
  68.7 30.3 %slice-start.3 = ((s8[6291456]{0:T(1024)(128)(4,1)}), s8[2097152]{0:T(1024)(128)(4,1)S(1)}, s32[]{:S(2)}) async-start(s8[6291456]{0:T(1024)(128)(4,1)} %bitcast.8), calls=%async_computation.5 | async-start | bytes 4194304
  95.7 9.1 %copy-start.12 = (f32[192,1024]{1,0:T(8,128)}, f32[192,1024]{1,0:T(8,128)S(1)}, u32[]{:S(2)}) copy-start(f32[192,1024]{1,0:T(8,128)S(1)} %get-tuple-element.55.after_ref) | copy-start | bytes 2359300
  95.7 9.1 %copy-start.14 = (bf16[192,2048]{1,0:T(8,128)(2,1)}, bf16[192,2048]{1,0:T(8,128)(2,1)S(1)}, u32[]{:S(2)}) copy-start(bf16[192,2048]{1,0:T(8,128)(2,1)S(1)} %get-tuple-element.56.hid_ref) | copy-start | bytes 2359300
  95.7 9.1 %collective-permute-start.4 = (bf16[144,1024]{1,0:T(8,128)(2,1)S(1)}, bf16[144,1024]{1,0:T(8,128)(2,1)S(1)}, u32[]{:S(2)}, u32[]{:S(2)}) collective-permute-start(bf16[144,1024]{1,0:T(8,128)(2,1)S(1)} %get-tuple-element.64), channel_id=1, source_target_pairs={{0,15},{1,0},{2,1},{3,2},{4,3},{5,4},{6,5},{7,6},{8,7},{9,8},{10,9... | collective-permute-start | bytes 884744 | tf_op jit(solution)/shard_map/ppermute | solution.py:732
  95.8 9.0 %collective-permute-start.5 = (bf16[144,1024]{1,0:T(8,128)(2,1)S(1)}, bf16[144,1024]{1,0:T(8,128)(2,1)S(1)}, u32[]{:S(2)}, u32[]{:S(2)}) collective-permute-start(bf16[144,1024]{1,0:T(8,128)(2,1)S(1)} %get-tuple-element.65), channel_id=1, source_target_pairs={{0,1},{1,2},{2,3},{3,4},{4,5},{5,6},{6,7},{7,8},{8,9},{9,10},{10,1... | collective-permute-start | bytes 884744 | tf_op jit(solution)/shard_map/ppermute | solution.py:732
  99.0 5.8 %copy-start.24 = (bf16[288,192]{1,0:T(8,128)(2,1)S(1)}, bf16[288,192]{1,0:T(8,128)(2,1)}, u32[]{:S(2)}) copy-start(bf16[288,192]{1,0:T(8,128)(2,1)} %constant.32.clone.sel_ref) | copy-start | bytes 331780
  99.0 11.8 %copy-start.25 = (bf16[288,192]{1,0:T(8,128)(2,1)S(1)}, bf16[288,192]{1,0:T(8,128)(2,1)}, u32[]{:S(2)}) copy-start(bf16[288,192]{1,0:T(8,128)(2,1)} %constant.33.clone.sel_ref) | copy-start | bytes 331780
  104.8 12.4 %copy-start.19 = (bf16[192,1024]{1,0:T(8,128)(2,1)S(1)}, bf16[192,1024]{1,0:T(8,128)(2,1)}, u32[]{:S(2)}) copy-start(bf16[192,1024]{1,0:T(8,128)(2,1)} %get-tuple-element.42.q_hbm.q_ref) | copy-start | bytes 1179652
  104.8 12.4 %copy-start.20 = (bf16[192,1024]{1,0:T(8,128)(2,1)S(1)}, bf16[192,1024]{1,0:T(8,128)(2,1)}, u32[]{:S(2)}) copy-start(bf16[192,1024]{1,0:T(8,128)(2,1)} %get-tuple-element.72.mix_ref) | copy-start | bytes 1179652
  104.8 12.4 %copy-start.21 = (bf16[192,1024]{1,0:T(8,128)(2,1)S(1)}, bf16[192,1024]{1,0:T(8,128)(2,1)}, u32[]{:S(2)}) copy-start(bf16[192,1024]{1,0:T(8,128)(2,1)} %get-tuple-element.73.ow_ref) | copy-start | bytes 1179652
  105.2 12.0 %collective-permute-start.6 = (bf16[96,1024]{1,0:T(8,128)(2,1)S(1)}, bf16[96,1024]{1,0:T(8,128)(2,1)S(1)}, u32[]{:S(2)}, u32[]{:S(2)}) collective-permute-start(bf16[96,1024]{1,0:T(8,128)(2,1)S(1)} %get-tuple-element.68), channel_id=1, source_target_pairs={{0,16},{16,32},{32,48},{48,64},{64,80},{80,96},{96,112},{1,17},{17... | collective-permute-start | bytes 589832 | tf_op jit(solution)/shard_map/ppermute | solution.py:738
  109.3 7.9 %collective-permute-start.7 = (bf16[96,1024]{1,0:T(8,128)(2,1)S(1)}, bf16[96,1024]{1,0:T(8,128)(2,1)S(1)}, u32[]{:S(2)}, u32[]{:S(2)}) collective-permute-start(bf16[96,1024]{1,0:T(8,128)(2,1)S(1)} %get-tuple-element.67._), channel_id=1, source_target_pairs={{16,0},{32,16},{48,32},{64,48},{80,64},{96,80},{112,96},{17,1},{33... | collective-permute-start | bytes 589832 | tf_op jit(solution)/shard_map/ppermute | solution.py:738
  110.9 6.4 %copy-start = (bf16[1024,2048]{1,0:T(8,128)(2,1)S(1)}, bf16[1024,2048]{1,0:T(8,128)(2,1)}, u32[]{:S(2)}) copy-start(bf16[1024,2048]{1,0:T(8,128)(2,1)} %wp_hbm.7) | copy-start | bytes 12582916
  110.9 6.4 %copy-start.4 = (bf16[8,384,512]{2,1,0:T(8,128)(2,1)S(1)}, bf16[8,384,512]{2,1,0:T(8,128)(2,1)}, u32[]{:S(2)}) copy-start(bf16[8,384,512]{2,1,0:T(8,128)(2,1)} %get-tuple-element.71.wts_ref) | copy-start | bytes 9437188
  110.9 6.4 %copy-start.5 = (bf16[1024,1024]{1,0:T(8,128)(2,1)S(1)}, bf16[1024,1024]{1,0:T(8,128)(2,1)}, u32[]{:S(2)}) copy-start(bf16[1024,1024]{1,0:T(8,128)(2,1)} %wo_hbm.5) | copy-start | bytes 6291460
  110.9 6.4 %copy-start.6 = (bf16[512,2048]{1,0:T(8,128)(2,1)S(1)}, bf16[512,2048]{1,0:T(8,128)(2,1)}, u32[]{:S(2)}) copy-start(bf16[512,2048]{1,0:T(8,128)(2,1)} %get-tuple-element.70.pairs_ref) | copy-start | bytes 6291460
  110.9 6.4 %copy-start.9 = (bf16[192,2048]{1,0:T(8,128)(2,1)S(1)}, bf16[192,2048]{1,0:T(8,128)(2,1)}, u32[]{:S(2)}) copy-start(bf16[192,2048]{1,0:T(8,128)(2,1)} %get-tuple-element.43.own_hbm.own_ref) | copy-start | bytes 2359300
  110.9 6.4 %copy-start.11 = (f32[192,1024]{1,0:T(8,128)S(1)}, f32[192,1024]{1,0:T(8,128)}, u32[]{:S(2)}) copy-start(f32[192,1024]{1,0:T(8,128)} %get-tuple-element.50.state_ref) | copy-start | bytes 2359300
  117.3 23.1 %copy-start.15 = (bf16[192,2048]{1,0:T(8,128)(2,1)S(1)}, bf16[192,2048]{1,0:T(8,128)(2,1)}, u32[]{:S(2)}) copy-start(bf16[192,2048]{1,0:T(8,128)(2,1)} %copy-done.14) | copy-start | bytes 2359300
  127.6 12.8 %copy-start.8 = (bf16[192,1024]{1,0:T(8,128)(2,1)S(1)}, bf16[192,1024]{1,0:T(8,128)(2,1)}, u32[]{:S(2)}) copy-start(bf16[192,1024]{1,0:T(8,128)(2,1)} %get-tuple-element.74._.dq_ref) | copy-start | bytes 1179652
  127.6 12.8 %copy-start.13 = (f32[192,1024]{1,0:T(8,128)S(1)}, f32[192,1024]{1,0:T(8,128)}, u32[]{:S(2)}) copy-start(f32[192,1024]{1,0:T(8,128)} %copy-done.12) | copy-start | bytes 2359300
  127.6 17.1 %copy-start.7 = (bf16[12,16,1024]{2,1,0:T(8,128)(2,1)S(1)}, bf16[12,16,1024]{2,1,0:T(8,128)(2,1)}, u32[]{:S(2)}) copy-start(bf16[12,16,1024]{2,1,0:T(8,128)(2,1)} %param.19) | copy-start | bytes 1179652
  127.6 31.7 %all-to-all-start.1 = ((bf16[128,4,1024]{2,1,0:T(4,128)(2,1)}), bf16[128,4,1024]{2,1,0:T(4,128)(2,1)S(1)}, u32[]{:S(2)}, u32[]{:S(2)}) async-start(bf16[128,4,1024]{2,1,0:T(4,128)(2,1)} %get-tuple-element.78), calls=%async_computation.1 | async-start | bytes 2097152 | tf_op jit(solution)/shard_map/all_to_all | solution.py:915
  140.4 2.2 %copy-start.2 = (bf16[2048,1024]{1,0:T(8,128)(2,1)S(1)}, bf16[2048,1024]{1,0:T(8,128)(2,1)}, u32[]{:S(2)}) copy-start(bf16[2048,1024]{1,0:T(8,128)(2,1)} %wd_hbm.3) | copy-start | bytes 12582916
  142.6 2.2 %copy-start.1 = (bf16[1024,2048]{1,0:T(8,128)(2,1)S(1)}, bf16[1024,2048]{1,0:T(8,128)(2,1)}, u32[]{:S(2)}) copy-start(bf16[1024,2048]{1,0:T(8,128)(2,1)} %wp_hbm.7) | copy-start | bytes 12582916
  142.6 3.0 %copy-start.3 = (bf16[1024,1024]{1,0:T(8,128)(2,1)S(1)}, bf16[1024,1024]{1,0:T(8,128)(2,1)}, u32[]{:S(2)}) copy-start(bf16[1024,1024]{1,0:T(8,128)(2,1)} %wq_hbm.3) | copy-start | bytes 6291460
  145.6 1.1 copy-start.16
  146.7 1.1 copy-start.17

commit v6 on v5

--- a/solution.py
+++ b/solution.py
@@ -373,18 +373,16 @@
             heads.append((h, keys, vals))
             scores[k] = dot(stacked(q_ref[:, keys]), kv[:, keys], NT)
         for k, (h, keys, vals) in enumerate(heads):
-            for i in range(0, cells, SOFT):
-                peaks, sums = [], []
-                for side in range(2):
-                    rows = pl.ds(side * cells + i, SOFT)
-                    v = scores[k, rows, :] + bias[pl.ds(i, SOFT), :]
-                    peak = jnp.max(v, -1, keepdims=True)
-                    v = jnp.exp(v - peak)
-                    wts[h, rows, :] = v.astype(BF)
-                    peaks.append(peak)
-                    sums.append(jnp.sum(v, -1, keepdims=True))
-                peak_ref[pl.ds(i, SOFT), keys] = spread(*peaks)
-                sum_ref[pl.ds(i, SOFT), keys] = spread(*sums)
+            for start in range(0, 2 * cells, SOFT):
+                rows = pl.ds(start, SOFT)
+                v = scores[k, rows, :] + bias[pl.ds(start % cells, SOFT), :]
+                peak = jnp.max(v, -1, keepdims=True)
+                v = jnp.exp(v - peak)
+                wts[h, rows, :] = v.astype(BF)
+                peak_ref[h, rows, :] = jnp.broadcast_to(peak, (SOFT, PAIR))
+                sum_ref[h, rows, :] = jnp.broadcast_to(
+                    jnp.sum(v, -1, keepdims=True), (SOFT, PAIR)
+                )
         for k, (h, keys, vals) in enumerate(heads):
             mix_ref[:, keys] = merged(dot(wts[h], kv[:, vals]))
 
@@ -430,19 +428,21 @@
     keys_all = kv.shape[0]
     side = west_ref.shape[0]
     ends = 2 * side
-    copies = fetch(
-        [wn_hbm.at[:, pl.ds(model, 2 * model)], wo_hbm, wu_hbm], [wkv, wo, wu], sems
-    )
+    copies = fetch([wn_hbm.at[:, pl.ds(model, 2 * model)]], [wkv], sems.at[pl.ds(0, 1)])
     x[pl.ds(0, side), :] = west_ref[...]
     x[pl.ds(side, side), :] = east_ref[...]
     kv[pl.ds(ends, keys_all - ends), :] = jnp.zeros((keys_all - ends, 2 * model), BF)
     bias[...] = base_ref[...].astype(F32) + inside_ref[0:1, :]
     copies[0].wait()
+    copies += fetch([wo_hbm, wu_hbm], [wo, wu], sems.at[pl.ds(1, 2)])
 
     def project(j):
         kv[pl.ds(0, ends), pl.ds(j, TILE)] = dot(x[...], wkv[:, pl.ds(j, TILE)]).astype(BF)
 
     tiles_of(2 * model, project)
+
+    def widened(values):
+        return jnp.concatenate([values] * (keys_all // PAIR), axis=1)
 
     @pl.loop(0, model // (PAIR * GROUP))
     def _(g):
@@ -456,19 +456,17 @@
         for k, (h, keys, vals) in enumerate(heads):
             for i in range(0, cells, SOFT):
                 here = pl.ds(i, SOFT)
-                peaks, sums = peak_ref[here, keys], sum_ref[here, keys]
                 shares = []
                 for s in range(2):
                     rows = pl.ds(s * cells + i, SOFT)
-                    before = peaks[:, s * HALF : s * HALF + 1]
+                    before = peak_ref[h, rows, :]
                     v = scores[k, rows, :] + bias[here, :]
                     peak = jnp.maximum(jnp.max(v, -1, keepdims=True), before)
-                    v = jnp.exp(v - peak)
+                    v = jnp.exp(v - widened(peak))
                     part = jnp.exp(before - peak)
-                    total = jnp.sum(v, -1, keepdims=True)
-                    total = total + part * sums[:, s * HALF : s * HALF + 1]
+                    total = jnp.sum(v, -1, keepdims=True) + part * sum_ref[h, rows, :]
                     inverse = 1.0 / total
-                    wts[h, rows, :] = (v * inverse).astype(BF)
+                    wts[h, rows, :] = (v * widened(inverse)).astype(BF)
                     shares.append(part * inverse)
                 share[here, keys] = spread(*shares)
         for k, (h, keys, vals) in enumerate(heads):
@@ -846,7 +844,8 @@
         (north, south, q_n, kv_own, jnp.asarray(base[:, : 2 * cells]), inside[:, : 2 * cells],
          w_near_proj), "vvvvvva",
         [((2 * rim, 2 * model), BF), ((pairs_n, 2 * cells, 2 * cells), BF, "h"),
-         ((cells, model), F32), ((cells, model), F32), ((cells, model), F32)],
+         ((cells, model), F32), ((pairs_n, 2 * cells, PAIR), F32),
+         ((pairs_n, 2 * cells, PAIR), F32)],
         [vm((2 * rim, model), BF), vm((model, 2 * model), BF), vm((2 * cells, 2 * model), BF),
          vm((cells, 2 * cells), F32), vm((GROUP, 2 * cells, 2 * cells), F32),
          vm((pairs_n, 2 * cells, 2 * cells), BF), dma((1,)), dma((1,))],

time: 162 us -> 153 us (0.944)
  Pallas kernels: 87.3 us -> 78 us
    pallas_call x14, Pallas kernels: 87.3 us -> 78 us  [call(): pl.pallas_call(body, name=name, out_shape=shapes[0] if single else shapes...]
    unnamed x70 -> x60, local copies, waits for them, and re-layouts: 5.57 us -> 5.54 us
  transfers between devices with their start and end apart: 10 -> 10, of which waited for: 5 -> 5; matrix products, arithmetic and copies ran while one was open for 0% -> 0% of each run, Pallas kernels for 21% -> 22%
where the time goes in v6:
time: 153 us
  Pallas kernels  78 us (51%)
  starting transfers between devices  40.4 us (26%)
  waiting for transfers between devices  27.5 us (18%)
  local copies, waits for them, and re-layouts  5.54 us (4%)
    pallas_call x14, Pallas kernels, call(): pl.pallas_call(body, name=name, out_shape=shapes[0] if single else shapes...  78 us
    all_to_all x1, waiting for transfers between devices, per_device(): arrived = lax.all_to_all(payload, ('lat', 'lon'), 0, 0, tiled=True)  13.5 us
    all_to_all x1, starting transfers between devices, per_device(): returned = lax.all_to_all(slot_grads, ('lat', 'lon'), 0, 0, tiled=True)  12.8 us
    all_to_all x1, starting transfers between devices, per_device(): arrived = lax.all_to_all(payload, ('lat', 'lon'), 0, 0, tiled=True)  11.5 us
    ppermute x4, starting transfers between devices, line(): return lax.ppermute(value, 'lat', pairs)  10.9 us
    all_to_all x1, waiting for transfers between devices, per_device(): returned = lax.all_to_all(slot_grads, ('lat', 'lon'), 0, 0, tiled=True)  7.75 us
    unnamed x60, local copies, waits for them, and re-layouts  5.54 us
    ppermute x4, starting transfers between devices, ring(): lax.ppermute(value, 'lon', [(i, (i + by) % size) for i in range(size)])  5.12 us
  transfers between devices with their start and end apart: 10, of which 5 were waited for; matrix products, arithmetic and copies ran while one was open for 0% of the time, Pallas kernels for 22%

profile of v6, /device:TPU:1, one launch (start us, length us, event | category | flops | bytes accessed | tf_op | source)
XLA Modules:
  0.0 152.7 jit_solution(8167853743537319400)
XLA Ops:
  0.6 0.0 copy-start.18
  0.6 2.8 %place.1 = (bf16[128,4,1152]{2,1,0:T(4,128)(2,1)}, bf16[512,256]{1,0:T(8,128)(2,1)}) custom-call(s32[1,256]{1,0:T(1,128)} %bitcast.17, s32[1,256]{1,0:T(1,128)} %bitcast.18, bf16[256,1024]{1,0:T(8,128)(2,1)} %obs_hbm.1), custom_call_target="tpu_custom_call" | custom-call | flops 268435456 | bytes 1968128 | tf_op jit(solution)/shard_map/place/pallas_call | solution.py:120
  3.4 11.5 %all-to-all-start = ((bf16[128,4,1152]{2,1,0:T(4,128)(2,1)}), bf16[128,4,1152]{2,1,0:T(4,128)(2,1)S(1)}, u32[]{:S(2)}, u32[]{:S(2)}) async-start(bf16[128,4,1152]{2,1,0:T(4,128)(2,1)} %get-tuple-element.41), calls=%async_computation | async-start | bytes 2359296 | tf_op jit(solution)/shard_map/all_to_all | solution.py:802
  14.9 0.0 copy-done.18
  14.9 6.8 %grid_proj.1 = (bf16[192,1024]{1,0:T(8,128)(2,1)}, bf16[192,2048]{1,0:T(8,128)(2,1)}, bf16[192,2048]{1,0:T(8,128)(2,1)}) custom-call(bf16[192,1024]{1,0:T(8,128)(2,1)} %bitcast.10, bf16[192,1024]{1,0:T(8,128)(2,1)} %bitcast.13, f32[3,1024]{1,0:T(4,128)S(1)} %copy-done.18, bf16[1024,1024]{1,0:T(8,128)(2,1)} %wq_hbm.3, bf16[1024,2048]{1,0:T(8,128)(2,1)} %wp_hbm.7, ...), custom_call_target="tpu_custom_call" | custom-call | flops 2013265920 | bytes 13250560 | tf_op jit(solution)/shard_map/grid_proj/pallas_call | solution.py:120
  21.8 13.5 %all-to-all-done.arr_ref = bf16[128,4,1152]{2,1,0:T(4,128)(2,1)S(1)} async-done(((bf16[128,4,1152]{2,1,0:T(4,128)(2,1)}), bf16[128,4,1152]{2,1,0:T(4,128)(2,1)S(1)}, u32[]{:S(2)}, u32[]{:S(2)}) %all-to-all-start) | async-done | bytes 1179680 | tf_op jit(solution)/shard_map/all_to_all | solution.py:802
  35.3 10.7 %cross.1 = (f32[192,1024]{1,0:T(8,128)}, bf16[96,1024]{1,0:T(8,128)(2,1)S(1)}, bf16[96,1024]{1,0:T(8,128)(2,1)S(1)}, bf16[512,2048]{1,0:T(8,128)(2,1)}, bf16[8,3...) custom-call(bf16[128,4,1152]{2,1,0:T(4,128)(2,1)S(1)} %all-to-all-done.arr_ref, ...), custom_call_target="tpu_custom_call" | custom-call | flops 4294967296 | bytes 16265216 | tf_op jit(solution)/shard_map/cross/pallas_call | solution.py:120
  46.0 1.3 collective-permute-start.1
  47.3 4.0 %collective-permute-start = (bf16[96,1024]{1,0:T(8,128)(2,1)S(1)}, bf16[96,1024]{1,0:T(8,128)(2,1)S(1)}, u32[]{:S(2)}, u32[]{:S(2)}) collective-permute-start(bf16[96,1024]{1,0:T(8,128)(2,1)S(1)} %get-tuple-element.45.bottom_ref), channel_id=1, source_target_pairs={{0,16},{16,32},{32,48},{48,64},{64,80},{80,96},{96,112},{1,17},{17... | collective-permute-start | bytes 589832 | tf_op jit(solution)/shard_map/ppermute | solution.py:736
  51.3 0.0 copy-done.25
  51.3 0.0 slice-done
  51.3 0.0 slice-done.1
  51.4 0.0 copy-start.17
  51.4 0.0 copy-start.21
  51.4 2.7 %near_own.1 = (bf16[192,1024]{1,0:T(8,128)(2,1)S(1)}, bf16[192,2048]{1,0:T(8,128)(2,1)S(1)}) custom-call(bf16[96,1024]{1,0:T(8,128)(2,1)S(1)} %get-tuple-element.44.top_ref, bf16[96,1024]{1,0:T(8,128)(2,1)S(1)} %get-tuple-element.45.bottom_ref, bf16[1024,3072]{1,0:T(8,128)(2,1)S(1)} %bitcast.7), custom_call_target="tpu_custom_call" | custom-call | flops 1207959552 | bytes 7864320 | tf_op jit(solution)/shard_map/near_own/pallas_call | solution.py:120
  54.1 0.5 collective-permute-done.1.south_ref
  54.5 1.0 collective-permute-done.north_ref
  55.5 0.0 copy-done.17
  55.5 0.5 rim.1
  56.0 1.8 %collective-permute-start.2 = (bf16[144,1024]{1,0:T(8,128)(2,1)S(1)}, bf16[144,1024]{1,0:T(8,128)(2,1)S(1)}, u32[]{:S(2)}, u32[]{:S(2)}) collective-permute-start(bf16[144,1024]{1,0:T(8,128)(2,1)S(1)} %get-tuple-element.48), channel_id=1, source_target_pairs={{0,1},{1,2},{2,3},{3,4},{4,5},{5,6},{6,7},{7,8},{8,9},{9,10},{10,1... | collective-permute-start | bytes 884744 | tf_op jit(solution)/shard_map/ppermute | solution.py:730
  57.8 0.0 collective-permute-start.3
  57.8 0.0 copy-done.21
  57.8 0.0 copy-start.10
  57.8 0.0 copy-start.13
  57.9 0.0 copy-start.22
  57.9 0.0 copy-start.24
  57.9 6.0 %inner.1 = (bf16[192,2048]{1,0:T(8,128)(2,1)S(1)}, bf16[8,384,384]{2,1,0:T(8,128)(2,1)}, f32[192,1024]{1,0:T(8,128)S(1)}, f32[8,384,128]{2,1,0:T(8,128)S(1)}, f32[8,384,128]{2,1,0:T(8,128)S(1)}) custom-call(bf16[96,1024]{1,0:T(8,128)(2,1)S(1)} %collective-permute-done.north_ref, bf16[96,1024]{1,0:T(8,128)(2,1)S(1)} %collective-permute-done.1.south_ref, ...), custom_call_target="tpu_custom_call" | custom-call | flops 1610612736 | bytes 15101952 | tf_op jit(solution)/shard_map/inner/pallas_call | solution.py:120
  63.9 0.0 collective-permute-done.2.west_ref
  63.9 4.8 %collective-permute-done.3.east_ref = bf16[144,1024]{1,0:T(8,128)(2,1)S(1)} collective-permute-done((bf16[144,1024]{1,0:T(8,128)(2,1)S(1)}, bf16[144,1024]{1,0:T(8,128)(2,1)S(1)}, u32[]{:S(2)}, u32[]{:S(2)}) %collective-permute-start.3) | collective-permute-done | bytes 294944 | tf_op jit(solution)/shard_map/ppermute | solution.py:730
  68.6 0.0 copy-done.10
  68.7 0.0 slice-start.3
  68.7 18.1 %near.1 = (f32[192,1024]{1,0:T(8,128)S(1)}, bf16[192,2048]{1,0:T(8,128)(2,1)S(1)}, bf16[144,1024]{1,0:T(8,128)(2,1)S(1)}, bf16[144,1024]{1,0:T(8,128)(2,1)S(1)},...) custom-call(bf16[192,1024]{1,0:T(8,128)(2,1)S(1)} %get-tuple-element, ...), custom_call_target="tpu_custom_call" | custom-call | flops 20000000000 | bytes 24158208 | tf_op jit(solution)/shard_map/near/pallas_call | solution.py:120
  86.7 0.1 collective-permute-start.4
  86.8 3.2 %collective-permute-start.5 = (bf16[144,1024]{1,0:T(8,128)(2,1)S(1)}, bf16[144,1024]{1,0:T(8,128)(2,1)S(1)}, u32[]{:S(2)}, u32[]{:S(2)}) collective-permute-start(bf16[144,1024]{1,0:T(8,128)(2,1)S(1)} %get-tuple-element.65), channel_id=1, source_target_pairs={{0,1},{1,2},{2,3},{3,4},{4,5},{5,6},{6,7},{7,8},{8,9},{9,10},{10,1... | collective-permute-start | bytes 884744 | tf_op jit(solution)/shard_map/ppermute | solution.py:730
  90.1 0.0 slice-done.2
  90.1 0.0 copy-start.20
  90.1 5.7 %middle_back.1 = (f32[192,1024]{1,0:T(8,128)S(1)}, bf16[64,2048]{1,0:T(8,128)(2,1)S(1)}, f32[192,1024]{1,0:T(8,128)S(1)}) custom-call(bf16[192,1024]{1,0:T(8,128)(2,1)S(1)} %get-tuple-element.46.q_ref, bf16[192,2048]{1,0:T(8,128)(2,1)S(1)} %get-tuple-element.47._.kvo_ref, bf16[192,2048]{1,0:T(8,128)(2,1)S(1)} %get-tuple-element.59.kvr_ref, ...), custom_call_target="tpu_custom_call" | custom-call | flops 1610612736 | bytes 14024704 | tf_op jit(solution)/shard_map/middle_back/pallas_call | solution.py:120
  95.8 0.0 collective-permute-done.4.from_east_ref
  95.8 0.0 collective-permute-done.5.from_west_ref
  95.8 0.0 copy-start.16
  95.8 0.4 fold.1
  96.2 4.1 %collective-permute-start.6 = (bf16[96,1024]{1,0:T(8,128)(2,1)S(1)}, bf16[96,1024]{1,0:T(8,128)(2,1)S(1)}, u32[]{:S(2)}, u32[]{:S(2)}) collective-permute-start(bf16[96,1024]{1,0:T(8,128)(2,1)S(1)} %get-tuple-element.68), channel_id=1, source_target_pairs={{0,16},{16,32},{32,48},{48,64},{64,80},{80,96},{96,112},{1,17},{17... | collective-permute-start | bytes 589832 | tf_op jit(solution)/shard_map/ppermute | solution.py:736
  100.4 1.5 collective-permute-start.7
  101.9 0.0 copy-start
  101.9 0.0 copy-start.5
  101.9 0.0 copy-start.14
  102.0 0.0 copy-start.15
  102.0 6.3 %own_back.1.dn_ref = f32[192,1024]{1,0:T(8,128)S(1)} custom-call(bf16[192,1024]{1,0:T(8,128)(2,1)S(1)} %get-tuple-element.46.q_ref, bf16[192,2048]{1,0:T(8,128)(2,1)S(1)} %get-tuple-element.47._.kvo_ref, bf16[192,1024]{1,0:T(8,128)(2,1)S(1)} %get-tuple-element.57.mix, bf16[192,1024]{1,0:T(8,128)(2,1)S(1)} %get-tuple-element.58.dmix, ...), custom_call_target="tpu_custom_call" | custom-call | flops 1610612736 | bytes 13348864 | tf_op jit(solution)/shard_map/own_back/pallas_call | solution.py:120
  108.3 0.0 collective-permute-done.6.north_ref
  108.3 0.0 collective-permute-done.7.south_ref
  108.4 10.2 %cross_back.1 = (f32[192,1024]{1,0:T(8,128)}, bf16[128,4,1024]{2,1,0:T(4,128)(2,1)}, bf16[192,1024]{1,0:T(8,128)(2,1)}, bf16[192,2048]{1,0:T(8,128)(2,1)}) custom-call(f32[192,1024]{1,0:T(8,128)S(1)} %own_back.1.dn_ref, bf16[96,1024]{1,0:T(8,128)(2,1)S(1)} %collective-permute-done.6.north_ref, bf16[96,1024]{1,0:T(8,128)(2,1)S(1)} %collective-permute-done.7.south_ref, ...), custom_call_target="tpu_custom_call" | custom-call | flops 4294967296 | bytes 19279872 | tf_op jit(solution)/shard_map/cross_back/pallas_call | solution.py:120
  118.6 0.0 copy-start.8
  118.6 0.0 copy-start.7
  118.6 12.8 %all-to-all-start.1 = ((bf16[128,4,1024]{2,1,0:T(4,128)(2,1)}), bf16[128,4,1024]{2,1,0:T(4,128)(2,1)S(1)}, u32[]{:S(2)}, u32[]{:S(2)}) async-start(bf16[128,4,1024]{2,1,0:T(4,128)(2,1)} %get-tuple-element.78), calls=%async_computation.1 | async-start | bytes 2097152 | tf_op jit(solution)/shard_map/all_to_all | solution.py:914
  131.4 0.0 copy-start.2
  131.5 2.2 %copy-done.2 = bf16[2048,1024]{1,0:T(8,128)(2,1)S(1)} copy-done((bf16[2048,1024]{1,0:T(8,128)(2,1)S(1)}, bf16[2048,1024]{1,0:T(8,128)(2,1)}, u32[]{:S(2)}) %copy-start.2) | copy-done | bytes 4194328
  133.6 2.0 %encode.1 = bf16[192,1024]{1,0:T(8,128)(2,1)} custom-call(f32[192,1024]{1,0:T(8,128)S(1)} %get-tuple-element.55.after_ref, bf16[192,2048]{1,0:T(8,128)(2,1)S(1)} %get-tuple-element.56.hid_ref, bf16[2048,1024]{1,0:T(8,128)(2,1)S(1)} %copy-done.2, bf16[192,1024]{1,0:T(8,128)(2,1)S(1)} %copy-done.8), custom_call_target="tpu_custom_call" | custom-call | flops 805306368 | bytes 6553600 | tf_op jit(solution)/shard_map/encode/pallas_call | solution.py:120
  135.7 0.1 copy-done.1
  135.8 0.8 copy-done.3
  136.6 1.1 copy-done.11
  137.8 1.1 copy-done.12
  138.9 3.7 %grid_back.1 = bf16[192,1024]{1,0:T(8,128)(2,1)} custom-call(bf16[192,1024]{1,0:T(8,128)(2,1)S(1)} %bitcast.12, f32[192,1024]{1,0:T(8,128)S(1)} %copy-done.11, f32[3,1024]{1,0:T(4,128)S(1)} %copy-done.18, bf16[192,1024]{1,0:T(8,128)(2,1)S(1)} %copy-done.8, bf16[192,2048]{1,0:T(8,128)(2,1)S(1)} %copy-done.12, bf16[1024,1024]{1,0:T(8,128)(2,1)S(1)} %copy-done.3, ...), custom_call_target="tpu_custom_call" | custom-call | flops 1207959552 | bytes 9056256 | tf_op jit(solution)/shard_map/grid_back/pallas_call | solution.py:120
  142.6 7.7 %all-to-all-done.1.ret_ref = bf16[128,4,1024]{2,1,0:T(4,128)(2,1)S(1)} async-done(((bf16[128,4,1024]{2,1,0:T(4,128)(2,1)}), bf16[128,4,1024]{2,1,0:T(4,128)(2,1)S(1)}, u32[]{:S(2)}, u32[]{:S(2)}) %all-to-all-start.1) | async-done | bytes 1048608 | tf_op jit(solution)/shard_map/all_to_all | solution.py:914
  150.4 2.2 %gather.1 = bf16[256,1024]{1,0:T(8,128)(2,1)} custom-call(bf16[512,256]{1,0:T(8,128)(2,1)} %get-tuple-element.77.place_hbm, bf16[128,4,1024]{2,1,0:T(4,128)(2,1)S(1)} %all-to-all-done.1.ret_ref), custom_call_target="tpu_custom_call" | custom-call | flops 268435456 | bytes 1835008 | tf_op jit(solution)/shard_map/gather/pallas_call | solution.py:120
  (34 shorter events, 0.1 us)
Async XLA Ops:
  0.6 14.3 %copy-start.18 = (f32[3,1024]{1,0:T(4,128)S(1)}, f32[3,1024]{1,0:T(4,128)}, u32[]{:S(2)}) copy-start(f32[3,1024]{1,0:T(4,128)} %gain_ref.9) | copy-start | bytes 36868
  3.4 31.8 %all-to-all-start = ((bf16[128,4,1152]{2,1,0:T(4,128)(2,1)}), bf16[128,4,1152]{2,1,0:T(4,128)(2,1)S(1)}, u32[]{:S(2)}, u32[]{:S(2)}) async-start(bf16[128,4,1152]{2,1,0:T(4,128)(2,1)} %get-tuple-element.41), calls=%async_computation | async-start | bytes 2359296 | tf_op jit(solution)/shard_map/all_to_all | solution.py:802
  35.2 16.1 %slice-start = ((s8[6291456]{0:T(1024)(128)(4,1)}), s8[4194304]{0:T(1024)(128)(4,1)S(1)}, s32[]{:S(2)}) async-start(s8[6291456]{0:T(1024)(128)(4,1)} %bitcast.6), calls=%async_computation.2 | async-start | bytes 8388608
  35.2 16.1 %copy-start.25 = (s32[8,768]{1,0:T(8,128)S(1)}, s32[8,768]{1,0:T(8,128)}, u32[]{:S(2)}) copy-start(s32[8,768]{1,0:T(8,128)} %constant.28.clone) | copy-start | bytes 73732
  35.2 16.1 %slice-start.1 = ((s8[6291456]{0:T(1024)(128)(4,1)}), s8[2097152]{0:T(1024)(128)(4,1)S(1)}, s32[]{:S(2)}) async-start(s8[6291456]{0:T(1024)(128)(4,1)} %bitcast.6), calls=%async_computation.3 | async-start | bytes 4194304
  46.0 8.5 %collective-permute-start.1 = (bf16[96,1024]{1,0:T(8,128)(2,1)S(1)}, bf16[96,1024]{1,0:T(8,128)(2,1)S(1)}, u32[]{:S(2)}, u32[]{:S(2)}) collective-permute-start(bf16[96,1024]{1,0:T(8,128)(2,1)S(1)} %get-tuple-element.44.top_ref), channel_id=1, source_target_pairs={{16,0},{32,16},{48,32},{64,48},{80,64},{96,80},{112,96},{17,1},{33... | collective-permute-start | bytes 589832 | tf_op jit(solution)/shard_map/ppermute | solution.py:736
  47.3 8.2 %collective-permute-start = (bf16[96,1024]{1,0:T(8,128)(2,1)S(1)}, bf16[96,1024]{1,0:T(8,128)(2,1)S(1)}, u32[]{:S(2)}, u32[]{:S(2)}) collective-permute-start(bf16[96,1024]{1,0:T(8,128)(2,1)S(1)} %get-tuple-element.45.bottom_ref), channel_id=1, source_target_pairs={{0,16},{16,32},{32,48},{48,64},{64,80},{80,96},{96,112},{1,17},{17... | collective-permute-start | bytes 589832 | tf_op jit(solution)/shard_map/ppermute | solution.py:736
  51.4 4.2 %copy-start.17 = (bf16[288,384]{1,0:T(8,128)(2,1)S(1)}, bf16[288,384]{1,0:T(8,128)(2,1)}, u32[]{:S(2)}) copy-start(bf16[288,384]{1,0:T(8,128)(2,1)} %constant.29.clone.sel_ref) | copy-start | bytes 663556
  51.4 6.5 %copy-start.21 = (bf16[192,384]{1,0:T(8,128)(2,1)S(1)}, bf16[192,384]{1,0:T(8,128)(2,1)}, u32[]{:S(2)}) copy-start(bf16[192,384]{1,0:T(8,128)(2,1)} %constant.30.clone.base_ref) | copy-start | bytes 442372
  56.0 7.9 %collective-permute-start.2 = (bf16[144,1024]{1,0:T(8,128)(2,1)S(1)}, bf16[144,1024]{1,0:T(8,128)(2,1)S(1)}, u32[]{:S(2)}, u32[]{:S(2)}) collective-permute-start(bf16[144,1024]{1,0:T(8,128)(2,1)S(1)} %get-tuple-element.48), channel_id=1, source_target_pairs={{0,1},{1,2},{2,3},{3,4},{4,5},{5,6},{6,7},{7,8},{8,9},{9,10},{10,1... | collective-permute-start | bytes 884744 | tf_op jit(solution)/shard_map/ppermute | solution.py:730
  57.8 10.8 %collective-permute-start.3 = (bf16[144,1024]{1,0:T(8,128)(2,1)S(1)}, bf16[144,1024]{1,0:T(8,128)(2,1)S(1)}, u32[]{:S(2)}, u32[]{:S(2)}) collective-permute-start(bf16[144,1024]{1,0:T(8,128)(2,1)S(1)} %get-tuple-element.49), channel_id=1, source_target_pairs={{0,15},{1,0},{2,1},{3,2},{4,3},{5,4},{6,5},{7,6},{8,7},{9,8},{10,9... | collective-permute-start | bytes 884744 | tf_op jit(solution)/shard_map/ppermute | solution.py:730
  57.8 10.8 %copy-start.10 = (f32[192,1024]{1,0:T(8,128)S(1)}, f32[192,1024]{1,0:T(8,128)}, u32[]{:S(2)}) copy-start(f32[192,1024]{1,0:T(8,128)} %get-tuple-element.50.state_ref) | copy-start | bytes 2359300
  57.8 10.8 %copy-start.13 = (bf16[12,16,1024]{2,1,0:T(8,128)(2,1)S(1)}, bf16[12,16,1024]{2,1,0:T(8,128)(2,1)}, u32[]{:S(2)}) copy-start(bf16[12,16,1024]{2,1,0:T(8,128)(2,1)} %param.23) | copy-start | bytes 1179652
  57.9 10.8 %copy-start.22 = (bf16[1024,1024]{1,0:T(8,128)(2,1)S(1)}, bf16[1024,1024]{1,0:T(8,128)(2,1)}, u32[]{:S(2)}) copy-start(bf16[1024,1024]{1,0:T(8,128)(2,1)} %wo_hbm.4) | copy-start | bytes 6291460
  57.9 10.8 %copy-start.23 = (bf16[192,2048]{1,0:T(8,128)(2,1)S(1)}, bf16[192,2048]{1,0:T(8,128)(2,1)}, u32[]{:S(2)}) copy-start(bf16[192,2048]{1,0:T(8,128)(2,1)} %get-tuple-element.51.dh_ref) | copy-start | bytes 2359300
  57.9 10.8 %copy-start.24 = (bf16[192,384]{1,0:T(8,128)(2,1)S(1)}, bf16[192,384]{1,0:T(8,128)(2,1)}, u32[]{:S(2)}) copy-start(bf16[192,384]{1,0:T(8,128)(2,1)} %constant.31.clone.base_ref) | copy-start | bytes 442372
  68.6 21.4 %slice-start.2 = ((s8[6291456]{0:T(1024)(128)(4,1)}), s8[4194304]{0:T(1024)(128)(4,1)S(1)}, s32[]{:S(2)}) async-start(s8[6291456]{0:T(1024)(128)(4,1)} %bitcast.8), calls=%async_computation.4 | async-start | bytes 8388608
  68.7 21.4 %slice-start.3 = ((s8[6291456]{0:T(1024)(128)(4,1)}), s8[2097152]{0:T(1024)(128)(4,1)S(1)}, s32[]{:S(2)}) async-start(s8[6291456]{0:T(1024)(128)(4,1)} %bitcast.8), calls=%async_computation.5 | async-start | bytes 4194304
  86.7 9.1 %collective-permute-start.4 = (bf16[144,1024]{1,0:T(8,128)(2,1)S(1)}, bf16[144,1024]{1,0:T(8,128)(2,1)S(1)}, u32[]{:S(2)}, u32[]{:S(2)}) collective-permute-start(bf16[144,1024]{1,0:T(8,128)(2,1)S(1)} %get-tuple-element.64), channel_id=1, source_target_pairs={{0,15},{1,0},{2,1},{3,2},{4,3},{5,4},{6,5},{7,6},{8,7},{9,8},{10,9... | collective-permute-start | bytes 884744 | tf_op jit(solution)/shard_map/ppermute | solution.py:730
  86.8 9.0 %collective-permute-start.5 = (bf16[144,1024]{1,0:T(8,128)(2,1)S(1)}, bf16[144,1024]{1,0:T(8,128)(2,1)S(1)}, u32[]{:S(2)}, u32[]{:S(2)}) collective-permute-start(bf16[144,1024]{1,0:T(8,128)(2,1)S(1)} %get-tuple-element.65), channel_id=1, source_target_pairs={{0,1},{1,2},{2,3},{3,4},{4,5},{5,6},{6,7},{7,8},{8,9},{9,10},{10,1... | collective-permute-start | bytes 884744 | tf_op jit(solution)/shard_map/ppermute | solution.py:730
  90.1 5.8 %copy-start.19 = (bf16[288,192]{1,0:T(8,128)(2,1)S(1)}, bf16[288,192]{1,0:T(8,128)(2,1)}, u32[]{:S(2)}) copy-start(bf16[288,192]{1,0:T(8,128)(2,1)} %constant.32.clone.sel_ref) | copy-start | bytes 331780
  90.1 11.8 %copy-start.20 = (bf16[288,192]{1,0:T(8,128)(2,1)S(1)}, bf16[288,192]{1,0:T(8,128)(2,1)}, u32[]{:S(2)}) copy-start(bf16[288,192]{1,0:T(8,128)(2,1)} %constant.33.clone.sel_ref) | copy-start | bytes 331780
  95.8 12.5 %copy-start.16 = (bf16[192,1024]{1,0:T(8,128)(2,1)S(1)}, bf16[192,1024]{1,0:T(8,128)(2,1)}, u32[]{:S(2)}) copy-start(bf16[192,1024]{1,0:T(8,128)(2,1)} %get-tuple-element.73.ow_ref) | copy-start | bytes 1179652
  96.2 12.0 %collective-permute-start.6 = (bf16[96,1024]{1,0:T(8,128)(2,1)S(1)}, bf16[96,1024]{1,0:T(8,128)(2,1)S(1)}, u32[]{:S(2)}, u32[]{:S(2)}) collective-permute-start(bf16[96,1024]{1,0:T(8,128)(2,1)S(1)} %get-tuple-element.68), channel_id=1, source_target_pairs={{0,16},{16,32},{32,48},{48,64},{64,80},{80,96},{96,112},{1,17},{17... | collective-permute-start | bytes 589832 | tf_op jit(solution)/shard_map/ppermute | solution.py:736
  100.4 7.9 %collective-permute-start.7 = (bf16[96,1024]{1,0:T(8,128)(2,1)S(1)}, bf16[96,1024]{1,0:T(8,128)(2,1)S(1)}, u32[]{:S(2)}, u32[]{:S(2)}) collective-permute-start(bf16[96,1024]{1,0:T(8,128)(2,1)S(1)} %get-tuple-element.67._), channel_id=1, source_target_pairs={{16,0},{32,16},{48,32},{64,48},{80,64},{96,80},{112,96},{17,1},{33... | collective-permute-start | bytes 589832 | tf_op jit(solution)/shard_map/ppermute | solution.py:736
  101.9 6.4 %copy-start = (bf16[1024,2048]{1,0:T(8,128)(2,1)S(1)}, bf16[1024,2048]{1,0:T(8,128)(2,1)}, u32[]{:S(2)}) copy-start(bf16[1024,2048]{1,0:T(8,128)(2,1)} %wp_hbm.7) | copy-start | bytes 12582916
  101.9 6.4 %copy-start.4 = (bf16[8,384,512]{2,1,0:T(8,128)(2,1)S(1)}, bf16[8,384,512]{2,1,0:T(8,128)(2,1)}, u32[]{:S(2)}) copy-start(bf16[8,384,512]{2,1,0:T(8,128)(2,1)} %get-tuple-element.71.wts_ref) | copy-start | bytes 9437188
  101.9 6.4 %copy-start.5 = (bf16[1024,1024]{1,0:T(8,128)(2,1)S(1)}, bf16[1024,1024]{1,0:T(8,128)(2,1)}, u32[]{:S(2)}) copy-start(bf16[1024,1024]{1,0:T(8,128)(2,1)} %wo_hbm.5) | copy-start | bytes 6291460
  101.9 6.4 %copy-start.6 = (bf16[512,2048]{1,0:T(8,128)(2,1)S(1)}, bf16[512,2048]{1,0:T(8,128)(2,1)}, u32[]{:S(2)}) copy-start(bf16[512,2048]{1,0:T(8,128)(2,1)} %get-tuple-element.70.pairs_ref) | copy-start | bytes 6291460
  101.9 6.4 %copy-start.9 = (bf16[192,2048]{1,0:T(8,128)(2,1)S(1)}, bf16[192,2048]{1,0:T(8,128)(2,1)}, u32[]{:S(2)}) copy-start(bf16[192,2048]{1,0:T(8,128)(2,1)} %get-tuple-element.43.own_hbm.own_ref) | copy-start | bytes 2359300
  101.9 6.4 %copy-start.14 = (bf16[192,1024]{1,0:T(8,128)(2,1)S(1)}, bf16[192,1024]{1,0:T(8,128)(2,1)}, u32[]{:S(2)}) copy-start(bf16[192,1024]{1,0:T(8,128)(2,1)} %get-tuple-element.42.q_hbm.q_ref) | copy-start | bytes 1179652
  102.0 6.4 %copy-start.15 = (bf16[192,1024]{1,0:T(8,128)(2,1)S(1)}, bf16[192,1024]{1,0:T(8,128)(2,1)}, u32[]{:S(2)}) copy-start(bf16[192,1024]{1,0:T(8,128)(2,1)} %get-tuple-element.72.mix_ref) | copy-start | bytes 1179652
  118.6 12.9 %copy-start.8 = (bf16[192,1024]{1,0:T(8,128)(2,1)S(1)}, bf16[192,1024]{1,0:T(8,128)(2,1)}, u32[]{:S(2)}) copy-start(bf16[192,1024]{1,0:T(8,128)(2,1)} %get-tuple-element.74._.dq_ref) | copy-start | bytes 1179652
  118.6 17.1 %copy-start.7 = (bf16[12,16,1024]{2,1,0:T(8,128)(2,1)S(1)}, bf16[12,16,1024]{2,1,0:T(8,128)(2,1)}, u32[]{:S(2)}) copy-start(bf16[12,16,1024]{2,1,0:T(8,128)(2,1)} %param.19) | copy-start | bytes 1179652
  118.6 31.8 %all-to-all-start.1 = ((bf16[128,4,1024]{2,1,0:T(4,128)(2,1)}), bf16[128,4,1024]{2,1,0:T(4,128)(2,1)S(1)}, u32[]{:S(2)}, u32[]{:S(2)}) async-start(bf16[128,4,1024]{2,1,0:T(4,128)(2,1)} %get-tuple-element.78), calls=%async_computation.1 | async-start | bytes 2097152 | tf_op jit(solution)/shard_map/all_to_all | solution.py:914
  131.4 2.2 %copy-start.2 = (bf16[2048,1024]{1,0:T(8,128)(2,1)S(1)}, bf16[2048,1024]{1,0:T(8,128)(2,1)}, u32[]{:S(2)}) copy-start(bf16[2048,1024]{1,0:T(8,128)(2,1)} %wd_hbm.3) | copy-start | bytes 12582916
  133.6 2.2 %copy-start.1 = (bf16[1024,2048]{1,0:T(8,128)(2,1)S(1)}, bf16[1024,2048]{1,0:T(8,128)(2,1)}, u32[]{:S(2)}) copy-start(bf16[1024,2048]{1,0:T(8,128)(2,1)} %wp_hbm.7) | copy-start | bytes 12582916
  133.6 3.0 %copy-start.3 = (bf16[1024,1024]{1,0:T(8,128)(2,1)S(1)}, bf16[1024,1024]{1,0:T(8,128)(2,1)}, u32[]{:S(2)}) copy-start(bf16[1024,1024]{1,0:T(8,128)(2,1)} %wq_hbm.3) | copy-start | bytes 6291460
  136.6 1.1 copy-start.11
  137.8 1.1 copy-start.12

commit v7 on v6

--- a/solution.py
+++ b/solution.py
@@ -620,10 +620,10 @@
 
 
 def cross_back_kernel(
-    dn_ref, north_ref, south_ref, state_ref, dafter_ref, gain_ref, q_ref, own_ref, pairs_ref,
-    wts_ref, mix_ref, ow_ref, wp_hbm, wo_hbm,
-    dstate_hbm, slot_hbm, dq_hbm, down_hbm,
-    wp, wo, dsb, dmix, dpairs, scores, ds, dstate_ref, dq_ref, down_ref, slot_ref, sems, out_sems,
+    dn_ref, north_ref, south_ref, state_ref, dafter_ref, gain_ref, q_ref, pairs_ref,
+    wts_ref, mix_ref, wp_hbm, wo_hbm,
+    dstate_hbm, slot_hbm, dmix_hbm, ds_hbm,
+    wp, wo, dsb, dmix, dpairs, scores, ds, dstate_ref, slot_ref, sems, out_sems,
 ):
     copies = fetch([wo_hbm, wp_hbm], [wo, wp], sems)
     cells, model = state_ref.shape
@@ -644,43 +644,29 @@
 
     @pl.loop(0, model // (PAIR * GROUP))
     def _(g):
-        heads, deltas, own_dots = [], [], []
+        heads, deltas = [], []
         for k in range(GROUP):
             h = g * GROUP + k
             keys = pl.ds(pl.multiple_of(h * PAIR, PAIR), PAIR)
             vals = pl.ds(pl.multiple_of(model + h * PAIR, PAIR), PAIR)
             heads.append((h, keys, vals))
             grad = dmix[:, keys]
-            grad_f = grad.astype(F32)
             scores[k] = dot(stacked(grad), pairs_ref[:, vals], NT)
-            deltas.append(lane_sums(grad_f * mix_ref[:, keys].astype(F32)))
-            own_dots.append(lane_sums(grad_f * own_ref[:, vals].astype(F32)))
+            deltas.append(lane_sums(grad.astype(F32) * mix_ref[:, keys].astype(F32)))
         for k, (h, keys, vals) in enumerate(heads):
             for s in range(2):
                 for i in range(0, cells, SOFT):
                     rows = pl.ds(s * cells + i, SOFT)
-                    ds[k, rows, :] = (
+                    ds[h, rows, :] = (
                         wts_ref[h, rows, :].astype(F32)
                         * (scores[k, rows, :] - deltas[k][s][i : i + SOFT])
                     ).astype(BF)
         for k, (h, keys, vals) in enumerate(heads):
-            lanes = iota((cells, PAIR), 1) < HALF
-            weight = ow_ref[:, keys].astype(F32)
-            own_grad = weight * jnp.where(
-                lanes, own_dots[k][0] - deltas[k][0], own_dots[k][1] - deltas[k][1]
-            )
-            q = q_ref[:, keys]
-            grad = dmix[:, keys]
-            dq = merged(dot(ds[k], pairs_ref[:, keys]))
-            dq = dq + own_grad * own_ref[:, keys].astype(F32)
-            dq_ref[:, keys] = (dq * HALF ** (-0.5)).astype(BF)
-            down_ref[:, keys] = (own_grad * q.astype(F32)).astype(BF)
-            down_ref[:, vals] = (weight * grad.astype(F32)).astype(BF)
-            dpairs[:, keys] = dot(stacked(q), ds[k], TN).T.astype(BF)
-            dpairs[:, vals] = dot(stacked(grad), wts_ref[h], TN).T.astype(BF)
+            dpairs[:, keys] = dot(stacked(q_ref[:, keys]), ds[h], TN).T.astype(BF)
+            dpairs[:, vals] = dot(stacked(dmix[:, keys]), wts_ref[h], TN).T.astype(BF)
 
     leaving = fetch(
-        [dstate_ref, dq_ref, down_ref], [dstate_hbm, dq_hbm, down_hbm],
+        [dstate_ref, dmix, ds], [dstate_hbm, dmix_hbm, ds_hbm],
         out_sems.at[pl.ds(0, 3)],
     )
     copies[1].wait()
@@ -704,10 +690,42 @@
 
 
 def grid_back_kernel(
-    grid_ref, dstate_ref, gain_ref, dq_ref, down_ref, wq_hbm, wp_hbm, out_ref, wq, wp, acc, sems
-):
-    copies = fetch([wq_hbm, wp_hbm], [wq, wp], sems)
+    grid_hbm, dstate_hbm, gain_ref, q_hbm, own_hbm, mix_hbm, ow_hbm, dmix_hbm,
+    pairs_hbm, ds_hbm, wq_hbm, wp_hbm, out_ref,
+    grid_ref, dstate_ref, q_ref, own_ref, mix_ref, ow_ref, dmix,
+    pairs, ds, dq_ref, down_ref, wq, wp, acc, sems,
+):
     cells, model = grid_ref.shape
+    first = fetch(
+        [q_hbm, own_hbm, mix_hbm, ow_hbm, dmix_hbm, pairs_hbm.at[:, pl.ds(0, model)], ds_hbm],
+        [q_ref, own_ref, mix_ref, ow_ref, dmix, pairs, ds],
+        sems.at[pl.ds(0, 7)],
+    )
+    copies = fetch(
+        [wq_hbm, wp_hbm, grid_hbm, dstate_hbm],
+        [wq, wp, grid_ref, dstate_ref],
+        sems.at[pl.ds(7, 4)],
+    )
+    for copy in first:
+        copy.wait()
+
+    def one(h):
+        keys = pl.ds(pl.multiple_of(h * PAIR, PAIR), PAIR)
+        vals = pl.ds(pl.multiple_of(model + h * PAIR, PAIR), PAIR)
+        grad = dmix[:, keys].astype(F32)
+        weight = ow_ref[:, keys].astype(F32)
+        gap = own_ref[:, vals].astype(F32) - mix_ref[:, keys].astype(F32)
+        own_grad = weight * spread(*lane_sums(grad * gap))
+        dq = merged(dot(ds[h], pairs[:, keys])) + own_grad * own_ref[:, keys].astype(F32)
+        dq_ref[:, keys] = (dq * HALF ** (-0.5)).astype(BF)
+        down_ref[:, keys] = (own_grad * q_ref[:, keys].astype(F32)).astype(BF)
+        down_ref[:, vals] = (weight * grad).astype(BF)
+
+    @pl.loop(0, model // (PAIR * GROUP))
+    def _(g):
+        for k in range(GROUP):
+            one(g * GROUP + k)
+
     for copy in copies:
         copy.wait()
 
@@ -899,28 +917,33 @@
          vm((model, 3 * model), BF), dma((2,))],
         2 * cells * model * 4 * model, "own_back",
     )
-    dstate, slot_grads, dq, down = call(
+    dstate, slot_grads, dmix_c, ds_c = call(
         cross_back_kernel,
-        (dn_own, from_north, from_south, state, dafter, norm_gains, q_c, own_pairs, slot_pairs,
-         cross_w, cross_mix, own_w, w_cross_pairs, w_cross_out), "vvvvvvvvvvvvaa",
+        (dn_own, from_north, from_south, state, dafter, norm_gains, q_c, slot_pairs,
+         cross_w, cross_mix, w_cross_pairs, w_cross_out), "vvvvvvvvvvaa",
         [((cells, model), F32, "h"), ((devices, cap, model), BF, "h"),
-         ((cells, model), BF, "h"), ((cells, 2 * model), BF, "h")],
+         ((cells, model), BF, "h"), ((pairs_n, 2 * cells, slots), BF, "h")],
         [vm((model, 2 * model), BF), vm((model, model), BF), vm((cells, model), BF),
          vm((cells, model), BF), vm((slots, 2 * model), BF), vm((GROUP, 2 * cells, slots), F32),
-         vm((GROUP, 2 * cells, slots), BF), vm((cells, model), F32), vm((cells, model), BF),
-         vm((cells, 2 * model), BF), vm((devices, cap, model), BF), dma((2,)), dma((5,))],
+         vm((pairs_n, 2 * cells, slots), BF), vm((cells, model), F32),
+         vm((devices, cap, model), BF), dma((2,)), dma((5,))],
         2 * slots * model * 2 * model * 2, "cross_back",
     )
     returned = lax.all_to_all(slot_grads, ("lat", "lon"), 0, 0, tiled=True)
     encoded = call(
-        encode_kernel, (after, hidden, w_down, dq), "vvaa", [((cells, model), BF)],
+        encode_kernel, (after, hidden, w_down, dmix_c), "vvha", [((cells, model), BF)],
         [vm((ff, model), BF), dma((1,))], 2 * cells * model * ff, "encode",
     )
     grid_grad = call(
         grid_back_kernel,
-        (flat, dstate, norm_gains, dq, down, w_cross_query, w_cross_pairs), "vvvvvaa",
+        (flat, dstate, norm_gains, q_c, own_pairs, cross_mix, own_w, dmix_c, slot_pairs, ds_c,
+         w_cross_query, w_cross_pairs), "hhvhhhhhhhhh",
         [((cells, model), BF)],
-        [vm((model, model), BF), vm((model, 2 * model), BF), vm((cells, model), F32), dma((2,))],
+        [vm((cells, model), BF), vm((cells, model), F32), vm((cells, model), BF),
+         vm((cells, 2 * model), BF), vm((cells, model), BF), vm((cells, model), BF),
+         vm((cells, model), BF), vm((slots, model), BF), vm((pairs_n, 2 * cells, slots), BF), vm((cells, model), BF),
+         vm((cells, 2 * model), BF), vm((model, model), BF), vm((model, 2 * model), BF),
+         vm((cells, model), F32), dma((11,))],
         2 * cells * model * 3 * model, "grid_back",
     )
     obs_grad = call(

time: 153 us -> 152 us (level)
  Pallas kernels: 78 us -> 82.7 us
  local copies, waits for them, and re-layouts: 5.54 us -> 1.02 us
    pallas_call x14, Pallas kernels: 78 us -> 82.7 us  [call(): pl.pallas_call(body, name=name, out_shape=shapes[0] if single else shapes...]
    unnamed x60 -> x56, local copies, waits for them, and re-layouts: 5.54 us -> 1.02 us
  transfers between devices with their start and end apart: 10 -> 10, of which waited for: 5 -> 5; matrix products, arithmetic and copies ran while one was open for 0% -> 0% of each run, Pallas kernels for 22% -> 26%
where the time goes in v7:
time: 152 us
  Pallas kernels  82.7 us (54%)
  starting transfers between devices  40.3 us (27%)
  waiting for transfers between devices  26.4 us (17%)
    pallas_call x14, Pallas kernels, call(): pl.pallas_call(body, name=name, out_shape=shapes[0] if single else shapes...  82.7 us
    all_to_all x1, waiting for transfers between devices, per_device(): arrived = lax.all_to_all(payload, ('lat', 'lon'), 0, 0, tiled=True)  13.5 us
    all_to_all x1, starting transfers between devices, per_device(): returned = lax.all_to_all(slot_grads, ('lat', 'lon'), 0, 0, tiled=True)  12.8 us
    all_to_all x1, starting transfers between devices, per_device(): arrived = lax.all_to_all(payload, ('lat', 'lon'), 0, 0, tiled=True)  11.5 us
    ppermute x4, starting transfers between devices, line(): return lax.ppermute(value, 'lat', pairs)  10.9 us
    all_to_all x1, waiting for transfers between devices, per_device(): returned = lax.all_to_all(slot_grads, ('lat', 'lon'), 0, 0, tiled=True)  6.68 us
    ppermute x4, starting transfers between devices, ring(): lax.ppermute(value, 'lon', [(i, (i + by) % size) for i in range(size)])  5.05 us
    ppermute x4, waiting for transfers between devices, ring(): lax.ppermute(value, 'lon', [(i, (i + by) % size) for i in range(size)])  4.77 us
  transfers between devices with their start and end apart: 10, of which 5 were waited for; matrix products, arithmetic and copies ran while one was open for 0% of the time, Pallas kernels for 26%

profile of v7, /device:TPU:1, one launch (start us, length us, event | category | flops | bytes accessed | tf_op | source)
XLA Modules:
  0.0 151.8 jit_solution(6067318340821586215)
XLA Ops:
  0.6 0.0 copy-start.14
  0.6 2.8 %place.1 = (bf16[128,4,1152]{2,1,0:T(4,128)(2,1)}, bf16[512,256]{1,0:T(8,128)(2,1)}) custom-call(s32[1,256]{1,0:T(1,128)} %bitcast.17, s32[1,256]{1,0:T(1,128)} %bitcast.18, bf16[256,1024]{1,0:T(8,128)(2,1)} %obs_hbm.1), custom_call_target="tpu_custom_call" | custom-call | flops 268435456 | bytes 1968128 | tf_op jit(solution)/shard_map/place/pallas_call | solution.py:120
  3.4 11.5 %all-to-all-start = ((bf16[128,4,1152]{2,1,0:T(4,128)(2,1)}), bf16[128,4,1152]{2,1,0:T(4,128)(2,1)S(1)}, u32[]{:S(2)}, u32[]{:S(2)}) async-start(bf16[128,4,1152]{2,1,0:T(4,128)(2,1)} %get-tuple-element.41), calls=%async_computation | async-start | bytes 2359296 | tf_op jit(solution)/shard_map/all_to_all | solution.py:820
  15.0 0.0 copy-done.14
  15.0 6.8 %grid_proj.1 = (bf16[192,1024]{1,0:T(8,128)(2,1)}, bf16[192,2048]{1,0:T(8,128)(2,1)}, bf16[192,2048]{1,0:T(8,128)(2,1)}) custom-call(bf16[192,1024]{1,0:T(8,128)(2,1)} %bitcast.12, bf16[192,1024]{1,0:T(8,128)(2,1)} %bitcast.10, f32[3,1024]{1,0:T(4,128)S(1)} %copy-done.14, bf16[1024,1024]{1,0:T(8,128)(2,1)} %wq_hbm.3, bf16[1024,2048]{1,0:T(8,128)(2,1)} %wp_hbm.7, ...), custom_call_target="tpu_custom_call" | custom-call | flops 2013265920 | bytes 13250560 | tf_op jit(solution)/shard_map/grid_proj/pallas_call | solution.py:120
  21.8 13.5 %all-to-all-done.arr_ref = bf16[128,4,1152]{2,1,0:T(4,128)(2,1)S(1)} async-done(((bf16[128,4,1152]{2,1,0:T(4,128)(2,1)}), bf16[128,4,1152]{2,1,0:T(4,128)(2,1)S(1)}, u32[]{:S(2)}, u32[]{:S(2)}) %all-to-all-start) | async-done | bytes 1179680 | tf_op jit(solution)/shard_map/all_to_all | solution.py:820
  35.3 10.6 %cross.1 = (f32[192,1024]{1,0:T(8,128)}, bf16[96,1024]{1,0:T(8,128)(2,1)S(1)}, bf16[96,1024]{1,0:T(8,128)(2,1)S(1)}, bf16[512,2048]{1,0:T(8,128)(2,1)}, bf16[8,3...) custom-call(bf16[128,4,1152]{2,1,0:T(4,128)(2,1)S(1)} %all-to-all-done.arr_ref, ...), custom_call_target="tpu_custom_call" | custom-call | flops 4294967296 | bytes 16265216 | tf_op jit(solution)/shard_map/cross/pallas_call | solution.py:120
  45.9 1.3 collective-permute-start.1
  47.2 4.0 %collective-permute-start = (bf16[96,1024]{1,0:T(8,128)(2,1)S(1)}, bf16[96,1024]{1,0:T(8,128)(2,1)S(1)}, u32[]{:S(2)}, u32[]{:S(2)}) collective-permute-start(bf16[96,1024]{1,0:T(8,128)(2,1)S(1)} %get-tuple-element.45.bottom_ref), channel_id=1, source_target_pairs={{0,16},{16,32},{32,48},{48,64},{64,80},{80,96},{96,112},{1,17},{17... | collective-permute-start | bytes 589832 | tf_op jit(solution)/shard_map/ppermute | solution.py:754
  51.3 0.0 copy-done.23
  51.3 0.0 slice-done
  51.3 0.0 slice-done.1
  51.3 0.0 copy-start.10
  51.3 0.0 copy-start.13
  51.3 2.7 %near_own.1 = (bf16[192,1024]{1,0:T(8,128)(2,1)S(1)}, bf16[192,2048]{1,0:T(8,128)(2,1)S(1)}) custom-call(bf16[96,1024]{1,0:T(8,128)(2,1)S(1)} %get-tuple-element.44.top_ref, bf16[96,1024]{1,0:T(8,128)(2,1)S(1)} %get-tuple-element.45.bottom_ref, bf16[1024,3072]{1,0:T(8,128)(2,1)S(1)} %bitcast.7), custom_call_target="tpu_custom_call" | custom-call | flops 1207959552 | bytes 7864320 | tf_op jit(solution)/shard_map/near_own/pallas_call | solution.py:120
  54.0 0.5 collective-permute-done.1.south_ref
  54.5 1.0 collective-permute-done.north_ref
  55.5 0.0 copy-done.10
  55.5 0.5 rim.1
  56.0 1.8 %collective-permute-start.2 = (bf16[144,1024]{1,0:T(8,128)(2,1)S(1)}, bf16[144,1024]{1,0:T(8,128)(2,1)S(1)}, u32[]{:S(2)}, u32[]{:S(2)}) collective-permute-start(bf16[144,1024]{1,0:T(8,128)(2,1)S(1)} %get-tuple-element.48), channel_id=1, source_target_pairs={{0,1},{1,2},{2,3},{3,4},{4,5},{5,6},{6,7},{7,8},{8,9},{9,10},{10,1... | collective-permute-start | bytes 884744 | tf_op jit(solution)/shard_map/ppermute | solution.py:748
  57.8 0.0 collective-permute-start.3
  57.8 0.0 copy-done.13
  57.8 0.0 copy-start.7
  57.8 0.0 copy-start.15
  57.8 0.0 copy-start.17
  57.8 0.0 copy-start.18
  57.8 0.0 copy-start.20
  57.8 6.0 %inner.1 = (bf16[192,2048]{1,0:T(8,128)(2,1)S(1)}, bf16[8,384,384]{2,1,0:T(8,128)(2,1)}, f32[192,1024]{1,0:T(8,128)S(1)}, f32[8,384,128]{2,1,0:T(8,128)S(1)}, f32[8,384,128]{2,1,0:T(8,128)S(1)}) custom-call(bf16[96,1024]{1,0:T(8,128)(2,1)S(1)} %collective-permute-done.north_ref, bf16[96,1024]{1,0:T(8,128)(2,1)S(1)} %collective-permute-done.1.south_ref, ...), custom_call_target="tpu_custom_call" | custom-call | flops 1610612736 | bytes 15101952 | tf_op jit(solution)/shard_map/inner/pallas_call | solution.py:120
  63.8 0.0 collective-permute-done.2.west_ref
  63.8 4.8 %collective-permute-done.3.east_ref = bf16[144,1024]{1,0:T(8,128)(2,1)S(1)} collective-permute-done((bf16[144,1024]{1,0:T(8,128)(2,1)S(1)}, bf16[144,1024]{1,0:T(8,128)(2,1)S(1)}, u32[]{:S(2)}, u32[]{:S(2)}) %collective-permute-start.3) | collective-permute-done | bytes 294944 | tf_op jit(solution)/shard_map/ppermute | solution.py:748
  68.6 0.0 copy-done.7
  68.6 0.0 copy-done.15
  68.6 0.0 copy-done.17
  68.6 0.0 slice-start.3
  68.6 18.1 %near.1 = (f32[192,1024]{1,0:T(8,128)S(1)}, bf16[192,2048]{1,0:T(8,128)(2,1)S(1)}, bf16[144,1024]{1,0:T(8,128)(2,1)S(1)}, bf16[144,1024]{1,0:T(8,128)(2,1)S(1)},...) custom-call(bf16[192,1024]{1,0:T(8,128)(2,1)S(1)} %get-tuple-element, ...), custom_call_target="tpu_custom_call" | custom-call | flops 20000000000 | bytes 24158208 | tf_op jit(solution)/shard_map/near/pallas_call | solution.py:120
  86.7 0.9 copy-done.21
  87.6 0.0 collective-permute-start.4
  87.6 3.2 %collective-permute-start.5 = (bf16[144,1024]{1,0:T(8,128)(2,1)S(1)}, bf16[144,1024]{1,0:T(8,128)(2,1)S(1)}, u32[]{:S(2)}, u32[]{:S(2)}) collective-permute-start(bf16[144,1024]{1,0:T(8,128)(2,1)S(1)} %get-tuple-element.65), channel_id=1, source_target_pairs={{0,1},{1,2},{2,3},{3,4},{4,5},{5,6},{6,7},{7,8},{8,9},{9,10},{10,1... | collective-permute-start | bytes 884744 | tf_op jit(solution)/shard_map/ppermute | solution.py:748
  90.9 0.0 slice-done.2
  90.9 0.0 copy-start.12
  90.9 5.7 %middle_back.1 = (f32[192,1024]{1,0:T(8,128)S(1)}, bf16[64,2048]{1,0:T(8,128)(2,1)S(1)}, f32[192,1024]{1,0:T(8,128)S(1)}) custom-call(bf16[192,1024]{1,0:T(8,128)(2,1)S(1)} %get-tuple-element.46.q_ref, bf16[192,2048]{1,0:T(8,128)(2,1)S(1)} %get-tuple-element.47._.kvo_ref, bf16[192,2048]{1,0:T(8,128)(2,1)S(1)} %get-tuple-element.59.kvr_ref, ...), custom_call_target="tpu_custom_call" | custom-call | flops 1610612736 | bytes 14024704 | tf_op jit(solution)/shard_map/middle_back/pallas_call | solution.py:120
  96.6 0.0 collective-permute-done.4.from_east_ref
  96.6 0.0 collective-permute-done.5.from_west_ref
  96.7 0.0 copy-done.11
  96.7 0.4 fold.1
  97.1 4.1 %collective-permute-start.6 = (bf16[96,1024]{1,0:T(8,128)(2,1)S(1)}, bf16[96,1024]{1,0:T(8,128)(2,1)S(1)}, u32[]{:S(2)}, u32[]{:S(2)}) collective-permute-start(bf16[96,1024]{1,0:T(8,128)(2,1)S(1)} %get-tuple-element.68), channel_id=1, source_target_pairs={{0,16},{16,32},{32,48},{48,64},{64,80},{80,96},{96,112},{1,17},{17... | collective-permute-start | bytes 589832 | tf_op jit(solution)/shard_map/ppermute | solution.py:754
  101.2 1.5 collective-permute-start.7
  102.7 0.0 copy-start
  102.8 0.0 copy-start.8
  102.8 0.0 copy-start.16
  102.8 0.0 copy-start.19
  102.8 0.0 copy-start.22
  102.8 6.3 %own_back.1.dn_ref = f32[192,1024]{1,0:T(8,128)S(1)} custom-call(bf16[192,1024]{1,0:T(8,128)(2,1)S(1)} %get-tuple-element.46.q_ref, bf16[192,2048]{1,0:T(8,128)(2,1)S(1)} %get-tuple-element.47._.kvo_ref, bf16[192,1024]{1,0:T(8,128)(2,1)S(1)} %get-tuple-element.57.mix, bf16[192,1024]{1,0:T(8,128)(2,1)S(1)} %get-tuple-element.58.dmix, ...), custom_call_target="tpu_custom_call" | custom-call | flops 1610612736 | bytes 13348864 | tf_op jit(solution)/shard_map/own_back/pallas_call | solution.py:120
  109.1 0.0 collective-permute-done.6.north_ref
  109.1 0.0 collective-permute-done.7.south_ref
  109.2 8.5 %cross_back.1 = (f32[192,1024]{1,0:T(8,128)}, bf16[128,4,1024]{2,1,0:T(4,128)(2,1)}, bf16[192,1024]{1,0:T(8,128)(2,1)}, bf16[8,384,512]{2,1,0:T(8,128)(2,1)}) custom-call(f32[192,1024]{1,0:T(8,128)S(1)} %own_back.1.dn_ref, bf16[96,1024]{1,0:T(8,128)(2,1)S(1)} %collective-permute-done.6.north_ref, bf16[96,1024]{1,0:T(8,128)(2,1)S(1)} %collective-permute-done.7.south_ref, ...), custom_call_target="tpu_custom_call" | custom-call | flops 4294967296 | bytes 20459520 | tf_op jit(solution)/shard_map/cross_back/pallas_call | solution.py:120
  117.7 0.0 copy-start.2
  117.7 0.0 copy-start.4
  117.7 0.0 copy-start.6
  117.7 12.8 %all-to-all-start.1 = ((bf16[128,4,1024]{2,1,0:T(4,128)(2,1)}), bf16[128,4,1024]{2,1,0:T(4,128)(2,1)S(1)}, u32[]{:S(2)}, u32[]{:S(2)}) async-start(bf16[128,4,1024]{2,1,0:T(4,128)(2,1)} %get-tuple-element.78), calls=%async_computation.1 | async-start | bytes 2097152 | tf_op jit(solution)/shard_map/all_to_all | solution.py:932
  130.5 3.9 %encode.1 = bf16[192,1024]{1,0:T(8,128)(2,1)} custom-call(f32[192,1024]{1,0:T(8,128)S(1)} %copy-done.4, bf16[192,2048]{1,0:T(8,128)(2,1)S(1)} %copy-done.6, bf16[2048,1024]{1,0:T(8,128)(2,1)} %wd_hbm.3, bf16[192,1024]{1,0:T(8,128)(2,1)S(1)} %copy-done.2), custom_call_target="tpu_custom_call" | custom-call | flops 805306368 | bytes 6553600 | tf_op jit(solution)/shard_map/encode/pallas_call | solution.py:120
  134.5 8.3 %grid_back.1 = bf16[192,1024]{1,0:T(8,128)(2,1)} custom-call(bf16[192,1024]{1,0:T(8,128)(2,1)} %bitcast.14, f32[192,1024]{1,0:T(8,128)} %get-tuple-element.74.dstate_hbm, f32[3,1024]{1,0:T(4,128)S(1)} %copy-done.14, bf16[192,1024]{1,0:T(8,128)(2,1)} %get-tuple-element.42.q_hbm.q_ref, bf16[192,2048]{1,0:T(8,128)(2,1)} %get-tuple-element.43.own_hbm, ...), custom_call_target="tpu_custom_call" | custom-call | flops 1207959552 | bytes 15478784 | tf_op jit(solution)/shard_map/grid_back/pallas_call | solution.py:120
  142.8 6.7 %all-to-all-done.1.ret_ref = bf16[128,4,1024]{2,1,0:T(4,128)(2,1)S(1)} async-done(((bf16[128,4,1024]{2,1,0:T(4,128)(2,1)}), bf16[128,4,1024]{2,1,0:T(4,128)(2,1)S(1)}, u32[]{:S(2)}, u32[]{:S(2)}) %all-to-all-start.1) | async-done | bytes 1048608 | tf_op jit(solution)/shard_map/all_to_all | solution.py:932
  149.4 2.2 %gather.1 = bf16[256,1024]{1,0:T(8,128)(2,1)} custom-call(bf16[512,256]{1,0:T(8,128)(2,1)} %get-tuple-element.77.place_hbm, bf16[128,4,1024]{2,1,0:T(4,128)(2,1)S(1)} %all-to-all-done.1.ret_ref), custom_call_target="tpu_custom_call" | custom-call | flops 268435456 | bytes 1835008 | tf_op jit(solution)/shard_map/gather/pallas_call | solution.py:120
  (30 shorter events, 0.1 us)
Async XLA Ops:
  0.6 14.3 %copy-start.14 = (f32[3,1024]{1,0:T(4,128)S(1)}, f32[3,1024]{1,0:T(4,128)}, u32[]{:S(2)}) copy-start(f32[3,1024]{1,0:T(4,128)} %gain_ref.9) | copy-start | bytes 36868
  3.4 31.8 %all-to-all-start = ((bf16[128,4,1152]{2,1,0:T(4,128)(2,1)}), bf16[128,4,1152]{2,1,0:T(4,128)(2,1)S(1)}, u32[]{:S(2)}, u32[]{:S(2)}) async-start(bf16[128,4,1152]{2,1,0:T(4,128)(2,1)} %get-tuple-element.41), calls=%async_computation | async-start | bytes 2359296 | tf_op jit(solution)/shard_map/all_to_all | solution.py:820
  35.3 16.0 %slice-start = ((s8[6291456]{0:T(1024)(128)(4,1)}), s8[4194304]{0:T(1024)(128)(4,1)S(1)}, s32[]{:S(2)}) async-start(s8[6291456]{0:T(1024)(128)(4,1)} %bitcast.6), calls=%async_computation.2 | async-start | bytes 8388608
  35.3 16.0 %copy-start.23 = (s32[8,768]{1,0:T(8,128)S(1)}, s32[8,768]{1,0:T(8,128)}, u32[]{:S(2)}) copy-start(s32[8,768]{1,0:T(8,128)} %constant.28.clone) | copy-start | bytes 73732
  35.3 16.0 %slice-start.1 = ((s8[6291456]{0:T(1024)(128)(4,1)}), s8[2097152]{0:T(1024)(128)(4,1)S(1)}, s32[]{:S(2)}) async-start(s8[6291456]{0:T(1024)(128)(4,1)} %bitcast.6), calls=%async_computation.3 | async-start | bytes 4194304
  45.9 8.6 %collective-permute-start.1 = (bf16[96,1024]{1,0:T(8,128)(2,1)S(1)}, bf16[96,1024]{1,0:T(8,128)(2,1)S(1)}, u32[]{:S(2)}, u32[]{:S(2)}) collective-permute-start(bf16[96,1024]{1,0:T(8,128)(2,1)S(1)} %get-tuple-element.44.top_ref), channel_id=1, source_target_pairs={{16,0},{32,16},{48,32},{64,48},{80,64},{96,80},{112,96},{17,1},{33... | collective-permute-start | bytes 589832 | tf_op jit(solution)/shard_map/ppermute | solution.py:754
  47.2 8.3 %collective-permute-start = (bf16[96,1024]{1,0:T(8,128)(2,1)S(1)}, bf16[96,1024]{1,0:T(8,128)(2,1)S(1)}, u32[]{:S(2)}, u32[]{:S(2)}) collective-permute-start(bf16[96,1024]{1,0:T(8,128)(2,1)S(1)} %get-tuple-element.45.bottom_ref), channel_id=1, source_target_pairs={{0,16},{16,32},{32,48},{48,64},{64,80},{80,96},{96,112},{1,17},{17... | collective-permute-start | bytes 589832 | tf_op jit(solution)/shard_map/ppermute | solution.py:754
  51.3 4.2 %copy-start.10 = (bf16[288,384]{1,0:T(8,128)(2,1)S(1)}, bf16[288,384]{1,0:T(8,128)(2,1)}, u32[]{:S(2)}) copy-start(bf16[288,384]{1,0:T(8,128)(2,1)} %constant.29.clone.sel_ref) | copy-start | bytes 663556
  51.3 6.4 %copy-start.13 = (bf16[192,384]{1,0:T(8,128)(2,1)S(1)}, bf16[192,384]{1,0:T(8,128)(2,1)}, u32[]{:S(2)}) copy-start(bf16[192,384]{1,0:T(8,128)(2,1)} %constant.30.clone.base_ref) | copy-start | bytes 442372
  56.0 7.8 %collective-permute-start.2 = (bf16[144,1024]{1,0:T(8,128)(2,1)S(1)}, bf16[144,1024]{1,0:T(8,128)(2,1)S(1)}, u32[]{:S(2)}, u32[]{:S(2)}) collective-permute-start(bf16[144,1024]{1,0:T(8,128)(2,1)S(1)} %get-tuple-element.48), channel_id=1, source_target_pairs={{0,1},{1,2},{2,3},{3,4},{4,5},{5,6},{6,7},{7,8},{8,9},{9,10},{10,1... | collective-permute-start | bytes 884744 | tf_op jit(solution)/shard_map/ppermute | solution.py:748
  57.8 10.8 %collective-permute-start.3 = (bf16[144,1024]{1,0:T(8,128)(2,1)S(1)}, bf16[144,1024]{1,0:T(8,128)(2,1)S(1)}, u32[]{:S(2)}, u32[]{:S(2)}) collective-permute-start(bf16[144,1024]{1,0:T(8,128)(2,1)S(1)} %get-tuple-element.49), channel_id=1, source_target_pairs={{0,15},{1,0},{2,1},{3,2},{4,3},{5,4},{6,5},{7,6},{8,7},{9,8},{10,9... | collective-permute-start | bytes 884744 | tf_op jit(solution)/shard_map/ppermute | solution.py:748
  57.8 10.8 %copy-start.7 = (bf16[12,16,1024]{2,1,0:T(8,128)(2,1)S(1)}, bf16[12,16,1024]{2,1,0:T(8,128)(2,1)}, u32[]{:S(2)}) copy-start(bf16[12,16,1024]{2,1,0:T(8,128)(2,1)} %param.23) | copy-start | bytes 1179652
  57.8 10.8 %copy-start.15 = (bf16[1024,1024]{1,0:T(8,128)(2,1)S(1)}, bf16[1024,1024]{1,0:T(8,128)(2,1)}, u32[]{:S(2)}) copy-start(bf16[1024,1024]{1,0:T(8,128)(2,1)} %wo_hbm.4) | copy-start | bytes 6291460
  57.8 10.8 %copy-start.17 = (bf16[192,2048]{1,0:T(8,128)(2,1)S(1)}, bf16[192,2048]{1,0:T(8,128)(2,1)}, u32[]{:S(2)}) copy-start(bf16[192,2048]{1,0:T(8,128)(2,1)} %get-tuple-element.51.dh_ref) | copy-start | bytes 2359300
  57.8 10.8 %copy-start.18 = (bf16[192,384]{1,0:T(8,128)(2,1)S(1)}, bf16[192,384]{1,0:T(8,128)(2,1)}, u32[]{:S(2)}) copy-start(bf16[192,384]{1,0:T(8,128)(2,1)} %constant.31.clone.base_ref) | copy-start | bytes 442372
  57.8 10.8 %copy-start.20 = (f32[192,1024]{1,0:T(8,128)S(1)}, f32[192,1024]{1,0:T(8,128)}, u32[]{:S(2)}) copy-start(f32[192,1024]{1,0:T(8,128)} %get-tuple-element.50.state_ref) | copy-start | bytes 2359300
  68.6 22.3 %slice-start.2 = ((s8[6291456]{0:T(1024)(128)(4,1)}), s8[4194304]{0:T(1024)(128)(4,1)S(1)}, s32[]{:S(2)}) async-start(s8[6291456]{0:T(1024)(128)(4,1)} %bitcast.8), calls=%async_computation.4 | async-start | bytes 8388608
  68.6 22.3 %slice-start.3 = ((s8[6291456]{0:T(1024)(128)(4,1)}), s8[2097152]{0:T(1024)(128)(4,1)S(1)}, s32[]{:S(2)}) async-start(s8[6291456]{0:T(1024)(128)(4,1)} %bitcast.8), calls=%async_computation.5 | async-start | bytes 4194304
  86.7 0.9 copy-start.21
  87.6 9.0 %copy-start.3 = (f32[192,1024]{1,0:T(8,128)}, f32[192,1024]{1,0:T(8,128)S(1)}, u32[]{:S(2)}) copy-start(f32[192,1024]{1,0:T(8,128)S(1)} %get-tuple-element.55.after_ref) | copy-start | bytes 2359300
  87.6 9.0 %copy-start.5 = (bf16[192,2048]{1,0:T(8,128)(2,1)}, bf16[192,2048]{1,0:T(8,128)(2,1)S(1)}, u32[]{:S(2)}) copy-start(bf16[192,2048]{1,0:T(8,128)(2,1)S(1)} %get-tuple-element.56.hid_ref) | copy-start | bytes 2359300
  87.6 9.0 %collective-permute-start.4 = (bf16[144,1024]{1,0:T(8,128)(2,1)S(1)}, bf16[144,1024]{1,0:T(8,128)(2,1)S(1)}, u32[]{:S(2)}, u32[]{:S(2)}) collective-permute-start(bf16[144,1024]{1,0:T(8,128)(2,1)S(1)} %get-tuple-element.64), channel_id=1, source_target_pairs={{0,15},{1,0},{2,1},{3,2},{4,3},{5,4},{6,5},{7,6},{8,7},{9,8},{10,9... | collective-permute-start | bytes 884744 | tf_op jit(solution)/shard_map/ppermute | solution.py:748
  87.6 9.0 %collective-permute-start.5 = (bf16[144,1024]{1,0:T(8,128)(2,1)S(1)}, bf16[144,1024]{1,0:T(8,128)(2,1)S(1)}, u32[]{:S(2)}, u32[]{:S(2)}) collective-permute-start(bf16[144,1024]{1,0:T(8,128)(2,1)S(1)} %get-tuple-element.65), channel_id=1, source_target_pairs={{0,1},{1,2},{2,3},{3,4},{4,5},{5,6},{6,7},{7,8},{8,9},{9,10},{10,1... | collective-permute-start | bytes 884744 | tf_op jit(solution)/shard_map/ppermute | solution.py:748
  90.9 5.8 %copy-start.11 = (bf16[288,192]{1,0:T(8,128)(2,1)S(1)}, bf16[288,192]{1,0:T(8,128)(2,1)}, u32[]{:S(2)}) copy-start(bf16[288,192]{1,0:T(8,128)(2,1)} %constant.32.clone.sel_ref) | copy-start | bytes 331780
  90.9 11.8 %copy-start.12 = (bf16[288,192]{1,0:T(8,128)(2,1)S(1)}, bf16[288,192]{1,0:T(8,128)(2,1)}, u32[]{:S(2)}) copy-start(bf16[288,192]{1,0:T(8,128)(2,1)} %constant.33.clone.sel_ref) | copy-start | bytes 331780
  97.1 12.0 %collective-permute-start.6 = (bf16[96,1024]{1,0:T(8,128)(2,1)S(1)}, bf16[96,1024]{1,0:T(8,128)(2,1)S(1)}, u32[]{:S(2)}, u32[]{:S(2)}) collective-permute-start(bf16[96,1024]{1,0:T(8,128)(2,1)S(1)} %get-tuple-element.68), channel_id=1, source_target_pairs={{0,16},{16,32},{32,48},{48,64},{64,80},{80,96},{96,112},{1,17},{17... | collective-permute-start | bytes 589832 | tf_op jit(solution)/shard_map/ppermute | solution.py:754
  101.2 7.9 %collective-permute-start.7 = (bf16[96,1024]{1,0:T(8,128)(2,1)S(1)}, bf16[96,1024]{1,0:T(8,128)(2,1)S(1)}, u32[]{:S(2)}, u32[]{:S(2)}) collective-permute-start(bf16[96,1024]{1,0:T(8,128)(2,1)S(1)} %get-tuple-element.67._), channel_id=1, source_target_pairs={{16,0},{32,16},{48,32},{64,48},{80,64},{96,80},{112,96},{17,1},{33... | collective-permute-start | bytes 589832 | tf_op jit(solution)/shard_map/ppermute | solution.py:754
  102.7 6.4 %copy-start = (bf16[1024,2048]{1,0:T(8,128)(2,1)S(1)}, bf16[1024,2048]{1,0:T(8,128)(2,1)}, u32[]{:S(2)}) copy-start(bf16[1024,2048]{1,0:T(8,128)(2,1)} %wp_hbm.7) | copy-start | bytes 12582916
  102.7 6.4 %copy-start.1 = (bf16[512,2048]{1,0:T(8,128)(2,1)S(1)}, bf16[512,2048]{1,0:T(8,128)(2,1)}, u32[]{:S(2)}) copy-start(bf16[512,2048]{1,0:T(8,128)(2,1)} %get-tuple-element.70.pairs_ref.pairs_hbm) | copy-start | bytes 6291460
  102.8 6.4 %copy-start.8 = (bf16[192,1024]{1,0:T(8,128)(2,1)S(1)}, bf16[192,1024]{1,0:T(8,128)(2,1)}, u32[]{:S(2)}) copy-start(bf16[192,1024]{1,0:T(8,128)(2,1)} %get-tuple-element.42.q_hbm.q_ref) | copy-start | bytes 1179652
  102.8 6.4 %copy-start.9 = (bf16[192,1024]{1,0:T(8,128)(2,1)S(1)}, bf16[192,1024]{1,0:T(8,128)(2,1)}, u32[]{:S(2)}) copy-start(bf16[192,1024]{1,0:T(8,128)(2,1)} %get-tuple-element.72.mix_ref.mix_hbm) | copy-start | bytes 1179652
  102.8 6.4 %copy-start.16 = (bf16[1024,1024]{1,0:T(8,128)(2,1)S(1)}, bf16[1024,1024]{1,0:T(8,128)(2,1)}, u32[]{:S(2)}) copy-start(bf16[1024,1024]{1,0:T(8,128)(2,1)} %wo_hbm.5) | copy-start | bytes 6291460
  102.8 6.4 %copy-start.19 = (bf16[8,384,512]{2,1,0:T(8,128)(2,1)S(1)}, bf16[8,384,512]{2,1,0:T(8,128)(2,1)}, u32[]{:S(2)}) copy-start(bf16[8,384,512]{2,1,0:T(8,128)(2,1)} %get-tuple-element.71.wts_ref) | copy-start | bytes 9437188
  102.8 6.4 %copy-start.22 = (f32[192,1024]{1,0:T(8,128)S(1)}, f32[192,1024]{1,0:T(8,128)}, u32[]{:S(2)}) copy-start(f32[192,1024]{1,0:T(8,128)} %copy-done.21) | copy-start | bytes 2359300
  117.7 12.8 %copy-start.2 = (bf16[192,1024]{1,0:T(8,128)(2,1)S(1)}, bf16[192,1024]{1,0:T(8,128)(2,1)}, u32[]{:S(2)}) copy-start(bf16[192,1024]{1,0:T(8,128)(2,1)} %get-tuple-element.73._.dmix_hbm) | copy-start | bytes 1179652
  117.7 12.8 %copy-start.4 = (f32[192,1024]{1,0:T(8,128)S(1)}, f32[192,1024]{1,0:T(8,128)}, u32[]{:S(2)}) copy-start(f32[192,1024]{1,0:T(8,128)} %copy-done.3) | copy-start | bytes 2359300
  117.7 12.8 %copy-start.6 = (bf16[192,2048]{1,0:T(8,128)(2,1)S(1)}, bf16[192,2048]{1,0:T(8,128)(2,1)}, u32[]{:S(2)}) copy-start(bf16[192,2048]{1,0:T(8,128)(2,1)} %copy-done.5) | copy-start | bytes 2359300
  117.7 31.7 %all-to-all-start.1 = ((bf16[128,4,1024]{2,1,0:T(4,128)(2,1)}), bf16[128,4,1024]{2,1,0:T(4,128)(2,1)S(1)}, u32[]{:S(2)}, u32[]{:S(2)}) async-start(bf16[128,4,1024]{2,1,0:T(4,128)(2,1)} %get-tuple-element.78), calls=%async_computation.1 | async-start | bytes 2097152 | tf_op jit(solution)/shard_map/all_to_all | solution.py:932

commit v8 on v7

--- a/solution.py
+++ b/solution.py
@@ -144,21 +144,29 @@
     earlier = (iota((rows, rows), 0) < iota((rows, rows), 1)).astype(F32).astype(BF)
     before = dot(member.astype(F32).astype(BF), earlier)
     rank = jnp.sum(jnp.where(member, before, 0.0), 0, keepdims=True).astype(jnp.int32)
-    slot = tile * cap + rank
+    share = 2 * devices
+    slot = (rank >> 1) * share + tile * 2 + (rank & 1)
     placing = (slot == iota((slots, rows), 0)).astype(F32).astype(BF)
     place_ref[...] = placing
     copies[1].wait()
     copies[2].wait()
     cell = cell_ref[...]
     shift = wide.bit_length() - 1
-    line_no = iota((128, rows), 0)
-    codes = jnp.where(
-        line_no == 0, (cell >> shift) + 1, jnp.where(line_no == 1, (cell & (wide - 1)) + 1, 0)
-    )
-    code_rows = dot(placing, codes.astype(F32).astype(BF), NT).astype(BF)
-    pay_ref[:, :, model:] = code_rows.reshape(devices, cap, 128)
+    line_no = iota((PAIR, rows), 0)
     moved = dot(placing, obs_ref[...]).astype(BF)
-    pay_ref[:, :, :model] = moved.reshape(devices, cap, model)
+    code_rows = jnp.zeros((share, PAIR), F32)
+    for part in range(cap // 2):
+        rows_here = slice(part * share, (part + 1) * share)
+        for j in range(model // PAIR):
+            piece = moved[rows_here, j * PAIR : (j + 1) * PAIR]
+            pay_ref[:, j * (cap // 2) + part] = piece.reshape(devices, 2, PAIR)
+        codes = jnp.where(
+            line_no == 2 * part,
+            (cell >> shift) + 1,
+            jnp.where(line_no == 2 * part + 1, (cell & (wide - 1)) + 1, 0),
+        )
+        code_rows = code_rows + dot(placing[rows_here], codes.astype(F32).astype(BF), NT)
+    pay_ref[:, pay_ref.shape[1] - 1] = code_rows.astype(BF).reshape(devices, 2, PAIR)
     for copy in fetch([pay_ref, place_ref], [pay_hbm, place_hbm], sems):
         copy.wait()
 
@@ -212,22 +220,33 @@
     lates = out_sems.at[pl.ds(5, 4)]
     rim = top_ref.shape[0]
     slots = arr.shape[0]
-    arr[...] = arr_ref[...].reshape(arr.shape)
+    devices = arr_ref.shape[0]
+    share = 2 * devices
+    halves = slots // share
+    for part in range(halves):
+        for j in range(model // PAIR):
+            arr[part * share : (part + 1) * share, j * PAIR : (j + 1) * PAIR] = arr_ref[
+                :, j * halves + part
+            ].reshape(share, PAIR)
     pick = (iota((8, 128), 0) == iota((8, 128), 1)).astype(F32).astype(BF)
-    codes = dot(pick, arr[:, model:], NT)
+    lines = dot(pick, arr_ref[:, arr_ref.shape[1] - 1].reshape(share, PAIR), NT)
+    codes = [
+        jnp.concatenate([lines[2 * p + i : 2 * p + i + 1] for p in range(halves)], axis=1)
+        for i in range(2)
+    ]
     cell = iota((cells, slots), 0)
     shift = wide.bit_length() - 1
-    row_gap = (cell >> shift).astype(F32) - (codes[0:1] - 1.0)
-    col_gap = (cell & (wide - 1)).astype(F32) - (codes[1:2] - 1.0)
+    row_gap = (cell >> shift).astype(F32) - (codes[0] - 1.0)
+    col_gap = (cell & (wide - 1)).astype(F32) - (codes[1] - 1.0)
     near = -(row_gap * row_gap + col_gap * col_gap) * (1.0 / SPREAD)
-    bias[...] = jnp.where(codes[0:1] > 0.5, near, LOW_SCORE)
+    bias[...] = jnp.where(codes[0] > 0.5, near, LOW_SCORE)
     for i, cols in enumerate(parts):
         copies[i].wait()
         if i == 0:
             late = fetch(
                 [q_hbm, own_hbm, wo_hbm, grid_hbm], [q_ref, own_ref, wo, grid_ref], lates
             )
-        pairs_ref[:, cols] = dot(arr[:, :model], wp[:, cols]).astype(BF)
+        pairs_ref[:, cols] = dot(arr[...], wp[:, cols]).astype(BF)
     leaving = fetch([pairs_ref], [pairs_hbm], out_sems.at[pl.ds(0, 1)])
     late[0].wait()
     late[1].wait()
@@ -421,8 +440,9 @@
 def near_kernel(
     q_ref, west_ref, east_ref, base_ref, inside_ref, state_ref, cot_ref, dh_ref, gain_ref,
     mix_in_ref, peak_ref, sum_ref, wn_hbm, wo_hbm, wu_hbm,
-    after_ref, hid_ref, dwest_ref, deast_ref, dq_ref, mix, dscaled_ref, dafter_ref,
-    wkv, wo, wu, kv, dkv, x, wts, scores, ds, bias, share, nrm, du, acc, dab, dmix, sems,
+    after_hbm, hid_hbm, dwest_ref, deast_ref, dq_ref, mix, dscaled_ref, dafter_ref,
+    wkv, wo, wu, kv, dkv, x, wts, scores, ds, bias, share, nrm, du, acc, dab, dmix,
+    after_ref, hid_ref, sems, out_sems,
 ):
     cells, model = state_ref.shape
     keys_all = kv.shape[0]
@@ -497,6 +517,7 @@
         du[:, cols] = (dh_ref[:, cols].astype(F32) * slope).astype(BF)
 
     tiles_of(du.shape[1], feed, FEED_TILE)
+    leaving = fetch([after_ref, hid_ref], [after_hbm, hid_hbm], out_sems)
 
     def feed_back(j):
         acc[:, pl.ds(j, TILE)] = dot(du[...], wu[pl.ds(j, TILE), :], NT)
@@ -530,6 +551,8 @@
         deast_ref[:, pl.ds(j, TILE)] = both[side:]
 
     tiles_of(model, rim_back)
+    for copy in leaving:
+        copy.wait()
 
 
 def middle_back_kernel(
@@ -674,7 +697,11 @@
     for i in range(2):
         cols = pl.ds(i * half, half)
         grads = dot(dpairs[...], wp[cols, :], NT).astype(BF)
-        slot_ref[:, :, cols] = grads.reshape(slot_ref.shape[:2] + (half,))
+        for part in range(slot_ref.shape[1] // 2):
+            count = 2 * slot_ref.shape[0]
+            slot_ref[:, 2 * part : 2 * part + 2, cols] = grads[
+                part * count : (part + 1) * count
+            ].reshape(slot_ref.shape[0], 2, half)
         leaving += fetch(
             [slot_ref.at[:, :, cols]], [slot_hbm.at[:, :, cols]], out_sems.at[pl.ds(3 + i, 1)]
         )
@@ -684,7 +711,11 @@
 
 def gather_kernel(place_hbm, ret_ref, out_ref, place_ref, ret, sems):
     copies = fetch([place_hbm], [place_ref], sems)
-    ret[...] = ret_ref[...].reshape(ret.shape)
+    count = 2 * ret_ref.shape[0]
+    for part in range(ret_ref.shape[1] // 2):
+        ret[part * count : (part + 1) * count] = ret_ref[:, 2 * part : 2 * part + 2].reshape(
+            count, ret.shape[1]
+        )
     copies[0].wait()
     out_ref[...] = dot(place_ref[...], ret[...], TN).astype(BF)
 
@@ -809,12 +840,13 @@
     flat = grid_state.reshape(cells, model)
     cot = cotangent.reshape(cells, model)
 
+    sent = (devices, cap // 2 * (model // PAIR) + 1, 2, PAIR)
     payload, placing = call(
         functools.partial(place_kernel, devices=devices, cap=cap, wide=rows_lon),
         (obs_tile.reshape(1, rows_obs), obs_cell.reshape(1, rows_obs), observations), "hhh",
-        [((devices, cap, model + 128), BF, "h"), ((slots, rows_obs), BF, "h")],
+        [(sent, BF, "h"), ((slots, rows_obs), BF, "h")],
         [vm((1, rows_obs), jnp.int32), vm((1, rows_obs), jnp.int32), vm((rows_obs, model), BF),
-         vm((devices, cap, model + 128), BF), vm((slots, rows_obs), BF), dma((3,))],
+         vm(sent, BF), vm((slots, rows_obs), BF), dma((3,))],
         2 * rows_obs * slots * model, "place",
     )
     arrived = lax.all_to_all(payload, ("lat", "lon"), 0, 0, tiled=True)
@@ -834,7 +866,7 @@
         [((cells, model), F32, "h"), ((rim, model), BF), ((rim, model), BF),
          ((slots, 2 * model), BF, "h"), ((pairs_n, 2 * cells, slots), BF, "h"),
          ((cells, model), BF, "h"), ((cells, model), BF, "h")],
-        [vm((slots, model + 128), BF), vm((model, 2 * model), BF), vm((model, model), BF),
+        [vm((slots, model), BF), vm((model, 2 * model), BF), vm((model, model), BF),
          vm((GROUP, 2 * cells, slots), F32), vm((cells, slots), F32), vm((cells, model), BF),
          vm((cells, model), BF), vm((cells, 2 * model), BF), vm((cells, model), F32),
          vm((slots, 2 * model), BF), vm((pairs_n, 2 * cells, slots), BF), vm((cells, model), BF),
@@ -875,15 +907,16 @@
         (q_n, west, east, jnp.asarray(base[:, 2 * cells :]), inside[:, 2 * cells :], state, cot,
          dhid, norm_gains, inner_mix, inner_peak, inner_sum, w_near_proj, w_near_out, w_up),
         "vvvvvvvvvvvvaaa",
-        [((cells, model), F32), ((cells, ff), BF), ((side, model), BF), ((side, model), BF),
-         ((cells, model), F32), ((cells, model), BF), ((cells, model), BF),
+        [((cells, model), F32, "h"), ((cells, ff), BF, "h"), ((side, model), BF),
+         ((side, model), BF), ((cells, model), F32), ((cells, model), BF), ((cells, model), BF),
          ((cells, model), F32)],
         [vm((model, 2 * model), BF), vm((model, model), BF), vm((model, ff), BF),
          vm((outer, 2 * model), BF), vm((outer, 2 * model), BF), vm((2 * side, model), BF),
          vm((pairs_n, 2 * cells, outer), BF), vm((GROUP, 2 * cells, outer), F32),
          vm((GROUP, 2 * cells, outer), BF), vm((cells, outer), F32), vm((cells, model), F32),
          vm((cells, model), BF), vm((cells, ff), BF), vm((cells, model), F32),
-         vm((cells, model), BF), vm((cells, model), BF), dma((3,))],
+         vm((cells, model), BF), vm((cells, model), BF), vm((cells, model), F32),
+         vm((cells, ff), BF), dma((3,)), dma((2,))],
         2e10, "near",
     )
     from_east = ring(dwest, -1)

time: 152 us -> 152 us (level)
  no operation moved by 1% of the time
where the time goes in v8:
time: 152 us; the launch traced here: 151 us
  Pallas kernels  83.7 us (55%)
  starting transfers between devices  40.5 us (27%)
  waiting for transfers between devices  25.6 us (17%)
    pallas_call x14, Pallas kernels, call(): pl.pallas_call(body, name=name, out_shape=shapes[0] if single else shapes...  83.7 us
    all_to_all x1, starting transfers between devices, per_device(): returned = lax.all_to_all(slot_grads, ('lat', 'lon'), 0, 0, tiled=True)  12.8 us
    all_to_all x1, waiting for transfers between devices, per_device(): arrived = lax.all_to_all(payload, ('lat', 'lon'), 0, 0, tiled=True)  12.8 us
    all_to_all x1, starting transfers between devices, per_device(): arrived = lax.all_to_all(payload, ('lat', 'lon'), 0, 0, tiled=True)  11.5 us
    ppermute x4, starting transfers between devices, line(): return lax.ppermute(value, 'lat', pairs)  10.9 us
    all_to_all x1, waiting for transfers between devices, per_device(): returned = lax.all_to_all(slot_grads, ('lat', 'lon'), 0, 0, tiled=True)  6.68 us
    ppermute x4, starting transfers between devices, ring(): lax.ppermute(value, 'lon', [(i, (i + by) % size) for i in range(size)])  5.26 us
    ppermute x4, waiting for transfers between devices, ring(): lax.ppermute(value, 'lon', [(i, (i + by) % size) for i in range(size)])  4.79 us
  transfers between devices with their start and end apart: 10, of which 5 were waited for; matrix products, arithmetic and copies ran while one was open for 0% of the time, Pallas kernels for 26%

profile of v8, /device:TPU:1, one launch (start us, length us, event | category | flops | bytes accessed | tf_op | source)
XLA Modules:
  0.0 151.2 jit_solution(18425346757670938611)
XLA Ops:
  0.6 0.0 copy-start.12
  0.6 3.1 %place.1 = (bf16[128,17,2,128]{3,2,1,0:T(2,128)(2,1)}, bf16[512,256]{1,0:T(8,128)(2,1)}) custom-call(s32[1,256]{1,0:T(1,128)} %bitcast.17, s32[1,256]{1,0:T(1,128)} %bitcast.18, bf16[256,1024]{1,0:T(8,128)(2,1)} %obs_hbm.1), custom_call_target="tpu_custom_call" | custom-call | flops 268435456 | bytes 1902592 | tf_op jit(solution)/shard_map/place/pallas_call | solution.py:120
  3.7 11.5 %all-to-all-start = ((bf16[128,17,2,128]{3,2,1,0:T(2,128)(2,1)}), bf16[128,17,2,128]{3,2,1,0:T(2,128)(2,1)S(1)}, u32[]{:S(2)}, u32[]{:S(2)}) async-start(bf16[128,17,2,128]{3,2,1,0:T(2,128)(2,1)} %get-tuple-element.41), calls=%async_computation | async-start | bytes 2228224 | tf_op jit(solution)/shard_map/all_to_all | solution.py:852
  15.3 0.0 copy-done.12
  15.3 6.8 %grid_proj.1 = (bf16[192,1024]{1,0:T(8,128)(2,1)}, bf16[192,2048]{1,0:T(8,128)(2,1)}, bf16[192,2048]{1,0:T(8,128)(2,1)}) custom-call(bf16[192,1024]{1,0:T(8,128)(2,1)} %bitcast.12, bf16[192,1024]{1,0:T(8,128)(2,1)} %bitcast.10, f32[3,1024]{1,0:T(4,128)S(1)} %copy-done.12, bf16[1024,1024]{1,0:T(8,128)(2,1)} %wq_hbm.3, bf16[1024,2048]{1,0:T(8,128)(2,1)} %wp_hbm.7, ...), custom_call_target="tpu_custom_call" | custom-call | flops 2013265920 | bytes 13250560 | tf_op jit(solution)/shard_map/grid_proj/pallas_call | solution.py:120
  22.1 12.8 %all-to-all-done.arr_ref = bf16[128,17,2,128]{3,2,1,0:T(2,128)(2,1)S(1)} async-done(((bf16[128,17,2,128]{3,2,1,0:T(2,128)(2,1)}), bf16[128,17,2,128]{3,2,1,0:T(2,128)(2,1)S(1)}, u32[]{:S(2)}, u32[]{:S(2)}) %all-to-all-start) | async-done | bytes 1114144 | tf_op jit(solution)/shard_map/all_to_all | solution.py:852
  34.9 11.2 %cross.1 = (f32[192,1024]{1,0:T(8,128)}, bf16[96,1024]{1,0:T(8,128)(2,1)S(1)}, bf16[96,1024]{1,0:T(8,128)(2,1)S(1)}, bf16[512,2048]{1,0:T(8,128)(2,1)}, bf16[8,3...) custom-call(bf16[128,17,2,128]{3,2,1,0:T(2,128)(2,1)S(1)} %all-to-all-done.arr_ref, ...), custom_call_target="tpu_custom_call" | custom-call | flops 4294967296 | bytes 16199680 | tf_op jit(solution)/shard_map/cross/pallas_call | solution.py:120
  46.1 1.3 collective-permute-start.1
  47.4 4.0 %collective-permute-start = (bf16[96,1024]{1,0:T(8,128)(2,1)S(1)}, bf16[96,1024]{1,0:T(8,128)(2,1)S(1)}, u32[]{:S(2)}, u32[]{:S(2)}) collective-permute-start(bf16[96,1024]{1,0:T(8,128)(2,1)S(1)} %get-tuple-element.45.bottom_ref), channel_id=1, source_target_pairs={{0,16},{16,32},{32,48},{48,64},{64,80},{80,96},{96,112},{1,17},{17... | collective-permute-start | bytes 589832 | tf_op jit(solution)/shard_map/ppermute | solution.py:785
  51.4 0.0 copy-done.19
  51.5 0.0 slice-done
  51.5 0.0 slice-done.1
  51.5 0.0 copy-start.8
  51.5 0.0 copy-start.11
  51.5 2.7 %near_own.1 = (bf16[192,1024]{1,0:T(8,128)(2,1)S(1)}, bf16[192,2048]{1,0:T(8,128)(2,1)S(1)}) custom-call(bf16[96,1024]{1,0:T(8,128)(2,1)S(1)} %get-tuple-element.44.top_ref, bf16[96,1024]{1,0:T(8,128)(2,1)S(1)} %get-tuple-element.45.bottom_ref, bf16[1024,3072]{1,0:T(8,128)(2,1)S(1)} %bitcast.7), custom_call_target="tpu_custom_call" | custom-call | flops 1207959552 | bytes 7864320 | tf_op jit(solution)/shard_map/near_own/pallas_call | solution.py:120
  54.2 0.4 collective-permute-done.1.south_ref
  54.6 1.0 collective-permute-done.north_ref
  55.6 0.0 copy-done.8
  55.6 0.5 rim.1
  56.0 1.9 %collective-permute-start.2 = (bf16[144,1024]{1,0:T(8,128)(2,1)S(1)}, bf16[144,1024]{1,0:T(8,128)(2,1)S(1)}, u32[]{:S(2)}, u32[]{:S(2)}) collective-permute-start(bf16[144,1024]{1,0:T(8,128)(2,1)S(1)} %get-tuple-element.48), channel_id=1, source_target_pairs={{0,1},{1,2},{2,3},{3,4},{4,5},{5,6},{6,7},{7,8},{8,9},{9,10},{10,1... | collective-permute-start | bytes 884744 | tf_op jit(solution)/shard_map/ppermute | solution.py:779
  58.0 0.0 collective-permute-start.3
  58.0 0.0 copy-done.11
  58.0 0.0 copy-start.5
  58.0 0.0 copy-start.13
  58.0 0.0 copy-start.15
  58.0 0.0 copy-start.16
  58.0 0.0 copy-start.18
  58.0 5.9 %inner.1 = (bf16[192,2048]{1,0:T(8,128)(2,1)S(1)}, bf16[8,384,384]{2,1,0:T(8,128)(2,1)}, f32[192,1024]{1,0:T(8,128)S(1)}, f32[8,384,128]{2,1,0:T(8,128)S(1)}, f32[8,384,128]{2,1,0:T(8,128)S(1)}) custom-call(bf16[96,1024]{1,0:T(8,128)(2,1)S(1)} %collective-permute-done.north_ref, bf16[96,1024]{1,0:T(8,128)(2,1)S(1)} %collective-permute-done.1.south_ref, ...), custom_call_target="tpu_custom_call" | custom-call | flops 1610612736 | bytes 15101952 | tf_op jit(solution)/shard_map/inner/pallas_call | solution.py:120
  64.0 0.0 collective-permute-done.2.west_ref
  64.0 4.8 %collective-permute-done.3.east_ref = bf16[144,1024]{1,0:T(8,128)(2,1)S(1)} collective-permute-done((bf16[144,1024]{1,0:T(8,128)(2,1)S(1)}, bf16[144,1024]{1,0:T(8,128)(2,1)S(1)}, u32[]{:S(2)}, u32[]{:S(2)}) %collective-permute-start.3) | collective-permute-done | bytes 294944 | tf_op jit(solution)/shard_map/ppermute | solution.py:779
  68.8 0.0 copy-done.5
  68.8 0.0 copy-done.13
  68.8 0.0 copy-done.15
  68.8 0.0 copy-done.16
  68.8 0.0 slice-start.3
  68.8 18.1 %near.1 = (f32[192,1024]{1,0:T(8,128)}, bf16[192,2048]{1,0:T(8,128)(2,1)}, bf16[144,1024]{1,0:T(8,128)(2,1)S(1)}, bf16[144,1024]{1,0:T(8,128)(2,1)S(1)}, f32[192...) custom-call(bf16[192,1024]{1,0:T(8,128)(2,1)S(1)} %get-tuple-element., ...), custom_call_target="tpu_custom_call" | custom-call | flops 20000000000 | bytes 24158208 | tf_op jit(solution)/shard_map/near/pallas_call | solution.py:120
  86.9 0.1 collective-permute-start.4
  87.0 3.2 %collective-permute-start.5 = (bf16[144,1024]{1,0:T(8,128)(2,1)S(1)}, bf16[144,1024]{1,0:T(8,128)(2,1)S(1)}, u32[]{:S(2)}, u32[]{:S(2)}) collective-permute-start(bf16[144,1024]{1,0:T(8,128)(2,1)S(1)} %get-tuple-element.65), channel_id=1, source_target_pairs={{0,1},{1,2},{2,3},{3,4},{4,5},{5,6},{6,7},{7,8},{8,9},{9,10},{10,1... | collective-permute-start | bytes 884744 | tf_op jit(solution)/shard_map/ppermute | solution.py:779
  90.3 0.0 copy-start.10
  90.3 5.7 %middle_back.1 = (f32[192,1024]{1,0:T(8,128)S(1)}, bf16[64,2048]{1,0:T(8,128)(2,1)S(1)}, f32[192,1024]{1,0:T(8,128)S(1)}) custom-call(bf16[192,1024]{1,0:T(8,128)(2,1)S(1)} %get-tuple-element.46.q_ref, bf16[192,2048]{1,0:T(8,128)(2,1)S(1)} %get-tuple-element.47._.kvo_ref, bf16[192,2048]{1,0:T(8,128)(2,1)S(1)} %get-tuple-element.59.kvr_ref, ...), custom_call_target="tpu_custom_call" | custom-call | flops 1610612736 | bytes 14024704 | tf_op jit(solution)/shard_map/middle_back/pallas_call | solution.py:120
  96.0 0.0 collective-permute-done.4.from_east_ref
  96.0 0.0 collective-permute-done.5.from_west_ref
  96.0 0.4 fold.1
  96.4 4.1 %collective-permute-start.6 = (bf16[96,1024]{1,0:T(8,128)(2,1)S(1)}, bf16[96,1024]{1,0:T(8,128)(2,1)S(1)}, u32[]{:S(2)}, u32[]{:S(2)}) collective-permute-start(bf16[96,1024]{1,0:T(8,128)(2,1)S(1)} %get-tuple-element.68), channel_id=1, source_target_pairs={{0,16},{16,32},{32,48},{48,64},{64,80},{80,96},{96,112},{1,17},{17... | collective-permute-start | bytes 589832 | tf_op jit(solution)/shard_map/ppermute | solution.py:785
  100.5 1.5 %collective-permute-start.7 = (bf16[96,1024]{1,0:T(8,128)(2,1)S(1)}, bf16[96,1024]{1,0:T(8,128)(2,1)S(1)}, u32[]{:S(2)}, u32[]{:S(2)}) collective-permute-start(bf16[96,1024]{1,0:T(8,128)(2,1)S(1)} %get-tuple-element.67._), channel_id=1, source_target_pairs={{16,0},{32,16},{48,32},{64,48},{80,64},{96,80},{112,96},{17,1},{33... | collective-permute-start | bytes 589832 | tf_op jit(solution)/shard_map/ppermute | solution.py:785
  102.1 0.0 copy-start
  102.1 0.0 copy-start.6
  102.1 0.0 copy-start.7
  102.1 0.0 copy-start.14
  102.1 6.3 %own_back.1.dn_ref = f32[192,1024]{1,0:T(8,128)S(1)} custom-call(bf16[192,1024]{1,0:T(8,128)(2,1)S(1)} %get-tuple-element.46.q_ref, bf16[192,2048]{1,0:T(8,128)(2,1)S(1)} %get-tuple-element.47._.kvo_ref, bf16[192,1024]{1,0:T(8,128)(2,1)S(1)} %get-tuple-element.57.mix, bf16[192,1024]{1,0:T(8,128)(2,1)S(1)} %get-tuple-element.58.dmix, ...), custom_call_target="tpu_custom_call" | custom-call | flops 1610612736 | bytes 13348864 | tf_op jit(solution)/shard_map/own_back/pallas_call | solution.py:120
  108.4 0.0 collective-permute-done.6.north_ref
  108.4 0.0 collective-permute-done.7.south_ref
  108.5 8.5 %cross_back.1 = (f32[192,1024]{1,0:T(8,128)}, bf16[128,4,1024]{2,1,0:T(4,128)(2,1)}, bf16[192,1024]{1,0:T(8,128)(2,1)}, bf16[8,384,512]{2,1,0:T(8,128)(2,1)}) custom-call(f32[192,1024]{1,0:T(8,128)S(1)} %own_back.1.dn_ref, bf16[96,1024]{1,0:T(8,128)(2,1)S(1)} %collective-permute-done.6.north_ref, bf16[96,1024]{1,0:T(8,128)(2,1)S(1)} %collective-permute-done.7.south_ref, ...), custom_call_target="tpu_custom_call" | custom-call | flops 4294967296 | bytes 20459520 | tf_op jit(solution)/shard_map/cross_back/pallas_call | solution.py:120
  117.1 0.0 copy-start.2
  117.1 0.0 copy-start.3
  117.1 0.0 copy-start.4
  117.1 12.8 %all-to-all-start.1 = ((bf16[128,4,1024]{2,1,0:T(4,128)(2,1)}), bf16[128,4,1024]{2,1,0:T(4,128)(2,1)S(1)}, u32[]{:S(2)}, u32[]{:S(2)}) async-start(bf16[128,4,1024]{2,1,0:T(4,128)(2,1)} %get-tuple-element.78), calls=%async_computation.1 | async-start | bytes 2097152 | tf_op jit(solution)/shard_map/all_to_all | solution.py:965
  129.9 0.0 copy-done.2
  129.9 0.0 copy-done.3
  129.9 0.0 copy-done.4
  129.9 3.9 %encode.1 = bf16[192,1024]{1,0:T(8,128)(2,1)} custom-call(f32[192,1024]{1,0:T(8,128)S(1)} %copy-done.3, bf16[192,2048]{1,0:T(8,128)(2,1)S(1)} %copy-done.4, bf16[2048,1024]{1,0:T(8,128)(2,1)} %wd_hbm.3, bf16[192,1024]{1,0:T(8,128)(2,1)S(1)} %copy-done.2), custom_call_target="tpu_custom_call" | custom-call | flops 805306368 | bytes 6553600 | tf_op jit(solution)/shard_map/encode/pallas_call | solution.py:120
  133.9 8.3 %grid_back.1 = bf16[192,1024]{1,0:T(8,128)(2,1)} custom-call(bf16[192,1024]{1,0:T(8,128)(2,1)} %bitcast.14, f32[192,1024]{1,0:T(8,128)} %get-tuple-element.74.dstate_hbm, f32[3,1024]{1,0:T(4,128)S(1)} %copy-done.12, bf16[192,1024]{1,0:T(8,128)(2,1)} %get-tuple-element.42.q_hbm.q_ref, bf16[192,2048]{1,0:T(8,128)(2,1)} %get-tuple-element.43.own_hbm, ...), custom_call_target="tpu_custom_call" | custom-call | flops 1207959552 | bytes 15478784 | tf_op jit(solution)/shard_map/grid_back/pallas_call | solution.py:120
  142.2 6.7 %all-to-all-done.1.ret_ref = bf16[128,4,1024]{2,1,0:T(4,128)(2,1)S(1)} async-done(((bf16[128,4,1024]{2,1,0:T(4,128)(2,1)}), bf16[128,4,1024]{2,1,0:T(4,128)(2,1)S(1)}, u32[]{:S(2)}, u32[]{:S(2)}) %all-to-all-start.1) | async-done | bytes 1048608 | tf_op jit(solution)/shard_map/all_to_all | solution.py:965
  148.8 2.2 %gather.1 = bf16[256,1024]{1,0:T(8,128)(2,1)} custom-call(bf16[512,256]{1,0:T(8,128)(2,1)} %get-tuple-element.77.place_hbm, bf16[128,4,1024]{2,1,0:T(4,128)(2,1)S(1)} %all-to-all-done.1.ret_ref), custom_call_target="tpu_custom_call" | custom-call | flops 268435456 | bytes 1835008 | tf_op jit(solution)/shard_map/gather/pallas_call | solution.py:120
  (22 shorter events, 0.0 us)
Async XLA Ops:
  0.6 14.6 %copy-start.12 = (f32[3,1024]{1,0:T(4,128)S(1)}, f32[3,1024]{1,0:T(4,128)}, u32[]{:S(2)}) copy-start(f32[3,1024]{1,0:T(4,128)} %gain_ref.9) | copy-start | bytes 36868
  3.7 31.1 %all-to-all-start = ((bf16[128,17,2,128]{3,2,1,0:T(2,128)(2,1)}), bf16[128,17,2,128]{3,2,1,0:T(2,128)(2,1)S(1)}, u32[]{:S(2)}, u32[]{:S(2)}) async-start(bf16[128,17,2,128]{3,2,1,0:T(2,128)(2,1)} %get-tuple-element.41), calls=%async_computation | async-start | bytes 2228224 | tf_op jit(solution)/shard_map/all_to_all | solution.py:852
  34.9 16.6 %slice-start = ((s8[6291456]{0:T(1024)(128)(4,1)}), s8[4194304]{0:T(1024)(128)(4,1)S(1)}, s32[]{:S(2)}) async-start(s8[6291456]{0:T(1024)(128)(4,1)} %bitcast.6), calls=%async_computation.2 | async-start | bytes 8388608
  34.9 16.6 %copy-start.19 = (s32[8,768]{1,0:T(8,128)S(1)}, s32[8,768]{1,0:T(8,128)}, u32[]{:S(2)}) copy-start(s32[8,768]{1,0:T(8,128)} %constant.28.clone) | copy-start | bytes 73732
  34.9 16.6 %slice-start.1 = ((s8[6291456]{0:T(1024)(128)(4,1)}), s8[2097152]{0:T(1024)(128)(4,1)S(1)}, s32[]{:S(2)}) async-start(s8[6291456]{0:T(1024)(128)(4,1)} %bitcast.6), calls=%async_computation.3 | async-start | bytes 4194304
  46.1 8.5 %collective-permute-start.1 = (bf16[96,1024]{1,0:T(8,128)(2,1)S(1)}, bf16[96,1024]{1,0:T(8,128)(2,1)S(1)}, u32[]{:S(2)}, u32[]{:S(2)}) collective-permute-start(bf16[96,1024]{1,0:T(8,128)(2,1)S(1)} %get-tuple-element.44.top_ref), channel_id=1, source_target_pairs={{16,0},{32,16},{48,32},{64,48},{80,64},{96,80},{112,96},{17,1},{33... | collective-permute-start | bytes 589832 | tf_op jit(solution)/shard_map/ppermute | solution.py:785
  47.4 8.1 %collective-permute-start = (bf16[96,1024]{1,0:T(8,128)(2,1)S(1)}, bf16[96,1024]{1,0:T(8,128)(2,1)S(1)}, u32[]{:S(2)}, u32[]{:S(2)}) collective-permute-start(bf16[96,1024]{1,0:T(8,128)(2,1)S(1)} %get-tuple-element.45.bottom_ref), channel_id=1, source_target_pairs={{0,16},{16,32},{32,48},{48,64},{64,80},{80,96},{96,112},{1,17},{17... | collective-permute-start | bytes 589832 | tf_op jit(solution)/shard_map/ppermute | solution.py:785
  51.5 4.1 %copy-start.8 = (bf16[288,384]{1,0:T(8,128)(2,1)S(1)}, bf16[288,384]{1,0:T(8,128)(2,1)}, u32[]{:S(2)}) copy-start(bf16[288,384]{1,0:T(8,128)(2,1)} %constant.29.clone.sel_ref) | copy-start | bytes 663556
  51.5 6.5 %copy-start.11 = (bf16[192,384]{1,0:T(8,128)(2,1)S(1)}, bf16[192,384]{1,0:T(8,128)(2,1)}, u32[]{:S(2)}) copy-start(bf16[192,384]{1,0:T(8,128)(2,1)} %constant.30.clone.base_ref) | copy-start | bytes 442372
  56.0 8.0 %collective-permute-start.2 = (bf16[144,1024]{1,0:T(8,128)(2,1)S(1)}, bf16[144,1024]{1,0:T(8,128)(2,1)S(1)}, u32[]{:S(2)}, u32[]{:S(2)}) collective-permute-start(bf16[144,1024]{1,0:T(8,128)(2,1)S(1)} %get-tuple-element.48), channel_id=1, source_target_pairs={{0,1},{1,2},{2,3},{3,4},{4,5},{5,6},{6,7},{7,8},{8,9},{9,10},{10,1... | collective-permute-start | bytes 884744 | tf_op jit(solution)/shard_map/ppermute | solution.py:779
  58.0 10.8 %collective-permute-start.3 = (bf16[144,1024]{1,0:T(8,128)(2,1)S(1)}, bf16[144,1024]{1,0:T(8,128)(2,1)S(1)}, u32[]{:S(2)}, u32[]{:S(2)}) collective-permute-start(bf16[144,1024]{1,0:T(8,128)(2,1)S(1)} %get-tuple-element.49), channel_id=1, source_target_pairs={{0,15},{1,0},{2,1},{3,2},{4,3},{5,4},{6,5},{7,6},{8,7},{9,8},{10,9... | collective-permute-start | bytes 884744 | tf_op jit(solution)/shard_map/ppermute | solution.py:779
  58.0 10.8 %copy-start.5 = (bf16[12,16,1024]{2,1,0:T(8,128)(2,1)S(1)}, bf16[12,16,1024]{2,1,0:T(8,128)(2,1)}, u32[]{:S(2)}) copy-start(bf16[12,16,1024]{2,1,0:T(8,128)(2,1)} %param.23) | copy-start | bytes 1179652
  58.0 10.8 %copy-start.13 = (bf16[1024,1024]{1,0:T(8,128)(2,1)S(1)}, bf16[1024,1024]{1,0:T(8,128)(2,1)}, u32[]{:S(2)}) copy-start(bf16[1024,1024]{1,0:T(8,128)(2,1)} %wo_hbm.4) | copy-start | bytes 6291460
  58.0 10.8 %copy-start.15 = (bf16[192,2048]{1,0:T(8,128)(2,1)S(1)}, bf16[192,2048]{1,0:T(8,128)(2,1)}, u32[]{:S(2)}) copy-start(bf16[192,2048]{1,0:T(8,128)(2,1)} %get-tuple-element.51.dh_ref) | copy-start | bytes 2359300
  58.0 10.8 %copy-start.16 = (bf16[192,384]{1,0:T(8,128)(2,1)S(1)}, bf16[192,384]{1,0:T(8,128)(2,1)}, u32[]{:S(2)}) copy-start(bf16[192,384]{1,0:T(8,128)(2,1)} %constant.31.clone.base_ref) | copy-start | bytes 442372
  58.0 10.8 %copy-start.18 = (f32[192,1024]{1,0:T(8,128)S(1)}, f32[192,1024]{1,0:T(8,128)}, u32[]{:S(2)}) copy-start(f32[192,1024]{1,0:T(8,128)} %get-tuple-element.50.state_ref) | copy-start | bytes 2359300
  68.8 21.5 %slice-start.2 = ((s8[6291456]{0:T(1024)(128)(4,1)}), s8[4194304]{0:T(1024)(128)(4,1)S(1)}, s32[]{:S(2)}) async-start(s8[6291456]{0:T(1024)(128)(4,1)} %bitcast.8), calls=%async_computation.4 | async-start | bytes 8388608
  68.8 21.4 %slice-start.3 = ((s8[6291456]{0:T(1024)(128)(4,1)}), s8[2097152]{0:T(1024)(128)(4,1)S(1)}, s32[]{:S(2)}) async-start(s8[6291456]{0:T(1024)(128)(4,1)} %bitcast.8), calls=%async_computation.5 | async-start | bytes 4194304
  86.9 9.1 %collective-permute-start.4 = (bf16[144,1024]{1,0:T(8,128)(2,1)S(1)}, bf16[144,1024]{1,0:T(8,128)(2,1)S(1)}, u32[]{:S(2)}, u32[]{:S(2)}) collective-permute-start(bf16[144,1024]{1,0:T(8,128)(2,1)S(1)} %get-tuple-element.64), channel_id=1, source_target_pairs={{0,15},{1,0},{2,1},{3,2},{4,3},{5,4},{6,5},{7,6},{8,7},{9,8},{10,9... | collective-permute-start | bytes 884744 | tf_op jit(solution)/shard_map/ppermute | solution.py:779
  87.0 9.0 %collective-permute-start.5 = (bf16[144,1024]{1,0:T(8,128)(2,1)S(1)}, bf16[144,1024]{1,0:T(8,128)(2,1)S(1)}, u32[]{:S(2)}, u32[]{:S(2)}) collective-permute-start(bf16[144,1024]{1,0:T(8,128)(2,1)S(1)} %get-tuple-element.65), channel_id=1, source_target_pairs={{0,1},{1,2},{2,3},{3,4},{4,5},{5,6},{6,7},{7,8},{8,9},{9,10},{10,1... | collective-permute-start | bytes 884744 | tf_op jit(solution)/shard_map/ppermute | solution.py:779
  90.3 5.8 %copy-start.9 = (bf16[288,192]{1,0:T(8,128)(2,1)S(1)}, bf16[288,192]{1,0:T(8,128)(2,1)}, u32[]{:S(2)}) copy-start(bf16[288,192]{1,0:T(8,128)(2,1)} %constant.32.clone.sel_ref) | copy-start | bytes 331780
  90.3 11.8 %copy-start.10 = (bf16[288,192]{1,0:T(8,128)(2,1)S(1)}, bf16[288,192]{1,0:T(8,128)(2,1)}, u32[]{:S(2)}) copy-start(bf16[288,192]{1,0:T(8,128)(2,1)} %constant.33.clone.sel_ref) | copy-start | bytes 331780
  96.4 12.0 %collective-permute-start.6 = (bf16[96,1024]{1,0:T(8,128)(2,1)S(1)}, bf16[96,1024]{1,0:T(8,128)(2,1)S(1)}, u32[]{:S(2)}, u32[]{:S(2)}) collective-permute-start(bf16[96,1024]{1,0:T(8,128)(2,1)S(1)} %get-tuple-element.68), channel_id=1, source_target_pairs={{0,16},{16,32},{32,48},{48,64},{64,80},{80,96},{96,112},{1,17},{17... | collective-permute-start | bytes 589832 | tf_op jit(solution)/shard_map/ppermute | solution.py:785
  100.5 7.9 %collective-permute-start.7 = (bf16[96,1024]{1,0:T(8,128)(2,1)S(1)}, bf16[96,1024]{1,0:T(8,128)(2,1)S(1)}, u32[]{:S(2)}, u32[]{:S(2)}) collective-permute-start(bf16[96,1024]{1,0:T(8,128)(2,1)S(1)} %get-tuple-element.67._), channel_id=1, source_target_pairs={{16,0},{32,16},{48,32},{64,48},{80,64},{96,80},{112,96},{17,1},{33... | collective-permute-start | bytes 589832 | tf_op jit(solution)/shard_map/ppermute | solution.py:785
  102.1 6.4 %copy-start = (bf16[1024,2048]{1,0:T(8,128)(2,1)S(1)}, bf16[1024,2048]{1,0:T(8,128)(2,1)}, u32[]{:S(2)}) copy-start(bf16[1024,2048]{1,0:T(8,128)(2,1)} %wp_hbm.7) | copy-start | bytes 12582916
  102.1 6.4 %copy-start.1 = (bf16[512,2048]{1,0:T(8,128)(2,1)S(1)}, bf16[512,2048]{1,0:T(8,128)(2,1)}, u32[]{:S(2)}) copy-start(bf16[512,2048]{1,0:T(8,128)(2,1)} %get-tuple-element.70.pairs_ref.pairs_hbm) | copy-start | bytes 6291460
  102.1 6.4 %copy-start.6 = (bf16[192,1024]{1,0:T(8,128)(2,1)S(1)}, bf16[192,1024]{1,0:T(8,128)(2,1)}, u32[]{:S(2)}) copy-start(bf16[192,1024]{1,0:T(8,128)(2,1)} %get-tuple-element.42.q_hbm.q_ref) | copy-start | bytes 1179652
  102.1 6.4 %copy-start.7 = (bf16[192,1024]{1,0:T(8,128)(2,1)S(1)}, bf16[192,1024]{1,0:T(8,128)(2,1)}, u32[]{:S(2)}) copy-start(bf16[192,1024]{1,0:T(8,128)(2,1)} %get-tuple-element.72.mix_ref.mix_hbm) | copy-start | bytes 1179652
  102.1 6.4 %copy-start.14 = (bf16[1024,1024]{1,0:T(8,128)(2,1)S(1)}, bf16[1024,1024]{1,0:T(8,128)(2,1)}, u32[]{:S(2)}) copy-start(bf16[1024,1024]{1,0:T(8,128)(2,1)} %wo_hbm.5) | copy-start | bytes 6291460
  102.1 6.4 %copy-start.17 = (bf16[8,384,512]{2,1,0:T(8,128)(2,1)S(1)}, bf16[8,384,512]{2,1,0:T(8,128)(2,1)}, u32[]{:S(2)}) copy-start(bf16[8,384,512]{2,1,0:T(8,128)(2,1)} %get-tuple-element.71.wts_ref) | copy-start | bytes 9437188
  117.1 12.9 %copy-start.2 = (bf16[192,1024]{1,0:T(8,128)(2,1)S(1)}, bf16[192,1024]{1,0:T(8,128)(2,1)}, u32[]{:S(2)}) copy-start(bf16[192,1024]{1,0:T(8,128)(2,1)} %get-tuple-element.73._.dmix_hbm) | copy-start | bytes 1179652
  117.1 12.9 %copy-start.3 = (f32[192,1024]{1,0:T(8,128)S(1)}, f32[192,1024]{1,0:T(8,128)}, u32[]{:S(2)}) copy-start(f32[192,1024]{1,0:T(8,128)} %get-tuple-element.55.after_ref) | copy-start | bytes 2359300
  117.1 12.9 %copy-start.4 = (bf16[192,2048]{1,0:T(8,128)(2,1)S(1)}, bf16[192,2048]{1,0:T(8,128)(2,1)}, u32[]{:S(2)}) copy-start(bf16[192,2048]{1,0:T(8,128)(2,1)} %get-tuple-element.56.hid_ref) | copy-start | bytes 2359300
  117.1 31.7 %all-to-all-start.1 = ((bf16[128,4,1024]{2,1,0:T(4,128)(2,1)}), bf16[128,4,1024]{2,1,0:T(4,128)(2,1)S(1)}, u32[]{:S(2)}, u32[]{:S(2)}) async-start(bf16[128,4,1024]{2,1,0:T(4,128)(2,1)} %get-tuple-element.78), calls=%async_computation.1 | async-start | bytes 2097152 | tf_op jit(solution)/shard_map/all_to_all | solution.py:965
